TPU v7x, 32 devices: a whole 2x2x4 slice. The times are simulated.
32 devices in a mesh: batch: 16 (over z, y, core), mem: 2 (over x).
Axes of the slice: x: 2, y: 2, z: 4, core: 2. Of those that a mesh axis runs over, the one named last changes fastest.
Arguments:
- hidden: bfloat16 [16, 1024, 768], P('batch', 'mem'), may hold values from -6 to 6
- memory: bfloat16 [16, 2048, 768], P('batch', 'mem'), may hold values from -6 to 6
- decoder_lengths: int32 [16, 4], P('batch'), may hold values from 1 to 768, as said below
- memory_lengths: int32 [16, 4], P('batch'), may hold values from 1 to 1536, as said below
- distance_buckets: int32 [1024], replicated, may hold values from 0 to 31, as said below
- norm_gains: float32 [3, 768], replicated, may hold values from 0.5 to 1.5
- position_bias: float32 [32, 12], replicated, may hold values from -4 to 4
- self_weights: bfloat16 [3, 768, 768], P(None, 'batch', 'mem'), may hold values from -0.078125 to 0.078125
- self_output: bfloat16 [768, 768], P('batch', 'mem'), may hold values from -12 to 12
- cross_weights: bfloat16 [3, 768, 768], P(None, 'batch', 'mem'), may hold values from -0.078125 to 0.078125
- cross_output: bfloat16 [768, 768], P('batch', 'mem'), may hold values from -16 to 16
- expand_weights: bfloat16 [2, 768, 2048], P(None, 'batch', 'mem'), may hold values from -0.21875 to 0.21875
- contract_weight: bfloat16 [2048, 768], P('batch', 'mem'), may hold values from -0.125 to 0.125
- cotangent: bfloat16 [16, 1024, 768], P('batch', 'mem'), may hold values from -6 to 6
Outputs:
- output: bfloat16 [16, 1024, 768], P('batch', 'mem')
- hidden_grad: float32 [16, 1024, 768], P('batch', 'mem')
- memory_grad: float32 [16, 2048, 768], P('batch', 'mem')
- gains_grad: float32 [3, 768], replicated
- bias_grad: float32 [32, 12], replicated
- self_weights_grad: float32 [3, 768, 768], P(None, 'batch', 'mem')
- self_output_grad: float32 [768, 768], P('batch', 'mem')
- cross_weights_grad: float32 [3, 768, 768], P(None, 'batch', 'mem')
- cross_output_grad: float32 [768, 768], P('batch', 'mem')
- expand_grad: float32 [2, 768, 2048], P(None, 'batch', 'mem')
- contract_grad: float32 [2048, 768], P('batch', 'mem')
Inputs may be any that keep to these rules, and one draw needn't show every extreme that they name: `decoder_lengths`: in each group the 4 lengths sum to 1024; one of them, in a slot drawn from the seed, is 768. `memory_lengths`: in each group the 4 lengths sum to 2048; the slot of length 1536 is the slot of the group's longest decoder sequence. `distance_buckets`: Non-decreasing along the distance; 0 at distance 0, 31 from distance 768 - 1 on.
All inputs are finite; a program needn't handle non-finite values.
Results may differ from a plain program's by a relative error of at most 0.028.
Values may be sent and summed in bfloat16 or wider, within the bound.
No kernel may reach another device: no remote copies, remote signals or barrier semaphores. Data moves between devices by JAX's collectives and lax.ppermute only.
A program may use at most 128 MiB of HBM per device.

v0:
```python
import jax
import jax.numpy as jnp
from jax import lax
from jax.sharding import PartitionSpec as P

EPSILON = 1e-06
NEGATIVE = -1e30


def rms_norm(values, gain_row):
    return (
        values * lax.rsqrt(jnp.mean(values * values, axis=-1, keepdims=True) + EPSILON) * gain_row
    )


def activate(gate_part, up_part):
    return jax.nn.gelu(gate_part, approximate=True) * up_part


def segment_ids(lengths, first_row, count):
    boundary = jnp.cumsum(lengths)
    places = first_row + jnp.arange(count, dtype=jnp.int32)
    return jnp.sum((places[:, None] >= boundary[None, :]).astype(jnp.int32), axis=1)


def bucket_starts(distance_buckets, bucket_count):
    levels = jnp.arange(1, bucket_count, dtype=jnp.int32)
    return jnp.sum((distance_buckets[None, :] < levels[:, None]).astype(jnp.int32), axis=1)


def bucket_of(distance_index, starts):
    return jnp.sum((distance_index[None, :, :] >= starts[:, None, None]).astype(jnp.int32), axis=0)


def bucket_bias(table_row, bucket_index):
    bucket_range = jnp.arange(table_row.shape[0], dtype=jnp.int32)
    return jnp.sum(
        jnp.where(
            bucket_index[None, :, :] == bucket_range[:, None, None], table_row[:, None, None], 0.0
        ),
        axis=0,
    )


def bucket_sums(grad_scores, bucket_index, bucket_count):
    bucket_range = jnp.arange(bucket_count, dtype=jnp.int32)
    return jnp.sum(
        jnp.where(
            bucket_index[None, :, :] == bucket_range[:, None, None],
            grad_scores.astype(jnp.float32)[None, :, :],
            0.0,
        ),
        axis=(1, 2),
    )


def head_columns(matrix, head_index, head_width):
    return lax.dynamic_slice_in_dim(matrix, head_index * head_width, head_width, 1)


def join_heads(stacked):
    return stacked.transpose(1, 0, 2).reshape(stacked.shape[1], stacked.shape[0] * stacked.shape[2])


def masked_scores(queries, key_rows, bias_rows, allowed):
    scores = (
        jnp.einsum("qd,kd->qk", queries, key_rows, preferred_element_type=jnp.float32) + bias_rows
    )
    return jnp.where(allowed, scores, NEGATIVE)


def head_forward(queries, key_rows, value_rows, bias_rows, allowed):
    scores = masked_scores(queries, key_rows, bias_rows, allowed)
    row_max = jnp.max(scores, axis=1, keepdims=True)
    exponent = jnp.exp(scores - row_max)
    row_total = jnp.sum(exponent, axis=1, keepdims=True)
    attn_probs = (exponent / row_total).astype(jnp.bfloat16)
    result = jnp.einsum("qk,kd->qd", attn_probs, value_rows, preferred_element_type=jnp.float32)
    return (result, (row_max + jnp.log(row_total))[:, 0])


def head_backward(queries, key_rows, value_rows, grad_result, log_total, bias_rows, allowed):
    scores = masked_scores(queries, key_rows, bias_rows, allowed)
    attn_probs = jnp.exp(scores - log_total[:, None])
    value_grads = jnp.einsum(
        "qk,qd->kd",
        attn_probs.astype(jnp.bfloat16),
        grad_result,
        preferred_element_type=jnp.float32,
    )
    grad_probs = jnp.einsum(
        "qd,kd->qk", grad_result, value_rows, preferred_element_type=jnp.float32
    )
    inner_sum = jnp.sum(attn_probs * grad_probs, axis=1, keepdims=True)
    grad_scores = (attn_probs * (grad_probs - inner_sum)).astype(jnp.bfloat16)
    query_grads = jnp.einsum("qk,kd->qd", grad_scores, key_rows, preferred_element_type=jnp.float32)
    key_grads = jnp.einsum("qk,qd->kd", grad_scores, queries, preferred_element_type=jnp.float32)
    return (query_grads, key_grads, value_grads, grad_scores)


def shards(
    hidden,
    memory,
    decoder_lengths,
    memory_lengths,
    distance_buckets,
    norm_gains,
    position_bias,
    self_weights,
    self_output,
    cross_weights,
    cross_output,
    expand_weights,
    contract_weight,
    cotangent,
):
    mem_count = lax.axis_size("mem")
    mem_index = lax.axis_index("mem")
    row_count = hidden.shape[1]
    memory_count = memory.shape[1]
    model_width = hidden.shape[2]
    head_count = position_bias.shape[1]
    head_width = model_width // head_count
    bucket_count = position_bias.shape[0]
    key_count = row_count * mem_count
    memory_total = memory_count * mem_count
    first_row = mem_index * row_count
    head_range = jnp.arange(head_count)
    within = (
        lax.all_gather(self_weights, "mem", axis=2, tiled=True),
        lax.all_gather(self_output, "mem", axis=1, tiled=True),
        lax.all_gather(cross_weights, "mem", axis=2, tiled=True),
        lax.all_gather(cross_output, "mem", axis=1, tiled=True),
        lax.all_gather(expand_weights, "mem", axis=2, tiled=True),
        lax.all_gather(contract_weight, "mem", axis=1, tiled=True),
    )
    full_weights = (
        lax.all_gather(within[0], "batch", axis=1, tiled=True),
        lax.all_gather(within[1], "batch", axis=0, tiled=True),
        lax.all_gather(within[2], "batch", axis=1, tiled=True),
        lax.all_gather(within[3], "batch", axis=0, tiled=True),
        lax.all_gather(within[4], "batch", axis=1, tiled=True),
        lax.all_gather(within[5], "batch", axis=0, tiled=True),
    )
    self_full, self_out_full, cross_full, cross_out_full, expand_full, contract_full = full_weights
    decoder_sizes = decoder_lengths[0]
    memory_sizes = memory_lengths[0]
    query_seq = segment_ids(decoder_sizes, first_row, row_count)
    key_seq = segment_ids(decoder_sizes, 0, key_count)
    memory_seq = segment_ids(memory_sizes, 0, memory_total)
    query_place = first_row + jnp.arange(row_count, dtype=jnp.int32)
    key_place = jnp.arange(key_count, dtype=jnp.int32)
    self_allowed = (key_place[None, :] <= query_place[:, None]) & (
        key_seq[None, :] == query_seq[:, None]
    )
    cross_allowed = memory_seq[None, :] == query_seq[:, None]
    distance_index = jnp.clip(query_place[:, None] - key_place[None, :], 0, key_count - 1)
    bucket_index = bucket_of(distance_index, bucket_starts(distance_buckets, bucket_count))
    head_tables = position_bias.T
    tokens = hidden[0].astype(jnp.float32)
    normed_self, pull_self = jax.vjp(rms_norm, tokens, norm_gains[0])
    input_self = normed_self.astype(jnp.bfloat16)
    query_self = jnp.dot(input_self, self_full[0], preferred_element_type=jnp.float32).astype(
        jnp.bfloat16
    )
    key_self = jnp.dot(input_self, self_full[1], preferred_element_type=jnp.float32).astype(
        jnp.bfloat16
    )
    value_self = jnp.dot(input_self, self_full[2], preferred_element_type=jnp.float32).astype(
        jnp.bfloat16
    )
    self_pairs = lax.all_gather(jnp.stack([key_self, value_self]), "mem", axis=1, tiled=True)

    def self_forward(head_index):
        return head_forward(
            head_columns(query_self, head_index, head_width),
            head_columns(self_pairs[0], head_index, head_width),
            head_columns(self_pairs[1], head_index, head_width),
            bucket_bias(head_tables[head_index], bucket_index),
            self_allowed,
        )

    self_heads, self_totals = lax.map(self_forward, head_range)
    attn_self = join_heads(self_heads).astype(jnp.bfloat16)
    middle_one = tokens + jnp.dot(attn_self, self_out_full, preferred_element_type=jnp.float32)
    normed_cross, pull_cross = jax.vjp(rms_norm, middle_one, norm_gains[1])
    input_cross = normed_cross.astype(jnp.bfloat16)
    query_cross = jnp.dot(input_cross, cross_full[0], preferred_element_type=jnp.float32).astype(
        jnp.bfloat16
    )
    memory_local = memory[0]
    key_memory = jnp.dot(memory_local, cross_full[1], preferred_element_type=jnp.float32).astype(
        jnp.bfloat16
    )
    value_memory = jnp.dot(memory_local, cross_full[2], preferred_element_type=jnp.float32).astype(
        jnp.bfloat16
    )
    memory_pairs = lax.all_gather(jnp.stack([key_memory, value_memory]), "mem", axis=1, tiled=True)

    def cross_forward(head_index):
        return head_forward(
            head_columns(query_cross, head_index, head_width),
            head_columns(memory_pairs[0], head_index, head_width),
            head_columns(memory_pairs[1], head_index, head_width),
            0.0,
            cross_allowed,
        )

    cross_heads, cross_totals = lax.map(cross_forward, head_range)
    attn_cross = join_heads(cross_heads).astype(jnp.bfloat16)
    middle_two = middle_one + jnp.dot(
        attn_cross, cross_out_full, preferred_element_type=jnp.float32
    )
    normed_feed, pull_feed = jax.vjp(rms_norm, middle_two, norm_gains[2])
    input_feed = normed_feed.astype(jnp.bfloat16)
    gate_part = jnp.dot(input_feed, expand_full[0], preferred_element_type=jnp.float32)
    up_part = jnp.dot(input_feed, expand_full[1], preferred_element_type=jnp.float32)
    activated, pull_activate = jax.vjp(activate, gate_part, up_part)
    hidden_act = activated.astype(jnp.bfloat16)
    result_rows = middle_two + jnp.dot(
        hidden_act, contract_full, preferred_element_type=jnp.float32
    )
    grad_branch_three = cotangent[0]
    grad_out = grad_branch_three.astype(jnp.float32)
    grad_contract = jnp.einsum(
        "rf,rd->fd", hidden_act, grad_branch_three, preferred_element_type=jnp.float32
    )
    grad_activated = jnp.einsum(
        "rd,fd->rf", grad_branch_three, contract_full, preferred_element_type=jnp.float32
    )
    grad_gate, grad_up = pull_activate(grad_activated)
    gate_rounded = grad_gate.astype(jnp.bfloat16)
    up_rounded = grad_up.astype(jnp.bfloat16)
    grad_expand = jnp.stack(
        [
            jnp.einsum("rd,rf->df", input_feed, gate_rounded, preferred_element_type=jnp.float32),
            jnp.einsum("rd,rf->df", input_feed, up_rounded, preferred_element_type=jnp.float32),
        ]
    )
    grad_input_feed = jnp.einsum(
        "rf,df->rd", gate_rounded, expand_full[0], preferred_element_type=jnp.float32
    ) + jnp.einsum("rf,df->rd", up_rounded, expand_full[1], preferred_element_type=jnp.float32)
    grad_norm_two, gain_grad_three = pull_feed(grad_input_feed)
    grad_middle_two = grad_out + grad_norm_two
    grad_branch_two = grad_middle_two.astype(jnp.bfloat16)
    grad_cross_out = jnp.einsum(
        "rd,re->de", attn_cross, grad_branch_two, preferred_element_type=jnp.float32
    )
    grad_attn_cross = jnp.einsum(
        "re,de->rd", grad_branch_two, cross_out_full, preferred_element_type=jnp.float32
    ).astype(jnp.bfloat16)

    def cross_backward(head_index):
        gradients = head_backward(
            head_columns(query_cross, head_index, head_width),
            head_columns(memory_pairs[0], head_index, head_width),
            head_columns(memory_pairs[1], head_index, head_width),
            head_columns(grad_attn_cross, head_index, head_width),
            cross_totals[head_index],
            0.0,
            cross_allowed,
        )
        return (gradients[0], gradients[1], gradients[2])

    cross_query_grads, cross_key_grads, cross_value_grads = lax.map(cross_backward, head_range)
    own_memory = lax.psum_scatter(
        jnp.stack([join_heads(cross_key_grads), join_heads(cross_value_grads)]).astype(
            jnp.bfloat16
        ),
        "mem",
        scatter_dimension=1,
        tiled=True,
    )
    grad_query_cross = join_heads(cross_query_grads).astype(jnp.bfloat16)
    grad_cross = jnp.stack(
        [
            jnp.einsum(
                "rd,re->de", input_cross, grad_query_cross, preferred_element_type=jnp.float32
            ),
            jnp.einsum(
                "md,me->de", memory_local, own_memory[0], preferred_element_type=jnp.float32
            ),
            jnp.einsum(
                "md,me->de", memory_local, own_memory[1], preferred_element_type=jnp.float32
            ),
        ]
    )
    memory_gradient = jnp.einsum(
        "me,de->md", own_memory[0], cross_full[1], preferred_element_type=jnp.float32
    ) + jnp.einsum("me,de->md", own_memory[1], cross_full[2], preferred_element_type=jnp.float32)
    grad_input_cross = jnp.einsum(
        "re,de->rd", grad_query_cross, cross_full[0], preferred_element_type=jnp.float32
    )
    grad_norm_one, gain_grad_two = pull_cross(grad_input_cross)
    grad_middle_one = grad_middle_two + grad_norm_one
    grad_branch_one = grad_middle_one.astype(jnp.bfloat16)
    grad_self_out = jnp.einsum(
        "rd,re->de", attn_self, grad_branch_one, preferred_element_type=jnp.float32
    )
    grad_attn_self = jnp.einsum(
        "re,de->rd", grad_branch_one, self_out_full, preferred_element_type=jnp.float32
    ).astype(jnp.bfloat16)

    def self_backward(head_index):
        bias_rows = bucket_bias(head_tables[head_index], bucket_index)
        gradients = head_backward(
            head_columns(query_self, head_index, head_width),
            head_columns(self_pairs[0], head_index, head_width),
            head_columns(self_pairs[1], head_index, head_width),
            head_columns(grad_attn_self, head_index, head_width),
            self_totals[head_index],
            bias_rows,
            self_allowed,
        )
        table_grad = bucket_sums(gradients[3], bucket_index, bucket_count)
        return (gradients[0], gradients[1], gradients[2], table_grad)

    self_query_grads, self_key_grads, self_value_grads, table_grads = lax.map(
        self_backward, head_range
    )
    own_self = lax.psum_scatter(
        jnp.stack([join_heads(self_key_grads), join_heads(self_value_grads)]).astype(jnp.bfloat16),
        "mem",
        scatter_dimension=1,
        tiled=True,
    )
    grad_query_self = join_heads(self_query_grads).astype(jnp.bfloat16)
    bias_partial = table_grads.T
    grad_self = jnp.stack(
        [
            jnp.einsum(
                "rd,re->de", input_self, grad_query_self, preferred_element_type=jnp.float32
            ),
            jnp.einsum("rd,re->de", input_self, own_self[0], preferred_element_type=jnp.float32),
            jnp.einsum("rd,re->de", input_self, own_self[1], preferred_element_type=jnp.float32),
        ]
    )
    grad_input_self = (
        jnp.einsum("re,de->rd", grad_query_self, self_full[0], preferred_element_type=jnp.float32)
        + jnp.einsum("re,de->rd", own_self[0], self_full[1], preferred_element_type=jnp.float32)
        + jnp.einsum("re,de->rd", own_self[1], self_full[2], preferred_element_type=jnp.float32)
    )
    grad_norm_zero, gain_grad_one = pull_self(grad_input_self)
    grad_tokens = grad_middle_one + grad_norm_zero
    gain_sums, bias_sums = lax.psum(
        (jnp.stack([gain_grad_one, gain_grad_two, gain_grad_three]), bias_partial), ("batch", "mem")
    )
    summed_groups = (
        lax.psum_scatter(
            grad_self.astype(jnp.bfloat16), "batch", scatter_dimension=1, tiled=True
        ).astype(jnp.float32),
        lax.psum_scatter(
            grad_self_out.astype(jnp.bfloat16), "batch", scatter_dimension=0, tiled=True
        ).astype(jnp.float32),
        lax.psum_scatter(
            grad_cross.astype(jnp.bfloat16), "batch", scatter_dimension=1, tiled=True
        ).astype(jnp.float32),
        lax.psum_scatter(
            grad_cross_out.astype(jnp.bfloat16), "batch", scatter_dimension=0, tiled=True
        ).astype(jnp.float32),
        lax.psum_scatter(
            grad_expand.astype(jnp.bfloat16), "batch", scatter_dimension=1, tiled=True
        ).astype(jnp.float32),
        lax.psum_scatter(
            grad_contract.astype(jnp.bfloat16), "batch", scatter_dimension=0, tiled=True
        ).astype(jnp.float32),
    )
    final_grads = (
        lax.psum_scatter(
            summed_groups[0].astype(jnp.bfloat16), "mem", scatter_dimension=2, tiled=True
        ).astype(jnp.float32),
        lax.psum_scatter(
            summed_groups[1].astype(jnp.bfloat16), "mem", scatter_dimension=1, tiled=True
        ).astype(jnp.float32),
        lax.psum_scatter(
            summed_groups[2].astype(jnp.bfloat16), "mem", scatter_dimension=2, tiled=True
        ).astype(jnp.float32),
        lax.psum_scatter(
            summed_groups[3].astype(jnp.bfloat16), "mem", scatter_dimension=1, tiled=True
        ).astype(jnp.float32),
        lax.psum_scatter(
            summed_groups[4].astype(jnp.bfloat16), "mem", scatter_dimension=2, tiled=True
        ).astype(jnp.float32),
        lax.psum_scatter(
            summed_groups[5].astype(jnp.bfloat16), "mem", scatter_dimension=1, tiled=True
        ).astype(jnp.float32),
    )
    return (
        result_rows.astype(jnp.bfloat16)[None],
        grad_tokens[None],
        memory_gradient[None],
        gain_sums,
        bias_sums,
        final_grads[0],
        final_grads[1],
        final_grads[2],
        final_grads[3],
        final_grads[4],
        final_grads[5],
    )


def solution(mesh):
    placed = (
        P("batch", "mem", None),
        P("batch", "mem", None),
        P("batch", None),
        P("batch", None),
        P(),
        P(),
        P(),
        P(None, "batch", "mem"),
        P("batch", "mem"),
        P(None, "batch", "mem"),
        P("batch", "mem"),
        P(None, "batch", "mem"),
        P("batch", "mem"),
        P("batch", "mem", None),
    )
    return jax.shard_map(
        shards,
        mesh=mesh,
        in_specs=placed,
        out_specs=(
            P("batch", "mem", None),
            P("batch", "mem", None),
            P("batch", "mem", None),
            P(),
            P(),
            P(None, "batch", "mem"),
            P("batch", "mem"),
            P(None, "batch", "mem"),
            P("batch", "mem"),
            P(None, "batch", "mem"),
            P("batch", "mem"),
        ),
        check_vma=False,
    )
```

profile of v0, /device:TPU:0, one launch (start us, length us, event | category | flops | bytes accessed | tf_op | source)
XLA Modules:
  0.0 2073.5 jit_solution(13779350863169390127)
XLA Ops:
  7.2 8.6 all_gather.42
  24.1 39.6 %all-gather.9.cloned.1.call-done = bf16[3,768,768]{2,1,0:T(8,128)(2,1)} async-done(((bf16[3,48,768]{2,1,0:T(8,128)(2,1)}), bf16[3,768,768]{2,1,0:T(8,128)(2,1)}) %all-gather.9.cloned.1.call-update) | async-done | bytes 3538960 | tf_op jit(solution)/shard_map/all_gather | solution.py:138
  74.4 37.8 %all-gather.15.cloned.1.call-done = bf16[3,768,768]{2,1,0:T(8,128)(2,1)} async-done(((bf16[3,48,768]{2,1,0:T(8,128)(2,1)}), bf16[3,768,768]{2,1,0:T(8,128)(2,1)}) %all-gather.15.cloned.1.call-update) | async-done | bytes 3538960 | tf_op jit(solution)/shard_map/all_gather | solution.py:140
  125.6 12.1 all_gather.52
  137.8 7.6 all_gather.54
  148.5 10.2 convert_reduce_fusion
  165.9 288.8 %while.58 = (s32[]{:T(128)}, bf16[12,512,64]{1,2,0:T(8,128)(2,1)}, f32[12,512]{1,0:T(8,128)S(1)}, s32[12]{0:T(128)S(1)}, bf16[512,768]{1,0:T(8,128)(2,1)}, /*ind...) while((s32[]{:T(128)}, bf16[12,512,64]{1,2,0:T(8,128)(2,1)}, ...), condition=%wide.region_10.11_spmd.clone, body=%wide.region_6.0_spmd.clone.sunk | while | flops 189791744 | bytes 32274084 | solution.py:183
  169.1 13.4 select_reduce_fusion.6
  193.2 13.4 select_reduce_fusion.6
  217.3 13.4 select_reduce_fusion.6
  241.3 13.4 select_reduce_fusion.6
  265.4 13.4 select_reduce_fusion.6
  289.4 13.4 select_reduce_fusion.6
  313.4 13.4 select_reduce_fusion.6
  337.5 13.4 select_reduce_fusion.6
  361.5 13.4 select_reduce_fusion.6
  385.8 13.4 select_reduce_fusion.6
  409.9 13.4 select_reduce_fusion.6
  433.9 13.4 select_reduce_fusion.6
  462.1 160.8 %while.59 = (s32[]{:T(128)}, bf16[12,512,64]{1,2,0:T(8,128)(2,1)}, f32[12,512]{1,0:T(8,128)S(1)}, s32[12]{0:T(128)S(1)}, bf16[512,768]{1,0:T(8,128)(2,1)}, /*ind...) while((s32[]{:T(128)}, bf16[12,512,64]{1,2,0:T(8,128)(2,1)}, ...), condition=%wide.region_17.18_spmd.clone, body=%wide.region_14.17_spmd.clone.sunk | while | flops 281017856 | bytes 26528964 | solution.py:209
  636.5 8.6 multiply_convert_fusion.2
  659.1 291.3 %while.60 = (s32[]{:T(128)}, bf16[12,512,64]{1,2,0:T(8,128)(2,1)}, bf16[12,2048,64]{1,2,0:T(8,128)(2,1)}, bf16[12,2048,64]{1,2,0:T(8,128)(2,1)}, s32[12]{0:T(128...) while((s32[]{:T(128)}, bf16[12,512,64]{1,2,0:T(8,128)(2,1)}, ...), condition=%wide.region_22.23_spmd.clone, body=%wide.region_20.22_spmd.clone.sunk | while | flops 680525312 | bytes 64117040 | solution.py:265
  659.3 6.1 fusion.248
  683.6 6.1 fusion.248
  707.8 6.1 fusion.248
  732.1 6.1 fusion.248
  957.7 470.1 %while.61 = (s32[]{:T(128)}, bf16[12,512,64]{1,2,0:T(8,128)(2,1)}, bf16[12,1024,64]{1,2,0:T(8,128)(2,1)}, bf16[12,1024,64]{1,2,0:T(8,128)(2,1)}, f32[12,32]{1,0:...) while((s32[]{:T(128)}, bf16[12,512,64]{1,2,0:T(8,128)(2,1)}, ...), condition=%wide.region_28.29_spmd.clone, body=%wide.region_24.28_spmd.clone.sunk | while | flops 442498528 | bytes 53367924 | solution.py:318
  968.4 12.1 select_reduce_fusion.7
  988.1 8.7 select_reduce_fusion.8
  1007.6 12.1 select_reduce_fusion.7
  1027.3 8.7 select_reduce_fusion.8
  1046.8 12.1 select_reduce_fusion.7
  1066.5 8.7 select_reduce_fusion.8
  1085.9 12.1 select_reduce_fusion.7
  1105.6 8.7 select_reduce_fusion.8
  1125.1 12.1 select_reduce_fusion.7
  1144.8 8.7 select_reduce_fusion.8
  1164.3 12.1 select_reduce_fusion.7
  1184.0 8.7 select_reduce_fusion.8
  1203.4 12.1 select_reduce_fusion.7
  1223.2 8.7 select_reduce_fusion.8
  1242.6 12.1 select_reduce_fusion.7
  1262.4 8.7 select_reduce_fusion.8
  1281.8 12.1 select_reduce_fusion.7
  1301.5 8.7 select_reduce_fusion.8
  1321.0 12.1 select_reduce_fusion.7
  1340.7 8.7 select_reduce_fusion.8
  1360.2 12.1 select_reduce_fusion.7
  1379.9 8.7 select_reduce_fusion.8
  1399.3 12.1 select_reduce_fusion.7
  1419.1 8.7 select_reduce_fusion.8
  1458.4 16.3 reduce-scatter.25.cloned.1.call-done
  1480.6 6.1 pad_maximum_fusion
  1486.7 50.0 %reduce-scatter.31.cloned.1.call-done = bf16[48,768]{1,0:T(8,128)(2,1)} async-done(((bf16[768,768]{1,0:T(8,128)(2,1)}), bf16[48,768]{1,0:T(8,128)(2,1)}) %reduce-scatter.31.cloned.1.call-update) | async-done | bytes 73744 | tf_op jit(solution)/shard_map/reduce_scatter | solution.py:352
  1538.5 59.4 %reduce-scatter.35.cloned.1.call-done = bf16[48,768]{1,0:T(8,128)(2,1)} async-done(((bf16[768,768]{1,0:T(8,128)(2,1)}), bf16[48,768]{1,0:T(8,128)(2,1)}) %reduce-scatter.35.cloned.1.call-update) | async-done | bytes 73744 | tf_op jit(solution)/shard_map/reduce_scatter | solution.py:358
  1599.6 67.6 %reduce-scatter.41.cloned.1.call-done = bf16[128,768]{1,0:T(8,128)(2,1)} async-done(((bf16[2048,768]{1,0:T(8,128)(2,1)}), bf16[128,768]{1,0:T(8,128)(2,1)}) %reduce-scatter.41.cloned.1.call-update) | async-done | bytes 196624 | tf_op jit(solution)/shard_map/reduce_scatter | solution.py:364
  1669.1 86.8 %reduce-scatter.37.cloned.1.call-done = bf16[2,48,2048]{2,1,0:T(8,128)(2,1)} async-done(((bf16[2,768,2048]{2,1,0:T(8,128)(2,1)}), bf16[2,48,2048]{2,1,0:T(8,128)(2,1)}) %reduce-scatter.37.cloned.1.call-update) | async-done | bytes 393232 | tf_op jit(solution)/shard_map/reduce_scatter | solution.py:361
  1759.9 66.9 %reduce-scatter.29.cloned.1.call-done = bf16[3,48,768]{2,1,0:T(8,128)(2,1)} async-done(((bf16[3,768,768]{2,1,0:T(8,128)(2,1)}), bf16[3,48,768]{2,1,0:T(8,128)(2,1)}) %reduce-scatter.29.cloned.1.call-update) | async-done | bytes 221200 | tf_op jit(solution)/shard_map/reduce_scatter | solution.py:349
  1831.2 73.8 %reduce-scatter.27.cloned.1.call-done = bf16[2,1024,768]{1,2,0:T(8,128)(2,1)} async-done(((bf16[2,2048,768]{1,2,0:T(8,128)(2,1)}), bf16[2,1024,768]{1,2,0:T(8,128)(2,1)}) %reduce-scatter.27.cloned.1.call-update) | async-done | bytes 3145744 | tf_op jit(solution)/shard_map/reduce_scatter | solution.py:266
  1922.2 10.2 reduce-scatter.49.cloned.1.call-done
  1934.0 12.1 reduce-scatter.51.cloned.1.call-done
  1954.3 40.1 %all-reduce = (f32[3,768]{1,0:T(4,128)}, f32[32,12]{0,1:T(8,128)}) all-reduce(f32[3,768]{1,0:T(4,128)S(1)} %pad_maximum_fusion.7, f32[32,12]{0,1:T(8,128)S(1)} %bitcast.397), channel_id=1, replica_groups=mesh['batch'=16,'mem'=2] {'batch','mem'}, use_global_device_ids=true, to_apply=%region_35.36 | all-reduce | flops 2688 | bytes 21504 | tf_op jit(solution)/shard_map/psum | solution.py:345
  2006.3 43.4 %reduce-scatter.33.cloned.1.call-done = bf16[3,48,768]{2,1,0:T(8,128)(2,1)} async-done(((bf16[3,768,768]{2,1,0:T(8,128)(2,1)}), bf16[3,48,768]{2,1,0:T(8,128)(2,1)}) %reduce-scatter.33.cloned.1.call-update) | async-done | bytes 221200 | tf_op jit(solution)/shard_map/reduce_scatter | solution.py:355
  2058.1 6.3 reduce-scatter.47.cloned.1.call-done
  (776 shorter events, 860.4 us)
Async XLA Ops:
  7.2 105.0 %copy-start = (bf16[1,1024,768]{2,1,0:T(8,128)(2,1)S(1)}, bf16[1,1024,768]{2,1,0:T(8,128)(2,1)}, u32[]{:S(2)}) copy-start(bf16[1,1024,768]{2,1,0:T(8,128)(2,1)} %param.23) | copy-start | bytes 4718596
  7.2 56.4 %all-gather.9.cloned.1.call-start = ((), (), s32[]{:S(2)}) async-start(), calls=%async_computation.14 | async-start | bytes 3760128 | tf_op jit(solution)/shard_map/all_gather | solution.py:138
  15.9 96.2 %all-gather.15.cloned.1.call-start = ((), (), s32[]{:S(2)}) async-start(), calls=%async_computation.17 | async-start | bytes 3760128 | tf_op jit(solution)/shard_map/all_gather | solution.py:140
  21.7 143.2 %all-gather.11.cloned.1.call-start = ((), (), s32[]{:S(2)}) async-start(), calls=%async_computation.15 | async-start | bytes 4718592 | tf_op jit(solution)/shard_map/all_gather | solution.py:172
  22.6 136.0 %copy-start.36 = (f32[768]{0:T(1024)}, f32[768]{0:T(1024)S(1)}, u32[]{:S(2)}) copy-start(f32[768]{0:T(1024)S(1)} %get-tuple-element.347) | copy-start | bytes 9220
  22.6 435.4 %copy-start.38 = (f32[768]{0:T(1024)}, f32[768]{0:T(1024)S(1)}, u32[]{:S(2)}) copy-start(f32[768]{0:T(1024)S(1)} %get-tuple-element.348) | copy-start | bytes 9220
  24.0 42.0 %copy-start.42 = (f32[512]{0:T(512)}, f32[512]{0:T(512)S(1)}, u32[]{:S(2)}) copy-start(f32[512]{0:T(512)S(1)} %fusion.93) | copy-start | bytes 6148
  24.1 134.6 %copy-start.44 = (f32[512]{0:T(512)}, f32[512]{0:T(512)S(1)}, u32[]{:S(2)}) copy-start(f32[512]{0:T(512)S(1)} %fusion.147) | copy-start | bytes 6148
  69.5 385.3 %all-gather.13.cloned.1.call-start = ((), (), s32[]{:S(2)}) async-start(), calls=%async_computation.16 | async-start | bytes 1253376 | tf_op jit(solution)/shard_map/all_gather | solution.py:139
  74.3 386.8 %all-gather.17.cloned.1.call-start = ((), (), s32[]{:S(2)}) async-start(), calls=%async_computation.18 | async-start | bytes 9437184 | tf_op jit(solution)/shard_map/all_gather | solution.py:198
  119.4 6.2 copy-start.31
  119.4 18.4 copy-start.32
  119.5 28.1 %copy-start.53 = (s32[1,4]{1,0:T(1,128)S(1)}, s32[1,4]{1,0:T(1,128)}, u32[]{:S(2)}) copy-start(s32[1,4]{1,0:T(1,128)} %param.24) | copy-start | bytes 52
  119.5 28.5 %copy-start.54 = (s32[1,4]{1,0:T(1,128)S(1)}, s32[1,4]{1,0:T(1,128)}, u32[]{:S(2)}) copy-start(s32[1,4]{1,0:T(1,128)} %param.25) | copy-start | bytes 52
  119.5 28.8 %copy-start.49 = (s32[1024]{0:T(1024)S(1)}, s32[1024]{0:T(1024)}, u32[]{:S(2)}) copy-start(s32[1024]{0:T(1024)} %param.26) | copy-start | bytes 12292
  119.5 503.4 %all-gather.19.cloned.1.call-start = ((), (), s32[]{:S(2)}) async-start(), calls=%async_computation.19 | async-start | bytes 1253376 | tf_op jit(solution)/shard_map/all_gather | solution.py:141
  125.6 501.2 %all-gather.21.cloned.1.call-start = ((), (), s32[]{:S(2)}) async-start(), calls=%async_computation.20 | async-start | bytes 6684672 | tf_op jit(solution)/shard_map/all_gather | solution.py:142
  137.7 498.8 %all-gather.23.cloned.1.call-start = ((), (), s32[]{:S(2)}) async-start(), calls=%async_computation.21 | async-start | bytes 3342336 | tf_op jit(solution)/shard_map/all_gather | solution.py:143
  145.4 1329.3 %reduce-scatter.25.cloned.1.call-start = ((), (), s32[]{:S(2)}) async-start(), calls=%async_computation.22 | async-start | bytes 4718592 | tf_op jit(solution)/shard_map/reduce_scatter | solution.py:321
  169.1 13.4 copy-start.4
  193.2 13.4 copy-start.4
  217.3 13.4 copy-start.4
  241.3 13.4 copy-start.4
  265.4 13.4 copy-start.4
  289.4 13.4 copy-start.4
  313.4 13.4 copy-start.4
  337.5 13.4 copy-start.4
  361.5 13.4 copy-start.4
  385.8 13.4 copy-start.4
  409.9 13.4 copy-start.4
  433.9 13.4 copy-start.4
  457.5 165.4 %copy-start.8 = (f32[512,768]{1,0:T(8,128)}, f32[512,768]{1,0:T(8,128)S(1)}, u32[]{:S(2)}) copy-start(f32[512,768]{1,0:T(8,128)S(1)} %get-tuple-element.463) | copy-start | bytes 4718596
  626.7 6.0 copy-start.20
  626.8 5.9 copy-start.51
  645.1 5.3 copy-start.11
  656.4 297.3 %copy-start.7 = (f32[512,768]{1,0:T(8,128)}, f32[512,768]{1,0:T(8,128)S(1)}, u32[]{:S(2)}) copy-start(f32[512,768]{1,0:T(8,128)S(1)} %fusion.99) | copy-start | bytes 4718596
  659.1 291.3 %copy-start.39 = (f32[768]{0:T(1024)S(1)}, f32[768]{0:T(1024)}, u32[]{:S(2)}) copy-start(f32[768]{0:T(1024)} %copy-done.38) | copy-start | bytes 9220
  659.1 291.3 %copy-start.41 = (f32[512]{0:T(512)S(1)}, f32[512]{0:T(512)}, u32[]{:S(2)}) copy-start(f32[512]{0:T(512)} %copy-done.40) | copy-start | bytes 6148
  968.4 12.1 copy-start.3
  1007.6 12.1 copy-start.3
  1046.7 12.1 copy-start.3
  1085.9 12.1 copy-start.3
  1125.1 12.1 copy-start.3
  1164.3 12.1 copy-start.3
  1203.4 12.1 copy-start.3
  1242.6 12.1 copy-start.3
  1281.8 12.1 copy-start.3
  1321.0 12.1 copy-start.3
  1360.2 12.1 copy-start.3
  1399.3 12.1 copy-start.3
  1431.7 105.0 %reduce-scatter.31.cloned.1.call-start = ((), (), s32[]{:S(2)}) async-start(), calls=%async_computation.25 | async-start | bytes 1253376 | tf_op jit(solution)/shard_map/reduce_scatter | solution.py:352
  1436.0 161.8 %reduce-scatter.35.cloned.1.call-start = ((), (), s32[]{:S(2)}) async-start(), calls=%async_computation.27 | async-start | bytes 1253376 | tf_op jit(solution)/shard_map/reduce_scatter | solution.py:358
  1440.1 227.1 %reduce-scatter.41.cloned.1.call-start = ((), (), s32[]{:S(2)}) async-start(), calls=%async_computation.30 | async-start | bytes 3342336 | tf_op jit(solution)/shard_map/reduce_scatter | solution.py:364
  1445.4 310.5 %reduce-scatter.37.cloned.1.call-start = ((), (), s32[]{:S(2)}) async-start(), calls=%async_computation.28 | async-start | bytes 6684672 | tf_op jit(solution)/shard_map/reduce_scatter | solution.py:361
  1454.4 372.4 %reduce-scatter.29.cloned.1.call-start = ((), (), s32[]{:S(2)}) async-start(), calls=%async_computation.24 | async-start | bytes 3760128 | tf_op jit(solution)/shard_map/reduce_scatter | solution.py:349
  1480.5 424.4 %reduce-scatter.27.cloned.1.call-start = ((), (), s32[]{:S(2)}) async-start(), calls=%async_computation.23 | async-start | bytes 9437184 | tf_op jit(solution)/shard_map/reduce_scatter | solution.py:266
  1486.7 433.9 %reduce-scatter.45.cloned.1.call-start = ((), (), s32[]{:S(2)}) async-start(), calls=%async_computation.32 | async-start | bytes 294912
  1538.4 394.0 %reduce-scatter.49.cloned.1.call-start = ((), (), s32[]{:S(2)}) async-start(), calls=%async_computation.34 | async-start | bytes 294912
  1599.6 346.5 %reduce-scatter.51.cloned.1.call-start = ((), (), s32[]{:S(2)}) async-start(), calls=%async_computation.35 | async-start | bytes 294912
  1669.0 328.7 %reduce-scatter.39.cloned.1.call-start = ((), (), s32[]{:S(2)}) async-start(), calls=%async_computation.29 | async-start | bytes 589824 | tf_op jit(solution)/shard_map/reduce_scatter | solution.py:381
  1755.9 243.5 %reduce-scatter.43.cloned.1.call-start = ((), (), s32[]{:S(2)}) async-start(), calls=%async_computation.31 | async-start | bytes 589824
  1831.1 218.6 %reduce-scatter.33.cloned.1.call-start = ((), (), s32[]{:S(2)}) async-start(), calls=%async_computation.26 | async-start | bytes 3760128 | tf_op jit(solution)/shard_map/reduce_scatter | solution.py:355
  1911.4 153.0 %reduce-scatter.47.cloned.1.call-start = ((), (), s32[]{:S(2)}) async-start(), calls=%async_computation.33 | async-start | bytes 589824
  1950.6 43.7 %copy-start.43 = (f32[512]{0:T(512)S(1)}, f32[512]{0:T(512)}, u32[]{:S(2)}) copy-start(f32[512]{0:T(512)} %copy-done.42) | copy-start | bytes 6148
  (61 other events, 194.5 us)
Sparse Core Ops, SparseCore 0:
  16.0 47.5 all-gather.8
  65.9 46.2 all-gather.14
  114.3 50.6 all-gather.10
  167.1 37.9 all-gather.12
  207.0 79.3 all-gather.16
  288.5 38.4 all-gather.18
  329.2 60.8 all-gather.20
  392.4 43.7 all-gather.22
  1431.8 42.9 reduce-scatter.24
  1478.6 58.0 reduce-scatter.30
  1540.7 57.0 reduce-scatter.34
  1602.0 65.1 reduce-scatter.40
  1671.7 84.1 reduce-scatter.36
  1759.6 67.1 reduce-scatter.28
  1828.9 75.9 reduce-scatter.26
  1907.7 10.9 reduce-scatter.44
  1921.4 10.9 reduce-scatter.48
  1935.1 10.9 reduce-scatter.50
  1948.4 13.1 reduce-scatter.38
  1963.7 13.5 reduce-scatter.42
  1981.6 67.9 reduce-scatter.32
  2052.4 12.0 reduce-scatter.46
where the time goes:
time: 2090 us; the launch traced here: 2070 us
  waiting for transfers between devices  574 us (27%)
  matrix products  534 us (26%)
  other arithmetic  481 us (23%)
  local copies, waits for them, and re-layouts  283 us (14%)
  loops' own time  99.8 us (5%)
  blocking collectives  84.2 us (4%)
    reduce_sum x24, other arithmetic, bucket_bias(): jnp.sum(jnp.where(bucket_index[None, :, :] == bucket_range[:, None, None]...  306 us
    dot_general x48, matrix products, masked_scores(): jnp.einsum('qd,kd->qk', queries, key_rows, preferred_element_type=jnp.flo...  126 us
    reduce_sum x12, other arithmetic, bucket_sums(): jnp.sum(jnp.where(bucket_index[None, :, :] == bucket_range[:, None, None]...  104 us
    reduce_scatter x1, waiting for transfers between devices, shards(): lax.psum_scatter(grad_expand.astype(jnp.bfloat16), 'batch', scatter_dimen...  86.8 us
    dot_general x24, matrix products, head_backward(): jnp.einsum('qd,kd->qk', grad_result, value_rows, preferred_element_type=j...  81.7 us
    reduce_scatter x1, waiting for transfers between devices, shards(): lax.psum_scatter(jnp.stack([join_heads(cross_key_grads), join_heads(cross...  73.8 us
    slice x12, local copies, waits for them, and re-layouts, cross_backward(): memory_pairs[1]  72.6 us
    slice x12, local copies, waits for them, and re-layouts, cross_forward(): memory_pairs[1]  71.3 us
  transfers between devices with their start and end apart: 22, of which 14 were waited for; matrix products, arithmetic and copies ran while one was open for 27% of the time, Pallas kernels for 0%

commit v1 on v0

--- a/solution.py
+++ b/solution.py
@@ -1,10 +1,19 @@
+import functools
+
 import jax
 import jax.numpy as jnp
 from jax import lax
+from jax.experimental import pallas as pl
+from jax.experimental.pallas import tpu as pltpu
 from jax.sharding import PartitionSpec as P
 
 EPSILON = 1e-06
 NEGATIVE = -1e30
+F32 = jnp.float32
+BF16 = jnp.bfloat16
+EXACT = lax.Precision.HIGHEST
+NT = (((1,), (1,)), ((), ()))
+NN = (((1,), (0,)), ((), ()))
 
 
 def rms_norm(values, gain_row):
@@ -17,85 +26,292 @@
     return jax.nn.gelu(gate_part, approximate=True) * up_part
 
 
-def segment_ids(lengths, first_row, count):
-    boundary = jnp.cumsum(lengths)
-    places = first_row + jnp.arange(count, dtype=jnp.int32)
-    return jnp.sum((places[:, None] >= boundary[None, :]).astype(jnp.int32), axis=1)
-
-
-def bucket_starts(distance_buckets, bucket_count):
-    levels = jnp.arange(1, bucket_count, dtype=jnp.int32)
-    return jnp.sum((distance_buckets[None, :] < levels[:, None]).astype(jnp.int32), axis=1)
-
-
-def bucket_of(distance_index, starts):
-    return jnp.sum((distance_index[None, :, :] >= starts[:, None, None]).astype(jnp.int32), axis=0)
-
-
-def bucket_bias(table_row, bucket_index):
-    bucket_range = jnp.arange(table_row.shape[0], dtype=jnp.int32)
-    return jnp.sum(
-        jnp.where(
-            bucket_index[None, :, :] == bucket_range[:, None, None], table_row[:, None, None], 0.0
-        ),
-        axis=0,
-    )
-
-
-def bucket_sums(grad_scores, bucket_index, bucket_count):
-    bucket_range = jnp.arange(bucket_count, dtype=jnp.int32)
-    return jnp.sum(
-        jnp.where(
-            bucket_index[None, :, :] == bucket_range[:, None, None],
-            grad_scores.astype(jnp.float32)[None, :, :],
-            0.0,
-        ),
-        axis=(1, 2),
-    )
-
-
-def head_columns(matrix, head_index, head_width):
-    return lax.dynamic_slice_in_dim(matrix, head_index * head_width, head_width, 1)
-
-
-def join_heads(stacked):
-    return stacked.transpose(1, 0, 2).reshape(stacked.shape[1], stacked.shape[0] * stacked.shape[2])
-
-
-def masked_scores(queries, key_rows, bias_rows, allowed):
-    scores = (
-        jnp.einsum("qd,kd->qk", queries, key_rows, preferred_element_type=jnp.float32) + bias_rows
-    )
-    return jnp.where(allowed, scores, NEGATIVE)
-
-
-def head_forward(queries, key_rows, value_rows, bias_rows, allowed):
-    scores = masked_scores(queries, key_rows, bias_rows, allowed)
-    row_max = jnp.max(scores, axis=1, keepdims=True)
-    exponent = jnp.exp(scores - row_max)
-    row_total = jnp.sum(exponent, axis=1, keepdims=True)
-    attn_probs = (exponent / row_total).astype(jnp.bfloat16)
-    result = jnp.einsum("qk,kd->qd", attn_probs, value_rows, preferred_element_type=jnp.float32)
-    return (result, (row_max + jnp.log(row_total))[:, 0])
-
-
-def head_backward(queries, key_rows, value_rows, grad_result, log_total, bias_rows, allowed):
-    scores = masked_scores(queries, key_rows, bias_rows, allowed)
-    attn_probs = jnp.exp(scores - log_total[:, None])
-    value_grads = jnp.einsum(
-        "qk,qd->kd",
-        attn_probs.astype(jnp.bfloat16),
-        grad_result,
-        preferred_element_type=jnp.float32,
-    )
-    grad_probs = jnp.einsum(
-        "qd,kd->qk", grad_result, value_rows, preferred_element_type=jnp.float32
-    )
-    inner_sum = jnp.sum(attn_probs * grad_probs, axis=1, keepdims=True)
-    grad_scores = (attn_probs * (grad_probs - inner_sum)).astype(jnp.bfloat16)
-    query_grads = jnp.einsum("qk,kd->qd", grad_scores, key_rows, preferred_element_type=jnp.float32)
-    key_grads = jnp.einsum("qk,qd->kd", grad_scores, queries, preferred_element_type=jnp.float32)
-    return (query_grads, key_grads, value_grads, grad_scores)
+def dot(left, right, dims):
+    return lax.dot_general(left, right, dims, preferred_element_type=F32)
+
+
+def bounds_of(sizes_ref):
+    edges = [jnp.int32(0)]
+    for slot in range(sizes_ref.shape[1]):
+        edges.append(edges[-1] + sizes_ref[0, slot])
+    return edges
+
+
+def pick(place, edges, values):
+    chosen = jnp.zeros_like(place) + values[0]
+    for slot in range(1, len(edges) - 1):
+        chosen = jnp.where(place >= edges[slot], values[slot], chosen)
+    return chosen
+
+
+def stack_heads(block, width):
+    lane = lax.broadcasted_iota(jnp.int32, block.shape, 1)
+    zero = jnp.zeros_like(block)
+    return jnp.concatenate(
+        [jnp.where(lane < width, block, zero), jnp.where(lane < width, zero, block)], axis=0
+    )
+
+
+def transposed_blocks(source_ref, scratch, step):
+    for index in range(scratch.shape[0]):
+        scratch[index] = source_ref[index * step : (index + 1) * step, :].T
+
+
+def ranges(first, rows, q_edges, k_edges, causal, step):
+    last = first + rows - 1
+    starts, ends = k_edges[:-1], k_edges[1:]
+    low_start = pick(first, q_edges, starts)
+    high_start = pick(last, q_edges, starts)
+    low_end = pick(first, q_edges, ends)
+    high_end = pick(last, q_edges, ends)
+    if causal:
+        low_end = jnp.minimum(low_end, first + 1)
+        high_end = jnp.minimum(high_end, last + 1)
+    low = low_start // step
+    high = (high_end + step - 1) // step
+    clear_low = (high_start + step - 1) // step
+    clear_high = low_end // step
+    return low, high, clear_low, clear_high
+
+
+def limits(first, rows, q_edges, k_edges, causal):
+    place = lax.rem(lax.broadcasted_iota(jnp.int32, (1, 2 * rows), 1), rows) + first
+    begin = pick(place, q_edges, k_edges[:-1])
+    end = pick(place, q_edges, k_edges[1:])
+    if causal:
+        end = jnp.minimum(end, place + 1)
+    return begin, end
+
+
+def toeplitz(table_ref, tiles, rows):
+    for delta in range(tiles.shape[0]):
+        for head in range(2):
+            base = table_ref[0, head : head + 1, delta * rows : (delta + 2) * rows]
+            wide = jnp.broadcast_to(base, (rows, 2 * rows))
+            wide = pltpu.roll(wide, 0, 1, stride=1, stride_axis=0)
+            tiles[delta, :, head * rows : (head + 1) * rows] = wide[:, rows:]
+
+
+def masked(scores, index, step, begin, end):
+    place = lax.broadcasted_iota(jnp.int32, scores.shape, 0) + index * step
+    return jnp.where((place >= begin) & (place < end), scores, NEGATIVE)
+
+
+def forward_kernel(
+    causal, step, width, first_ref, q_sizes, k_sizes, q_ref, k_ref, v_ref, *rest
+):
+    if causal:
+        table_ref, out_ref, total_ref, value_t, scores, tiles = rest
+    else:
+        out_ref, total_ref, value_t, scores = rest
+    blocks, rows = total_ref.shape[1], total_ref.shape[3] // 2
+    q_edges = bounds_of(q_sizes)
+    k_edges = bounds_of(k_sizes)
+    transposed_blocks(v_ref, value_t, step)
+    if causal:
+        toeplitz(table_ref, tiles, rows)
+    for block in range(blocks):
+        first = first_ref[0] + block * rows
+        low, high, clear_low, clear_high = ranges(first, rows, q_edges, k_edges, causal, step)
+        begin, end = limits(first, rows, q_edges, k_edges, causal)
+        queries = stack_heads(q_ref[block * rows : (block + 1) * rows, :], width)
+
+        def measure(index, top):
+            keys = k_ref[pl.ds(pl.multiple_of(index * step, step), step), :]
+            block_scores = dot(keys, queries, NT)
+            if causal:
+                block_scores = block_scores + tiles[first // rows - index]
+            clear = (index >= clear_low) & (index < clear_high)
+
+            def plain():
+                scores[index] = block_scores
+                return jnp.max(block_scores, axis=0, keepdims=True)
+
+            def cut():
+                kept = masked(block_scores, index, step, begin, end)
+                scores[index] = kept
+                return jnp.max(kept, axis=0, keepdims=True)
+
+            return jnp.maximum(top, lax.cond(clear, plain, cut))
+
+        top = lax.fori_loop(low, high, measure, jnp.full((1, 2 * rows), NEGATIVE, F32))
+
+        def gather(index, carry):
+            total, out_a, out_b = carry
+            weights = jnp.exp(scores[index] - top)
+            total = total + jnp.sum(weights, axis=0, keepdims=True)
+            rounded = weights.astype(BF16)
+            out_a = out_a + dot(value_t[index, :width, :], rounded[:, :rows], NN)
+            out_b = out_b + dot(value_t[index, width:, :], rounded[:, rows:], NN)
+            return total, out_a, out_b
+
+        zero = jnp.zeros((width, rows), F32)
+        total, out_a, out_b = lax.fori_loop(
+            low, high, gather, (jnp.zeros((1, 2 * rows), F32), zero, zero)
+        )
+        joined = jnp.concatenate([out_a / total[:, :rows], out_b / total[:, rows:]], axis=0)
+        out_ref[block * rows : (block + 1) * rows, :] = joined.T.astype(BF16)
+        total_ref[0, block] = top + jnp.log(total)
+
+
+def backward_kernel(
+    causal, step, width, first_ref, q_sizes, k_sizes, q_ref, k_ref, v_ref, g_ref, total_ref, *rest
+):
+    if causal:
+        table_ref, dq_ref, dk_ref, dv_ref, diag_ref, key_t, probs, grads, dk, dv, tiles, sums = rest
+    else:
+        dq_ref, dk_ref, dv_ref, key_t, probs, grads, dk, dv = rest
+    blocks, rows = total_ref.shape[1], total_ref.shape[3] // 2
+    q_edges = bounds_of(q_sizes)
+    k_edges = bounds_of(k_sizes)
+    transposed_blocks(k_ref, key_t, step)
+    dk[...] = jnp.zeros_like(dk)
+    dv[...] = jnp.zeros_like(dv)
+    if causal:
+        toeplitz(table_ref, tiles, rows)
+        sums[...] = jnp.zeros_like(sums)
+    for block in range(blocks):
+        first = first_ref[0] + block * rows
+        low, high, clear_low, clear_high = ranges(first, rows, q_edges, k_edges, causal, step)
+        begin, end = limits(first, rows, q_edges, k_edges, causal)
+        queries = stack_heads(q_ref[block * rows : (block + 1) * rows, :], width)
+        targets = stack_heads(g_ref[block * rows : (block + 1) * rows, :], width)
+        total = total_ref[0, block]
+
+        def measure(index, inner):
+            here = pl.ds(pl.multiple_of(index * step, step), step)
+            block_scores = dot(k_ref[here, :], queries, NT)
+            if causal:
+                block_scores = block_scores + tiles[first // rows - index]
+            weights = jnp.exp(block_scores - total)
+            clear = (index >= clear_low) & (index < clear_high)
+            place = lax.broadcasted_iota(jnp.int32, weights.shape, 0) + index * step
+            weights = jnp.where((place >= begin) & (place < end), weights, 0.0)
+            pulled = dot(v_ref[here, :], targets, NT)
+            probs[index] = weights
+            grads[index] = pulled
+            dv[here, :] += dot(weights.astype(BF16), targets, NN)
+            return inner + jnp.sum(weights * pulled, axis=0, keepdims=True)
+
+        inner = lax.fori_loop(low, high, measure, jnp.zeros((1, 2 * rows), F32))
+
+        def gather(index, carry):
+            out_a, out_b = carry
+            here = pl.ds(pl.multiple_of(index * step, step), step)
+            rounded = (probs[index] * (grads[index] - inner)).astype(BF16)
+            dk[here, :] += dot(rounded, queries, NN)
+            if causal:
+                sums[first // rows - index] += rounded.astype(F32)
+            out_a = out_a + dot(key_t[index, :width, :], rounded[:, :rows], NN)
+            out_b = out_b + dot(key_t[index, width:, :], rounded[:, rows:], NN)
+            return out_a, out_b
+
+        zero = jnp.zeros((width, rows), F32)
+        out_a, out_b = lax.fori_loop(low, high, gather, (zero, zero))
+        joined = jnp.concatenate([out_a, out_b], axis=0)
+        dq_ref[block * rows : (block + 1) * rows, :] = joined.T.astype(BF16)
+    dk_ref[...] = dk[...].astype(BF16)
+    dv_ref[...] = dv[...].astype(BF16)
+    if causal:
+        for delta in range(sums.shape[0]):
+            for head in range(2):
+                parts = jnp.zeros((8, 2 * rows), F32)
+                for chunk in range(rows // 8):
+                    piece = sums[delta, chunk * 8 : chunk * 8 + 8, head * rows : (head + 1) * rows]
+                    piece = jnp.concatenate([jnp.zeros_like(piece), piece], axis=1)
+                    parts = parts + (pltpu.roll(piece, 2 * rows - 8 * chunk, 1) if chunk else piece)
+                line = parts[0:1]
+                for row in range(1, 8):
+                    line = line + pltpu.roll(parts[row : row + 1], 2 * rows - row, 1)
+                diag_ref[0, head, delta : delta + 1, :] = line
+
+
+def smem():
+    return pl.BlockSpec(memory_space=pltpu.SMEM)
+
+
+def attention_forward(first, q_sizes, k_sizes, queries, keys, values, table, width, step):
+    causal = table is not None
+    count, model = queries.shape
+    key_count = keys.shape[0]
+    rows = min(256, count)
+    step = rows if causal else step
+    pairs, blocks = model // (2 * width), count // rows
+    column = lambda size: pl.BlockSpec((size, 2 * width), lambda pair: (0, pair))
+    scratch = [
+        pltpu.VMEM((key_count // step, 2 * width, step), BF16),
+        pltpu.VMEM((key_count // step, step, 2 * rows), F32),
+    ]
+    in_specs = [smem(), smem(), smem(), column(count), column(key_count), column(key_count)]
+    args = [first, q_sizes, k_sizes, queries, keys, values]
+    if causal:
+        in_specs.append(pl.BlockSpec((1, 2, table.shape[2]), lambda pair: (pair, 0, 0)))
+        args.append(table)
+        scratch.append(pltpu.VMEM((key_count // rows, rows, 2 * rows), F32))
+    return pl.pallas_call(
+        functools.partial(forward_kernel, causal, step, width),
+        grid=(pairs,),
+        in_specs=in_specs,
+        out_specs=[
+            column(count),
+            pl.BlockSpec((1, blocks, 1, 2 * rows), lambda pair: (pair, 0, 0, 0)),
+        ],
+        out_shape=[
+            jax.ShapeDtypeStruct((count, model), BF16),
+            jax.ShapeDtypeStruct((pairs, blocks, 1, 2 * rows), F32),
+        ],
+        scratch_shapes=scratch,
+        compiler_params=pltpu.CompilerParams(vmem_limit_bytes=56 << 20),
+        name="self_forward" if causal else "cross_forward",
+    )(*args)
+
+
+def attention_backward(
+    first, q_sizes, k_sizes, queries, keys, values, grads, totals, table, width, step
+):
+    causal = table is not None
+    count, model = queries.shape
+    key_count = keys.shape[0]
+    rows = min(256, count)
+    step = rows if causal else step
+    pairs, blocks = model // (2 * width), count // rows
+    column = lambda size: pl.BlockSpec((size, 2 * width), lambda pair: (0, pair))
+    n_step = key_count // step
+    scratch = [
+        pltpu.VMEM((n_step, 2 * width, step), BF16),
+        pltpu.VMEM((n_step, step, 2 * rows), F32),
+        pltpu.VMEM((n_step, step, 2 * rows), F32),
+        pltpu.VMEM((key_count, 2 * width), F32),
+        pltpu.VMEM((key_count, 2 * width), F32),
+    ]
+    in_specs = [
+        smem(), smem(), smem(), column(count), column(key_count), column(key_count), column(count),
+        pl.BlockSpec((1, blocks, 1, 2 * rows), lambda pair: (pair, 0, 0, 0)),
+    ]
+    args = [first, q_sizes, k_sizes, queries, keys, values, grads, totals]
+    out_specs = [column(count), column(key_count), column(key_count)]
+    out_shape = [
+        jax.ShapeDtypeStruct((count, model), BF16),
+        jax.ShapeDtypeStruct((key_count, model), BF16),
+        jax.ShapeDtypeStruct((key_count, model), BF16),
+    ]
+    if causal:
+        in_specs.append(pl.BlockSpec((1, 2, table.shape[2]), lambda pair: (pair, 0, 0)))
+        args.append(table)
+        deltas = key_count // rows
+        scratch += [pltpu.VMEM((deltas, rows, 2 * rows), F32), pltpu.VMEM((deltas, rows, 2 * rows), F32)]
+        out_specs.append(pl.BlockSpec((1, 2, deltas, 2 * rows), lambda pair: (pair, 0, 0, 0)))
+        out_shape.append(jax.ShapeDtypeStruct((pairs, 2, deltas, 2 * rows), F32))
+    return pl.pallas_call(
+        functools.partial(backward_kernel, causal, step, width),
+        grid=(pairs,),
+        in_specs=in_specs,
+        out_specs=out_specs,
+        out_shape=out_shape,
+        scratch_shapes=scratch,
+        compiler_params=pltpu.CompilerParams(vmem_limit_bytes=60 << 20),
+        name="self_backward" if causal else "cross_backward",
+    )(*args)
 
 
 def shards(
@@ -123,9 +339,7 @@
     head_width = model_width // head_count
     bucket_count = position_bias.shape[0]
     key_count = row_count * mem_count
-    memory_total = memory_count * mem_count
     first_row = mem_index * row_count
-    head_range = jnp.arange(head_count)
     within = (
         lax.all_gather(self_weights, "mem", axis=2, tiled=True),
         lax.all_gather(self_output, "mem", axis=1, tiled=True),
@@ -143,20 +357,13 @@
         lax.all_gather(within[5], "batch", axis=0, tiled=True),
     )
     self_full, self_out_full, cross_full, cross_out_full, expand_full, contract_full = full_weights
-    decoder_sizes = decoder_lengths[0]
-    memory_sizes = memory_lengths[0]
-    query_seq = segment_ids(decoder_sizes, first_row, row_count)
-    key_seq = segment_ids(decoder_sizes, 0, key_count)
-    memory_seq = segment_ids(memory_sizes, 0, memory_total)
-    query_place = first_row + jnp.arange(row_count, dtype=jnp.int32)
-    key_place = jnp.arange(key_count, dtype=jnp.int32)
-    self_allowed = (key_place[None, :] <= query_place[:, None]) & (
-        key_seq[None, :] == query_seq[:, None]
-    )
-    cross_allowed = memory_seq[None, :] == query_seq[:, None]
-    distance_index = jnp.clip(query_place[:, None] - key_place[None, :], 0, key_count - 1)
-    bucket_index = bucket_of(distance_index, bucket_starts(distance_buckets, bucket_count))
-    head_tables = position_bias.T
+    first = jnp.reshape(first_row, (1,)).astype(jnp.int32)
+    rows = min(256, row_count)
+    buckets = jnp.arange(bucket_count, dtype=jnp.int32)
+    one_hot = (distance_buckets[:, None] == buckets[None, :]).astype(F32)
+    distance_table = jnp.einsum("db,bh->hd", one_hot, position_bias, precision=EXACT)
+    distance_table = jnp.pad(distance_table, ((0, 0), (rows, 0)))
+    distance_table = distance_table.reshape(head_count // 2, 2, key_count + rows)
     tokens = hidden[0].astype(jnp.float32)
     normed_self, pull_self = jax.vjp(rms_norm, tokens, norm_gains[0])
     input_self = normed_self.astype(jnp.bfloat16)
@@ -171,17 +378,10 @@
     )
     self_pairs = lax.all_gather(jnp.stack([key_self, value_self]), "mem", axis=1, tiled=True)
 
-    def self_forward(head_index):
-        return head_forward(
-            head_columns(query_self, head_index, head_width),
-            head_columns(self_pairs[0], head_index, head_width),
-            head_columns(self_pairs[1], head_index, head_width),
-            bucket_bias(head_tables[head_index], bucket_index),
-            self_allowed,
-        )
-
-    self_heads, self_totals = lax.map(self_forward, head_range)
-    attn_self = join_heads(self_heads).astype(jnp.bfloat16)
+    attn_self, self_totals = attention_forward(
+        first, decoder_lengths, decoder_lengths, query_self, self_pairs[0], self_pairs[1],
+        distance_table, head_width, rows,
+    )
     middle_one = tokens + jnp.dot(attn_self, self_out_full, preferred_element_type=jnp.float32)
     normed_cross, pull_cross = jax.vjp(rms_norm, middle_one, norm_gains[1])
     input_cross = normed_cross.astype(jnp.bfloat16)
@@ -197,17 +397,10 @@
     )
     memory_pairs = lax.all_gather(jnp.stack([key_memory, value_memory]), "mem", axis=1, tiled=True)
 
-    def cross_forward(head_index):
-        return head_forward(
-            head_columns(query_cross, head_index, head_width),
-            head_columns(memory_pairs[0], head_index, head_width),
-            head_columns(memory_pairs[1], head_index, head_width),
-            0.0,
-            cross_allowed,
-        )
-
-    cross_heads, cross_totals = lax.map(cross_forward, head_range)
-    attn_cross = join_heads(cross_heads).astype(jnp.bfloat16)
+    attn_cross, cross_totals = attention_forward(
+        first, decoder_lengths, memory_lengths, query_cross, memory_pairs[0], memory_pairs[1],
+        None, head_width, 512,
+    )
     middle_two = middle_one + jnp.dot(
         attn_cross, cross_out_full, preferred_element_type=jnp.float32
     )
@@ -250,28 +443,16 @@
         "re,de->rd", grad_branch_two, cross_out_full, preferred_element_type=jnp.float32
     ).astype(jnp.bfloat16)
 
-    def cross_backward(head_index):
-        gradients = head_backward(
-            head_columns(query_cross, head_index, head_width),
-            head_columns(memory_pairs[0], head_index, head_width),
-            head_columns(memory_pairs[1], head_index, head_width),
-            head_columns(grad_attn_cross, head_index, head_width),
-            cross_totals[head_index],
-            0.0,
-            cross_allowed,
-        )
-        return (gradients[0], gradients[1], gradients[2])
-
-    cross_query_grads, cross_key_grads, cross_value_grads = lax.map(cross_backward, head_range)
+    grad_query_cross, cross_key_grads, cross_value_grads = attention_backward(
+        first, decoder_lengths, memory_lengths, query_cross, memory_pairs[0], memory_pairs[1],
+        grad_attn_cross, cross_totals, None, head_width, 512,
+    )
     own_memory = lax.psum_scatter(
-        jnp.stack([join_heads(cross_key_grads), join_heads(cross_value_grads)]).astype(
-            jnp.bfloat16
-        ),
+        jnp.stack([cross_key_grads, cross_value_grads]),
         "mem",
         scatter_dimension=1,
         tiled=True,
     )
-    grad_query_cross = join_heads(cross_query_grads).astype(jnp.bfloat16)
     grad_cross = jnp.stack(
         [
             jnp.einsum(
@@ -301,31 +482,22 @@
         "re,de->rd", grad_branch_one, self_out_full, preferred_element_type=jnp.float32
     ).astype(jnp.bfloat16)
 
-    def self_backward(head_index):
-        bias_rows = bucket_bias(head_tables[head_index], bucket_index)
-        gradients = head_backward(
-            head_columns(query_self, head_index, head_width),
-            head_columns(self_pairs[0], head_index, head_width),
-            head_columns(self_pairs[1], head_index, head_width),
-            head_columns(grad_attn_self, head_index, head_width),
-            self_totals[head_index],
-            bias_rows,
-            self_allowed,
-        )
-        table_grad = bucket_sums(gradients[3], bucket_index, bucket_count)
-        return (gradients[0], gradients[1], gradients[2], table_grad)
-
-    self_query_grads, self_key_grads, self_value_grads, table_grads = lax.map(
-        self_backward, head_range
-    )
+    grad_query_self, self_key_grads, self_value_grads, diagonals = attention_backward(
+        first, decoder_lengths, decoder_lengths, query_self, self_pairs[0], self_pairs[1],
+        grad_attn_self, self_totals, distance_table, head_width, rows,
+    )
+    diagonals = diagonals.reshape(head_count, key_count // rows, 2 * rows)
+    by_distance = jnp.zeros((head_count, key_count + rows), F32)
+    for delta in range(key_count // rows):
+        here = slice(delta * rows, delta * rows + 2 * rows)
+        by_distance = by_distance.at[:, here].add(diagonals[:, delta])
+    bias_partial = jnp.einsum("db,hd->bh", one_hot, by_distance[:, rows:], precision=EXACT)
     own_self = lax.psum_scatter(
-        jnp.stack([join_heads(self_key_grads), join_heads(self_value_grads)]).astype(jnp.bfloat16),
+        jnp.stack([self_key_grads, self_value_grads]),
         "mem",
         scatter_dimension=1,
         tiled=True,
     )
-    grad_query_self = join_heads(self_query_grads).astype(jnp.bfloat16)
-    bias_partial = table_grads.T
     grad_self = jnp.stack(
         [
             jnp.einsum(

time: 2090 us -> 1220 us (0.58)
  other arithmetic: 481 us -> 36.4 us
  matrix products: 534 us -> 115 us
  local copies, waits for them, and re-layouts: 283 us -> 31.6 us
  waiting for transfers between devices: 574 us -> 783 us
  Pallas kernels: 0 us -> 145 us
  loops' own time: 99.8 us -> 0 us
    reduce_sum x65 -> x0, other arithmetic: 439 us -> none  [the longest x24 306 us: bucket_bias(): jnp.sum(jnp.where(bucket_index[None, :, :] == bucket_range[:, None, None]...]
    dot_general x168 -> x2, matrix products: 420 us -> 0.83 us  [the longest x1 0.45 us: shards(): jnp.einsum('db,bh->hd', one_hot, position_bias, precision=EXACT)]
    slice x48 -> x1, local copies, waits for them, and re-layouts: 199 us -> 0.07 us  [shards(): by_distance = by_distance.at[:, here].add(diagonals[:, delta])]
    pallas_call x0 -> x4, Pallas kernels: none -> 145 us  [the longest x2 84.5 us: attention_backward(): pl.pallas_call(functools.partial(backward_kernel, causal, step, width), g...]
    another operation x4 -> x0, loops' own time: 99.8 us -> none  [the longest x1 31.6 us: shards(): lax.map(self_backward, head_range)]
    all_gather x1, waiting for transfers between devices: 0.01 us -> 75.2 us  [shards(): lax.all_gather(jnp.stack([key_memory, value_memory]), 'mem', axis=1, tile...]
    all_gather x1, waiting for transfers between devices: 0.02 us -> 51 us  [shards(): lax.all_gather(within[4], 'batch', axis=1, tiled=True)]
    dynamic_slice x72 -> x0, local copies, waits for them, and re-layouts: 36.7 us -> none  [the longest x48 27.9 us: shards(): self_heads, self_totals = lax.map(self_forward, head_range)]
  transfers between devices with their start and end apart: 22 -> 22, of which waited for: 14 -> 18; matrix products, arithmetic and copies ran while one was open for 27% -> 12% of each run, Pallas kernels for 0% -> 5%
where the time goes in v1:
time: 1220 us; the launch traced here: 1210 us
  waiting for transfers between devices  783 us (64%)
  Pallas kernels  145 us (12%)
  matrix products  115 us (9%)
  blocking collectives  84.2 us (7%)
  other arithmetic  36.4 us (3%)
  local copies, waits for them, and re-layouts  31.6 us (3%)
  between operations  15.2 us (1%)
    reduce_scatter x1, waiting for transfers between devices, shards(): lax.psum_scatter(grad_expand.astype(jnp.bfloat16), 'batch', scatter_dimen...  86.8 us
    pallas_call x2, Pallas kernels, attention_backward(): pl.pallas_call(functools.partial(backward_kernel, causal, step, width), g...  84.5 us
    all_gather x1, waiting for transfers between devices, shards(): lax.all_gather(jnp.stack([key_memory, value_memory]), 'mem', axis=1, tile...  75.2 us
    reduce_scatter x1, waiting for transfers between devices, shards(): lax.psum_scatter(jnp.stack([cross_key_grads, cross_value_grads]), 'mem',...  73.7 us
    reduce_scatter x1, waiting for transfers between devices, shards(): lax.psum_scatter(grad_contract.astype(jnp.bfloat16), 'batch', scatter_dim...  67.6 us
    reduce_scatter x1, waiting for transfers between devices, shards(): lax.psum_scatter(grad_self.astype(jnp.bfloat16), 'batch', scatter_dimensi...  66.9 us
    pallas_call x2, Pallas kernels, attention_forward(): pl.pallas_call(functools.partial(forward_kernel, causal, step, width), gr...  60.8 us
    reduce_scatter x1, waiting for transfers between devices, shards(): lax.psum_scatter(grad_cross_out.astype(jnp.bfloat16), 'batch', scatter_di...  59.4 us
  transfers between devices with their start and end apart: 22, of which 18 were waited for; matrix products, arithmetic and copies ran while one was open for 12% of the time, Pallas kernels for 5%

profile of v1, /device:TPU:0, one launch (start us, length us, event | category | flops | bytes accessed | tf_op | source)
XLA Modules:
  0.0 1211.6 jit_solution(14124382894339254070)
XLA Ops:
  7.3 8.6 all_gather.42
  16.0 5.7 all_gather.47
  22.9 40.7 %all-gather.9.cloned.1.call-done = bf16[3,768,768]{2,1,0:T(8,128)(2,1)} async-done(((bf16[3,48,768]{2,1,0:T(8,128)(2,1)}), bf16[3,768,768]{2,1,0:T(8,128)(2,1)}) %all-gather.9.cloned.1.call-update) | async-done | bytes 3538960 | tf_op jit(solution)/shard_map/all_gather | solution.py:352
  63.6 2.1 fusion.61
  65.7 2.1 fusion.60
  69.9 4.7 all_gather.45
  74.7 37.5 %all-gather.15.cloned.1.call-done = bf16[3,768,768]{2,1,0:T(8,128)(2,1)} async-done(((bf16[3,48,768]{2,1,0:T(8,128)(2,1)}), bf16[3,768,768]{2,1,0:T(8,128)(2,1)}) %all-gather.15.cloned.1.call-update) | async-done | bytes 3538960 | tf_op jit(solution)/shard_map/all_gather | solution.py:354
  112.2 2.7 fusion.45
  114.8 2.7 fusion.42
  120.2 5.3 all_gather.50
  125.6 12.1 all_gather.52
  137.8 7.6 all_gather.54
  146.7 3.0 convolution_convert_fusion.16.q_ref
  149.6 15.3 %all-gather.11.cloned.1.call-done = bf16[2,1024,768]{2,1,0:T(8,128)(2,1)} async-done(((bf16[2,512,768]{2,1,0:T(8,128)(2,1)}), bf16[2,1024,768]{2,1,0:T(8,128)(2,1)}) %all-gather.11.cloned.1.call-update) | async-done | bytes 3145744 | tf_op jit(solution)/shard_map/all_gather | solution.py:379
  164.9 3.7 slice_bitcast_fusion.10
  168.7 18.2 %self_forward.1 = (bf16[512,768]{1,0:T(8,128)(2,1)}, f32[6,2,1,512]{3,2,1,0:T(1,128)}) custom-call(s32[1]{0:T(128)} %bitcast.1.first_ref, s32[1,4]{1,0:T(1,128)} %k_sizes.7, s32[1,4]{1,0:T(1,128)} %k_sizes.7, bf16[512,768]{1,0:T(8,128)(2,1)} %convolution_convert_fusion.16.q_ref, bf16[1024,768]{1,0:T(8,128)(2,1)} %get-tuple-element.98.k_ref, ...), custom_call_target="tpu_custom_call" | custom-call | tf_op jit(solution)/shard_map/self_forward/pallas_call | solution.py:251
  186.8 18.3 %all-gather.13.cloned.1.call-done = bf16[768,768]{1,0:T(8,128)(2,1)} async-done(((bf16[48,768]{1,0:T(8,128)(2,1)}), bf16[768,768]{1,0:T(8,128)(2,1)}) %all-gather.13.cloned.1.call-update) | async-done | bytes 1179664 | tf_op jit(solution)/shard_map/all_gather | solution.py:353
  205.2 2.6 multiply_reduce_fusion.5
  207.8 3.6 convolution_convert_fusion.13.q_ref
  211.4 75.2 %all-gather.17.cloned.1.call-done = bf16[2,2048,768]{2,1,0:T(8,128)(2,1)} async-done(((bf16[2,1024,768]{2,1,0:T(8,128)(2,1)}), bf16[2,2048,768]{2,1,0:T(8,128)(2,1)}) %all-gather.17.cloned.1.call-update) | async-done | bytes 6291472 | tf_op jit(solution)/shard_map/all_gather | solution.py:398
  286.6 5.9 slice_bitcast_fusion.2
  292.5 42.7 %cross_forward.1 = (bf16[512,768]{1,0:T(8,128)(2,1)}, f32[6,2,1,512]{3,2,1,0:T(1,128)}) custom-call(s32[1]{0:T(128)} %bitcast.1.first_ref, s32[1,4]{1,0:T(1,128)} %k_sizes.7, s32[1,4]{1,0:T(1,128)} %k_sizes.6, bf16[512,768]{1,0:T(8,128)(2,1)} %convolution_convert_fusion.13.q_ref, bf16[2048,768]{1,0:T(8,128)(2,1)} %get-tuple-element.96.k_ref, ...), custom_call_target="tpu_custom_call" | custom-call | tf_op jit(solution)/shard_map/cross_forward/pallas_call | solution.py:251
  335.2 3.0 multiply_reduce_fusion.4
  339.5 51.0 %all-gather.21.cloned.1.call-done = bf16[2,768,2048]{2,1,0:T(8,128)(2,1)} async-done(((bf16[2,48,2048]{2,1,0:T(8,128)(2,1)}), bf16[2,768,2048]{2,1,0:T(8,128)(2,1)}) %all-gather.21.cloned.1.call-update) | async-done | bytes 6291472 | tf_op jit(solution)/shard_map/all_gather | solution.py:356
  390.5 6.1 fusion.10
  396.7 3.9 fusion.12
  400.5 36.1 %all-gather.23.cloned.1.call-done = bf16[2048,768]{1,0:T(8,128)(2,1)} async-done(((bf16[128,768]{1,0:T(8,128)(2,1)}), bf16[2048,768]{1,0:T(8,128)(2,1)}) %all-gather.23.cloned.1.call-update) | async-done | bytes 3145744 | tf_op jit(solution)/shard_map/all_gather | solution.py:357
  436.6 9.3 multiply_convert_fusion
  446.0 5.2 fusion.9
  451.3 4.1 multiply_reduce_fusion
  459.1 55.1 %cross_backward.1 = (bf16[512,768]{1,0:T(8,128)(2,1)}, bf16[2048,768]{1,0:T(8,128)(2,1)}, bf16[2048,768]{1,0:T(8,128)(2,1)}) custom-call(s32[1]{0:T(128)} %bitcast.1.first_ref, s32[1,4]{1,0:T(1,128)} %k_sizes.7, s32[1,4]{1,0:T(1,128)} %k_sizes.6, bf16[512,768]{1,0:T(8,128)(2,1)} %convolution_convert_fusion.13.q_ref, ...), custom_call_target="tpu_custom_call" | custom-call | tf_op jit(solution)/shard_map/cross_backward/pallas_call | solution.py:305
  514.2 2.6 multiply_reduce_fusion.1
  519.9 29.4 %self_backward.1 = (bf16[512,768]{1,0:T(8,128)(2,1)}, bf16[1024,768]{1,0:T(8,128)(2,1)}, bf16[1024,768]{1,0:T(8,128)(2,1)}, f32[6,2,4,512]{3,2,1,0:T(4,128)}) custom-call(s32[1]{0:T(128)} %bitcast.1.first_ref, s32[1,4]{1,0:T(1,128)} %k_sizes.7, s32[1,4]{1,0:T(1,128)} %k_sizes.7, bf16[512,768]{1,0:T(8,128)(2,1)} %convolution_convert_fusion.16.q_ref, ...), custom_call_target="tpu_custom_call" | custom-call | tf_op jit(solution)/shard_map/self_backward/pallas_call | solution.py:305
  549.3 3.8 pad_maximum_fusion.5
  553.2 3.0 convolution_convert_fusion.7
  556.3 3.5 convolution_convert_fusion.5
  559.8 5.3 convolution_convert_fusion
  565.2 3.8 fusion.8
  570.9 3.2 pad_maximum_fusion.1
  574.2 3.8 fusion.49
  577.9 34.4 %reduce-scatter.25.cloned.1.call-done = bf16[2,512,768]{2,1,0:T(8,128)(2,1)} async-done(((bf16[2,1024,768]{2,1,0:T(8,128)(2,1)}), bf16[2,512,768]{2,1,0:T(8,128)(2,1)}) %reduce-scatter.25.cloned.1.call-update) | async-done | bytes 1572880 | tf_op jit(solution)/shard_map/reduce_scatter | solution.py:495
  612.3 2.4 fusion.51
  618.1 6.1 pad_maximum_fusion
  624.2 50.1 %reduce-scatter.31.cloned.1.call-done = bf16[48,768]{1,0:T(8,128)(2,1)} async-done(((bf16[768,768]{1,0:T(8,128)(2,1)}), bf16[48,768]{1,0:T(8,128)(2,1)}) %reduce-scatter.31.cloned.1.call-update) | async-done | bytes 73744 | tf_op jit(solution)/shard_map/reduce_scatter | solution.py:524
  676.0 59.4 %reduce-scatter.35.cloned.1.call-done = bf16[48,768]{1,0:T(8,128)(2,1)} async-done(((bf16[768,768]{1,0:T(8,128)(2,1)}), bf16[48,768]{1,0:T(8,128)(2,1)}) %reduce-scatter.35.cloned.1.call-update) | async-done | bytes 73744 | tf_op jit(solution)/shard_map/reduce_scatter | solution.py:530
  737.2 67.6 %reduce-scatter.41.cloned.1.call-done = bf16[128,768]{1,0:T(8,128)(2,1)} async-done(((bf16[2048,768]{1,0:T(8,128)(2,1)}), bf16[128,768]{1,0:T(8,128)(2,1)}) %reduce-scatter.41.cloned.1.call-update) | async-done | bytes 196624 | tf_op jit(solution)/shard_map/reduce_scatter | solution.py:536
  806.6 86.8 %reduce-scatter.37.cloned.1.call-done = bf16[2,48,2048]{2,1,0:T(8,128)(2,1)} async-done(((bf16[2,768,2048]{2,1,0:T(8,128)(2,1)}), bf16[2,48,2048]{2,1,0:T(8,128)(2,1)}) %reduce-scatter.37.cloned.1.call-update) | async-done | bytes 393232 | tf_op jit(solution)/shard_map/reduce_scatter | solution.py:533
  893.8 3.5 fusion.52
  897.4 66.9 %reduce-scatter.29.cloned.1.call-done = bf16[3,48,768]{2,1,0:T(8,128)(2,1)} async-done(((bf16[3,768,768]{2,1,0:T(8,128)(2,1)}), bf16[3,48,768]{2,1,0:T(8,128)(2,1)}) %reduce-scatter.29.cloned.1.call-update) | async-done | bytes 221200 | tf_op jit(solution)/shard_map/reduce_scatter | solution.py:521
  966.4 2.2 reshape.284
  968.7 73.7 %reduce-scatter.27.cloned.1.call-done = bf16[2,1024,768]{2,1,0:T(8,128)(2,1)} async-done(((bf16[2,2048,768]{2,1,0:T(8,128)(2,1)}), bf16[2,1024,768]{2,1,0:T(8,128)(2,1)}) %reduce-scatter.27.cloned.1.call-update) | async-done | bytes 3145744 | tf_op jit(solution)/shard_map/reduce_scatter | solution.py:450
  1042.4 3.0 fusion.53
  1053.4 3.6 fusion.63
  1057.0 4.6 fusion.62
  1063.2 6.6 reduce-scatter.49.cloned.1.call-done
  1071.5 12.1 reduce-scatter.51.cloned.1.call-done
  1085.3 2.5 fusion.64
  1087.8 3.6 fusion.20
  1091.4 40.1 %all-reduce.2 = (f32[3,768]{1,0:T(4,128)}, f32[32,12]{0,1:T(8,128)}) all-reduce(f32[3,768]{1,0:T(4,128)S(1)} %pad_maximum_fusion.7, f32[32,12]{0,1:T(8,128)S(1)} %fusion.73), channel_id=1, replica_groups=mesh['batch'=16,'mem'=2] {'batch','mem'}, use_global_device_ids=true, to_apply=%region_11.12 | all-reduce | flops 2688 | bytes 21504 | tf_op jit(solution)/shard_map/psum | solution.py:517
  1131.5 3.3 fusion.29
  1138.6 4.9 fusion.59
  1143.4 44.5 %reduce-scatter.33.cloned.1.call-done = bf16[3,48,768]{2,1,0:T(8,128)(2,1)} async-done(((bf16[3,768,768]{2,1,0:T(8,128)(2,1)}), bf16[3,48,768]{2,1,0:T(8,128)(2,1)}) %reduce-scatter.33.cloned.1.call-update) | async-done | bytes 221200 | tf_op jit(solution)/shard_map/reduce_scatter | solution.py:527
  1190.5 5.8 add_bitcast_fusion
  1196.3 6.3 reduce-scatter.47.cloned.1.call-done
  (172 shorter events, 50.0 us)
Async XLA Ops:
  7.2 105.0 %copy-start = (bf16[1,1024,768]{2,1,0:T(8,128)(2,1)S(1)}, bf16[1,1024,768]{2,1,0:T(8,128)(2,1)}, u32[]{:S(2)}) copy-start(bf16[1,1024,768]{2,1,0:T(8,128)(2,1)} %param.23) | copy-start | bytes 4718596
  7.2 15.4 %copy-start.8 = (bf16[1,512,768]{2,1,0:T(8,128)(2,1)S(1)}, bf16[1,512,768]{2,1,0:T(8,128)(2,1)}, u32[]{:S(2)}) copy-start(bf16[1,512,768]{2,1,0:T(8,128)(2,1)} %param.22) | copy-start | bytes 2359300
  7.2 56.4 %all-gather.9.cloned.1.call-start = ((), (), s32[]{:S(2)}) async-start(), calls=%async_computation.14 | async-start | bytes 3760128 | tf_op jit(solution)/shard_map/all_gather | solution.py:352
  15.9 96.2 %all-gather.15.cloned.1.call-start = ((), (), s32[]{:S(2)}) async-start(), calls=%async_computation.17 | async-start | bytes 3760128 | tf_op jit(solution)/shard_map/all_gather | solution.py:354
  21.7 143.2 %all-gather.11.cloned.1.call-start = ((), (), s32[]{:S(2)}) async-start(), calls=%async_computation.15 | async-start | bytes 4718592 | tf_op jit(solution)/shard_map/all_gather | solution.py:379
  69.1 0.8 copy-start.24
  69.2 136.0 %all-gather.13.cloned.1.call-start = ((), (), s32[]{:S(2)}) async-start(), calls=%async_computation.16 | async-start | bytes 1253376 | tf_op jit(solution)/shard_map/all_gather | solution.py:353
  74.7 211.9 %all-gather.17.cloned.1.call-start = ((), (), s32[]{:S(2)}) async-start(), calls=%async_computation.18 | async-start | bytes 9437184 | tf_op jit(solution)/shard_map/all_gather | solution.py:398
  119.4 0.8 copy-start.25
  119.4 6.2 copy-start.21
  119.4 18.4 %copy-start.23 = (bf16[128,384]{1,0:T(8,128)(2,1)S(1)}, bf16[128,384]{1,0:T(8,128)(2,1)}, u32[]{:S(2)}) copy-start(bf16[128,384]{1,0:T(8,128)(2,1)} %param.34) | copy-start | bytes 294916
  119.5 26.0 %copy-start.28 = (f32[32,12]{0,1:T(8,128)S(1)}, f32[32,12]{0,1:T(8,128)}, u32[]{:S(2)}) copy-start(f32[32,12]{0,1:T(8,128)} %param.28) | copy-start | bytes 4612
  119.5 26.0 %copy-start.29 = (s32[1024]{0:T(1024)S(1)}, s32[1024]{0:T(1024)}, u32[]{:S(2)}) copy-start(s32[1024]{0:T(1024)} %param.26) | copy-start | bytes 12292
  119.5 215.7 %all-gather.19.cloned.1.call-start = ((), (), s32[]{:S(2)}) async-start(), calls=%async_computation.19 | async-start | bytes 1253376 | tf_op jit(solution)/shard_map/all_gather | solution.py:355
  125.6 264.9 %all-gather.21.cloned.1.call-start = ((), (), s32[]{:S(2)}) async-start(), calls=%async_computation.20 | async-start | bytes 6684672 | tf_op jit(solution)/shard_map/all_gather | solution.py:356
  137.7 298.9 %all-gather.23.cloned.1.call-start = ((), (), s32[]{:S(2)}) async-start(), calls=%async_computation.21 | async-start | bytes 3342336 | tf_op jit(solution)/shard_map/all_gather | solution.py:357
  145.4 466.8 %reduce-scatter.25.cloned.1.call-start = ((), (), s32[]{:S(2)}) async-start(), calls=%async_computation.22 | async-start | bytes 4718592 | tf_op jit(solution)/shard_map/reduce_scatter | solution.py:495
  207.8 3.6 copy-start.5
  338.2 113.0 %copy-start.3 = (f32[512,768]{1,0:T(8,128)}, f32[512,768]{1,0:T(8,128)S(1)}, u32[]{:S(2)}) copy-start(f32[512,768]{1,0:T(8,128)S(1)} %get-tuple-element.106) | copy-start | bytes 4718596
  390.5 6.2 copy-start.15
  390.5 6.2 copy-start.26
  446.0 5.3 copy-start.31
  446.0 5.3 copy-start.30
  451.2 4.2 copy-start.18
  455.4 1.9 copy-start.14
  457.4 1.8 copy-start.1
  459.1 55.1 %copy-start.6 = (f32[512,768]{1,0:T(8,128)S(1)}, f32[512,768]{1,0:T(8,128)}, u32[]{:S(2)}) copy-start(f32[512,768]{1,0:T(8,128)} %copy-done.5) | copy-start | bytes 4718596
  514.2 2.7 copy-start.2
  514.2 2.7 copy-start.7
  516.9 1.3 copy-start.27
  553.2 121.1 %reduce-scatter.31.cloned.1.call-start = ((), (), s32[]{:S(2)}) async-start(), calls=%async_computation.25 | async-start | bytes 1253376 | tf_op jit(solution)/shard_map/reduce_scatter | solution.py:524
  556.2 179.2 %reduce-scatter.35.cloned.1.call-start = ((), (), s32[]{:S(2)}) async-start(), calls=%async_computation.27 | async-start | bytes 1253376 | tf_op jit(solution)/shard_map/reduce_scatter | solution.py:530
  559.8 245.0 %reduce-scatter.41.cloned.1.call-start = ((), (), s32[]{:S(2)}) async-start(), calls=%async_computation.30 | async-start | bytes 3342336 | tf_op jit(solution)/shard_map/reduce_scatter | solution.py:536
  565.2 328.2 %reduce-scatter.37.cloned.1.call-start = ((), (), s32[]{:S(2)}) async-start(), calls=%async_computation.28 | async-start | bytes 6684672 | tf_op jit(solution)/shard_map/reduce_scatter | solution.py:533
  565.2 3.8 copy-start.16
  565.2 3.8 copy-start.32
  574.1 390.2 %reduce-scatter.29.cloned.1.call-start = ((), (), s32[]{:S(2)}) async-start(), calls=%async_computation.24 | async-start | bytes 3760128 | tf_op jit(solution)/shard_map/reduce_scatter | solution.py:521
  612.3 2.4 copy-start.9
  612.3 2.4 copy-start.19
  614.7 1.3 copy-start.13
  618.0 424.4 %reduce-scatter.27.cloned.1.call-start = ((), (), s32[]{:S(2)}) async-start(), calls=%async_computation.23 | async-start | bytes 9437184 | tf_op jit(solution)/shard_map/reduce_scatter | solution.py:450
  624.2 437.5 %reduce-scatter.45.cloned.1.call-start = ((), (), s32[]{:S(2)}) async-start(), calls=%async_computation.32 | async-start | bytes 294912
  676.0 393.9 %reduce-scatter.49.cloned.1.call-start = ((), (), s32[]{:S(2)}) async-start(), calls=%async_computation.34 | async-start | bytes 294912
  737.1 346.5 %reduce-scatter.51.cloned.1.call-start = ((), (), s32[]{:S(2)}) async-start(), calls=%async_computation.35 | async-start | bytes 294912
  806.5 328.3 %reduce-scatter.39.cloned.1.call-start = ((), (), s32[]{:S(2)}) async-start(), calls=%async_computation.29 | async-start | bytes 589824 | tf_op jit(solution)/shard_map/reduce_scatter | solution.py:553
  893.4 243.1 %reduce-scatter.43.cloned.1.call-start = ((), (), s32[]{:S(2)}) async-start(), calls=%async_computation.31 | async-start | bytes 589824
  968.6 219.3 %reduce-scatter.33.cloned.1.call-start = ((), (), s32[]{:S(2)}) async-start(), calls=%async_computation.26 | async-start | bytes 3760128 | tf_op jit(solution)/shard_map/reduce_scatter | solution.py:527
  1042.4 3.0 copy-start.17
  1045.4 1.5 copy-start.11
  1048.9 2.0 copy-start.22
  1048.9 153.6 %reduce-scatter.47.cloned.1.call-start = ((), (), s32[]{:S(2)}) async-start(), calls=%async_computation.33 | async-start | bytes 589824
  1053.4 3.6 copy-start.4
  1053.4 3.6 copy-start.33
  1084.6 3.2 copy-start.20
  1085.3 2.5 copy-start.10
  1085.3 2.5 copy-start.12
Sparse Core Ops, SparseCore 0:
  16.0 47.5 all-gather.8
  65.9 46.2 all-gather.14
  114.3 50.6 all-gather.10
  167.1 38.0 all-gather.12
  207.2 79.3 all-gather.16
  288.7 38.4 all-gather.18
  329.4 61.0 all-gather.20
  392.8 43.7 all-gather.22
  553.3 58.9 reduce-scatter.24
  616.2 58.0 reduce-scatter.30
  678.3 57.0 reduce-scatter.34
  739.5 65.1 reduce-scatter.40
  809.2 84.0 reduce-scatter.36
  897.1 67.1 reduce-scatter.28
  966.5 75.9 reduce-scatter.26
  1045.2 10.9 reduce-scatter.44
  1058.9 10.9 reduce-scatter.48
  1072.6 10.9 reduce-scatter.50
  1085.9 13.1 reduce-scatter.38
  1101.8 13.5 reduce-scatter.42
  1119.8 68.0 reduce-scatter.32
  1190.6 11.9 reduce-scatter.46

commit v2 on v1

v2 whole, which is shorter than its diff:
```python
import functools
import math

import jax
import jax.numpy as jnp
from jax import lax
from jax.experimental import pallas as pl
from jax.experimental.pallas import tpu as pltpu
from jax.sharding import PartitionSpec as P

EPSILON = 1e-06
NEGATIVE = -1e30
F32 = jnp.float32
BF16 = jnp.bfloat16
EXACT = lax.Precision.HIGHEST
GELU_SCALE = (2 / math.pi) ** 0.5
GELU_CUBE = 0.044715
LONG = pl.CostEstimate(flops=20_000_000_000, bytes_accessed=1_000, transcendentals=0)
MEDIUM = pl.CostEstimate(flops=6_000_000_000, bytes_accessed=1_000, transcendentals=0)
BRIEF = pl.CostEstimate(flops=2_000_000_000, bytes_accessed=1_000, transcendentals=0)
SHORT = pl.CostEstimate(flops=100_000, bytes_accessed=1_000, transcendentals=0)
NT = (((1,), (1,)), ((), ()))
NN = (((1,), (0,)), ((), ()))


def rms_norm(values, gain_row):
    return (
        values * lax.rsqrt(jnp.mean(values * values, axis=-1, keepdims=True) + EPSILON) * gain_row
    )


def activate(gate_part, up_part):
    return jax.nn.gelu(gate_part, approximate=True) * up_part


def dot(left, right, dims):
    return lax.dot_general(left, right, dims, preferred_element_type=F32)


def bounds_of(sizes_ref):
    edges = [jnp.int32(0)]
    for slot in range(sizes_ref.shape[1]):
        edges.append(edges[-1] + sizes_ref[0, slot])
    return edges


def pick(place, edges, values):
    chosen = jnp.zeros_like(place) + values[0]
    for slot in range(1, len(edges) - 1):
        chosen = jnp.where(place >= edges[slot], values[slot], chosen)
    return chosen


def stack_heads(block, width):
    lane = lax.broadcasted_iota(jnp.int32, block.shape, 1)
    zero = jnp.zeros_like(block)
    return jnp.concatenate(
        [jnp.where(lane < width, block, zero), jnp.where(lane < width, zero, block)], axis=0
    )


def transposed_blocks(source_ref, scratch, step):
    for index in range(scratch.shape[0]):
        scratch[index] = source_ref[index * step : (index + 1) * step, :].T


def ranges(first, rows, q_edges, k_edges, causal, step):
    last = first + rows - 1
    starts, ends = k_edges[:-1], k_edges[1:]
    low_start = pick(first, q_edges, starts)
    high_start = pick(last, q_edges, starts)
    low_end = pick(first, q_edges, ends)
    high_end = pick(last, q_edges, ends)
    if causal:
        low_end = jnp.minimum(low_end, first + 1)
        high_end = jnp.minimum(high_end, last + 1)
    low = low_start // step
    high = (high_end + step - 1) // step
    clear_low = (high_start + step - 1) // step
    clear_high = low_end // step
    return low, high, clear_low, clear_high


def limits(first, rows, q_edges, k_edges, causal):
    place = lax.rem(lax.broadcasted_iota(jnp.int32, (1, 2 * rows), 1), rows) + first
    begin = pick(place, q_edges, k_edges[:-1])
    end = pick(place, q_edges, k_edges[1:])
    if causal:
        end = jnp.minimum(end, place + 1)
    return begin, end


def toeplitz(table_ref, tiles, rows):
    for delta in range(tiles.shape[0]):
        for head in range(2):
            base = table_ref[0, head : head + 1, delta * rows : (delta + 2) * rows]
            wide = jnp.broadcast_to(base, (rows, 2 * rows))
            wide = pltpu.roll(wide, 0, 1, stride=1, stride_axis=0)
            tiles[delta, :, head * rows : (head + 1) * rows] = wide[:, rows:]


def masked(scores, index, step, begin, end):
    place = lax.broadcasted_iota(jnp.int32, scores.shape, 0) + index * step
    return jnp.where((place >= begin) & (place < end), scores, NEGATIVE)


def forward_kernel(
    causal, step, width, first_ref, q_sizes, k_sizes, q_ref, k_ref, v_ref, *rest
):
    if causal:
        table_ref, out_ref, total_ref, value_t, scores, tiles = rest
    else:
        out_ref, total_ref, value_t, scores = rest
    blocks, rows = total_ref.shape[1], total_ref.shape[3] // 2
    q_edges = bounds_of(q_sizes)
    k_edges = bounds_of(k_sizes)
    transposed_blocks(v_ref, value_t, step)
    if causal:
        toeplitz(table_ref, tiles, rows)
    for block in range(blocks):
        first = first_ref[0] + block * rows
        low, high, clear_low, clear_high = ranges(first, rows, q_edges, k_edges, causal, step)
        begin, end = limits(first, rows, q_edges, k_edges, causal)
        queries = stack_heads(q_ref[block * rows : (block + 1) * rows, :], width)

        def measure(index, top):
            keys = k_ref[pl.ds(pl.multiple_of(index * step, step), step), :]
            block_scores = dot(keys, queries, NT)
            if causal:
                block_scores = block_scores + tiles[first // rows - index]
            clear = (index >= clear_low) & (index < clear_high)

            def plain():
                scores[index] = block_scores
                return jnp.max(block_scores, axis=0, keepdims=True)

            def cut():
                kept = masked(block_scores, index, step, begin, end)
                scores[index] = kept
                return jnp.max(kept, axis=0, keepdims=True)

            return jnp.maximum(top, lax.cond(clear, plain, cut))

        top = lax.fori_loop(low, high, measure, jnp.full((1, 2 * rows), NEGATIVE, F32))

        def gather(index, carry):
            total, out_a, out_b = carry
            weights = jnp.exp(scores[index] - top)
            total = total + jnp.sum(weights, axis=0, keepdims=True)
            rounded = weights.astype(BF16)
            out_a = out_a + dot(value_t[index, :width, :], rounded[:, :rows], NN)
            out_b = out_b + dot(value_t[index, width:, :], rounded[:, rows:], NN)
            return total, out_a, out_b

        zero = jnp.zeros((width, rows), F32)
        total, out_a, out_b = lax.fori_loop(
            low, high, gather, (jnp.zeros((1, 2 * rows), F32), zero, zero)
        )
        joined = jnp.concatenate([out_a / total[:, :rows], out_b / total[:, rows:]], axis=0)
        out_ref[block * rows : (block + 1) * rows, :] = joined.T.astype(BF16)
        total_ref[0, block] = top + jnp.log(total)


def backward_kernel(
    causal, step, width, first_ref, q_sizes, k_sizes, q_ref, k_ref, v_ref, g_ref, total_ref, *rest
):
    if causal:
        table_ref, dq_ref, dk_ref, dv_ref, diag_ref, key_t, probs, grads, dk, dv, tiles, sums = rest
    else:
        dq_ref, dk_ref, dv_ref, key_t, probs, grads, dk, dv = rest
    blocks, rows = total_ref.shape[1], total_ref.shape[3] // 2
    q_edges = bounds_of(q_sizes)
    k_edges = bounds_of(k_sizes)
    transposed_blocks(k_ref, key_t, step)
    dk[...] = jnp.zeros_like(dk)
    dv[...] = jnp.zeros_like(dv)
    if causal:
        toeplitz(table_ref, tiles, rows)
        sums[...] = jnp.zeros_like(sums)
    for block in range(blocks):
        first = first_ref[0] + block * rows
        low, high, clear_low, clear_high = ranges(first, rows, q_edges, k_edges, causal, step)
        begin, end = limits(first, rows, q_edges, k_edges, causal)
        queries = stack_heads(q_ref[block * rows : (block + 1) * rows, :], width)
        targets = stack_heads(g_ref[block * rows : (block + 1) * rows, :], width)
        total = total_ref[0, block]

        def measure(index, inner):
            here = pl.ds(pl.multiple_of(index * step, step), step)
            block_scores = dot(k_ref[here, :], queries, NT)
            if causal:
                block_scores = block_scores + tiles[first // rows - index]
            weights = jnp.exp(block_scores - total)
            clear = (index >= clear_low) & (index < clear_high)
            place = lax.broadcasted_iota(jnp.int32, weights.shape, 0) + index * step
            weights = jnp.where((place >= begin) & (place < end), weights, 0.0)
            pulled = dot(v_ref[here, :], targets, NT)
            probs[index] = weights
            grads[index] = pulled
            dv[here, :] += dot(weights.astype(BF16), targets, NN)
            return inner + jnp.sum(weights * pulled, axis=0, keepdims=True)

        inner = lax.fori_loop(low, high, measure, jnp.zeros((1, 2 * rows), F32))

        def gather(index, carry):
            out_a, out_b = carry
            here = pl.ds(pl.multiple_of(index * step, step), step)
            rounded = (probs[index] * (grads[index] - inner)).astype(BF16)
            dk[here, :] += dot(rounded, queries, NN)
            if causal:
                sums[first // rows - index] += rounded.astype(F32)
            out_a = out_a + dot(key_t[index, :width, :], rounded[:, :rows], NN)
            out_b = out_b + dot(key_t[index, width:, :], rounded[:, rows:], NN)
            return out_a, out_b

        zero = jnp.zeros((width, rows), F32)
        out_a, out_b = lax.fori_loop(low, high, gather, (zero, zero))
        joined = jnp.concatenate([out_a, out_b], axis=0)
        dq_ref[block * rows : (block + 1) * rows, :] = joined.T.astype(BF16)
    dk_ref[...] = dk[...].astype(BF16)
    dv_ref[...] = dv[...].astype(BF16)
    if causal:
        for delta in range(sums.shape[0]):
            for head in range(2):
                parts = jnp.zeros((8, 2 * rows), F32)
                for chunk in range(rows // 8):
                    piece = sums[delta, chunk * 8 : chunk * 8 + 8, head * rows : (head + 1) * rows]
                    piece = jnp.concatenate([jnp.zeros_like(piece), piece], axis=1)
                    parts = parts + (pltpu.roll(piece, 2 * rows - 8 * chunk, 1) if chunk else piece)
                line = parts[0:1]
                for row in range(1, 8):
                    line = line + pltpu.roll(parts[row : row + 1], 2 * rows - row, 1)
                diag_ref[0, head, delta : delta + 1, :] = line


def unread():
    return pl.BlockSpec(memory_space=pl.ANY)


def ignoring(body, first, count):
    return lambda *refs: body(*refs[:first], *refs[first + count :])


def hold(values, after):
    count = len(values)
    return pl.pallas_call(
        lambda *refs: None,
        in_specs=[unread()] * (count + len(after)),
        out_specs=[unread()] * count,
        out_shape=[jax.ShapeDtypeStruct(value.shape, value.dtype) for value in values],
        input_output_aliases={index: index for index in range(count)},
        cost_estimate=SHORT,
        name="hold",
    )(*values, *after)


def smem():
    return pl.BlockSpec(memory_space=pltpu.SMEM)


def attention_forward(
    first, q_sizes, k_sizes, queries, keys, values, table, width, step, span, after=(), cost=LONG
):
    causal = table is not None
    count, model = queries.shape
    key_count = keys.shape[0]
    rows = min(256, count)
    step = rows if causal else step
    pair_first, pairs = span
    blocks = count // rows
    column = lambda size: pl.BlockSpec((size, 2 * width), lambda pair: (0, pair + pair_first))
    result = lambda size: pl.BlockSpec((size, 2 * width), lambda pair: (0, pair))
    scratch = [
        pltpu.VMEM((key_count // step, 2 * width, step), BF16),
        pltpu.VMEM((key_count // step, step, 2 * rows), F32),
    ]
    in_specs = [smem(), smem(), smem(), column(count), column(key_count), column(key_count)]
    args = [first, q_sizes, k_sizes, queries, keys, values]
    if causal:
        in_specs.append(
            pl.BlockSpec((1, 2, table.shape[2]), lambda pair: (pair + pair_first, 0, 0))
        )
        args.append(table)
        scratch.append(pltpu.VMEM((key_count // rows, rows, 2 * rows), F32))
    return pl.pallas_call(
        ignoring(functools.partial(forward_kernel, causal, step, width), len(args), len(after)),
        grid=(pairs,),
        in_specs=in_specs + [unread()] * len(after),
        out_specs=[
            result(count),
            pl.BlockSpec((1, blocks, 1, 2 * rows), lambda pair: (pair, 0, 0, 0)),
        ],
        out_shape=[
            jax.ShapeDtypeStruct((count, pairs * 2 * width), BF16),
            jax.ShapeDtypeStruct((pairs, blocks, 1, 2 * rows), F32),
        ],
        scratch_shapes=scratch,
        compiler_params=pltpu.CompilerParams(vmem_limit_bytes=56 << 20),
        cost_estimate=cost,
        name="self_forward" if causal else "cross_forward",
    )(*args, *after)


def attention_backward(
    first, q_sizes, k_sizes, queries, keys, values, grads, totals, table, width, step, span, after=()
):
    causal = table is not None
    count, model = queries.shape
    key_count = keys.shape[0]
    rows = min(256, count)
    step = rows if causal else step
    pair_first, pairs = span
    blocks = count // rows
    column = lambda size: pl.BlockSpec((size, 2 * width), lambda pair: (0, pair + pair_first))
    result = lambda size: pl.BlockSpec((size, 2 * width), lambda pair: (0, pair))
    n_step = key_count // step
    scratch = [
        pltpu.VMEM((n_step, 2 * width, step), BF16),
        pltpu.VMEM((n_step, step, 2 * rows), F32),
        pltpu.VMEM((n_step, step, 2 * rows), F32),
        pltpu.VMEM((key_count, 2 * width), F32),
        pltpu.VMEM((key_count, 2 * width), F32),
    ]
    in_specs = [
        smem(), smem(), smem(), column(count), column(key_count), column(key_count), column(count),
        pl.BlockSpec((1, blocks, 1, 2 * rows), lambda pair: (pair + pair_first, 0, 0, 0)),
    ]
    args = [first, q_sizes, k_sizes, queries, keys, values, grads, totals]
    out_specs = [result(count), result(key_count), result(key_count)]
    out_shape = [
        jax.ShapeDtypeStruct((count, pairs * 2 * width), BF16),
        jax.ShapeDtypeStruct((key_count, pairs * 2 * width), BF16),
        jax.ShapeDtypeStruct((key_count, pairs * 2 * width), BF16),
    ]
    if causal:
        in_specs.append(
            pl.BlockSpec((1, 2, table.shape[2]), lambda pair: (pair + pair_first, 0, 0))
        )
        args.append(table)
        deltas = key_count // rows
        scratch += [pltpu.VMEM((deltas, rows, 2 * rows), F32), pltpu.VMEM((deltas, rows, 2 * rows), F32)]
        out_specs.append(pl.BlockSpec((1, 2, deltas, 2 * rows), lambda pair: (pair, 0, 0, 0)))
        out_shape.append(jax.ShapeDtypeStruct((pairs, 2, deltas, 2 * rows), F32))
    return pl.pallas_call(
        ignoring(functools.partial(backward_kernel, causal, step, width), len(args), len(after)),
        grid=(pairs,),
        in_specs=in_specs + [unread()] * len(after),
        out_specs=out_specs,
        out_shape=out_shape,
        scratch_shapes=scratch,
        compiler_params=pltpu.CompilerParams(vmem_limit_bytes=60 << 20),
        cost_estimate=LONG,
        name="self_backward" if causal else "cross_backward",
    )(*args, *after)


def send_batch(block, distance):
    count = lax.axis_size("batch")
    return lax.ppermute(block, "batch", [(i, i ^ distance) for i in range(count)])


def send_mem(block):
    return lax.ppermute(block, "mem", [(0, 1), (1, 0)])


def place(pieces, mine):
    ordered = []
    for index in range(len(pieces)):
        chosen = pieces[0]
        for distance in range(1, len(pieces)):
            chosen = jnp.where(mine == (index ^ distance), pieces[distance], chosen)
        ordered.append(chosen)
    return jnp.stack(ordered)


def grid_place():
    batch_index = lax.axis_index("batch")
    return batch_index >> 2, (batch_index >> 1) & 1, batch_index & 1, lax.axis_index("mem")


def gather_plain(shard):
    within = lax.all_gather(shard, "mem", axis=2, tiled=True)
    return lax.all_gather(within, "batch", axis=1, tiled=True)


def scatter_plain(whole):
    part = lax.psum_scatter(whole, "batch", scatter_dimension=1, tiled=True)
    return lax.psum_scatter(part, "mem", scatter_dimension=2, tiled=True).astype(F32)


def whole_spec(shape):
    return pl.BlockSpec(tuple(shape), lambda *_: (0,) * len(shape))


def kernel_call(
    body, name, grid, in_specs, out_specs, out_shape, args, scratch=(), after=()
):
    return pl.pallas_call(
        ignoring(body, len(args), len(after)),
        grid=grid,
        in_specs=in_specs + [unread()] * len(after),
        out_specs=out_specs,
        out_shape=out_shape,
        scratch_shapes=list(scratch),
        compiler_params=pltpu.CompilerParams(vmem_limit_bytes=60 << 20),
        cost_estimate=MEDIUM if name.endswith("kernel") else SHORT,
        name=name,
    )(*args, *after)


def simple_call(body, name, out_shape, args, after=(), spot=None):
    lead = [] if spot is None else [spot]
    return kernel_call(
        body, name, (1,), [smem()] * len(lead) + [whole_spec(arg.shape) for arg in args],
        [whole_spec(shape.shape) for shape in out_shape], out_shape, (*lead, *args), after=after,
    )


def place_line(spot, pieces, after=()):
    count = len(pieces)
    half = count // 2
    shape = jax.ShapeDtypeStruct((half, *pieces[0].shape), BF16)

    def body(spot_ref, *refs):
        low_ref, high_ref = refs[count:]
        for distance in range(count):
            z = spot_ref[0] ^ distance

            @pl.when(z < half)
            def lower():
                low_ref[z] = refs[distance][...]

            @pl.when(z >= half)
            def upper():
                high_ref[z - half] = refs[distance][...]

    return simple_call(body, "place_line", [shape, shape], pieces, after, spot)


def place_pairs(spot, axes, pairs, after=()):
    shapes = [jax.ShapeDtypeStruct((2, *own.shape), BF16) for own, _ in pairs]

    def body(spot_ref, *refs):
        for index, axis in enumerate(axes):
            own_ref, far_ref, out_ref = refs[2 * index], refs[2 * index + 1], refs[2 * len(axes) + index]
            mine = spot_ref[axis]
            out_ref[mine] = own_ref[...]
            out_ref[1 - mine] = far_ref[...]

    return simple_call(body, "place_pairs", shapes, [part for pair in pairs for part in pair], after, spot)


def line_of(shard):
    return [shard] + [send_batch(shard, 4 * d) for d in range(1, lax.axis_size("batch") // 4)]


def gather_first(spot, low, high, after=()):
    return place_pairs(spot, (3, 1), ((low, send_mem(low)), (high, send_batch(high, 2))), after)


def gather_second(spot, low, high, after=()):
    return place_pairs(spot, (1, 3), ((low, send_batch(low, 2)), (high, send_mem(high))), after)


def gather_cores(low, high):
    return low, send_batch(low, 1), high, send_batch(high, 1)


def add_refs(refs):
    total = refs[0][...].astype(F32)
    for ref in refs[1:]:
        total = total + ref[...].astype(F32)
    return total


def scatter_step(groups, after, axes):
    def body(*refs):
        outs = refs[2 * len(groups) :]
        for index, axis in enumerate(axes):
            total = add_refs(refs[2 * index : 2 * index + 2]).astype(BF16)
            cut = (slice(None),) * axis
            outs[2 * index][...] = total[(*cut, 0)]
            outs[2 * index + 1][...] = total[(*cut, 1)]

    in_specs, out_specs, shapes, args = [], [], [], []
    for (kept, received), axis in zip(groups, axes):
        args += [kept, received]
        block = (1, *kept.shape[1:])
        zeros = (0,) * (len(block) - 1)
        in_specs += [pl.BlockSpec(block, lambda z, zeros=zeros: (z, *zeros))] * 2
        rest = kept.shape[:axis] + kept.shape[axis + 1 :]
        out_specs += [pl.BlockSpec((1, *rest[1:]), lambda z, zeros=zeros: (z, *zeros[1:]))] * 2
        shapes += [jax.ShapeDtypeStruct(rest, BF16)] * 2
    outs = kernel_call(
        body, "scatter_step", (args[0].shape[0],), in_specs, out_specs, shapes, args, after=after
    )
    return [tuple(outs[2 * index : 2 * index + 2]) for index in range(len(groups))]


def scatter_to_line(groups, after):
    count = groups[0][0].shape[0]

    def body(*refs):
        outs = refs[2 * len(groups) :]
        for index in range(len(groups)):
            total = add_refs(refs[2 * index : 2 * index + 2]).astype(BF16)
            for distance in range(count):
                outs[count * index + distance][...] = total[distance]

    shapes = [jax.ShapeDtypeStruct(kept.shape[1:], BF16) for kept, _ in groups for _ in range(count)]
    outs = simple_call(body, "scatter_to_line", shapes, [part for group in groups for part in group], after)
    return [outs[count * index : count * (index + 1)] for index in range(len(groups))]


def send_line(pieces):
    return [pieces[0]] + [send_batch(pieces[d], 4 * d) for d in range(1, len(pieces))]


def scatter_end(groups, out_shapes, moves, after):
    def body(*refs):
        outs = refs[sum(len(group) for group in groups) :]
        totals, start = [], 0
        for group in groups:
            totals.append(add_refs(refs[start : start + len(group)]))
            start += len(group)
        for group, first, rows, out, index in moves:
            outs[out][index] = totals[group][first : first + rows]

    shapes = [jax.ShapeDtypeStruct(shape, F32) for shape in out_shapes]
    return simple_call(body, "scatter_end", shapes, [part for group in groups for part in group], after)


def square_moves(units, slab, columns, outputs):
    moves, used = [], {}
    for group, matrix, block in units:
        first = used.get(group, 0)
        used[group] = first + slab
        out, index = outputs[matrix]
        span = slice(block * 128, (block + 1) * 128)
        moves.append((group, first, slab, out, (slice(None), span) if index is None else (index, slice(None), span)))
    return moves


def sum_small(block, distances, after):
    count = lax.axis_size("batch") * 2
    parts = [block]
    for distance in distances:
        pairs = [(i, i ^ distance) for i in range(count)]
        parts.append(lax.ppermute(block, ("batch", "mem"), pairs))

    def body(*refs):
        values = [ref[...] for ref in refs[:-1]]
        while len(values) > 1:
            values = [values[i] + values[i + 1] for i in range(0, len(values), 2)]
        refs[-1][...] = values[0]

    return simple_call(body, "sum_small", [jax.ShapeDtypeStruct(block.shape, F32)], parts, after)[0]


def add_rows(block, far, after):
    rows, width = block.shape

    def body(one_ref, two_ref, out_ref):
        out_ref[...] = one_ref[...] + two_ref[...].astype(F32)

    spec = pl.BlockSpec((rows // 4, width), lambda i: (i, 0))
    shape = jax.ShapeDtypeStruct(block.shape, F32)
    return kernel_call(body, "add_rows", (4,), [spec, spec], spec, shape, (block, far), after=after)


def chosen(block, axis, index):
    return lax.dynamic_index_in_dim(block, index, axis, keepdims=False)


def all_rows(block):
    if lax.axis_size("mem") == 2:
        return place([block, send_mem(block)], lax.axis_index("mem")).reshape(-1, block.shape[1])
    return lax.all_gather(block, "mem", axis=0, tiled=True)


def own_rows(partial_rows):
    mem_count = lax.axis_size("mem")
    if mem_count == 2:
        halves = partial_rows.reshape(2, -1, partial_rows.shape[1])
        index = lax.axis_index("mem")
        far = send_mem(chosen(halves, 0, 1 - index).astype(BF16))
        return chosen(halves, 0, index) + far.astype(F32)
    return lax.psum_scatter(
        partial_rows.astype(BF16), "mem", scatter_dimension=0, tiled=True
    ).astype(F32)


def mm(left, right):
    return dot(left, right, NN)


def mm_t(left, right):
    return dot(left, right, NT)


def t_mm(left, right):
    return dot(left, right, (((0,), (0,)), ((), ())))


def weight_specs(pack, index):
    return [
        pl.BlockSpec(
            part.shape[:3] + (1,) + part.shape[4:], lambda *_: (0, 0, 0, index, 0, 0)
        )
        for part in pack
    ]


def columns_of(spot_ref, refs, index, column):
    low_own, low_far, high_own, high_far = refs
    half = low_own.shape[2]
    pieces = []
    for z in range(2 * half):
        for y in range(2):
            for core in range(2):
                if z < half:
                    spot = (y, column, z, index)
                    own, far = low_own[spot], low_far[spot]
                else:
                    spot = (column, y, z - half, index)
                    own, far = high_own[spot], high_far[spot]
                pieces.append(jnp.where(spot_ref[2] == core, own, far))
    return jnp.concatenate(pieces, axis=0)


def matrix_of(spot_ref, refs, index=0):
    return jnp.concatenate(
        [columns_of(spot_ref, refs, index, 0), columns_of(spot_ref, refs, index, 1)], axis=1
    )


def join(parts):
    return jnp.concatenate([part[...] for part in parts], axis=1)


def store_shard(place_ref, keep_ref, send_ref, z, y, x, unit, even, odd):
    at_z, at_y, at_core, at_x = (place_ref[axis] for axis in range(4))
    rows = even.shape[0]
    span = slice(unit, unit + rows)
    keep_ref[z ^ at_z, y ^ at_y, x ^ at_x, span, :] = jnp.where(at_core == 0, even, odd)
    send_ref[z ^ at_z, y ^ at_y, x ^ at_x, span, :] = jnp.where(at_core == 0, odd, even)


def store_square(place_ref, targets, matrix, z_count):
    rounded = matrix.astype(BF16)
    rows, columns = rounded.shape[0] // (4 * z_count), rounded.shape[1] // 2
    for z in range(z_count):
        for y in range(2):
            start = (z * 2 + y) * 2 * rows
            for x in range(2):
                for index, (keep_ref, send_ref, unit) in enumerate(targets):
                    span = slice(x * columns + index * 128, x * columns + (index + 1) * 128)
                    store_shard(
                        place_ref, keep_ref, send_ref, z, y, x, unit,
                        rounded[start : start + rows, span],
                        rounded[start + rows : start + 2 * rows, span],
                    )


def piece_shape(z_count, rows):
    return jax.ShapeDtypeStruct((z_count, 2, 2, rows, 128), BF16)


def inverse_rms(values):
    return lax.rsqrt(jnp.mean(values * values, axis=1, keepdims=True) + EPSILON)


def norm_backward(values, gain_row, grads):
    scale = inverse_rms(values)
    normed = values * scale
    gain_grad = jnp.sum(grads * normed, axis=0, keepdims=True)
    pulled = grads * gain_row
    inner = jnp.mean(pulled * normed, axis=1, keepdims=True)
    return scale * (pulled - normed * inner), gain_grad


def project_self(place, own, far, gains, pack, after):
    rows, width = own.shape
    columns = width // 2

    def body(place_ref, own_ref, far_ref, gains_ref, *refs):
        weights, (q_ref, k_ref, v_ref, normed_ref) = refs[:4], refs[4:]
        at_x = place_ref[3]
        here = pl.ds(pl.multiple_of(at_x * rows, rows), rows)
        there = pl.ds(pl.multiple_of((1 - at_x) * rows, rows), rows)

        @pl.when(pl.program_id(0) == 0)
        def normalise():
            for source, span in ((own_ref, here), (far_ref, there)):
                values = source[...].astype(F32)
                normed_ref[span, :] = (values * inverse_rms(values) * gains_ref[0:1, :]).astype(BF16)

        q_ref[...] = mm(normed_ref[here, :], columns_of(place_ref, weights, 0, 0)).astype(BF16)
        normed = normed_ref[...]
        k_ref[...] = mm(normed, columns_of(place_ref, weights, 1, 0)).astype(BF16)
        v_ref[...] = mm(normed, columns_of(place_ref, weights, 2, 0)).astype(BF16)

    low, high = pack[0], pack[2]
    low_spec = pl.BlockSpec(low.shape[:1] + (1,) + low.shape[2:], lambda m: (0, m, 0, 0, 0, 0))
    high_spec = pl.BlockSpec((1,) + high.shape[1:], lambda m: (m, 0, 0, 0, 0, 0))
    return kernel_call(
        body, "project_self_kernel", (2,),
        [
            smem(), whole_spec(own.shape), whole_spec(far.shape), whole_spec(gains.shape),
            low_spec, low_spec, high_spec, high_spec,
        ],
        [
            pl.BlockSpec((rows, columns), lambda m: (0, m)),
            pl.BlockSpec((2 * rows, columns), lambda m: (0, m)),
            pl.BlockSpec((2 * rows, columns), lambda m: (0, m)),
            whole_spec((2 * rows, width)),
        ],
        [
            jax.ShapeDtypeStruct((rows, width), BF16),
            jax.ShapeDtypeStruct((2 * rows, width), BF16),
            jax.ShapeDtypeStruct((2 * rows, width), BF16),
            jax.ShapeDtypeStruct((2 * rows, width), BF16),
        ],
        (place, own, far, gains, *pack),
        after=after,
    )


def specs_of(arrays):
    return [whole_spec(array.shape) for array in arrays]


def after_self(place, own, attn, gains, pack):
    rows, width = own.shape
    count = len(attn)

    def body(place_ref, own_ref, gains_ref, *refs):
        attended = join(refs[:count])
        out_weight, q_weight = refs[count : count + 4], refs[count + 4 : count + 8]
        middle_ref, normed_ref, q_ref = refs[count + 8 :]
        middle = own_ref[...].astype(F32) + mm(attended, matrix_of(place_ref, out_weight))
        middle_ref[...] = middle
        normed = (middle * inverse_rms(middle) * gains_ref[1:2, :]).astype(BF16)
        normed_ref[...] = normed
        q_ref[...] = mm(normed, matrix_of(place_ref, q_weight)).astype(BF16)

    return kernel_call(
        body, "after_self_kernel", (1,),
        [smem(), whole_spec(own.shape), whole_spec(gains.shape), *specs_of(attn)]
        + weight_specs(pack, 3) + weight_specs(pack, 0),
        [whole_spec(own.shape)] * 3,
        [
            jax.ShapeDtypeStruct((rows, width), F32),
            jax.ShapeDtypeStruct((rows, width), BF16),
            jax.ShapeDtypeStruct((rows, width), BF16),
        ],
        (place, own, gains, *attn, *pack, *pack),
    )


def three_way(step, own_ref, far_a, far_b):
    return jnp.where(step < 2, own_ref[...], jnp.where(step == 2, far_a[...], far_b[...]))


def project_memory(place, own, far, pack):
    rows, width = own.shape
    step = rows // 2

    def body(place_ref, own_ref, far_a, far_b, *refs):
        k_ref, v_ref = refs[8:]
        source = three_way(pl.program_id(0), own_ref, far_a, far_b)
        k_ref[...] = mm(source, matrix_of(place_ref, refs[:4])).astype(BF16)
        v_ref[...] = mm(source, matrix_of(place_ref, refs[4:8])).astype(BF16)

    def result(i, place_ref):
        return ((place_ref[3] ^ (i // 2)) * 2 + i % 2, 0)

    shape = jax.ShapeDtypeStruct((2 * rows, width), BF16)
    return pl.pallas_call(
        body,
        grid_spec=pltpu.PrefetchScalarGridSpec(
            num_scalar_prefetch=1,
            grid=(4,),
            in_specs=[
                pl.BlockSpec((step, width), lambda i, _: (jnp.minimum(i, 1), 0)),
                whole_spec((step, width)),
                whole_spec((step, width)),
            ]
            + weight_specs(pack, 1) + weight_specs(pack, 2),
            out_specs=[pl.BlockSpec((step, width), result)] * 2,
        ),
        out_shape=[shape, shape],
        compiler_params=pltpu.CompilerParams(vmem_limit_bytes=60 << 20),
        cost_estimate=MEDIUM,
        name="project_memory_kernel",
    )(place, own, *far, *pack, *pack)


def feed_forward(place, middle_one, attn, cotangent, gains, pack, wide, half):
    rows, width = cotangent.shape
    batch_count = wide.shape[0]
    slab = width // batch_count
    chunk = half // 2
    across = chunk // 128
    down_rows = half * 2 // batch_count
    down_across = width // 256
    down_units = down_across * down_rows

    def body(
        place_ref, middle_ref, attn_ref, cot_ref, gains_ref, co_one, co_two, co_three, co_four,
        gate_ref, up_ref, down_ref, out_ref, grad_middle_ref, grad_attn_ref, gain_ref, wide_grad,
        middle_two, normed, normed_t, grad_normed, result,
    ):
        step = pl.program_id(0)
        co_refs = (co_one, co_two, co_three, co_four)

        @pl.when(step == 0)
        def start():
            middle = middle_ref[...] + mm(attn_ref[...], matrix_of(place_ref, co_refs))
            middle_two[...] = middle
            rounded = (middle * inverse_rms(middle) * gains_ref[2:3, :]).astype(BF16)
            normed[...] = rounded
            normed_t[...] = rounded.T
            grad_normed[...] = jnp.zeros_like(grad_normed)
            result[...] = middle

        def wide_weight(ref):
            blocks = [
                ref[:, 0, index * slab : (index + 1) * slab, :].reshape(width, 128)
                for index in range(across)
            ]
            return jnp.concatenate(blocks, axis=1)

        cot = cot_ref[...]
        gate_weight, up_weight = wide_weight(gate_ref), wide_weight(up_ref)
        down_weight = jnp.concatenate(
            [
                down_ref[:, x, index * down_rows : (index + 1) * down_rows, :].reshape(chunk, 128)
                for x in range(2)
                for index in range(down_across)
            ],
            axis=1,
        )
        gate = mm(normed[...], gate_weight)
        up = mm(normed[...], up_weight)
        square = gate * gate
        bend = jnp.tanh(GELU_SCALE * (gate + GELU_CUBE * (gate * square)))
        half_one = 0.5 * (1.0 + bend)
        gelu = gate * half_one
        slope = half_one + 0.5 * gate * (1.0 - bend * bend) * (
            GELU_SCALE * (1.0 + 3.0 * GELU_CUBE * square)
        )
        act = (gelu * up).astype(BF16)
        result[...] += mm(act, down_weight)
        grad_act = mm_t(cot, down_weight)
        grad_gate = (grad_act * up * slope).astype(BF16)
        grad_up = (grad_act * gelu).astype(BF16)
        grad_normed[...] += mm_t(grad_gate, gate_weight) + mm_t(grad_up, up_weight)
        down_grad = t_mm(act, cot).astype(BF16)
        gate_rows = 2 * across * slab
        for block in range(chunk // down_rows):
            for x in range(2):
                for index in range(down_across):
                    span = slice((x * down_across + index) * 128, (x * down_across + index + 1) * 128)
                    start_row = 2 * gate_rows + index * down_rows
                    wide_grad[step * (chunk // down_rows) + block, x, start_row : start_row + down_rows, :] = (
                        down_grad[block * down_rows : (block + 1) * down_rows, span]
                    )
        for which, grad in enumerate((grad_gate, grad_up)):
            whole = mm(normed_t[...], grad).astype(BF16).reshape(batch_count, slab, chunk)
            for index in range(across):
                start_row = pl.multiple_of(
                    which * gate_rows + (step % 2) * across * slab + index * slab, slab
                )
                wide_grad[:, step // 2, pl.ds(start_row, slab), :] = whole[
                    :, :, index * 128 : (index + 1) * 128
                ]

        @pl.when(step == pl.num_programs(0) - 1)
        def finish():
            out_ref[...] = result[...].astype(BF16)
            pulled, gain_grad = norm_backward(middle_two[...], gains_ref[2:3, :], grad_normed[...])
            gain_ref[...] = gain_grad
            grad_middle = cot_ref[...].astype(F32) + pulled
            grad_middle_ref[...] = grad_middle
            branch = grad_middle.astype(BF16)
            grad_attn_ref[...] = mm_t(branch, matrix_of(place_ref, co_refs)).astype(BF16)

    row_shape = (rows, width)
    wide_spec = lambda which: pl.BlockSpec(
        (batch_count, 1, across * slab, 128), lambda i: (0, i // 2, 2 * which + i % 2, 0)
    )
    down_spec = pl.BlockSpec(
        (chunk // down_rows, 2, down_units, 128), lambda i: (i, 0, 4 * across * slab // down_units, 0)
    )
    return kernel_call(
        body, "feed_forward_kernel", (4,),
        [smem(), *[whole_spec(row_shape)] * 3, whole_spec(gains.shape)] + weight_specs(pack, 4) + [wide_spec(0), wide_spec(1), down_spec],
        [whole_spec(row_shape)] * 3 + [whole_spec((1, width)), whole_spec(wide.shape)],
        [
            jax.ShapeDtypeStruct(row_shape, BF16),
            jax.ShapeDtypeStruct(row_shape, F32),
            jax.ShapeDtypeStruct(row_shape, BF16),
            jax.ShapeDtypeStruct((1, width), F32),
            jax.ShapeDtypeStruct(wide.shape, BF16),
        ],
        (place, middle_one, attn, cotangent, gains, *pack, wide, wide, wide),
        scratch=[
            pltpu.VMEM(row_shape, F32), pltpu.VMEM(row_shape, BF16), pltpu.VMEM((width, rows), BF16),
            pltpu.VMEM(row_shape, F32), pltpu.VMEM(row_shape, F32),
        ],
    )


def after_cross(
    place, grad_query, middle_one, grad_middle_two, normed_cross, attn_self, attn_cross, gains, pack, after
):
    rows, width = middle_one.shape
    z_count = pack[0].shape[2] * 2
    slab = pack[0].shape[4]
    one, two = len(grad_query), len(attn_self)

    def body(place_ref, middle_ref, grad_ref, normed_ref, cross_ref, gains_ref, *refs):
        grad_query = join(refs[:one])
        attended = join(refs[one : one + two])
        so_refs, q_refs = refs[one + two : one + two + 4], refs[one + two + 4 : one + two + 8]
        grad_middle_ref, grad_attn_ref, gain_ref, keep_ref, send_ref = refs[one + two + 8 :]
        grads = mm_t(grad_query, matrix_of(place_ref, q_refs))
        pulled, gain_grad = norm_backward(middle_ref[...], gains_ref[1:2, :], grads)
        gain_ref[...] = gain_grad
        grad_middle = grad_ref[...] + pulled
        grad_middle_ref[...] = grad_middle
        branch = grad_middle.astype(BF16)
        grad_attn_ref[...] = mm_t(branch, matrix_of(place_ref, so_refs)).astype(BF16)
        branch_two = grad_ref[...].astype(BF16)
        for index, (left, right) in enumerate(
            ((normed_ref[...], grad_query), (attended, branch), (cross_ref[...], branch_two))
        ):
            targets = [(keep_ref, send_ref, (3 * index + part) * slab) for part in range(3)]
            store_square(place_ref, targets, t_mm(left, right), z_count)

    pieces = piece_shape(z_count, 9 * slab)
    row_shape = (rows, width)
    return kernel_call(
        body, "after_cross_kernel", (1,),
        [smem()] + [whole_spec(row_shape)] * 4 + [whole_spec(gains.shape)]
        + specs_of(grad_query) + specs_of(attn_self)
        + weight_specs(pack, 3) + weight_specs(pack, 0),
        [whole_spec(row_shape), whole_spec(row_shape), whole_spec((1, width))]
        + [whole_spec(pieces.shape)] * 2,
        [
            jax.ShapeDtypeStruct(row_shape, F32),
            jax.ShapeDtypeStruct(row_shape, BF16),
            jax.ShapeDtypeStruct((1, width), F32),
            pieces,
            pieces,
        ],
        (
            place, middle_one, grad_middle_two, normed_cross, attn_cross, gains,
            *grad_query, *attn_self, *pack, *pack,
        ),
        after=after,
    )


def memory_backward(place, grad_key, grad_value, own, far, pack):
    rows, width = own.shape
    step = rows // 2
    z_count = pack[0].shape[2] * 2
    slab = pack[0].shape[4]

    def body(
        place_ref, dk_ref, dv_ref, own_ref, far_a, far_b, *refs,
    ):
        k_refs, v_refs = refs[:4], refs[4:8]
        grad_own_ref, grad_far_ref, keep_ref, send_ref, key_total, value_total = refs[8:]
        i = pl.program_id(0)
        source = three_way(i ^ 2, own_ref, far_a, far_b)
        source_t = source.T

        @pl.when(i == 0)
        def clear():
            key_total[...] = jnp.zeros_like(key_total)
            value_total[...] = jnp.zeros_like(value_total)

        grad_key, grad_value = dk_ref[...], dv_ref[...]
        key_total[...] += mm(source_t, grad_key)
        value_total[...] += mm(source_t, grad_value)
        grads = mm_t(grad_key, matrix_of(place_ref, k_refs)) + mm_t(
            grad_value, matrix_of(place_ref, v_refs)
        )

        @pl.when(i < 2)
        def here():
            grad_far_ref[...] = grads.astype(BF16)

        @pl.when(i >= 2)
        def there():
            grad_own_ref[...] = grads

        @pl.when(i == 3)
        def finish():
            for index, total in enumerate((key_total, value_total)):
                targets = [(keep_ref, send_ref, (3 * index + part) * slab) for part in range(3)]
                store_square(place_ref, targets, total[...], z_count)

    def block(i, place_ref):
        return ((place_ref[3] ^ (1 - i // 2)) * 2 + i % 2, 0)

    pieces = piece_shape(z_count, 6 * slab)
    return pl.pallas_call(
        body,
        grid_spec=pltpu.PrefetchScalarGridSpec(
            num_scalar_prefetch=1,
            grid=(4,),
            in_specs=[
                *[pl.BlockSpec((step, width), block)] * 2,
                pl.BlockSpec((step, width), lambda i, _: (jnp.maximum(i - 2, 0), 0)),
                whole_spec((step, width)),
                whole_spec((step, width)),
            ]
            + weight_specs(pack, 1) + weight_specs(pack, 2),
            out_specs=[
                pl.BlockSpec((step, width), lambda i, _: (jnp.maximum(i - 2, 0), 0)),
                pl.BlockSpec((step, width), lambda i, _: (jnp.minimum(i, 1), 0)),
                whole_spec(pieces.shape),
                whole_spec(pieces.shape),
            ],
            scratch_shapes=[pltpu.VMEM((width, width), F32), pltpu.VMEM((width, width), F32)],
        ),
        out_shape=[
            jax.ShapeDtypeStruct((rows, width), F32),
            jax.ShapeDtypeStruct((rows, width), BF16),
            pieces,
            pieces,
        ],
        compiler_params=pltpu.CompilerParams(vmem_limit_bytes=60 << 20),
        cost_estimate=MEDIUM,
        name="memory_backward_kernel",
    )(place, grad_key, grad_value, own, *far, *pack, *pack)


def self_weight_grads(place, grad_query, grad_key, grad_value, normed, z_count, after):
    rows, half = grad_query[0].shape
    width = 2 * half
    slab = width // (4 * z_count)

    def body(place_ref, dq_a, dq_b, dk_a, dk_b, dv_a, dv_b, normed_ref, keep_a, send_a, keep_b, send_b):
        here = pl.ds(pl.multiple_of(place_ref[3] * rows, rows), rows)
        normed_t = normed_ref[...].T
        grads = (
            t_mm(normed_ref[here, :], join((dq_a, dq_b))),
            mm(normed_t, join((dk_a, dk_b))),
            mm(normed_t, join((dv_a, dv_b))),
        )
        for index, grad in enumerate(grads):
            targets = []
            for unit in range(3 * index, 3 * index + 3):
                first = unit < 5
                targets.append(
                    (keep_a if first else keep_b, send_a if first else send_b, (unit if first else unit - 5) * slab)
                )
            store_square(place_ref, targets, grad, z_count)

    shapes = [piece_shape(z_count, count * slab) for count in (5, 5, 4, 4)]
    return kernel_call(
        body, "self_weight_grads_kernel", (1,),
        [smem()] + [whole_spec((rows, half))] * 2 + [whole_spec((2 * rows, half))] * 4
        + [whole_spec((2 * rows, width))],
        [whole_spec(shape.shape) for shape in shapes],
        shapes,
        (place, *grad_query, *grad_key, *grad_value, normed),
        after=after,
    )


def self_row_grads(place, own, far, gains, grad_query, grad_key, grad_value, pack, after):
    rows, half = grad_query[0].shape
    width = 2 * half

    def body(place_ref, own_rows, far_rows, dq_a, dq_b, dk_a, dk_b, dv_a, dv_b, *refs):
        weights, (own_ref, far_ref, gain_ref) = refs[:4], refs[4:]
        key_weight = matrix_of(place_ref, weights, 1)
        value_weight = matrix_of(place_ref, weights, 2)
        here = pl.ds(pl.multiple_of(place_ref[3] * rows, rows), rows)
        there = pl.ds(pl.multiple_of((1 - place_ref[3]) * rows, rows), rows)
        split = lambda pair, span: jnp.concatenate([pair[0][span, :], pair[1][span, :]], axis=1)
        keys, values = (dk_a, dk_b), (dv_a, dv_b)

        def gain_of(rows_ref, grads):
            values = rows_ref[...].astype(F32)
            return jnp.sum(grads * (values * inverse_rms(values)), axis=0, keepdims=True)

        far_grads = mm_t(split(keys, there), key_weight) + mm_t(split(values, there), value_weight)
        far_ref[...] = far_grads.astype(BF16)
        own_grads = (
            mm_t(split(keys, here), key_weight)
            + mm_t(split(values, here), value_weight)
            + mm_t(join((dq_a, dq_b)), matrix_of(place_ref, weights, 0))
        )
        own_ref[...] = own_grads
        gain_ref[...] = gain_of(own_rows, own_grads) + gain_of(far_rows, far_grads)

    row_shape = (rows, width)
    return kernel_call(
        body, "self_row_grads_kernel", (1,),
        [smem()] + [whole_spec(row_shape)] * 2
        + specs_of(grad_query) + specs_of(grad_key) + specs_of(grad_value) + specs_of(pack),
        [whole_spec(row_shape)] * 2 + [whole_spec((1, width))],
        [
            jax.ShapeDtypeStruct(row_shape, F32),
            jax.ShapeDtypeStruct(row_shape, BF16),
            jax.ShapeDtypeStruct((1, width), F32),
        ],
        (place, own, far, *grad_query, *grad_key, *grad_value, *pack),
        after=after,
    )


def finish_rows(own, grads, far_grads, grad_middle, gains, after):
    def body(own_ref, grads_ref, far_ref, middle_ref, gains_ref, out_ref):
        total = grads_ref[...] + far_ref[...].astype(F32)
        pulled, _ = norm_backward(own_ref[...].astype(F32), gains_ref[0:1, :], total)
        out_ref[...] = middle_ref[...] + pulled

    shape = jax.ShapeDtypeStruct(own.shape, F32)
    return simple_call(body, "finish_rows_kernel", [shape], [own, grads, far_grads, grad_middle, gains], after)[0]


def shards_plain(
    hidden,
    memory,
    decoder_lengths,
    memory_lengths,
    distance_buckets,
    norm_gains,
    position_bias,
    self_weights,
    self_output,
    cross_weights,
    cross_output,
    expand_weights,
    contract_weight,
    cotangent,
):
    mem_count = lax.axis_size("mem")
    mem_index = lax.axis_index("mem")
    row_count, model_width = hidden.shape[1:]
    head_count = position_bias.shape[1]
    head_width = model_width // head_count
    bucket_count = position_bias.shape[0]
    key_count = row_count * mem_count
    first_row = mem_index * row_count
    first = jnp.reshape(first_row, (1,)).astype(jnp.int32)
    rows = min(256, row_count)

    self_full = gather_plain(self_weights)
    tokens_all = all_rows(hidden[0])
    memory_all = all_rows(memory[0])
    square_full = gather_plain(
        jnp.concatenate([cross_weights, self_output[None], cross_output[None]])
    )
    cross_full, self_out_full, cross_out_full = square_full[:3], square_full[3], square_full[4]
    expand_full = gather_plain(expand_weights)
    contract_full = gather_plain(contract_weight[None])[0]

    buckets = jnp.arange(bucket_count, dtype=jnp.int32)
    one_hot = (distance_buckets[:, None] == buckets[None, :]).astype(F32)
    distance_table = jnp.einsum("db,bh->hd", one_hot, position_bias, precision=EXACT)
    distance_table = jnp.pad(distance_table, ((0, 0), (rows, 0)))
    distance_table = distance_table.reshape(head_count // 2, 2, key_count + rows)

    tokens = hidden[0].astype(F32)
    normed_self, pull_self = jax.vjp(rms_norm, tokens, norm_gains[0])
    input_self = normed_self.astype(BF16)
    input_all = rms_norm(tokens_all.astype(F32), norm_gains[0]).astype(BF16)
    query_self = mm(input_self, self_full[0]).astype(BF16)
    key_self = mm(input_all, self_full[1]).astype(BF16)
    value_self = mm(input_all, self_full[2]).astype(BF16)
    attn_self, self_totals = attention_forward(
        first, decoder_lengths, decoder_lengths, query_self, key_self, value_self,
        distance_table, head_width, rows, (0, head_count // 2),
    )
    middle_one = tokens + mm(attn_self, self_out_full)
    normed_cross, pull_cross = jax.vjp(rms_norm, middle_one, norm_gains[1])
    input_cross = normed_cross.astype(BF16)
    query_cross = mm(input_cross, cross_full[0]).astype(BF16)
    key_memory = mm(memory_all, cross_full[1]).astype(BF16)
    value_memory = mm(memory_all, cross_full[2]).astype(BF16)
    attn_cross, cross_totals = attention_forward(
        first, decoder_lengths, memory_lengths, query_cross, key_memory, value_memory,
        None, head_width, 512, (0, head_count // 2),
    )
    middle_two = middle_one + mm(attn_cross, cross_out_full)
    normed_feed, pull_feed = jax.vjp(rms_norm, middle_two, norm_gains[2])
    input_feed = normed_feed.astype(BF16)
    gate_part = mm(input_feed, expand_full[0])
    up_part = mm(input_feed, expand_full[1])
    activated, pull_activate = jax.vjp(activate, gate_part, up_part)
    hidden_act = activated.astype(BF16)
    result_rows = middle_two + mm(hidden_act, contract_full)
    grad_branch_three = cotangent[0]
    grad_out = grad_branch_three.astype(F32)
    grad_gate, grad_up = pull_activate(mm_t(grad_branch_three, contract_full))
    grad_gate, grad_up = grad_gate.astype(BF16), grad_up.astype(BF16)
    contract_grad = scatter_plain(t_mm(hidden_act, grad_branch_three).astype(BF16)[None])[0]
    expand_grad = scatter_plain(
        jnp.stack([t_mm(input_feed, grad_gate), t_mm(input_feed, grad_up)]).astype(BF16)
    )
    grad_norm_two, gain_grad_three = pull_feed(
        mm_t(grad_gate, expand_full[0]) + mm_t(grad_up, expand_full[1])
    )
    grad_middle_two = grad_out + grad_norm_two
    grad_branch_two = grad_middle_two.astype(BF16)
    grad_cross_out = t_mm(attn_cross, grad_branch_two)
    grad_attn_cross = mm_t(grad_branch_two, cross_out_full).astype(BF16)
    grad_query_cross, grad_key_memory, grad_value_memory = attention_backward(
        first, decoder_lengths, memory_lengths, query_cross, key_memory, value_memory,
        grad_attn_cross, cross_totals, None, head_width, 512, (0, head_count // 2),
    )
    cross_grads = scatter_plain(
        jnp.stack(
            [
                t_mm(input_cross, grad_query_cross),
                t_mm(memory_all, grad_key_memory),
                t_mm(memory_all, grad_value_memory),
                grad_cross_out,
            ]
        ).astype(BF16)
    )
    memory_gradient = own_rows(
        mm_t(grad_key_memory, cross_full[1]) + mm_t(grad_value_memory, cross_full[2])
    )
    grad_norm_one, gain_grad_two = pull_cross(mm_t(grad_query_cross, cross_full[0]))
    grad_middle_one = grad_middle_two + grad_norm_one
    grad_branch_one = grad_middle_one.astype(BF16)
    grad_self_out = t_mm(attn_self, grad_branch_one)
    grad_attn_self = mm_t(grad_branch_one, self_out_full).astype(BF16)
    grad_query_self, grad_key_self, grad_value_self, diagonals = attention_backward(
        first, decoder_lengths, decoder_lengths, query_self, key_self, value_self,
        grad_attn_self, self_totals, distance_table, head_width, rows, (0, head_count // 2),
    )
    diagonals = diagonals.reshape(head_count, key_count // rows, 2 * rows)
    by_distance = jnp.zeros((head_count, key_count + rows), F32)
    for delta in range(key_count // rows):
        here = slice(delta * rows, delta * rows + 2 * rows)
        by_distance = by_distance.at[:, here].add(diagonals[:, delta])
    bias_partial = jnp.einsum("db,hd->bh", one_hot, by_distance[:, rows:], precision=EXACT)
    self_grads = scatter_plain(
        jnp.stack(
            [
                t_mm(input_self, grad_query_self),
                t_mm(input_all, grad_key_self),
                t_mm(input_all, grad_value_self),
                grad_self_out,
            ]
        ).astype(BF16)
    )
    grad_input_self = own_rows(
        mm_t(grad_key_self, self_full[1]) + mm_t(grad_value_self, self_full[2])
    ) + mm_t(grad_query_self, self_full[0])
    grad_norm_zero, gain_grad_one = pull_self(grad_input_self)
    grad_tokens = grad_middle_one + grad_norm_zero
    gain_sums, bias_sums = lax.psum(
        (jnp.stack([gain_grad_one, gain_grad_two, gain_grad_three]), bias_partial), ("batch", "mem")
    )
    return (
        result_rows.astype(BF16)[None],
        grad_tokens[None],
        memory_gradient[None],
        gain_sums,
        bias_sums,
        self_grads[:3],
        self_grads[3],
        cross_grads[:3],
        cross_grads[3],
        expand_grad,
        contract_grad,
    )


def shards_hops(
    hidden,
    memory,
    decoder_lengths,
    memory_lengths,
    distance_buckets,
    norm_gains,
    position_bias,
    self_weights,
    self_output,
    cross_weights,
    cross_output,
    expand_weights,
    contract_weight,
    cotangent,
):
    batch_count, mem_count = lax.axis_size("batch"), lax.axis_size("mem")
    row_count, model_width = hidden.shape[1:]
    bucket_count, head_count = position_bias.shape
    head_width = model_width // head_count
    key_count = row_count * mem_count
    rows = min(256, row_count)
    spot = jnp.stack(grid_place()).astype(jnp.int32)
    first = jnp.reshape(lax.axis_index("mem") * row_count, (1,)).astype(jnp.int32)
    own, own_memory = hidden[0], memory[0]

    slab, columns = self_weights.shape[1:]
    z_count = batch_count // 4

    pairs = head_count // 2
    pairs = head_count // 2
    far = send_mem(own)
    low, high = place_line(spot, line_of(self_weights))
    across = expand_weights.shape[2] // 128
    wide = jnp.concatenate(
        [
            expand_weights.reshape(2, slab, across, 128).transpose(0, 2, 1, 3).reshape(-1, 128),
            contract_weight.reshape(-1, columns // 128, 128).transpose(1, 0, 2).reshape(-1, 128),
        ]
    )
    second = jnp.concatenate([cross_weights, self_output[None], cross_output[None]])
    (second,) = hold((second,), (low, high))
    line = line_of(second)
    low, high = gather_first(spot, low, high, (far,))
    next_low, next_high = place_line(spot, line, (low, high))
    low, high = gather_second(spot, low, high, (next_low, next_high))
    (memory_start,) = hold((own_memory[: own_memory.shape[0] // 2],), (low, high))
    far_memory_a = send_mem(memory_start)
    self_pack = gather_cores(low, high)
    low, high = next_low, next_high

    buckets = jnp.arange(bucket_count, dtype=jnp.int32)
    one_hot = (distance_buckets[:, None] == buckets[None, :]).astype(F32)
    distance_table = jnp.einsum("db,bh->hd", one_hot, position_bias, precision=EXACT)
    distance_table = jnp.pad(distance_table, ((0, 0), (rows, 0)))
    distance_table = distance_table.reshape(pairs, 2, key_count + rows)
    padded = jnp.pad(one_hot, ((rows, 0), (0, 0)))
    bucket_windows = jnp.concatenate(
        [padded[delta * rows : (delta + 2) * rows] for delta in range(key_count // rows)]
    )

    query_self, key_self, value_self, normed_self = project_self(
        spot, own, far, norm_gains, self_pack, (low, high)
    )

    def self_forward(span, after, cost):
        return attention_forward(
            first, decoder_lengths, decoder_lengths, query_self, key_self, value_self,
            distance_table, head_width, rows, span, after, cost,
        )

    low, high = gather_first(spot, low, high, (query_self, far_memory_a))
    (memory_start,) = hold((own_memory[own_memory.shape[0] // 2 :],), (low, high))
    far_memory = (far_memory_a, send_mem(memory_start))
    one = self_forward((0, 2 * pairs // 3), (low, high), LONG)
    low, high = gather_second(spot, low, high, (one[0],))
    (wide,) = hold((wide,), (low, high))
    square_pack = gather_cores(low, high)
    wide = lax.all_gather(wide, ("batch", "mem"), axis=0, tiled=False)
    wide = wide.reshape(batch_count, mem_count, *wide.shape[1:])
    two = self_forward((2 * pairs // 3, pairs // 3), (low, high), BRIEF)
    attn_self, self_totals = zip(one, two)
    self_totals = jnp.concatenate(self_totals, axis=0)
    middle_one, normed_cross, query_cross = after_self(spot, own, attn_self, norm_gains, square_pack)
    key_memory, value_memory = project_memory(spot, own_memory, far_memory, square_pack)
    attn_cross, cross_totals = attention_forward(
        first, decoder_lengths, memory_lengths, query_cross, key_memory, value_memory,
        None, head_width, 512, (0, pairs),
    )
    (
        result, grad_middle_two, grad_attn_cross, gain_three, wide_grad,
    ) = feed_forward(
        spot, middle_one, attn_cross, cotangent[0], norm_gains, square_pack, wide, expand_weights.shape[2]
    )
    halves = ((0, pairs // 2), (pairs // 2, pairs // 2))
    wide_grad = lax.psum_scatter(
        wide_grad.reshape(batch_count * mem_count, *wide_grad.shape[2:]),
        ("batch", "mem"), scatter_dimension=0, tiled=True,
    )[0]
    grad_query_cross, grad_key_memory, grad_value_memory = attention_backward(
        first, decoder_lengths, memory_lengths, query_cross, key_memory, value_memory,
        grad_attn_cross, cross_totals, None, head_width, 512, (0, pairs),
    )
    memory_own, memory_far, kv_keep, kv_send = memory_backward(
        spot, grad_key_memory, grad_value_memory, own_memory, far_memory, square_pack
    )
    grad_middle_one, grad_attn_self, gain_two, qo_keep, qo_send = after_cross(
        spot, (grad_query_cross,), middle_one, grad_middle_two, normed_cross, attn_self, attn_cross,
        norm_gains, square_pack, (memory_far,),
    )

    def self_backward(half, after):
        return attention_backward(
            first, decoder_lengths, decoder_lengths, query_self, key_self, value_self,
            grad_attn_self, self_totals, distance_table, head_width, rows, halves[half], after,
        )

    one = self_backward(0, (qo_keep,))
    (kv_keep, kv_send), (qo_keep, qo_send) = scatter_step(
        ((kv_keep, send_batch(kv_send, 1)), (qo_keep, send_batch(qo_send, 1))), (one[0],), (2, 1)
    )
    memory_far = send_mem(memory_far)
    two = self_backward(1, (kv_keep, one[0]))
    (kv_keep, kv_send), (qo_keep, qo_send) = scatter_step(
        ((kv_keep, send_mem(kv_send)), (qo_keep, send_batch(qo_send, 2))), (two[0],), (1, 1)
    )
    grad_query_self, grad_key_self, grad_value_self, diagonals = zip(one, two)
    rows_own, rows_far, gain_one = self_row_grads(
        spot, own, far, norm_gains, grad_query_self, grad_key_self, grad_value_self, self_pack,
        (kv_keep,),
    )
    line_kv, line_qo = scatter_to_line(
        ((kv_keep, send_batch(kv_send, 2)), (qo_keep, send_mem(qo_send))), (rows_far,)
    )
    diagonals = jnp.concatenate(diagonals, axis=0).reshape(head_count, -1)
    bias_partial = jnp.einsum("db,hd->bh", bucket_windows, diagonals, precision=EXACT)
    gains = jnp.concatenate([gain_one, gain_two, gain_three], axis=0)
    sums = jnp.concatenate([gains.reshape(-1), bias_partial.reshape(-1)]).reshape(-1, 128)
    keep_a, send_a, keep_b, send_b = self_weight_grads(
        spot, grad_query_self, grad_key_self, grad_value_self, normed_self, z_count, (line_kv[0],)
    )
    sums = sum_small(sums, (1, 2, 3), (keep_a,))
    memory_gradient = add_rows(memory_own, memory_far, (keep_a, sums))
    (keep_a, send_a), (keep_b, send_b) = scatter_step(
        ((keep_a, send_batch(send_a, 1)), (keep_b, send_batch(send_b, 1))), (memory_gradient,), (2, 1)
    )
    hidden_gradient = finish_rows(
        own, rows_own, send_mem(rows_far), grad_middle_one, norm_gains, (keep_a,)
    )
    sums = sum_small(sums, (4, 8, 12), (keep_a,))
    units = [(0, 0, block) for block in range(3)] + [(0, 1, block) for block in range(3)]
    units += [(1, matrix, block) for matrix in (2, 3, 4) for block in range(3)]
    cross_grad, self_out_grad, cross_out_grad = scatter_end(
        (send_line(line_kv), send_line(line_qo)),
        (cross_weights.shape, self_output.shape, cross_output.shape),
        square_moves(units, slab, columns, ((0, 1), (0, 2), (0, 0), (1, None), (2, None))),
        (hidden_gradient,),
    )
    (keep_a, send_a), (keep_b, send_b) = scatter_step(
        ((keep_a, send_mem(send_a)), (keep_b, send_batch(send_b, 2))), (cross_grad,), (1, 1)
    )
    sums = sum_small(sums, (16,), (keep_a,)).reshape(-1)
    line_a, line_b = scatter_to_line(
        ((keep_a, send_batch(send_a, 2)), (keep_b, send_mem(send_b))), ()
    )
    units = [(0 if unit < 5 else 1, unit // 3, unit % 3) for unit in range(9)]
    (self_grad,) = scatter_end(
        (send_line(line_a), send_line(line_b)), (self_weights.shape,),
        square_moves(units, slab, columns, ((0, 0), (0, 1), (0, 2))), (),
    )
    gate_rows, down_rows = across * slab, contract_weight.shape[0]
    moves = []
    for which in range(2):
        for block in range(across):
            span = (which, slice(None), slice(block * 128, block * 128 + 128))
            moves.append((0, which * gate_rows + block * slab, slab, 0, span))
    for block in range(columns // 128):
        span = (slice(None), slice(block * 128, block * 128 + 128))
        moves.append((0, 2 * gate_rows + block * down_rows, down_rows, 1, span))
    expand_grad, contract_grad = scatter_end(
        ((wide_grad,),), (expand_weights.shape, contract_weight.shape), moves, (line_a[0],)
    )
    return (
        result[None],
        hidden_gradient[None],
        memory_gradient[None],
        sums[: gains.size].reshape(gains.shape),
        sums[gains.size :].reshape(bucket_count, head_count),
        self_grad,
        self_out_grad,
        cross_grad,
        cross_out_grad,
        expand_grad,
        contract_grad,
    )


def shards(*arrays):
    row_count, slab, columns = arrays[0].shape[1], arrays[7].shape[1], arrays[7].shape[2]
    allowed = row_count % 256 == 0 and slab % 16 == 0 and columns % 128 == 0
    if lax.axis_size("mem") == 2 and lax.axis_size("batch") == 16 and allowed:
        return shards_hops(*arrays)
    return shards_plain(*arrays)


def solution(mesh):
    placed = (
        P("batch", "mem", None),
        P("batch", "mem", None),
        P("batch", None),
        P("batch", None),
        P(),
        P(),
        P(),
        P(None, "batch", "mem"),
        P("batch", "mem"),
        P(None, "batch", "mem"),
        P("batch", "mem"),
        P(None, "batch", "mem"),
        P("batch", "mem"),
        P("batch", "mem", None),
    )
    return jax.shard_map(
        shards,
        mesh=mesh,
        in_specs=placed,
        out_specs=(
            P("batch", "mem", None),
            P("batch", "mem", None),
            P("batch", "mem", None),
            P(),
            P(),
            P(None, "batch", "mem"),
            P("batch", "mem"),
            P(None, "batch", "mem"),
            P("batch", "mem"),
            P(None, "batch", "mem"),
            P("batch", "mem"),
        ),
        check_vma=False,
    )
```

time: 1220 us -> 515 us (0.42)
  waiting for transfers between devices: 783 us -> 99.8 us
  Pallas kernels: 145 us -> 298 us
  matrix products: 115 us -> 0.51 us
  blocking collectives: 84.2 us -> 0 us
  starting transfers between devices: 1.32 us -> 71.6 us
  other arithmetic: 36.4 us -> 2.08 us
    reduce_scatter x9 -> x1, waiting for transfers between devices: 483 us -> 0.01 us  [shards_hops(): lax.psum_scatter(wide_grad.reshape(batch_count * mem_count, *wide_grad.sh...]
    all_gather x8 -> x1, waiting for transfers between devices: 274 us -> 7.46 us  [shards_hops(): wide = lax.all_gather(wide, ('batch', 'mem'), axis=0, tiled=False)]
    pallas_call x4 -> x38, Pallas kernels: 145 us -> 298 us  [the longest x26 121 us: kernel_call(): pl.pallas_call(ignoring(body, len(args), len(after)), grid=grid, in_specs...]
    dot_general x35 -> x2, matrix products: 115 us -> 0.51 us  [the longest x1 0.35 us: shards_hops(): jnp.einsum('db,hd->bh', bucket_windows, diagonals, precision=EXACT)]
    ppermute x0 -> x54, waiting for transfers between devices: none -> 92.3 us  [the longest x13 38.2 us: send_mem(): return lax.ppermute(block, 'mem', [(0, 1), (1, 0)])]
    ppermute x0 -> x54, starting transfers between devices: none -> 71.3 us  [the longest x13 34.3 us: send_mem(): return lax.ppermute(block, 'mem', [(0, 1), (1, 0)])]
    all_gather x6 -> x0, blocking collectives: 44.2 us -> none  [the longest x1 12.1 us: shards(): lax.all_gather(expand_weights, 'mem', axis=2, tiled=True)]
    psum x1 -> x0, blocking collectives: 40.1 us -> none  [shards(): lax.psum((jnp.stack([gain_grad_one, gain_grad_two, gain_grad_three]), bia...]
  transfers between devices with their start and end apart: 22 -> 56, of which waited for: 18 -> 24; matrix products, arithmetic and copies ran while one was open for 12% -> 2% of each run, Pallas kernels for 5% -> 51%
where the time goes in v2:
time: 515 us; the launch traced here: 509 us
  Pallas kernels  298 us (58%)
  waiting for transfers between devices  99.8 us (19%)
  starting transfers between devices  71.6 us (14%)
  local copies, waits for them, and re-layouts  21.6 us (4%)
  between operations  14.8 us (3%)
    pallas_call x26, Pallas kernels, kernel_call(): pl.pallas_call(ignoring(body, len(args), len(after)), grid=grid, in_specs...  121 us
    pallas_call x3, Pallas kernels, attention_backward(): pl.pallas_call(ignoring(functools.partial(backward_kernel, causal, step,...  86.2 us
    pallas_call x3, Pallas kernels, attention_forward(): pl.pallas_call(ignoring(functools.partial(forward_kernel, causal, step, w...  62 us
    ppermute x13, waiting for transfers between devices, send_mem(): return lax.ppermute(block, 'mem', [(0, 1), (1, 0)])  38.2 us
    ppermute x13, starting transfers between devices, send_mem(): return lax.ppermute(block, 'mem', [(0, 1), (1, 0)])  34.3 us
    ppermute x34, waiting for transfers between devices, send_batch(): lax.ppermute(block, 'batch', [(i, i ^ distance) for i in range(count)])  32.1 us
    ppermute x34, starting transfers between devices, send_batch(): lax.ppermute(block, 'batch', [(i, i ^ distance) for i in range(count)])  30.7 us
    ppermute x7, waiting for transfers between devices, sum_small(): parts.append(lax.ppermute(block, ('batch', 'mem'), pairs))  22 us
  transfers between devices with their start and end apart: 56, of which 24 were waited for; matrix products, arithmetic and copies ran while one was open for 2% of the time, Pallas kernels for 51%

profile of v2, /device:TPU:0, one launch (start us, length us, event | category | flops | bytes accessed | tf_op | source)
XLA Modules:
  0.0 508.9 jit_solution(13799897000032842883)
XLA Ops:
  7.3 3.0 collective-permute-start
  10.3 1.6 collective-permute-start.1
  11.9 2.6 collective-permute-start.2
  16.3 6.9 %collective-permute-done.2.refs_3_ = bf16[3,48,384]{2,1,0:T(8,128)(2,1)S(1)} collective-permute-done((bf16[3,48,384]{2,1,0:T(8,128)(2,1)}, bf16[3,48,384]{2,1,0:T(8,128)(2,1)S(1)}, u32[]{:S(2)}, u32[]{:S(2)}) %collective-permute-start.2) | collective-permute-done | bytes 110624 | tf_op jit(solution)/shard_map/ppermute | solution.py:359
  24.5 1.9 place_line.2
  26.9 1.6 collective-permute-start.5
  28.4 4.3 collective-permute-done.4.refs_2_
  34.6 2.2 place_pairs.4
  36.9 1.6 collective-permute-start.6
  40.7 3.6 collective-permute-start.10
  45.1 5.3 %collective-permute-done.10.refs_4_ = bf16[5,48,384]{2,1,0:T(8,128)(2,1)S(1)} collective-permute-done((bf16[5,48,384]{2,1,0:T(8,128)(2,1)}, bf16[5,48,384]{2,1,0:T(8,128)(2,1)S(1)}, u32[]{:S(2)}, u32[]{:S(2)}) %collective-permute-start.10) | collective-permute-done | bytes 184352 | tf_op jit(solution)/shard_map/ppermute | solution.py:359
  50.4 2.7 collective-permute-done.8.refs_2_
  53.1 5.6 %collective-permute-done.9.refs_3_ = bf16[5,48,384]{2,1,0:T(8,128)(2,1)S(1)} collective-permute-done((bf16[5,48,384]{2,1,0:T(8,128)(2,1)}, bf16[5,48,384]{2,1,0:T(8,128)(2,1)S(1)}, u32[]{:S(2)}, u32[]{:S(2)}) %collective-permute-start.9) | collective-permute-done | bytes 184352 | tf_op jit(solution)/shard_map/ppermute | solution.py:359
  59.4 2.2 place_line.3
  62.5 2.9 place_pairs.5
  69.4 1.7 collective-permute-start.13
  71.6 8.1 %project_self_kernel.1 = (bf16[512,768]{1,0:T(8,128)(2,1)}, bf16[1024,768]{1,0:T(8,128)(2,1)}, bf16[1024,768]{1,0:T(8,128)(2,1)}, bf16[1024,768]{1,0:T(8,128)(2,1)}) custom-call(s32[4]{0:T(128)} %pad_add_fusion.refs_0_.place_ref, bf16[512,768]{1,0:T(8,128)(2,1)} %bitcast.63, bf16[512,768]{1,0:T(8,128)(2,1)} %copy-done.11, f32[3,768]{1,0:T(4,128)} %refs_4_.3, ...), custom_call_target="tpu_custom_call" | custom-call | flops 6000000000 | bytes 1000 | tf_op jit(solution)/shard_map/project_self_kernel/pallas_call | solution.py:398
  79.8 16.1 %collective-permute-done.13.refs_2_ = bf16[2,5,48,384]{3,2,1,0:T(8,128)(2,1)S(1)} collective-permute-done((bf16[2,5,48,384]{3,2,1,0:T(8,128)(2,1)S(1)}, bf16[2,5,48,384]{3,2,1,0:T(8,128)(2,1)S(1)}, u32[]{:S(2)}, u32[]{:S(2)}) %collective-permute-start.13) | collective-permute-done | bytes 368672 | tf_op jit(solution)/shard_map/ppermute | solution.py:363
  97.1 2.6 place_pairs.6
  100.5 12.3 %self_forward.2 = (bf16[512,512]{1,0:T(8,128)(2,1)}, f32[4,2,1,512]{3,2,1,0:T(1,128)}) custom-call(s32[1]{0:T(128)} %bitcast.5.refs_0_, s32[1,4]{1,0:T(1,128)} %refs_2_.13, s32[1,4]{1,0:T(1,128)} %refs_2_.13, bf16[512,768]{1,0:T(8,128)(2,1)} %get-tuple-element.115.refs_5_.refs_3_, bf16[1024,768]{1,0:T(8,128)(2,1)} %get-tuple-element.116.refs_4_, ...), custom_call_target="tpu_custom_call" | custom-call | flops 20000000000 | bytes 1000 | tf_op jit(solution)/shard_map/self_forward/pallas_call | solution.py:285
  112.8 4.6 collective-permute-done.16.refs_2_
  118.5 3.5 place_pairs.7
  124.0 5.9 %collective-permute-start.20 = (bf16[512,768]{1,0:T(8,128)(2,1)}, bf16[512,768]{1,0:T(8,128)(2,1)}, u32[]{:S(2)}, u32[]{:S(2)}) collective-permute-start(bf16[512,768]{1,0:T(8,128)(2,1)} %hold.6), channel_id=1, source_target_pairs={{0,1},{1,0},{2,3},{3,2},{4,5},{5,4},{6,7},{7,6},{8,9},{9,8},{10,11... | collective-permute-start | bytes 2359304 | tf_op jit(solution)/shard_map/ppermute | solution.py:363
  129.9 7.0 %self_forward.3 = (bf16[512,256]{1,0:T(8,128)(2,1)}, f32[2,2,1,512]{3,2,1,0:T(1,128)}) custom-call(s32[1]{0:T(128)} %bitcast.5.refs_0_, s32[1,4]{1,0:T(1,128)} %refs_2_.13, s32[1,4]{1,0:T(1,128)} %refs_2_.13, bf16[512,768]{1,0:T(8,128)(2,1)} %get-tuple-element.115.refs_5_.refs_3_, bf16[1024,768]{1,0:T(8,128)(2,1)} %get-tuple-element.116.refs_4_, ...), custom_call_target="tpu_custom_call" | custom-call | flops 2000000000 | bytes 1000 | tf_op jit(solution)/shard_map/self_forward/pallas_call | solution.py:285
  136.9 5.0 after_self_kernel.1
  141.9 8.5 %collective-permute-done.20.far_b = bf16[512,768]{1,0:T(8,128)(2,1)} collective-permute-done((bf16[512,768]{1,0:T(8,128)(2,1)}, bf16[512,768]{1,0:T(8,128)(2,1)}, u32[]{:S(2)}, u32[]{:S(2)}) %collective-permute-start.20) | collective-permute-done | bytes 786464 | tf_op jit(solution)/shard_map/ppermute | solution.py:363
  150.4 9.9 %project_memory_kernel.1 = (bf16[2048,768]{1,0:T(8,128)(2,1)}, bf16[2048,768]{1,0:T(8,128)(2,1)}) custom-call(s32[4]{0:T(128)} %pad_add_fusion.refs_0_.place_ref, bf16[1024,768]{1,0:T(8,128)(2,1)} %bitcast.48, bf16[512,768]{1,0:T(8,128)(2,1)} %copy-done.13, bf16[512,768]{1,0:T(8,128)(2,1)} %collective-permute-done.20.far_b, ...), custom_call_target="tpu_custom_call" | custom-call | flops 6000000000 | bytes 1000 | tf_op jit(solution)/shard_map/project_memory_kernel/pallas_call | solution.py:779
  160.4 42.6 %cross_forward.1 = (bf16[512,768]{1,0:T(8,128)(2,1)}, f32[6,2,1,512]{3,2,1,0:T(1,128)}) custom-call(s32[1]{0:T(128)} %bitcast.5.refs_0_, s32[1,4]{1,0:T(1,128)} %refs_2_.13, s32[1,4]{1,0:T(1,128)} %refs_2_.11, bf16[512,768]{1,0:T(8,128)(2,1)} %get-tuple-element.125.refs_3_, bf16[2048,768]{1,0:T(8,128)(2,1)} %get-tuple-element.126.refs_4_, ...), custom_call_target="tpu_custom_call" | custom-call | flops 20000000000 | bytes 1000 | tf_op jit(solution)/shard_map/cross_forward/pallas_call | solution.py:285
  203.0 7.5 %all-gather.3.cloned.1.call-done = bf16[36864,128]{1,0:T(8,128)(2,1)} async-done(((bf16[1152,128]{1,0:T(8,128)(2,1)}), bf16[36864,128]{1,0:T(8,128)(2,1)}) %all-gather.3.cloned.1.call-update) | async-done | bytes 9437200 | tf_op jit(solution)/shard_map/all_gather | solution.py:1360
  210.4 27.7 %feed_forward_kernel.1 = (bf16[512,768]{1,0:T(8,128)(2,1)}, f32[512,768]{1,0:T(8,128)}, bf16[512,768]{1,0:T(8,128)(2,1)}, f32[1,768]{1,0:T(1,128)}, bf16[16,2,1152,128]{3,2,1,0:T(8,128)(2,1)}) custom-call(s32[4]{0:T(128)} %pad_add_fusion.refs_0_.place_ref, f32[512,768]{1,0:T(8,128)} %get-tuple-element.124.refs_1_, ...), custom_call_target="tpu_custom_call" | custom-call | flops 6000000000 | bytes 1000 | tf_op jit(solution)/shard_map/feed_forward_kernel/pallas_call | solution.py:398
  238.8 55.0 %cross_backward.1 = (bf16[512,768]{1,0:T(8,128)(2,1)}, bf16[2048,768]{1,0:T(8,128)(2,1)}, bf16[2048,768]{1,0:T(8,128)(2,1)}) custom-call(s32[1]{0:T(128)} %bitcast.5.refs_0_, s32[1,4]{1,0:T(1,128)} %refs_2_.13, s32[1,4]{1,0:T(1,128)} %refs_2_.11, bf16[512,768]{1,0:T(8,128)(2,1)} %get-tuple-element.125.refs_3_, bf16[2048,768]{1,0:T(8,128)(2,1)} %get-tuple-element.126.refs_4_, ...), custom_call_target="tpu_custom_call" | custom-call | flops 20000000000 | bytes 1000 | tf_op jit(solution)/shard_map/cross_backward/pallas_call | solution.py:344
  293.8 19.0 %memory_backward_kernel.1 = (f32[1024,768]{1,0:T(8,128)}, bf16[1024,768]{1,0:T(8,128)(2,1)}, bf16[4,2,2,288,128]{4,3,2,1,0:T(8,128)(2,1)}, bf16[4,2,2,288,128]{4,3,2,1,0:T(8,128)(2,1)}) custom-call(s32[4]{0:T(128)} %pad_add_fusion.refs_0_.place_ref, bf16[2048,768]{1,0:T(8,128)(2,1)} %get-tuple-element.135.dk_ref, ...), custom_call_target="tpu_custom_call" | custom-call | flops 6000000000 | bytes 1000 | tf_op jit(solution)/shard_map/memory_backward_kernel/pallas_call | solution.py:1011
  314.3 10.5 %after_cross_kernel.1 = (f32[512,768]{1,0:T(8,128)}, bf16[512,768]{1,0:T(8,128)(2,1)}, f32[1,768]{1,0:T(1,128)}, bf16[4,2,2,432,128]{4,3,2,1,0:T(8,128)(2,1)}, bf16[4,2,2,432,128]{4,3,2,1,0:T(8,128)(2,1)}) custom-call(s32[4]{0:T(128)} %pad_add_fusion.refs_0_.place_ref, f32[512,768]{1,0:T(8,128)} %get-tuple-element.124.refs_1_, ...), custom_call_target="tpu_custom_call" | custom-call | flops 6000000000 | bytes 1000 | tf_op jit(solution)/shard_map/after_cross_kernel/pallas_call | solution.py:398
  325.3 15.6 %self_backward.2 = (bf16[512,384]{1,0:T(8,128)(2,1)}, bf16[1024,384]{1,0:T(8,128)(2,1)}, bf16[1024,384]{1,0:T(8,128)(2,1)}, f32[3,2,4,512]{3,2,1,0:T(4,128)}) custom-call(s32[1]{0:T(128)} %bitcast.5.refs_0_, s32[1,4]{1,0:T(1,128)} %refs_2_.13, s32[1,4]{1,0:T(1,128)} %refs_2_.13, bf16[512,768]{1,0:T(8,128)(2,1)} %get-tuple-element.115.refs_5_.refs_3_, ...), custom_call_target="tpu_custom_call" | custom-call | flops 20000000000 | bytes 1000 | tf_op jit(solution)/shard_map/self_backward/pallas_call | solution.py:344
  342.1 4.8 scatter_step.4
  347.3 8.6 %collective-permute-start.23 = (bf16[4,2,288,128]{3,2,1,0:T(8,128)(2,1)}, bf16[4,2,288,128]{3,2,1,0:T(8,128)(2,1)S(1)}, u32[]{:S(2)}, u32[]{:S(2)}) collective-permute-start(bf16[4,2,288,128]{3,2,1,0:T(8,128)(2,1)} %get-tuple-element.152), channel_id=1, source_target_pairs={{0,1},{1,0},{2,3},{3,2},{4,5},{5,4},{6,7},{7,6},{8,9},{9,8},{10,11... | collective-permute-start | bytes 1769480 | tf_op jit(solution)/shard_map/ppermute | solution.py:363
  355.9 15.7 %self_backward.3 = (bf16[512,384]{1,0:T(8,128)(2,1)}, bf16[1024,384]{1,0:T(8,128)(2,1)}, bf16[1024,384]{1,0:T(8,128)(2,1)}, f32[3,2,4,512]{3,2,1,0:T(4,128)}) custom-call(s32[1]{0:T(128)} %bitcast.5.refs_0_, s32[1,4]{1,0:T(1,128)} %refs_2_.13, s32[1,4]{1,0:T(1,128)} %refs_2_.13, bf16[512,768]{1,0:T(8,128)(2,1)} %get-tuple-element.115.refs_5_.refs_3_, ...), custom_call_target="tpu_custom_call" | custom-call | flops 20000000000 | bytes 1000 | tf_op jit(solution)/shard_map/self_backward/pallas_call | solution.py:344
  371.5 3.3 collective-permute-done.23.refs_1_
  376.0 4.1 scatter_step.5
  380.1 5.2 %collective-permute-start.27 = (bf16[4,432,128]{2,1,0:T(8,128)(2,1)}, bf16[4,432,128]{2,1,0:T(8,128)(2,1)S(1)}, u32[]{:S(2)}, u32[]{:S(2)}) collective-permute-start(bf16[4,432,128]{2,1,0:T(8,128)(2,1)} %get-tuple-element.162), channel_id=1, source_target_pairs={{0,1},{1,0},{2,3},{3,2},{4,5},{5,4},{6,7},{7,6},{8,9},{9,8},{10,11... | collective-permute-start | bytes 1327112 | tf_op jit(solution)/shard_map/ppermute | solution.py:363
  385.3 8.0 %self_row_grads_kernel.1 = (f32[512,768]{1,0:T(8,128)}, bf16[512,768]{1,0:T(8,128)(2,1)}, f32[1,768]{1,0:T(1,128)}) custom-call(s32[4]{0:T(128)} %pad_add_fusion.refs_0_.place_ref, bf16[512,768]{1,0:T(8,128)(2,1)} %bitcast.65, bf16[512,768]{1,0:T(8,128)(2,1)} %copy-done.11, bf16[512,384]{1,0:T(8,128)(2,1)} %get-tuple-element.142.refs_4_.refs_10_.refs_3_.refs_1_, ...), custom_call_target="tpu_custom_call" | custom-call | flops 6000000000 | bytes 1000 | tf_op jit(solution)/shard_map/self_row_grads_kernel/pallas_call | solution.py:398
  393.3 2.0 collective-permute-done.26.refs_1_
  396.9 2.2 scatter_to_line.2
  399.1 7.7 %self_weight_grads_kernel.1 = (bf16[4,2,2,240,128]{4,3,2,1,0:T(8,128)(2,1)}, bf16[4,2,2,240,128]{4,3,2,1,0:T(8,128)(2,1)}, bf16[4,2,2,192,128]{4,3,2,1,0:T(8,128)(2,1)}, bf16[4,2,2,192,128]{4,3,2,1,0:T(8,128)(2,1)}) custom-call(s32[4]{0:T(128)} %pad_add_fusion.refs_0_.place_ref, bf16[512,384]{1,0:T(8,128)(2,1)} %get-tuple-element.142.refs_4_.refs_10_.refs_3_.refs_1_, ...), custom_call_target="tpu_custom_call" | custom-call | flops 6000000000 | bytes 1000 | tf_op jit(solution)/shard_map/self_weight_grads_kernel/pallas_call | solution.py:398
  407.1 2.2 collective-permute-start.25
  410.7 16.9 %collective-permute-done.31.refs_1_ = f32[21,128]{1,0:T(8,128)S(1)} collective-permute-done((f32[21,128]{1,0:T(8,128)S(1)}, f32[21,128]{1,0:T(8,128)S(1)}, u32[]{:S(2)}, u32[]{:S(2)}) %collective-permute-start.31) | collective-permute-done | bytes 10784 | tf_op jit(solution)/shard_map/ppermute | solution.py:549
  430.8 3.0 collective-permute-start.42
  435.2 4.5 add_rows.1.refs_4_
  440.6 4.1 scatter_step.6
  445.4 3.0 collective-permute-start.45
  449.1 1.9 collective-permute-start.38
  450.9 4.2 finish_rows_kernel.1.refs_8_
  456.2 2.0 scatter_end.3
  458.1 2.4 collective-permute-done.39.refs_3_
  462.0 3.6 scatter_step.7
  465.6 1.8 collective-permute-start.47
  467.5 4.1 collective-permute-done.47.refs_3_
  472.7 2.1 scatter_to_line.3
  476.6 1.8 collective-permute-start.35
  481.5 2.0 collective-permute-start.50
  486.7 3.7 collective-permute-done.37.refs_1_
  491.5 1.6 collective-permute-start.53
  498.3 1.7 scatter_end.4
  500.0 1.8 scatter_end.5
  (260 shorter events, 52.9 us)
Async XLA Ops:
  7.2 59.9 %copy-start = (bf16[2,48,1024]{2,1,0:T(8,128)(2,1)S(1)}, bf16[2,48,1024]{2,1,0:T(8,128)(2,1)}, u32[]{:S(2)}) copy-start(bf16[2,48,1024]{2,1,0:T(8,128)(2,1)} %param.25) | copy-start | bytes 589828
  7.2 32.8 %copy-start.54 = (bf16[48,384]{1,0:T(8,128)(2,1)S(1)}, bf16[48,384]{1,0:T(8,128)(2,1)}, u32[]{:S(2)}) copy-start(bf16[48,384]{1,0:T(8,128)(2,1)} %param.22) | copy-start | bytes 110596
  7.2 32.8 %copy-start.53 = (bf16[48,384]{1,0:T(8,128)(2,1)S(1)}, bf16[48,384]{1,0:T(8,128)(2,1)}, u32[]{:S(2)}) copy-start(bf16[48,384]{1,0:T(8,128)(2,1)} %param.24) | copy-start | bytes 110596
  7.2 32.8 %copy-start.33 = (bf16[3,48,384]{2,1,0:T(8,128)(2,1)S(1)}, bf16[3,48,384]{2,1,0:T(8,128)(2,1)}, u32[]{:S(2)}) copy-start(bf16[3,48,384]{2,1,0:T(8,128)(2,1)} %param.23) | copy-start | bytes 331780
  7.2 203.2 %all-gather.3.cloned.1.call-start = ((), (), s32[]{:S(2)}) async-start(), calls=%async_computation.2 | async-start | bytes 9732096 | tf_op jit(solution)/shard_map/all_gather | solution.py:1360
  7.3 25.8 %collective-permute-start = (bf16[512,768]{1,0:T(8,128)(2,1)}, bf16[512,768]{1,0:T(8,128)(2,1)S(1)}, u32[]{:S(2)}, u32[]{:S(2)}) collective-permute-start(bf16[512,768]{1,0:T(8,128)(2,1)} %bitcast.62), channel_id=1, source_target_pairs={{0,1},{1,0},{2,3},{3,2},{4,5},{5,4},{6,7},{7,6},{8,9},{9,8},{10,11... | collective-permute-start | bytes 2359304 | tf_op jit(solution)/shard_map/ppermute | solution.py:363
  10.3 6.0 %collective-permute-start.1 = (bf16[3,48,384]{2,1,0:T(8,128)(2,1)}, bf16[3,48,384]{2,1,0:T(8,128)(2,1)S(1)}, u32[]{:S(2)}, u32[]{:S(2)}) collective-permute-start(bf16[3,48,384]{2,1,0:T(8,128)(2,1)} %refs_1_.7), channel_id=1, source_target_pairs={{0,8},{2,10},{4,12},{6,14},{8,0},{10,2},{12,4},{14,6},{16,24},{18,... | collective-permute-start | bytes 331784 | tf_op jit(solution)/shard_map/ppermute | solution.py:359
  11.9 11.3 %collective-permute-start.2 = (bf16[3,48,384]{2,1,0:T(8,128)(2,1)}, bf16[3,48,384]{2,1,0:T(8,128)(2,1)S(1)}, u32[]{:S(2)}, u32[]{:S(2)}) collective-permute-start(bf16[3,48,384]{2,1,0:T(8,128)(2,1)} %refs_1_.7), channel_id=1, source_target_pairs={{0,16},{2,18},{4,20},{6,22},{8,24},{10,26},{12,28},{14,30},{16,0},... | collective-permute-start | bytes 331784 | tf_op jit(solution)/shard_map/ppermute | solution.py:359
  14.4 8.7 %collective-permute-start.3 = (bf16[3,48,384]{2,1,0:T(8,128)(2,1)}, bf16[3,48,384]{2,1,0:T(8,128)(2,1)S(1)}, u32[]{:S(2)}, u32[]{:S(2)}) collective-permute-start(bf16[3,48,384]{2,1,0:T(8,128)(2,1)} %refs_1_.7), channel_id=1, source_target_pairs={{0,24},{2,26},{4,28},{6,30},{8,16},{10,18},{12,20},{14,22},{16,8},... | collective-permute-start | bytes 331784 | tf_op jit(solution)/shard_map/ppermute | solution.py:359
  26.4 6.4 %collective-permute-start.4 = (bf16[2,3,48,384]{3,2,1,0:T(8,128)(2,1)}, bf16[2,3,48,384]{3,2,1,0:T(8,128)(2,1)S(1)}, u32[]{:S(2)}, u32[]{:S(2)}) collective-permute-start(bf16[2,3,48,384]{3,2,1,0:T(8,128)(2,1)} %get-tuple-element.107.refs_1_), channel_id=1, source_target_pairs={{0,1},{1,0},{2,3},{3,2},{4,5},{5,4},{6,7},{7,6},{8,9},{9,8},{10,11... | collective-permute-start | bytes 663560 | tf_op jit(solution)/shard_map/ppermute | solution.py:363
  26.9 6.1 %collective-permute-start.5 = (bf16[2,3,48,384]{3,2,1,0:T(8,128)(2,1)}, bf16[2,3,48,384]{3,2,1,0:T(8,128)(2,1)S(1)}, u32[]{:S(2)}, u32[]{:S(2)}) collective-permute-start(bf16[2,3,48,384]{3,2,1,0:T(8,128)(2,1)} %get-tuple-element.108.refs_3_.refs_2_), channel_id=1, source_target_pairs={{0,4},{2,6},{4,0},{6,2},{8,12},{10,14},{12,8},{14,10},{16,20},{18,... | collective-permute-start | bytes 663560 | tf_op jit(solution)/shard_map/ppermute | solution.py:359
  36.9 24.7 %collective-permute-start.6 = (bf16[2,2,3,48,384]{4,3,2,1,0:T(8,128)(2,1)}, bf16[2,2,3,48,384]{4,3,2,1,0:T(8,128)(2,1)S(1)}, u32[]{:S(2)}, u32[]{:S(2)}) collective-permute-start(bf16[2,2,3,48,384]{4,3,2,1,0:T(8,128)(2,1)} %get-tuple-element.109.refs_5_.refs_1_), channel_id=1, source_target_pairs={{0,4},{2,6},{4,0},{6,2},{8,12},{10,14},{12,8},{14,10},{16,20},{18,... | collective-permute-start | bytes 1327112 | tf_op jit(solution)/shard_map/ppermute | solution.py:359
  38.5 23.1 %collective-permute-start.7 = (bf16[2,2,3,48,384]{4,3,2,1,0:T(8,128)(2,1)}, bf16[2,2,3,48,384]{4,3,2,1,0:T(8,128)(2,1)S(1)}, u32[]{:S(2)}, u32[]{:S(2)}) collective-permute-start(bf16[2,2,3,48,384]{4,3,2,1,0:T(8,128)(2,1)} %get-tuple-element.110.refs_6_.refs_3_), channel_id=1, source_target_pairs={{0,1},{1,0},{2,3},{3,2},{4,5},{5,4},{6,7},{7,6},{8,9},{9,8},{10,11... | collective-permute-start | bytes 1327112 | tf_op jit(solution)/shard_map/ppermute | solution.py:363
  40.7 9.7 %collective-permute-start.10 = (bf16[5,48,384]{2,1,0:T(8,128)(2,1)}, bf16[5,48,384]{2,1,0:T(8,128)(2,1)S(1)}, u32[]{:S(2)}, u32[]{:S(2)}) collective-permute-start(bf16[5,48,384]{2,1,0:T(8,128)(2,1)} %hold.4.refs_1_), channel_id=1, source_target_pairs={{0,24},{2,26},{4,28},{6,30},{8,16},{10,18},{12,20},{14,22},{16,8},... | collective-permute-start | bytes 552968 | tf_op jit(solution)/shard_map/ppermute | solution.py:359
  44.3 8.8 %collective-permute-start.8 = (bf16[5,48,384]{2,1,0:T(8,128)(2,1)}, bf16[5,48,384]{2,1,0:T(8,128)(2,1)S(1)}, u32[]{:S(2)}, u32[]{:S(2)}) collective-permute-start(bf16[5,48,384]{2,1,0:T(8,128)(2,1)} %hold.4.refs_1_), channel_id=1, source_target_pairs={{0,8},{2,10},{4,12},{6,14},{8,0},{10,2},{12,4},{14,6},{16,24},{18,... | collective-permute-start | bytes 552968 | tf_op jit(solution)/shard_map/ppermute | solution.py:359
  44.3 14.4 %collective-permute-start.9 = (bf16[5,48,384]{2,1,0:T(8,128)(2,1)}, bf16[5,48,384]{2,1,0:T(8,128)(2,1)S(1)}, u32[]{:S(2)}, u32[]{:S(2)}) collective-permute-start(bf16[5,48,384]{2,1,0:T(8,128)(2,1)} %hold.4.refs_1_), channel_id=1, source_target_pairs={{0,16},{2,18},{4,20},{6,22},{8,24},{10,26},{12,28},{14,30},{16,0},... | collective-permute-start | bytes 552968 | tf_op jit(solution)/shard_map/ppermute | solution.py:359
  65.4 6.2 %collective-permute-start.11 = (bf16[2,2,2,3,48,384]{5,4,3,2,1,0:T(8,128)(2,1)}, bf16[2,2,2,3,48,384]{5,4,3,2,1,0:T(8,128)(2,1)}, u32[]{:S(2)}, u32[]{:S(2)}) collective-permute-start(bf16[2,2,2,3,48,384]{5,4,3,2,1,0:T(8,128)(2,1)} %get-tuple-element.113.refs_4_.refs_1_.refs_9_), channel_id=1, source_target_pairs={{0,2},{2,0},{4,6},{6,4},{8,10},{10,8},{12,14},{14,12},{16,18},{18,... | collective-permute-start | bytes 2654216 | tf_op jit(solution)/shard_map/ppermute | solution.py:359
  65.4 6.2 %collective-permute-start.12 = (bf16[2,2,2,3,48,384]{5,4,3,2,1,0:T(8,128)(2,1)}, bf16[2,2,2,3,48,384]{5,4,3,2,1,0:T(8,128)(2,1)}, u32[]{:S(2)}, u32[]{:S(2)}) collective-permute-start(bf16[2,2,2,3,48,384]{5,4,3,2,1,0:T(8,128)(2,1)} %get-tuple-element.114.refs_6_.refs_2_.refs_11_), channel_id=1, source_target_pairs={{0,2},{2,0},{4,6},{6,4},{8,10},{10,8},{12,14},{14,12},{16,18},{18,... | collective-permute-start | bytes 2654216 | tf_op jit(solution)/shard_map/ppermute | solution.py:359
  68.3 27.6 %collective-permute-start.15 = (bf16[512,768]{1,0:T(8,128)(2,1)}, bf16[512,768]{1,0:T(8,128)(2,1)S(1)}, u32[]{:S(2)}, u32[]{:S(2)}) collective-permute-start(bf16[512,768]{1,0:T(8,128)(2,1)} %hold.5), channel_id=1, source_target_pairs={{0,1},{1,0},{2,3},{3,2},{4,5},{5,4},{6,7},{7,6},{8,9},{9,8},{10,11... | collective-permute-start | bytes 2359304 | tf_op jit(solution)/shard_map/ppermute | solution.py:363
  69.4 26.5 %collective-permute-start.13 = (bf16[2,5,48,384]{3,2,1,0:T(8,128)(2,1)S(1)}, bf16[2,5,48,384]{3,2,1,0:T(8,128)(2,1)S(1)}, u32[]{:S(2)}, u32[]{:S(2)}) collective-permute-start(bf16[2,5,48,384]{3,2,1,0:T(8,128)(2,1)S(1)} %copy-done.7), channel_id=1, source_target_pairs={{0,1},{1,0},{2,3},{3,2},{4,5},{5,4},{6,7},{7,6},{8,9},{9,8},{10,11... | collective-permute-start | bytes 1105928 | tf_op jit(solution)/shard_map/ppermute | solution.py:363
  71.1 24.8 %collective-permute-start.14 = (bf16[2,5,48,384]{3,2,1,0:T(8,128)(2,1)S(1)}, bf16[2,5,48,384]{3,2,1,0:T(8,128)(2,1)S(1)}, u32[]{:S(2)}, u32[]{:S(2)}) collective-permute-start(bf16[2,5,48,384]{3,2,1,0:T(8,128)(2,1)S(1)} %copy-done.8), channel_id=1, source_target_pairs={{0,4},{2,6},{4,0},{6,2},{8,12},{10,14},{12,8},{14,10},{16,20},{18,... | collective-permute-start | bytes 1105928 | tf_op jit(solution)/shard_map/ppermute | solution.py:359
  99.7 17.8 %collective-permute-start.16 = (bf16[2,2,5,48,384]{4,3,2,1,0:T(8,128)(2,1)}, bf16[2,2,5,48,384]{4,3,2,1,0:T(8,128)(2,1)S(1)}, u32[]{:S(2)}, u32[]{:S(2)}) collective-permute-start(bf16[2,2,5,48,384]{4,3,2,1,0:T(8,128)(2,1)} %get-tuple-element.118.refs_7_.refs_1_), channel_id=1, source_target_pairs={{0,4},{2,6},{4,0},{6,2},{8,12},{10,14},{12,8},{14,10},{16,20},{18,... | collective-permute-start | bytes 2211848 | tf_op jit(solution)/shard_map/ppermute | solution.py:359
  100.2 17.5 %collective-permute-start.17 = (bf16[2,2,5,48,384]{4,3,2,1,0:T(8,128)(2,1)}, bf16[2,2,5,48,384]{4,3,2,1,0:T(8,128)(2,1)S(1)}, u32[]{:S(2)}, u32[]{:S(2)}) collective-permute-start(bf16[2,2,5,48,384]{4,3,2,1,0:T(8,128)(2,1)} %get-tuple-element.119.refs_8_.refs_3_.refs_2_), channel_id=1, source_target_pairs={{0,1},{1,0},{2,3},{3,2},{4,5},{5,4},{6,7},{7,6},{8,9},{9,8},{10,11... | collective-permute-start | bytes 2211848 | tf_op jit(solution)/shard_map/ppermute | solution.py:363
  122.1 377.9 %reduce-scatter.2.cloned.1.call-start = ((), (), s32[]{:S(2)}) async-start(), calls=%async_computation.1 | async-start | bytes 9732096 | tf_op jit(solution)/shard_map/reduce_scatter | solution.py:1377
  123.5 13.4 %collective-permute-start.18 = (bf16[2,2,2,5,48,384]{5,4,3,2,1,0:T(8,128)(2,1)S(1)}, bf16[2,2,2,5,48,384]{5,4,3,2,1,0:T(8,128)(2,1)}, u32[]{:S(2)}, u32[]{:S(2)}) collective-permute-start(bf16[2,2,2,5,48,384]{5,4,3,2,1,0:T(8,128)(2,1)S(1)} %copy-done.2), channel_id=1, source_target_pairs={{0,2},{2,0},{4,6},{6,4},{8,10},{10,8},{12,14},{14,12},{16,18},{18,... | collective-permute-start | bytes 4423688 | tf_op jit(solution)/shard_map/ppermute | solution.py:359
  123.9 13.0 %collective-permute-start.19 = (bf16[2,2,2,5,48,384]{5,4,3,2,1,0:T(8,128)(2,1)S(1)}, bf16[2,2,2,5,48,384]{5,4,3,2,1,0:T(8,128)(2,1)}, u32[]{:S(2)}, u32[]{:S(2)}) collective-permute-start(bf16[2,2,2,5,48,384]{5,4,3,2,1,0:T(8,128)(2,1)S(1)} %copy-done.3), channel_id=1, source_target_pairs={{0,2},{2,0},{4,6},{6,4},{8,10},{10,8},{12,14},{14,12},{16,18},{18,... | collective-permute-start | bytes 4423688 | tf_op jit(solution)/shard_map/ppermute | solution.py:359
  124.0 26.4 %collective-permute-start.20 = (bf16[512,768]{1,0:T(8,128)(2,1)}, bf16[512,768]{1,0:T(8,128)(2,1)}, u32[]{:S(2)}, u32[]{:S(2)}) collective-permute-start(bf16[512,768]{1,0:T(8,128)(2,1)} %hold.6), channel_id=1, source_target_pairs={{0,1},{1,0},{2,3},{3,2},{4,5},{5,4},{6,7},{7,6},{8,9},{9,8},{10,11... | collective-permute-start | bytes 2359304 | tf_op jit(solution)/shard_map/ppermute | solution.py:363
  238.8 55.0 %copy-start.65 = (f32[6,2,1,512]{3,2,1,0:T(1,128)}, f32[6,2,1,512]{3,2,1,0:T(1,128)S(1)}, u32[]{:S(2)}) copy-start(f32[6,2,1,512]{3,2,1,0:T(1,128)S(1)} %constant_dynamic-update-slice_fusion.refs_7_) | copy-start | bytes 73732
  312.8 97.7 %collective-permute-start.30 = (bf16[1024,768]{1,0:T(8,128)(2,1)}, bf16[1024,768]{1,0:T(8,128)(2,1)S(1)}, u32[]{:S(2)}, u32[]{:S(2)}) collective-permute-start(bf16[1024,768]{1,0:T(8,128)(2,1)} %get-tuple-element.137.refs_17_), channel_id=1, source_target_pairs={{0,1},{1,0},{2,3},{3,2},{4,5},{5,4},{6,7},{7,6},{8,9},{9,8},{10,11... | collective-permute-start | bytes 4718600 | tf_op jit(solution)/shard_map/ppermute | solution.py:363
  324.7 16.1 %collective-permute-start.22 = (bf16[4,2,2,432,128]{4,3,2,1,0:T(8,128)(2,1)}, bf16[4,2,2,432,128]{4,3,2,1,0:T(8,128)(2,1)S(1)}, u32[]{:S(2)}, u32[]{:S(2)}) collective-permute-start(bf16[4,2,2,432,128]{4,3,2,1,0:T(8,128)(2,1)} %get-tuple-element.145), channel_id=1, source_target_pairs={{0,2},{2,0},{4,6},{6,4},{8,10},{10,8},{12,14},{14,12},{16,18},{18,... | collective-permute-start | bytes 5308424 | tf_op jit(solution)/shard_map/ppermute | solution.py:359
  324.7 16.1 %collective-permute-start.21 = (bf16[4,2,2,288,128]{4,3,2,1,0:T(8,128)(2,1)}, bf16[4,2,2,288,128]{4,3,2,1,0:T(8,128)(2,1)}, u32[]{:S(2)}, u32[]{:S(2)}) collective-permute-start(bf16[4,2,2,288,128]{4,3,2,1,0:T(8,128)(2,1)} %get-tuple-element.144), channel_id=1, source_target_pairs={{0,2},{2,0},{4,6},{6,4},{8,10},{10,8},{12,14},{14,12},{16,18},{18,... | collective-permute-start | bytes 3538952 | tf_op jit(solution)/shard_map/ppermute | solution.py:359
  346.8 28.1 %collective-permute-start.24 = (bf16[4,2,432,128]{3,2,1,0:T(8,128)(2,1)}, bf16[4,2,432,128]{3,2,1,0:T(8,128)(2,1)S(1)}, u32[]{:S(2)}, u32[]{:S(2)}) collective-permute-start(bf16[4,2,432,128]{3,2,1,0:T(8,128)(2,1)} %get-tuple-element.154), channel_id=1, source_target_pairs={{0,4},{2,6},{4,0},{6,2},{8,12},{10,14},{12,8},{14,10},{16,20},{18,... | collective-permute-start | bytes 2654216 | tf_op jit(solution)/shard_map/ppermute | solution.py:359
  347.3 27.6 %collective-permute-start.23 = (bf16[4,2,288,128]{3,2,1,0:T(8,128)(2,1)}, bf16[4,2,288,128]{3,2,1,0:T(8,128)(2,1)S(1)}, u32[]{:S(2)}, u32[]{:S(2)}) collective-permute-start(bf16[4,2,288,128]{3,2,1,0:T(8,128)(2,1)} %get-tuple-element.152), channel_id=1, source_target_pairs={{0,1},{1,0},{2,3},{3,2},{4,5},{5,4},{6,7},{7,6},{8,9},{9,8},{10,11... | collective-permute-start | bytes 1769480 | tf_op jit(solution)/shard_map/ppermute | solution.py:363
  380.1 16.0 %collective-permute-start.27 = (bf16[4,432,128]{2,1,0:T(8,128)(2,1)}, bf16[4,432,128]{2,1,0:T(8,128)(2,1)S(1)}, u32[]{:S(2)}, u32[]{:S(2)}) collective-permute-start(bf16[4,432,128]{2,1,0:T(8,128)(2,1)} %get-tuple-element.162), channel_id=1, source_target_pairs={{0,1},{1,0},{2,3},{3,2},{4,5},{5,4},{6,7},{7,6},{8,9},{9,8},{10,11... | collective-permute-start | bytes 1327112 | tf_op jit(solution)/shard_map/ppermute | solution.py:363
  385.3 10.0 %collective-permute-start.26 = (bf16[4,288,128]{2,1,0:T(8,128)(2,1)}, bf16[4,288,128]{2,1,0:T(8,128)(2,1)S(1)}, u32[]{:S(2)}, u32[]{:S(2)}) collective-permute-start(bf16[4,288,128]{2,1,0:T(8,128)(2,1)} %get-tuple-element.160), channel_id=1, source_target_pairs={{0,4},{2,6},{4,0},{6,2},{8,12},{10,14},{12,8},{14,10},{16,20},{18,... | collective-permute-start | bytes 884744 | tf_op jit(solution)/shard_map/ppermute | solution.py:359
  406.8 32.9 %collective-permute-start.28 = (bf16[4,2,2,240,128]{4,3,2,1,0:T(8,128)(2,1)}, bf16[4,2,2,240,128]{4,3,2,1,0:T(8,128)(2,1)S(1)}, u32[]{:S(2)}, u32[]{:S(2)}) collective-permute-start(bf16[4,2,2,240,128]{4,3,2,1,0:T(8,128)(2,1)} %get-tuple-element.165), channel_id=1, source_target_pairs={{0,2},{2,0},{4,6},{6,4},{8,10},{10,8},{12,14},{14,12},{16,18},{18,... | collective-permute-start | bytes 2949128 | tf_op jit(solution)/shard_map/ppermute | solution.py:359
  407.1 43.8 %collective-permute-start.25 = (bf16[512,768]{1,0:T(8,128)(2,1)S(1)}, bf16[512,768]{1,0:T(8,128)(2,1)}, u32[]{:S(2)}, u32[]{:S(2)}) collective-permute-start(bf16[512,768]{1,0:T(8,128)(2,1)S(1)} %copy-done.12), channel_id=1, source_target_pairs={{0,1},{1,0},{2,3},{3,2},{4,5},{5,4},{6,7},{7,6},{8,9},{9,8},{10,11... | collective-permute-start | bytes 2359304 | tf_op jit(solution)/shard_map/ppermute | solution.py:363
  409.4 21.5 %collective-permute-start.29 = (bf16[4,2,2,192,128]{4,3,2,1,0:T(8,128)(2,1)}, bf16[4,2,2,192,128]{4,3,2,1,0:T(8,128)(2,1)}, u32[]{:S(2)}, u32[]{:S(2)}) collective-permute-start(bf16[4,2,2,192,128]{4,3,2,1,0:T(8,128)(2,1)} %get-tuple-element.167), channel_id=1, source_target_pairs={{0,2},{2,0},{4,6},{6,4},{8,10},{10,8},{12,14},{14,12},{16,18},{18,... | collective-permute-start | bytes 2359304 | tf_op jit(solution)/shard_map/ppermute | solution.py:359
  410.1 23.7 %copy-start.47 = (f32[21,128]{1,0:T(8,128)}, f32[21,128]{1,0:T(8,128)S(1)}, u32[]{:S(2)}) copy-start(f32[21,128]{1,0:T(8,128)S(1)} %maximum_bitcast_fusion.refs_0_) | copy-start | bytes 32260
  410.1 17.5 %collective-permute-start.31 = (f32[21,128]{1,0:T(8,128)S(1)}, f32[21,128]{1,0:T(8,128)S(1)}, u32[]{:S(2)}, u32[]{:S(2)}) collective-permute-start(f32[21,128]{1,0:T(8,128)S(1)} %maximum_bitcast_fusion.refs_0_), channel_id=1, source_target_pairs={{0,1},{1,0},{2,3},{3,2},{4,5},{5,4},{6,7},{7,6},{8,9},{9,8},{10,11... | collective-permute-start | bytes 32264 | tf_op jit(solution)/shard_map/ppermute | solution.py:549
  410.6 24.7 %copy-start.5 = (bf16[1024,768]{1,0:T(8,128)(2,1)}, bf16[1024,768]{1,0:T(8,128)(2,1)S(1)}, u32[]{:S(2)}) copy-start(bf16[1024,768]{1,0:T(8,128)(2,1)S(1)} %collective-permute-done.30.refs_1_) | copy-start | bytes 4718596
  410.6 18.1 %collective-permute-start.32 = (f32[21,128]{1,0:T(8,128)S(1)}, f32[21,128]{1,0:T(8,128)S(1)}, u32[]{:S(2)}, u32[]{:S(2)}) collective-permute-start(f32[21,128]{1,0:T(8,128)S(1)} %maximum_bitcast_fusion.refs_0_), channel_id=1, source_target_pairs={{0,2},{1,3},{2,0},{3,1},{4,6},{5,7},{6,4},{7,5},{8,10},{9,11},{10,... | collective-permute-start | bytes 32264 | tf_op jit(solution)/shard_map/ppermute | solution.py:549
  427.7 3.1 collective-permute-start.33
  428.7 16.1 %collective-permute-start.40 = (bf16[288,128]{1,0:T(8,128)(2,1)}, bf16[288,128]{1,0:T(8,128)(2,1)S(1)}, u32[]{:S(2)}, u32[]{:S(2)}) collective-permute-start(bf16[288,128]{1,0:T(8,128)(2,1)} %get-tuple-element.178), channel_id=1, source_target_pairs={{0,8},{2,10},{4,12},{6,14},{8,0},{10,2},{12,4},{14,6},{16,24},{18,... | collective-permute-start | bytes 221192 | tf_op jit(solution)/shard_map/ppermute | solution.py:359
  430.8 14.6 %collective-permute-start.41 = (bf16[288,128]{1,0:T(8,128)(2,1)}, bf16[288,128]{1,0:T(8,128)(2,1)S(1)}, u32[]{:S(2)}, u32[]{:S(2)}) collective-permute-start(bf16[288,128]{1,0:T(8,128)(2,1)} %get-tuple-element.179), channel_id=1, source_target_pairs={{0,16},{2,18},{4,20},{6,22},{8,24},{10,26},{12,28},{14,30},{16,0},... | collective-permute-start | bytes 221192 | tf_op jit(solution)/shard_map/ppermute | solution.py:359
  430.8 17.6 %collective-permute-start.42 = (bf16[288,128]{1,0:T(8,128)(2,1)}, bf16[288,128]{1,0:T(8,128)(2,1)S(1)}, u32[]{:S(2)}, u32[]{:S(2)}) collective-permute-start(bf16[288,128]{1,0:T(8,128)(2,1)} %get-tuple-element.180), channel_id=1, source_target_pairs={{0,24},{2,26},{4,28},{6,30},{8,16},{10,18},{12,20},{14,22},{16,8},... | collective-permute-start | bytes 221192 | tf_op jit(solution)/shard_map/ppermute | solution.py:359
  439.7 15.4 %collective-permute-start.43 = (bf16[432,128]{1,0:T(8,128)(2,1)}, bf16[432,128]{1,0:T(8,128)(2,1)S(1)}, u32[]{:S(2)}, u32[]{:S(2)}) collective-permute-start(bf16[432,128]{1,0:T(8,128)(2,1)} %get-tuple-element.182), channel_id=1, source_target_pairs={{0,8},{2,10},{4,12},{6,14},{8,0},{10,2},{12,4},{14,6},{16,24},{18,... | collective-permute-start | bytes 331784 | tf_op jit(solution)/shard_map/ppermute | solution.py:359
  444.8 10.7 %collective-permute-start.44 = (bf16[432,128]{1,0:T(8,128)(2,1)S(1)}, bf16[432,128]{1,0:T(8,128)(2,1)S(1)}, u32[]{:S(2)}, u32[]{:S(2)}) collective-permute-start(bf16[432,128]{1,0:T(8,128)(2,1)S(1)} %copy-done.72), channel_id=1, source_target_pairs={{0,16},{2,18},{4,20},{6,22},{8,24},{10,26},{12,28},{14,30},{16,0},... | collective-permute-start | bytes 331784 | tf_op jit(solution)/shard_map/ppermute | solution.py:359
  445.4 10.1 %collective-permute-start.45 = (bf16[432,128]{1,0:T(8,128)(2,1)S(1)}, bf16[432,128]{1,0:T(8,128)(2,1)S(1)}, u32[]{:S(2)}, u32[]{:S(2)}) collective-permute-start(bf16[432,128]{1,0:T(8,128)(2,1)S(1)} %copy-done.71), channel_id=1, source_target_pairs={{0,24},{2,26},{4,28},{6,30},{8,16},{10,18},{12,20},{14,22},{16,8},... | collective-permute-start | bytes 331784 | tf_op jit(solution)/shard_map/ppermute | solution.py:359
  449.1 12.2 %collective-permute-start.38 = (bf16[4,2,240,128]{3,2,1,0:T(8,128)(2,1)}, bf16[4,2,240,128]{3,2,1,0:T(8,128)(2,1)S(1)}, u32[]{:S(2)}, u32[]{:S(2)}) collective-permute-start(bf16[4,2,240,128]{3,2,1,0:T(8,128)(2,1)} %get-tuple-element.175), channel_id=1, source_target_pairs={{0,1},{1,0},{2,3},{3,2},{4,5},{5,4},{6,7},{7,6},{8,9},{9,8},{10,11... | collective-permute-start | bytes 1474568 | tf_op jit(solution)/shard_map/ppermute | solution.py:363
  450.9 9.7 %collective-permute-start.39 = (bf16[4,2,192,128]{3,2,1,0:T(8,128)(2,1)}, bf16[4,2,192,128]{3,2,1,0:T(8,128)(2,1)S(1)}, u32[]{:S(2)}, u32[]{:S(2)}) collective-permute-start(bf16[4,2,192,128]{3,2,1,0:T(8,128)(2,1)} %get-tuple-element.177), channel_id=1, source_target_pairs={{0,4},{2,6},{4,0},{6,2},{8,12},{10,14},{12,8},{14,10},{16,20},{18,... | collective-permute-start | bytes 1179656 | tf_op jit(solution)/shard_map/ppermute | solution.py:359
  462.0 39.8 %copy-start.1 = (bf16[2,48,1024]{2,1,0:T(8,128)(2,1)S(1)}, bf16[2,48,1024]{2,1,0:T(8,128)(2,1)}, u32[]{:S(2)}) copy-start(bf16[2,48,1024]{2,1,0:T(8,128)(2,1)} %param.25) | copy-start | bytes 589828
  465.6 6.4 %collective-permute-start.46 = (bf16[4,240,128]{2,1,0:T(8,128)(2,1)}, bf16[4,240,128]{2,1,0:T(8,128)(2,1)S(1)}, u32[]{:S(2)}, u32[]{:S(2)}) collective-permute-start(bf16[4,240,128]{2,1,0:T(8,128)(2,1)} %get-tuple-element.187), channel_id=1, source_target_pairs={{0,4},{2,6},{4,0},{6,2},{8,12},{10,14},{12,8},{14,10},{16,20},{18,... | collective-permute-start | bytes 737288 | tf_op jit(solution)/shard_map/ppermute | solution.py:359
  465.6 5.9 %collective-permute-start.47 = (bf16[4,192,128]{2,1,0:T(8,128)(2,1)}, bf16[4,192,128]{2,1,0:T(8,128)(2,1)S(1)}, u32[]{:S(2)}, u32[]{:S(2)}) collective-permute-start(bf16[4,192,128]{2,1,0:T(8,128)(2,1)} %get-tuple-element.189), channel_id=1, source_target_pairs={{0,1},{1,0},{2,3},{3,2},{4,5},{5,4},{6,7},{7,6},{8,9},{9,8},{10,11... | collective-permute-start | bytes 589832 | tf_op jit(solution)/shard_map/ppermute | solution.py:363
  474.8 16.7 %collective-permute-start.51 = (bf16[192,128]{1,0:T(8,128)(2,1)}, bf16[192,128]{1,0:T(8,128)(2,1)S(1)}, u32[]{:S(2)}, u32[]{:S(2)}) collective-permute-start(bf16[192,128]{1,0:T(8,128)(2,1)} %get-tuple-element.195), channel_id=1, source_target_pairs={{0,8},{2,10},{4,12},{6,14},{8,0},{10,2},{12,4},{14,6},{16,24},{18,... | collective-permute-start | bytes 147464 | tf_op jit(solution)/shard_map/ppermute | solution.py:359
  475.6 4.7 collective-permute-start.34
  476.6 4.9 collective-permute-start.35
  478.4 5.1 %collective-permute-start.36 = (f32[21,128]{1,0:T(8,128)S(1)}, f32[21,128]{1,0:T(8,128)S(1)}, u32[]{:S(2)}, u32[]{:S(2)}) collective-permute-start(f32[21,128]{1,0:T(8,128)S(1)} %copy-done.32), channel_id=1, source_target_pairs={{0,12},{1,13},{2,14},{3,15},{4,8},{5,9},{6,10},{7,11},{8,4},{9,5},... | collective-permute-start | bytes 32264 | tf_op jit(solution)/shard_map/ppermute | solution.py:549
  479.1 18.5 %collective-permute-start.48 = (bf16[240,128]{1,0:T(8,128)(2,1)}, bf16[240,128]{1,0:T(8,128)(2,1)S(1)}, u32[]{:S(2)}, u32[]{:S(2)}) collective-permute-start(bf16[240,128]{1,0:T(8,128)(2,1)} %get-tuple-element.191), channel_id=1, source_target_pairs={{0,8},{2,10},{4,12},{6,14},{8,0},{10,2},{12,4},{14,6},{16,24},{18,... | collective-permute-start | bytes 184328 | tf_op jit(solution)/shard_map/ppermute | solution.py:359
  480.3 17.3 %collective-permute-start.49 = (bf16[240,128]{1,0:T(8,128)(2,1)}, bf16[240,128]{1,0:T(8,128)(2,1)S(1)}, u32[]{:S(2)}, u32[]{:S(2)}) collective-permute-start(bf16[240,128]{1,0:T(8,128)(2,1)} %get-tuple-element.192), channel_id=1, source_target_pairs={{0,16},{2,18},{4,20},{6,22},{8,24},{10,26},{12,28},{14,30},{16,0},... | collective-permute-start | bytes 184328 | tf_op jit(solution)/shard_map/ppermute | solution.py:359
  481.5 16.1 %collective-permute-start.50 = (bf16[240,128]{1,0:T(8,128)(2,1)}, bf16[240,128]{1,0:T(8,128)(2,1)S(1)}, u32[]{:S(2)}, u32[]{:S(2)}) collective-permute-start(bf16[240,128]{1,0:T(8,128)(2,1)} %get-tuple-element.193), channel_id=1, source_target_pairs={{0,24},{2,26},{4,28},{6,30},{8,16},{10,18},{12,20},{14,22},{16,8},... | collective-permute-start | bytes 184328 | tf_op jit(solution)/shard_map/ppermute | solution.py:359
  485.5 5.0 collective-permute-start.37
  490.4 6.8 %collective-permute-start.52 = (bf16[192,128]{1,0:T(8,128)(2,1)}, bf16[192,128]{1,0:T(8,128)(2,1)S(1)}, u32[]{:S(2)}, u32[]{:S(2)}) collective-permute-start(bf16[192,128]{1,0:T(8,128)(2,1)} %get-tuple-element.196), channel_id=1, source_target_pairs={{0,16},{2,18},{4,20},{6,22},{8,24},{10,26},{12,28},{14,30},{16,0},... | collective-permute-start | bytes 147464 | tf_op jit(solution)/shard_map/ppermute | solution.py:359
  491.5 6.1 %collective-permute-start.53 = (bf16[192,128]{1,0:T(8,128)(2,1)}, bf16[192,128]{1,0:T(8,128)(2,1)S(1)}, u32[]{:S(2)}, u32[]{:S(2)}) collective-permute-start(bf16[192,128]{1,0:T(8,128)(2,1)} %get-tuple-element.197), channel_id=1, source_target_pairs={{0,24},{2,26},{4,28},{6,30},{8,16},{10,18},{12,20},{14,22},{16,8},... | collective-permute-start | bytes 147464 | tf_op jit(solution)/shard_map/ppermute | solution.py:359
  (65 other events, 187.9 us)
Sparse Core Ops, SparseCore 0:
  122.2 88.1 all-gather.2
  238.2 145.3 reduce-scatter.1

commit v3 on v2

--- a/solution.py
+++ b/solution.py
@@ -64,25 +64,8 @@
         scratch[index] = source_ref[index * step : (index + 1) * step, :].T
 
 
-def ranges(first, rows, q_edges, k_edges, causal, step):
-    last = first + rows - 1
-    starts, ends = k_edges[:-1], k_edges[1:]
-    low_start = pick(first, q_edges, starts)
-    high_start = pick(last, q_edges, starts)
-    low_end = pick(first, q_edges, ends)
-    high_end = pick(last, q_edges, ends)
-    if causal:
-        low_end = jnp.minimum(low_end, first + 1)
-        high_end = jnp.minimum(high_end, last + 1)
-    low = low_start // step
-    high = (high_end + step - 1) // step
-    clear_low = (high_start + step - 1) // step
-    clear_high = low_end // step
-    return low, high, clear_low, clear_high
-
-
 def limits(first, rows, q_edges, k_edges, causal):
-    place = lax.rem(lax.broadcasted_iota(jnp.int32, (1, 2 * rows), 1), rows) + first
+    place = lax.broadcasted_iota(jnp.int32, (1, rows), 1) + first
     begin = pick(place, q_edges, k_edges[:-1])
     end = pick(place, q_edges, k_edges[1:])
     if causal:
@@ -90,73 +73,131 @@
     return begin, end
 
 
-def toeplitz(table_ref, tiles, rows):
-    for delta in range(tiles.shape[0]):
-        for head in range(2):
-            base = table_ref[0, head : head + 1, delta * rows : (delta + 2) * rows]
-            wide = jnp.broadcast_to(base, (rows, 2 * rows))
-            wide = pltpu.roll(wide, 0, 1, stride=1, stride_axis=0)
-            tiles[delta, :, head * rows : (head + 1) * rows] = wide[:, rows:]
-
-
-def masked(scores, index, step, begin, end):
-    place = lax.broadcasted_iota(jnp.int32, scores.shape, 0) + index * step
-    return jnp.where((place >= begin) & (place < end), scores, NEGATIVE)
-
-
-def forward_kernel(
-    causal, step, width, first_ref, q_sizes, k_sizes, q_ref, k_ref, v_ref, *rest
-):
+def fold(block, combine):
+    parts = [block[start : start + 8] for start in range(0, block.shape[0], 8)]
+    while len(parts) > 1:
+        joined = [combine(parts[i], parts[i + 1]) for i in range(0, len(parts) - 1, 2)]
+        parts = joined + parts[2 * len(joined) :]
+    return parts[0]
+
+
+def fill_mask(mask, first, q_edges, k_edges, causal):
+    blocks, key_count, rows = mask.shape
+    for block in range(blocks):
+        begin, end = limits(first + block * rows, rows, q_edges, k_edges, causal)
+        place = lax.broadcasted_iota(jnp.int32, (key_count, rows), 0)
+        mask[block] = jnp.where((place >= begin) & (place < end), 0.0, NEGATIVE)
+
+
+def fill_tiles(table_ref, tiles):
+    count, tile = tiles.shape[:2]
+    for head in range(2):
+        wide = jnp.broadcast_to(table_ref[0, head : head + 1, :], (8, (count + 1) * tile))
+        wide = pltpu.roll(wide, 0, 1, stride=1, stride_axis=0)
+        for start in range(0, tile, 8):
+            moved = pltpu.roll(wide, start, 1) if start else wide
+            for index in range(count):
+                tiles[index, start : start + 8, head * tile : (head + 1) * tile] = moved[
+                    :, (index + 1) * tile : (index + 2) * tile
+                ]
+
+
+def sum_diagonals(tiles, out_ref):
+    count, tile = tiles.shape[:2]
+    for head in range(2):
+        parts = jnp.zeros((8, (count + 1) * tile), F32)
+        for start in range(0, tile, 8):
+            line = [jnp.zeros((8, tile), F32)]
+            for index in range(count):
+                line.append(tiles[index, start : start + 8, head * tile : (head + 1) * tile])
+            line = jnp.concatenate(line, axis=1)
+            parts = parts + (pltpu.roll(line, line.shape[1] - start, 1) if start else line)
+        line = parts[0:1]
+        for row in range(1, 8):
+            line = line + pltpu.roll(parts[row : row + 1], parts.shape[1] - row, 1)
+        out_ref[0, head : head + 1, :] = line
+
+
+def tile_of(u, t, key_tiles, row_tiles):
+    return key_tiles - row_tiles + t - u
+
+
+def bias_of(tiles, key_tiles, row_tiles):
+    tile = tiles.shape[1]
+    lines = []
+    for u in range(key_tiles):
+        line = [
+            tiles[max(tile_of(u, t, key_tiles, row_tiles), 0), :, head * tile : (head + 1) * tile]
+            for head in range(2)
+            for t in range(row_tiles)
+        ]
+        lines.append(jnp.concatenate(line, axis=1))
+    return jnp.concatenate(lines, axis=0)
+
+
+def score_block(k_ref, queries, mask, tiles, block, index, step):
+    here = pl.ds(pl.multiple_of(index * step, step), step)
+    scores = dot(k_ref[here, :], queries, NT)
+    if tiles is not None:
+        tile = tiles.shape[1]
+        scores = scores + bias_of(tiles, step // tile, queries.shape[0] // 2 // tile)
+    hidden = mask[block, here, :]
+    return scores + jnp.concatenate([hidden, hidden], axis=1)
+
+
+def key_range(first, rows, q_edges, k_edges, step):
+    high = pick(first + rows - 1, q_edges, k_edges[1:])
+    return pick(first, q_edges, k_edges[:-1]) // step, (high + step - 1) // step
+
+
+def forward_kernel(causal, step, width, first_ref, q_sizes, k_sizes, q_ref, k_ref, v_ref, *rest):
     if causal:
-        table_ref, out_ref, total_ref, value_t, scores, tiles = rest
+        table_ref, out_ref, total_ref, tiles_ref, value_t, scores, mask = rest
+        tiles = tiles_ref.at[0]
     else:
-        out_ref, total_ref, value_t, scores = rest
+        out_ref, total_ref, value_t, scores, mask = rest
+        tiles = None
     blocks, rows = total_ref.shape[1], total_ref.shape[3] // 2
     q_edges = bounds_of(q_sizes)
     k_edges = bounds_of(k_sizes)
+
+    @pl.when(pl.program_id(0) == 0)
+    def once():
+        fill_mask(mask, first_ref[0], q_edges, k_edges, causal)
+
     transposed_blocks(v_ref, value_t, step)
     if causal:
-        toeplitz(table_ref, tiles, rows)
+        fill_tiles(table_ref, tiles)
     for block in range(blocks):
         first = first_ref[0] + block * rows
-        low, high, clear_low, clear_high = ranges(first, rows, q_edges, k_edges, causal, step)
-        begin, end = limits(first, rows, q_edges, k_edges, causal)
+        low, high = (0, 1) if causal else key_range(first, rows, q_edges, k_edges, step)
         queries = stack_heads(q_ref[block * rows : (block + 1) * rows, :], width)
 
         def measure(index, top):
-            keys = k_ref[pl.ds(pl.multiple_of(index * step, step), step), :]
-            block_scores = dot(keys, queries, NT)
-            if causal:
-                block_scores = block_scores + tiles[first // rows - index]
-            clear = (index >= clear_low) & (index < clear_high)
-
-            def plain():
-                scores[index] = block_scores
-                return jnp.max(block_scores, axis=0, keepdims=True)
-
-            def cut():
-                kept = masked(block_scores, index, step, begin, end)
-                scores[index] = kept
-                return jnp.max(kept, axis=0, keepdims=True)
-
-            return jnp.maximum(top, lax.cond(clear, plain, cut))
-
-        top = lax.fori_loop(low, high, measure, jnp.full((1, 2 * rows), NEGATIVE, F32))
+            block_scores = score_block(k_ref, queries, mask, tiles, block, index, step)
+            scores[index] = block_scores
+            return jnp.maximum(top, fold(block_scores, jnp.maximum))
+
+        top = lax.fori_loop(low, high, measure, jnp.full((8, 2 * rows), NEGATIVE, F32))
+        top = jnp.max(top, axis=0, keepdims=True)
 
         def gather(index, carry):
             total, out_a, out_b = carry
             weights = jnp.exp(scores[index] - top)
-            total = total + jnp.sum(weights, axis=0, keepdims=True)
+            total = total + fold(weights, jnp.add)
             rounded = weights.astype(BF16)
-            out_a = out_a + dot(value_t[index, :width, :], rounded[:, :rows], NN)
-            out_b = out_b + dot(value_t[index, width:, :], rounded[:, rows:], NN)
+            out_a = out_a + dot(value_t[index], rounded[:, :rows], NN)
+            out_b = out_b + dot(value_t[index], rounded[:, rows:], NN)
             return total, out_a, out_b
 
-        zero = jnp.zeros((width, rows), F32)
+        zero = jnp.zeros((2 * width, rows), F32)
         total, out_a, out_b = lax.fori_loop(
-            low, high, gather, (jnp.zeros((1, 2 * rows), F32), zero, zero)
+            low, high, gather, (jnp.zeros((8, 2 * rows), F32), zero, zero)
         )
-        joined = jnp.concatenate([out_a / total[:, :rows], out_b / total[:, rows:]], axis=0)
+        total = jnp.sum(total, axis=0, keepdims=True)
+        joined = jnp.concatenate(
+            [out_a[:width] / total[:, :rows], out_b[width:] / total[:, rows:]], axis=0
+        )
         out_ref[block * rows : (block + 1) * rows, :] = joined.T.astype(BF16)
         total_ref[0, block] = top + jnp.log(total)
 
@@ -165,42 +206,41 @@
     causal, step, width, first_ref, q_sizes, k_sizes, q_ref, k_ref, v_ref, g_ref, total_ref, *rest
 ):
     if causal:
-        table_ref, dq_ref, dk_ref, dv_ref, diag_ref, key_t, probs, grads, dk, dv, tiles, sums = rest
+        tiles_ref, dq_ref, dk_ref, dv_ref, diag_ref, key_t, probs, grads, dk, dv, mask, sums = rest
+        tiles = tiles_ref.at[0]
     else:
-        dq_ref, dk_ref, dv_ref, key_t, probs, grads, dk, dv = rest
+        dq_ref, dk_ref, dv_ref, key_t, probs, grads, dk, dv, mask = rest
+        tiles = None
     blocks, rows = total_ref.shape[1], total_ref.shape[3] // 2
     q_edges = bounds_of(q_sizes)
     k_edges = bounds_of(k_sizes)
+
+    @pl.when(pl.program_id(0) == 0)
+    def once():
+        fill_mask(mask, first_ref[0], q_edges, k_edges, causal)
+
     transposed_blocks(k_ref, key_t, step)
     dk[...] = jnp.zeros_like(dk)
     dv[...] = jnp.zeros_like(dv)
-    if causal:
-        toeplitz(table_ref, tiles, rows)
-        sums[...] = jnp.zeros_like(sums)
     for block in range(blocks):
         first = first_ref[0] + block * rows
-        low, high, clear_low, clear_high = ranges(first, rows, q_edges, k_edges, causal, step)
-        begin, end = limits(first, rows, q_edges, k_edges, causal)
+        low, high = (0, 1) if causal else key_range(first, rows, q_edges, k_edges, step)
         queries = stack_heads(q_ref[block * rows : (block + 1) * rows, :], width)
         targets = stack_heads(g_ref[block * rows : (block + 1) * rows, :], width)
         total = total_ref[0, block]
 
         def measure(index, inner):
             here = pl.ds(pl.multiple_of(index * step, step), step)
-            block_scores = dot(k_ref[here, :], queries, NT)
-            if causal:
-                block_scores = block_scores + tiles[first // rows - index]
+            block_scores = score_block(k_ref, queries, mask, tiles, block, index, step)
             weights = jnp.exp(block_scores - total)
-            clear = (index >= clear_low) & (index < clear_high)
-            place = lax.broadcasted_iota(jnp.int32, weights.shape, 0) + index * step
-            weights = jnp.where((place >= begin) & (place < end), weights, 0.0)
             pulled = dot(v_ref[here, :], targets, NT)
             probs[index] = weights
             grads[index] = pulled
             dv[here, :] += dot(weights.astype(BF16), targets, NN)
-            return inner + jnp.sum(weights * pulled, axis=0, keepdims=True)
-
-        inner = lax.fori_loop(low, high, measure, jnp.zeros((1, 2 * rows), F32))
+            return inner + fold(weights * pulled, jnp.add)
+
+        inner = lax.fori_loop(low, high, measure, jnp.zeros((8, 2 * rows), F32))
+        inner = jnp.sum(inner, axis=0, keepdims=True)
 
         def gather(index, carry):
             out_a, out_b = carry
@@ -208,29 +248,33 @@
             rounded = (probs[index] * (grads[index] - inner)).astype(BF16)
             dk[here, :] += dot(rounded, queries, NN)
             if causal:
-                sums[first // rows - index] += rounded.astype(F32)
-            out_a = out_a + dot(key_t[index, :width, :], rounded[:, :rows], NN)
-            out_b = out_b + dot(key_t[index, width:, :], rounded[:, rows:], NN)
+                tile = tiles.shape[1]
+                spots = [(u, t) for u in range(step // tile) for t in range(rows // tile)]
+                for which in range(sums.shape[0]):
+                    parts = [
+                        jnp.concatenate(
+                            [
+                                rounded[u * tile : (u + 1) * tile, start + t * tile : start + (t + 1) * tile]
+                                for start in (0, rows)
+                            ],
+                            axis=1,
+                        ).astype(F32)
+                        for u, t in spots
+                        if tile_of(u, t, step // tile, rows // tile) == which
+                    ]
+                    sums[which] = functools.reduce(jnp.add, parts)
+            out_a = out_a + dot(key_t[index], rounded[:, :rows], NN)
+            out_b = out_b + dot(key_t[index], rounded[:, rows:], NN)
             return out_a, out_b
 
-        zero = jnp.zeros((width, rows), F32)
+        zero = jnp.zeros((2 * width, rows), F32)
         out_a, out_b = lax.fori_loop(low, high, gather, (zero, zero))
-        joined = jnp.concatenate([out_a, out_b], axis=0)
+        joined = jnp.concatenate([out_a[:width], out_b[width:]], axis=0)
         dq_ref[block * rows : (block + 1) * rows, :] = joined.T.astype(BF16)
     dk_ref[...] = dk[...].astype(BF16)
     dv_ref[...] = dv[...].astype(BF16)
     if causal:
-        for delta in range(sums.shape[0]):
-            for head in range(2):
-                parts = jnp.zeros((8, 2 * rows), F32)
-                for chunk in range(rows // 8):
-                    piece = sums[delta, chunk * 8 : chunk * 8 + 8, head * rows : (head + 1) * rows]
-                    piece = jnp.concatenate([jnp.zeros_like(piece), piece], axis=1)
-                    parts = parts + (pltpu.roll(piece, 2 * rows - 8 * chunk, 1) if chunk else piece)
-                line = parts[0:1]
-                for row in range(1, 8):
-                    line = line + pltpu.roll(parts[row : row + 1], 2 * rows - row, 1)
-                diag_ref[0, head, delta : delta + 1, :] = line
+        sum_diagonals(sums, diag_ref)
 
 
 def unread():
@@ -264,8 +308,8 @@
     causal = table is not None
     count, model = queries.shape
     key_count = keys.shape[0]
-    rows = min(256, count)
-    step = rows if causal else step
+    rows, tile = min(512, count), min(256, count)
+    step = key_count if causal else min(step, key_count)
     pair_first, pairs = span
     blocks = count // rows
     column = lambda size: pl.BlockSpec((size, 2 * width), lambda pair: (0, pair + pair_first))
@@ -273,29 +317,32 @@
     scratch = [
         pltpu.VMEM((key_count // step, 2 * width, step), BF16),
         pltpu.VMEM((key_count // step, step, 2 * rows), F32),
+        pltpu.VMEM((count // rows, key_count, rows), F32),
     ]
     in_specs = [smem(), smem(), smem(), column(count), column(key_count), column(key_count)]
     args = [first, q_sizes, k_sizes, queries, keys, values]
+    out_specs = [
+        result(count),
+        pl.BlockSpec((1, blocks, 1, 2 * rows), lambda pair: (pair, 0, 0, 0)),
+    ]
+    out_shape = [
+        jax.ShapeDtypeStruct((count, pairs * 2 * width), BF16),
+        jax.ShapeDtypeStruct((pairs, blocks, 1, 2 * rows), F32),
+    ]
     if causal:
-        in_specs.append(
-            pl.BlockSpec((1, 2, table.shape[2]), lambda pair: (pair + pair_first, 0, 0))
-        )
+        in_specs.append(pl.BlockSpec((1, 2, table.shape[2]), lambda pair: (pair + pair_first, 0, 0)))
         args.append(table)
-        scratch.append(pltpu.VMEM((key_count // rows, rows, 2 * rows), F32))
+        tiles = (1, key_count // tile, tile, 2 * tile)
+        out_specs.append(pl.BlockSpec(tiles, lambda pair: (pair, 0, 0, 0)))
+        out_shape.append(jax.ShapeDtypeStruct((pairs, *tiles[1:]), F32))
     return pl.pallas_call(
         ignoring(functools.partial(forward_kernel, causal, step, width), len(args), len(after)),
         grid=(pairs,),
         in_specs=in_specs + [unread()] * len(after),
-        out_specs=[
-            result(count),
-            pl.BlockSpec((1, blocks, 1, 2 * rows), lambda pair: (pair, 0, 0, 0)),
-        ],
-        out_shape=[
-            jax.ShapeDtypeStruct((count, pairs * 2 * width), BF16),
-            jax.ShapeDtypeStruct((pairs, blocks, 1, 2 * rows), F32),
-        ],
+        out_specs=out_specs,
+        out_shape=out_shape,
         scratch_shapes=scratch,
-        compiler_params=pltpu.CompilerParams(vmem_limit_bytes=56 << 20),
+        compiler_params=pltpu.CompilerParams(vmem_limit_bytes=60 << 20),
         cost_estimate=cost,
         name="self_forward" if causal else "cross_forward",
     )(*args, *after)
@@ -307,8 +354,8 @@
     causal = table is not None
     count, model = queries.shape
     key_count = keys.shape[0]
-    rows = min(256, count)
-    step = rows if causal else step
+    rows, tile = min(512, count), min(256, count)
+    step = key_count if causal else min(step, key_count)
     pair_first, pairs = span
     blocks = count // rows
     column = lambda size: pl.BlockSpec((size, 2 * width), lambda pair: (0, pair + pair_first))
@@ -320,10 +367,11 @@
         pltpu.VMEM((n_step, step, 2 * rows), F32),
         pltpu.VMEM((key_count, 2 * width), F32),
         pltpu.VMEM((key_count, 2 * width), F32),
+        pltpu.VMEM((count // rows, key_count, rows), F32),
     ]
     in_specs = [
         smem(), smem(), smem(), column(count), column(key_count), column(key_count), column(count),
-        pl.BlockSpec((1, blocks, 1, 2 * rows), lambda pair: (pair + pair_first, 0, 0, 0)),
+        pl.BlockSpec((1, blocks, 1, 2 * rows), lambda pair: (pair, 0, 0, 0)),
     ]
     args = [first, q_sizes, k_sizes, queries, keys, values, grads, totals]
     out_specs = [result(count), result(key_count), result(key_count)]
@@ -333,14 +381,12 @@
         jax.ShapeDtypeStruct((key_count, pairs * 2 * width), BF16),
     ]
     if causal:
-        in_specs.append(
-            pl.BlockSpec((1, 2, table.shape[2]), lambda pair: (pair + pair_first, 0, 0))
-        )
+        in_specs.append(pl.BlockSpec((1, *table.shape[1:]), lambda pair: (pair, 0, 0, 0)))
         args.append(table)
-        deltas = key_count // rows
-        scratch += [pltpu.VMEM((deltas, rows, 2 * rows), F32), pltpu.VMEM((deltas, rows, 2 * rows), F32)]
-        out_specs.append(pl.BlockSpec((1, 2, deltas, 2 * rows), lambda pair: (pair, 0, 0, 0)))
-        out_shape.append(jax.ShapeDtypeStruct((pairs, 2, deltas, 2 * rows), F32))
+        deltas = key_count // tile
+        scratch.append(pltpu.VMEM((deltas, tile, 2 * tile), F32))
+        out_specs.append(pl.BlockSpec((1, 2, (deltas + 1) * tile), lambda pair: (pair, 0, 0)))
+        out_shape.append(jax.ShapeDtypeStruct((pairs, 2, (deltas + 1) * tile), F32))
     return pl.pallas_call(
         ignoring(functools.partial(backward_kernel, causal, step, width), len(args), len(after)),
         grid=(pairs,),
@@ -352,6 +398,23 @@
         cost_estimate=LONG,
         name="self_backward" if causal else "cross_backward",
     )(*args, *after)
+
+
+def bias_window(distance_buckets, position_bias, first, rows):
+    key_count = distance_buckets.shape[0]
+    tile = min(256, rows)
+    margin = key_count - rows + tile
+    buckets = jnp.arange(position_bias.shape[0], dtype=jnp.int32)
+    one_hot = (distance_buckets[:, None] == buckets[None, :]).astype(F32)
+    one_hot = jnp.pad(one_hot, ((margin, 0), (0, 0)))
+    one_hot = lax.dynamic_slice_in_dim(one_hot, first, key_count + tile, 0)
+    table = jnp.einsum("db,bh->hd", one_hot, position_bias, precision=EXACT)
+    return table.reshape(position_bias.shape[1] // 2, 2, key_count + tile), one_hot
+
+
+def bias_gradient(diagonals, one_hot):
+    diagonals = diagonals.reshape(-1, one_hot.shape[0])
+    return jnp.einsum("db,hd->bh", one_hot, diagonals, precision=EXACT)
 
 
 def send_batch(block, distance):
@@ -499,17 +562,19 @@
 
 def scatter_to_line(groups, after):
     count = groups[0][0].shape[0]
+    ends = [0]
+    for kept, _ in groups:
+        ends.append(ends[-1] + kept.shape[1])
 
     def body(*refs):
         outs = refs[2 * len(groups) :]
         for index in range(len(groups)):
             total = add_refs(refs[2 * index : 2 * index + 2]).astype(BF16)
             for distance in range(count):
-                outs[count * index + distance][...] = total[distance]
-
-    shapes = [jax.ShapeDtypeStruct(kept.shape[1:], BF16) for kept, _ in groups for _ in range(count)]
-    outs = simple_call(body, "scatter_to_line", shapes, [part for group in groups for part in group], after)
-    return [outs[count * index : count * (index + 1)] for index in range(len(groups))]
+                outs[distance][ends[index] : ends[index + 1], :] = total[distance]
+
+    shapes = [jax.ShapeDtypeStruct((ends[-1], 128), BF16)] * count
+    return simple_call(body, "scatter_to_line", shapes, [part for group in groups for part in group], after)
 
 
 def send_line(pieces):
@@ -560,12 +625,18 @@
 def add_rows(block, far, after):
     rows, width = block.shape
 
-    def body(one_ref, two_ref, out_ref):
-        out_ref[...] = one_ref[...] + two_ref[...].astype(F32)
-
-    spec = pl.BlockSpec((rows // 4, width), lambda i: (i, 0))
+    def body(one_ref, far_a, far_b, out_ref):
+        other = jnp.where(pl.program_id(0) < 2, far_a[...], far_b[...])
+        out_ref[...] = one_ref[...] + other.astype(F32)
+
+    part = (rows // 4, width)
+    spec = pl.BlockSpec(part, lambda i: (i, 0))
+    halves = [
+        pl.BlockSpec(part, lambda i: (jnp.minimum(i, 1), 0)),
+        pl.BlockSpec(part, lambda i: (jnp.maximum(i - 2, 0), 0)),
+    ]
     shape = jax.ShapeDtypeStruct(block.shape, F32)
-    return kernel_call(body, "add_rows", (4,), [spec, spec], spec, shape, (block, far), after=after)
+    return kernel_call(body, "add_rows", (4,), [spec, *halves], spec, shape, (block, *far), after=after)
 
 
 def chosen(block, axis, index):
@@ -973,7 +1044,7 @@
         place_ref, dk_ref, dv_ref, own_ref, far_a, far_b, *refs,
     ):
         k_refs, v_refs = refs[:4], refs[4:8]
-        grad_own_ref, grad_far_ref, keep_ref, send_ref, key_total, value_total = refs[8:]
+        grad_own_ref, grad_far_a, grad_far_b, keep_ref, send_ref, key_total, value_total = refs[8:]
         i = pl.program_id(0)
         source = three_way(i ^ 2, own_ref, far_a, far_b)
         source_t = source.T
@@ -990,12 +1061,16 @@
             grad_value, matrix_of(place_ref, v_refs)
         )
 
-        @pl.when(i < 2)
+        @pl.when(i == 0)
+        def there_first():
+            grad_far_a[...] = grads.astype(BF16)
+
+        @pl.when(i == 1)
+        def there_second():
+            grad_far_b[...] = grads.astype(BF16)
+
+        @pl.when(i >= 2)
         def here():
-            grad_far_ref[...] = grads.astype(BF16)
-
-        @pl.when(i >= 2)
-        def there():
             grad_own_ref[...] = grads
 
         @pl.when(i == 3)
@@ -1022,7 +1097,8 @@
             + weight_specs(pack, 1) + weight_specs(pack, 2),
             out_specs=[
                 pl.BlockSpec((step, width), lambda i, _: (jnp.maximum(i - 2, 0), 0)),
-                pl.BlockSpec((step, width), lambda i, _: (jnp.minimum(i, 1), 0)),
+                whole_spec((step, width)),
+                whole_spec((step, width)),
                 whole_spec(pieces.shape),
                 whole_spec(pieces.shape),
             ],
@@ -1030,7 +1106,8 @@
         ),
         out_shape=[
             jax.ShapeDtypeStruct((rows, width), F32),
-            jax.ShapeDtypeStruct((rows, width), BF16),
+            jax.ShapeDtypeStruct((step, width), BF16),
+            jax.ShapeDtypeStruct((step, width), BF16),
             pieces,
             pieces,
         ],
@@ -1148,11 +1225,9 @@
     row_count, model_width = hidden.shape[1:]
     head_count = position_bias.shape[1]
     head_width = model_width // head_count
-    bucket_count = position_bias.shape[0]
     key_count = row_count * mem_count
     first_row = mem_index * row_count
     first = jnp.reshape(first_row, (1,)).astype(jnp.int32)
-    rows = min(256, row_count)
 
     self_full = gather_plain(self_weights)
     tokens_all = all_rows(hidden[0])
@@ -1164,11 +1239,7 @@
     expand_full = gather_plain(expand_weights)
     contract_full = gather_plain(contract_weight[None])[0]
 
-    buckets = jnp.arange(bucket_count, dtype=jnp.int32)
-    one_hot = (distance_buckets[:, None] == buckets[None, :]).astype(F32)
-    distance_table = jnp.einsum("db,bh->hd", one_hot, position_bias, precision=EXACT)
-    distance_table = jnp.pad(distance_table, ((0, 0), (rows, 0)))
-    distance_table = distance_table.reshape(head_count // 2, 2, key_count + rows)
+    distance_table, one_hot = bias_window(distance_buckets, position_bias, first_row, row_count)
 
     tokens = hidden[0].astype(F32)
     normed_self, pull_self = jax.vjp(rms_norm, tokens, norm_gains[0])
@@ -1177,9 +1248,9 @@
     query_self = mm(input_self, self_full[0]).astype(BF16)
     key_self = mm(input_all, self_full[1]).astype(BF16)
     value_self = mm(input_all, self_full[2]).astype(BF16)
-    attn_self, self_totals = attention_forward(
+    attn_self, self_totals, tiles = attention_forward(
         first, decoder_lengths, decoder_lengths, query_self, key_self, value_self,
-        distance_table, head_width, rows, (0, head_count // 2),
+        distance_table, head_width, key_count, (0, head_count // 2),
     )
     middle_one = tokens + mm(attn_self, self_out_full)
     normed_cross, pull_cross = jax.vjp(rms_norm, middle_one, norm_gains[1])
@@ -1189,7 +1260,7 @@
     value_memory = mm(memory_all, cross_full[2]).astype(BF16)
     attn_cross, cross_totals = attention_forward(
         first, decoder_lengths, memory_lengths, query_cross, key_memory, value_memory,
-        None, head_width, 512, (0, head_count // 2),
+        None, head_width, memory_all.shape[0], (0, head_count // 2),
     )
     middle_two = middle_one + mm(attn_cross, cross_out_full)
     normed_feed, pull_feed = jax.vjp(rms_norm, middle_two, norm_gains[2])
@@ -1216,7 +1287,7 @@
     grad_attn_cross = mm_t(grad_branch_two, cross_out_full).astype(BF16)
     grad_query_cross, grad_key_memory, grad_value_memory = attention_backward(
         first, decoder_lengths, memory_lengths, query_cross, key_memory, value_memory,
-        grad_attn_cross, cross_totals, None, head_width, 512, (0, head_count // 2),
+        grad_attn_cross, cross_totals, None, head_width, memory_all.shape[0], (0, head_count // 2),
     )
     cross_grads = scatter_plain(
         jnp.stack(
@@ -1238,14 +1309,9 @@
     grad_attn_self = mm_t(grad_branch_one, self_out_full).astype(BF16)
     grad_query_self, grad_key_self, grad_value_self, diagonals = attention_backward(
         first, decoder_lengths, decoder_lengths, query_self, key_self, value_self,
-        grad_attn_self, self_totals, distance_table, head_width, rows, (0, head_count // 2),
-    )
-    diagonals = diagonals.reshape(head_count, key_count // rows, 2 * rows)
-    by_distance = jnp.zeros((head_count, key_count + rows), F32)
-    for delta in range(key_count // rows):
-        here = slice(delta * rows, delta * rows + 2 * rows)
-        by_distance = by_distance.at[:, here].add(diagonals[:, delta])
-    bias_partial = jnp.einsum("db,hd->bh", one_hot, by_distance[:, rows:], precision=EXACT)
+        grad_attn_self, self_totals, tiles, head_width, key_count, (0, head_count // 2),
+    )
+    bias_partial = bias_gradient(diagonals, one_hot)
     self_grads = scatter_plain(
         jnp.stack(
             [
@@ -1300,7 +1366,6 @@
     bucket_count, head_count = position_bias.shape
     head_width = model_width // head_count
     key_count = row_count * mem_count
-    rows = min(256, row_count)
     spot = jnp.stack(grid_place()).astype(jnp.int32)
     first = jnp.reshape(lax.axis_index("mem") * row_count, (1,)).astype(jnp.int32)
     own, own_memory = hidden[0], memory[0]
@@ -1323,131 +1388,122 @@
     (second,) = hold((second,), (low, high))
     line = line_of(second)
     low, high = gather_first(spot, low, high, (far,))
-    next_low, next_high = place_line(spot, line, (low, high))
-    low, high = gather_second(spot, low, high, (next_low, next_high))
-    (memory_start,) = hold((own_memory[: own_memory.shape[0] // 2],), (low, high))
-    far_memory_a = send_mem(memory_start)
+    low, high = gather_second(spot, low, high)
+    middle = own_memory.shape[0] // 2
+    memory_a, wide = hold((own_memory[:middle], wide), (low, high))
+    far_memory_a = send_mem(memory_a)
+    wide = lax.all_gather(wide, ("batch", "mem"), axis=0, tiled=False)
+    wide = wide.reshape(batch_count, mem_count, *wide.shape[1:])
     self_pack = gather_cores(low, high)
-    low, high = next_low, next_high
-
-    buckets = jnp.arange(bucket_count, dtype=jnp.int32)
-    one_hot = (distance_buckets[:, None] == buckets[None, :]).astype(F32)
-    distance_table = jnp.einsum("db,bh->hd", one_hot, position_bias, precision=EXACT)
-    distance_table = jnp.pad(distance_table, ((0, 0), (rows, 0)))
-    distance_table = distance_table.reshape(pairs, 2, key_count + rows)
-    padded = jnp.pad(one_hot, ((rows, 0), (0, 0)))
-    bucket_windows = jnp.concatenate(
-        [padded[delta * rows : (delta + 2) * rows] for delta in range(key_count // rows)]
+
+    distance_table, one_hot = bias_window(
+        distance_buckets, position_bias, lax.axis_index("mem") * row_count, row_count
     )
 
     query_self, key_self, value_self, normed_self = project_self(
-        spot, own, far, norm_gains, self_pack, (low, high)
-    )
+        spot, own, far, norm_gains, self_pack, ()
+    )
+
+    halves = ((0, pairs // 2), (pairs // 2, pairs // 2))
 
     def self_forward(span, after, cost):
         return attention_forward(
             first, decoder_lengths, decoder_lengths, query_self, key_self, value_self,
-            distance_table, head_width, rows, span, after, cost,
+            distance_table, head_width, key_count, span, after, cost,
         )
 
-    low, high = gather_first(spot, low, high, (query_self, far_memory_a))
-    (memory_start,) = hold((own_memory[own_memory.shape[0] // 2 :],), (low, high))
-    far_memory = (far_memory_a, send_mem(memory_start))
-    one = self_forward((0, 2 * pairs // 3), (low, high), LONG)
-    low, high = gather_second(spot, low, high, (one[0],))
-    (wide,) = hold((wide,), (low, high))
+    low, high = place_line(spot, line, (query_self,))
+    one = self_forward(halves[0], (low, high), LONG)
+    low, high = gather_first(spot, low, high, (one[0], far_memory_a))
+    two = self_forward(halves[1], (low, high), LONG)
+    low, high = gather_second(spot, low, high, (two[0],))
+    (memory_b,) = hold((own_memory[middle:],), (low, high))
+    far_memory = (far_memory_a, send_mem(memory_b))
     square_pack = gather_cores(low, high)
-    wide = lax.all_gather(wide, ("batch", "mem"), axis=0, tiled=False)
-    wide = wide.reshape(batch_count, mem_count, *wide.shape[1:])
-    two = self_forward((2 * pairs // 3, pairs // 3), (low, high), BRIEF)
-    attn_self, self_totals = zip(one, two)
-    self_totals = jnp.concatenate(self_totals, axis=0)
+    attn_self, self_totals, tiles = zip(one, two)
     middle_one, normed_cross, query_cross = after_self(spot, own, attn_self, norm_gains, square_pack)
     key_memory, value_memory = project_memory(spot, own_memory, far_memory, square_pack)
     attn_cross, cross_totals = attention_forward(
         first, decoder_lengths, memory_lengths, query_cross, key_memory, value_memory,
-        None, head_width, 512, (0, pairs),
+        None, head_width, key_memory.shape[0], (0, pairs),
     )
     (
         result, grad_middle_two, grad_attn_cross, gain_three, wide_grad,
     ) = feed_forward(
         spot, middle_one, attn_cross, cotangent[0], norm_gains, square_pack, wide, expand_weights.shape[2]
     )
-    halves = ((0, pairs // 2), (pairs // 2, pairs // 2))
     wide_grad = lax.psum_scatter(
         wide_grad.reshape(batch_count * mem_count, *wide_grad.shape[2:]),
         ("batch", "mem"), scatter_dimension=0, tiled=True,
     )[0]
     grad_query_cross, grad_key_memory, grad_value_memory = attention_backward(
         first, decoder_lengths, memory_lengths, query_cross, key_memory, value_memory,
-        grad_attn_cross, cross_totals, None, head_width, 512, (0, pairs),
-    )
-    memory_own, memory_far, kv_keep, kv_send = memory_backward(
+        grad_attn_cross, cross_totals, None, head_width, key_memory.shape[0], (0, pairs),
+    )
+    memory_own, memory_far_a, memory_far_b, kv_keep, kv_send = memory_backward(
         spot, grad_key_memory, grad_value_memory, own_memory, far_memory, square_pack
     )
     grad_middle_one, grad_attn_self, gain_two, qo_keep, qo_send = after_cross(
         spot, (grad_query_cross,), middle_one, grad_middle_two, normed_cross, attn_self, attn_cross,
-        norm_gains, square_pack, (memory_far,),
+        norm_gains, square_pack, (memory_far_a,),
     )
 
     def self_backward(half, after):
         return attention_backward(
             first, decoder_lengths, decoder_lengths, query_self, key_self, value_self,
-            grad_attn_self, self_totals, distance_table, head_width, rows, halves[half], after,
+            grad_attn_self, self_totals[half], tiles[half], head_width, key_count, halves[half], after,
         )
 
     one = self_backward(0, (qo_keep,))
     (kv_keep, kv_send), (qo_keep, qo_send) = scatter_step(
         ((kv_keep, send_batch(kv_send, 1)), (qo_keep, send_batch(qo_send, 1))), (one[0],), (2, 1)
     )
-    memory_far = send_mem(memory_far)
-    two = self_backward(1, (kv_keep, one[0]))
-    (kv_keep, kv_send), (qo_keep, qo_send) = scatter_step(
-        ((kv_keep, send_mem(kv_send)), (qo_keep, send_batch(qo_send, 2))), (two[0],), (1, 1)
-    )
+    (memory_far_b,) = hold((memory_far_b,), (kv_keep, qo_keep))
+    memory_far = (send_mem(memory_far_a), send_mem(memory_far_b))
+    two = self_backward(1, (kv_keep, one[0], memory_far[0]))
     grad_query_self, grad_key_self, grad_value_self, diagonals = zip(one, two)
     rows_own, rows_far, gain_one = self_row_grads(
-        spot, own, far, norm_gains, grad_query_self, grad_key_self, grad_value_self, self_pack,
-        (kv_keep,),
-    )
-    line_kv, line_qo = scatter_to_line(
-        ((kv_keep, send_batch(kv_send, 2)), (qo_keep, send_mem(qo_send))), (rows_far,)
-    )
-    diagonals = jnp.concatenate(diagonals, axis=0).reshape(head_count, -1)
-    bias_partial = jnp.einsum("db,hd->bh", bucket_windows, diagonals, precision=EXACT)
+        spot, own, far, norm_gains, grad_query_self, grad_key_self, grad_value_self, self_pack, ()
+    )
+    (kv_keep, kv_send), (qo_keep, qo_send) = scatter_step(
+        ((kv_keep, send_mem(kv_send)), (qo_keep, send_batch(qo_send, 2))),
+        (rows_own, memory_far[1]), (1, 1),
+    )
+    rows_far = send_mem(rows_far)
+    bias_partial = bias_gradient(jnp.concatenate(diagonals, axis=0), one_hot)
     gains = jnp.concatenate([gain_one, gain_two, gain_three], axis=0)
     sums = jnp.concatenate([gains.reshape(-1), bias_partial.reshape(-1)]).reshape(-1, 128)
     keep_a, send_a, keep_b, send_b = self_weight_grads(
-        spot, grad_query_self, grad_key_self, grad_value_self, normed_self, z_count, (line_kv[0],)
-    )
-    sums = sum_small(sums, (1, 2, 3), (keep_a,))
-    memory_gradient = add_rows(memory_own, memory_far, (keep_a, sums))
+        spot, grad_query_self, grad_key_self, grad_value_self, normed_self, z_count, (kv_keep, sums)
+    )
+    sums = sum_small(sums, (2, 4, 6), (keep_a,))
     (keep_a, send_a), (keep_b, send_b) = scatter_step(
-        ((keep_a, send_batch(send_a, 1)), (keep_b, send_batch(send_b, 1))), (memory_gradient,), (2, 1)
-    )
-    hidden_gradient = finish_rows(
-        own, rows_own, send_mem(rows_far), grad_middle_one, norm_gains, (keep_a,)
-    )
-    sums = sum_small(sums, (4, 8, 12), (keep_a,))
-    units = [(0, 0, block) for block in range(3)] + [(0, 1, block) for block in range(3)]
-    units += [(1, matrix, block) for matrix in (2, 3, 4) for block in range(3)]
+        ((keep_a, send_batch(send_a, 1)), (keep_b, send_batch(send_b, 1))), (sums,), (2, 1)
+    )
+    line = scatter_to_line(
+        ((kv_keep, send_batch(kv_send, 2)), (qo_keep, send_mem(qo_send))), (keep_a,)
+    )
+    sums = sum_small(sums, (8, 16, 24), (line[0],))
+    memory_gradient = add_rows(memory_own, memory_far, (sums,))
+    (keep_a, send_a), (keep_b, send_b) = scatter_step(
+        ((keep_a, send_mem(send_a)), (keep_b, send_batch(send_b, 2))), (memory_gradient,), (1, 1)
+    )
+    hidden_gradient = finish_rows(own, rows_own, rows_far, grad_middle_one, norm_gains, (keep_a,))
+    self_line = scatter_to_line(
+        ((keep_a, send_batch(send_a, 2)), (keep_b, send_mem(send_b))), (hidden_gradient,)
+    )
+    units = [(0, matrix, block) for matrix in range(5) for block in range(3)]
     cross_grad, self_out_grad, cross_out_grad = scatter_end(
-        (send_line(line_kv), send_line(line_qo)),
+        (send_line(line),),
         (cross_weights.shape, self_output.shape, cross_output.shape),
         square_moves(units, slab, columns, ((0, 1), (0, 2), (0, 0), (1, None), (2, None))),
-        (hidden_gradient,),
-    )
-    (keep_a, send_a), (keep_b, send_b) = scatter_step(
-        ((keep_a, send_mem(send_a)), (keep_b, send_batch(send_b, 2))), (cross_grad,), (1, 1)
-    )
-    sums = sum_small(sums, (16,), (keep_a,)).reshape(-1)
-    line_a, line_b = scatter_to_line(
-        ((keep_a, send_batch(send_a, 2)), (keep_b, send_mem(send_b))), ()
-    )
-    units = [(0 if unit < 5 else 1, unit // 3, unit % 3) for unit in range(9)]
+        (self_line[0],),
+    )
+    sums = sum_small(sums, (1,), (cross_grad,)).reshape(-1)
+    units = [(0, unit // 3, unit % 3) for unit in range(9)]
     (self_grad,) = scatter_end(
-        (send_line(line_a), send_line(line_b)), (self_weights.shape,),
-        square_moves(units, slab, columns, ((0, 0), (0, 1), (0, 2))), (),
+        (send_line(self_line),), (self_weights.shape,),
+        square_moves(units, slab, columns, ((0, 0), (0, 1), (0, 2))), (sums,),
     )
     gate_rows, down_rows = across * slab, contract_weight.shape[0]
     moves = []
@@ -1459,7 +1515,7 @@
         span = (slice(None), slice(block * 128, block * 128 + 128))
         moves.append((0, 2 * gate_rows + block * down_rows, down_rows, 1, span))
     expand_grad, contract_grad = scatter_end(
-        ((wide_grad,),), (expand_weights.shape, contract_weight.shape), moves, (line_a[0],)
+        ((wide_grad,),), (expand_weights.shape, contract_weight.shape), moves, (self_line[0],)
     )
     return (
         result[None],
@@ -1478,7 +1534,7 @@
 
 def shards(*arrays):
     row_count, slab, columns = arrays[0].shape[1], arrays[7].shape[1], arrays[7].shape[2]
-    allowed = row_count % 256 == 0 and slab % 16 == 0 and columns % 128 == 0
+    allowed = row_count == 512 and slab % 16 == 0 and columns % 128 == 0
     if lax.axis_size("mem") == 2 and lax.axis_size("batch") == 16 and allowed:
         return shards_hops(*arrays)
     return shards_plain(*arrays)

time: 515 us -> 459 us (0.89)
  Pallas kernels: 298 us -> 256 us
  starting transfers between devices: 71.6 us -> 49.3 us
    pallas_call x3, Pallas kernels: 62 us -> 40.3 us  [attention_forward(): pl.pallas_call(ignoring(functools.partial(forward_kernel, causal, step, w...]
    ppermute x34 -> x28, waiting for transfers between devices: 32.1 us -> 53.6 us  [send_batch(): lax.ppermute(block, 'batch', [(i, i ^ distance) for i in range(count)])]
    pallas_call x3, Pallas kernels: 86.2 us -> 65.1 us  [attention_backward(): pl.pallas_call(ignoring(functools.partial(backward_kernel, causal, step,...]
    ppermute x13 -> x14, starting transfers between devices: 34.3 us -> 17.9 us  [send_mem(): return lax.ppermute(block, 'mem', [(0, 1), (1, 0)])]
    ppermute x7, waiting for transfers between devices: 22 us -> 6.6 us  [sum_small(): parts.append(lax.ppermute(block, ('batch', 'mem'), pairs))]
    all_gather x1, waiting for transfers between devices: 7.46 us -> 0.01 us  [shards_hops(): wide = lax.all_gather(wide, ('batch', 'mem'), axis=0, tiled=False)]
    ppermute x13 -> x14, waiting for transfers between devices: 38.2 us -> 43.3 us  [send_mem(): return lax.ppermute(block, 'mem', [(0, 1), (1, 0)])]
    ppermute x34 -> x28, starting transfers between devices: 30.7 us -> 26.2 us  [send_batch(): lax.ppermute(block, 'batch', [(i, i ^ distance) for i in range(count)])]
  transfers between devices with their start and end apart: 56 -> 51, of which waited for: 24 -> 21; matrix products, arithmetic and copies ran while one was open for 2% -> 2% of each run, Pallas kernels for 51% -> 49%
where the time goes in v3:
time: 459 us; the launch traced here: 453 us
  Pallas kernels  256 us (56%)
  waiting for transfers between devices  103 us (22%)
  starting transfers between devices  49.3 us (11%)
  local copies, waits for them, and re-layouts  24.9 us (5%)
  between operations  14.8 us (3%)
    pallas_call x26, Pallas kernels, kernel_call(): pl.pallas_call(ignoring(body, len(args), len(after)), grid=grid, in_specs...  121 us
    pallas_call x3, Pallas kernels, attention_backward(): pl.pallas_call(ignoring(functools.partial(backward_kernel, causal, step,...  65.1 us
    ppermute x28, waiting for transfers between devices, send_batch(): lax.ppermute(block, 'batch', [(i, i ^ distance) for i in range(count)])  53.6 us
    ppermute x14, waiting for transfers between devices, send_mem(): return lax.ppermute(block, 'mem', [(0, 1), (1, 0)])  43.3 us
    pallas_call x3, Pallas kernels, attention_forward(): pl.pallas_call(ignoring(functools.partial(forward_kernel, causal, step, w...  40.3 us
    ppermute x28, starting transfers between devices, send_batch(): lax.ppermute(block, 'batch', [(i, i ^ distance) for i in range(count)])  26.2 us
    unnamed x140, local copies, waits for them, and re-layouts  20.6 us
    pallas_call x1, Pallas kernels, memory_backward(): pl.pallas_call(body, grid_spec=pltpu.PrefetchScalarGridSpec(num_scalar_pr...  19.2 us
  transfers between devices with their start and end apart: 51, of which 21 were waited for; matrix products, arithmetic and copies ran while one was open for 2% of the time, Pallas kernels for 49%

profile of v3, /device:TPU:0, one launch (start us, length us, event | category | flops | bytes accessed | tf_op | source)
XLA Modules:
  0.0 453.1 jit_solution(10033430083179708063)
XLA Ops:
  7.2 3.0 collective-permute-start
  10.2 2.6 collective-permute-start.2
  12.8 1.6 collective-permute-start.1
  16.4 4.0 collective-permute-done.2.refs_3_
  22.4 1.9 place_line.2
  24.8 1.5 collective-permute-start.5
  26.4 6.4 %collective-permute-done.4.refs_2_ = bf16[2,3,48,384]{3,2,1,0:T(8,128)(2,1)S(1)} collective-permute-done((bf16[2,3,48,384]{3,2,1,0:T(8,128)(2,1)}, bf16[2,3,48,384]{3,2,1,0:T(8,128)(2,1)S(1)}, u32[]{:S(2)}, u32[]{:S(2)}) %collective-permute-start.4) | collective-permute-done | bytes 221216 | tf_op jit(solution)/shard_map/ppermute | solution.py:426
  34.4 2.2 place_pairs.4
  36.6 1.8 collective-permute-start.6
  38.4 1.5 collective-permute-start.7
  41.9 6.3 %collective-permute-done.6.refs_2_ = bf16[2,2,3,48,384]{4,3,2,1,0:T(8,128)(2,1)S(1)} collective-permute-done((bf16[2,2,3,48,384]{4,3,2,1,0:T(8,128)(2,1)}, bf16[2,2,3,48,384]{4,3,2,1,0:T(8,128)(2,1)S(1)}, u32[]{:S(2)}, u32[]{:S(2)}) %collective-permute-start.6) | collective-permute-done | bytes 442400 | tf_op jit(solution)/shard_map/ppermute | solution.py:422
  50.1 2.7 place_pairs.5
  56.7 3.6 collective-permute-start.12
  61.0 1.5 collective-permute-start.15
  62.5 8.1 %project_self_kernel.1 = (bf16[512,768]{1,0:T(8,128)(2,1)}, bf16[1024,768]{1,0:T(8,128)(2,1)}, bf16[1024,768]{1,0:T(8,128)(2,1)}, bf16[1024,768]{1,0:T(8,128)(2,1)}) custom-call(s32[4]{0:T(128)} %pad_add_fusion.refs_0_.place_ref, bf16[512,768]{1,0:T(8,128)(2,1)} %bitcast.58, bf16[512,768]{1,0:T(8,128)(2,1)} %copy-done.14, f32[3,768]{1,0:T(4,128)} %refs_4_.3, ...), custom_call_target="tpu_custom_call" | custom-call | flops 6000000000 | bytes 1000 | tf_op jit(solution)/shard_map/project_self_kernel/pallas_call | solution.py:461
  70.7 12.5 %collective-permute-done.11.refs_3_ = bf16[5,48,384]{2,1,0:T(8,128)(2,1)S(1)} collective-permute-done((bf16[5,48,384]{2,1,0:T(8,128)(2,1)}, bf16[5,48,384]{2,1,0:T(8,128)(2,1)S(1)}, u32[]{:S(2)}, u32[]{:S(2)}) %collective-permute-start.11) | collective-permute-done | bytes 184352 | tf_op jit(solution)/shard_map/ppermute | solution.py:422
  83.9 2.2 place_line.3
  88.4 9.1 %self_forward.2 = (bf16[512,384]{1,0:T(8,128)(2,1)}, f32[3,1,1,1024]{3,2,1,0:T(1,128)}, f32[3,4,256,512]{3,2,1,0:T(8,128)}) custom-call(s32[1]{0:T(128)} %bitcast.5.refs_0_, s32[1,4]{1,0:T(1,128)} %refs_2_.13, s32[1,4]{1,0:T(1,128)} %refs_2_.13, bf16[512,768]{1,0:T(8,128)(2,1)} %get-tuple-element.110.refs_5_.refs_3_, ...), custom_call_target="tpu_custom_call" | custom-call | flops 20000000000 | bytes 1000 | tf_op jit(solution)/shard_map/self_forward/pallas_call | solution.py:338
  97.5 7.3 %collective-permute-done.13.refs_2_ = bf16[2,5,48,384]{3,2,1,0:T(8,128)(2,1)S(1)} collective-permute-done((bf16[2,5,48,384]{3,2,1,0:T(8,128)(2,1)}, bf16[2,5,48,384]{3,2,1,0:T(8,128)(2,1)S(1)}, u32[]{:S(2)}, u32[]{:S(2)}) %collective-permute-start.13) | collective-permute-done | bytes 368672 | tf_op jit(solution)/shard_map/ppermute | solution.py:426
  105.7 2.6 place_pairs.6
  109.1 1.4 collective-permute-start.17
  110.4 9.0 %self_forward.3 = (bf16[512,384]{1,0:T(8,128)(2,1)}, f32[3,1,1,1024]{3,2,1,0:T(1,128)}, f32[3,4,256,512]{3,2,1,0:T(8,128)}) custom-call(s32[1]{0:T(128)} %bitcast.5.refs_0_, s32[1,4]{1,0:T(1,128)} %refs_2_.13, s32[1,4]{1,0:T(1,128)} %refs_2_.13, bf16[512,768]{1,0:T(8,128)(2,1)} %get-tuple-element.110.refs_5_.refs_3_, ...), custom_call_target="tpu_custom_call" | custom-call | flops 20000000000 | bytes 1000 | tf_op jit(solution)/shard_map/self_forward/pallas_call | solution.py:338
  119.5 15.6 %collective-permute-done.16.refs_2_ = bf16[2,2,5,48,384]{4,3,2,1,0:T(8,128)(2,1)S(1)} collective-permute-done((bf16[2,2,5,48,384]{4,3,2,1,0:T(8,128)(2,1)}, bf16[2,2,5,48,384]{4,3,2,1,0:T(8,128)(2,1)S(1)}, u32[]{:S(2)}, u32[]{:S(2)}) %collective-permute-start.16) | collective-permute-done | bytes 737312 | tf_op jit(solution)/shard_map/ppermute | solution.py:422
  135.0 1.6 collective-permute-done.17.refs_4_
  137.5 3.6 place_pairs.7
  141.6 2.4 collective-permute-start.20
  144.6 2.7 collective-permute-done.19.refs_8_.refs_12_.refs_3_.refs_7_.refs_16_
  148.4 5.1 %after_self_kernel.1 = (f32[512,768]{1,0:T(8,128)}, bf16[512,768]{1,0:T(8,128)(2,1)}, bf16[512,768]{1,0:T(8,128)(2,1)}) custom-call(s32[4]{0:T(128)} %pad_add_fusion.refs_0_.place_ref, bf16[512,768]{1,0:T(8,128)(2,1)} %bitcast.59, f32[3,768]{1,0:T(4,128)} %refs_4_.3, bf16[512,384]{1,0:T(8,128)(2,1)} %get-tuple-element.115.refs_5_.refs_3_.refs_7_, ...), custom_call_target="tpu_custom_call" | custom-call | flops 6000000000 | bytes 1000 | tf_op jit(solution)/shard_map/after_self_kernel/pallas_call | solution.py:461
  153.6 8.4 %collective-permute-done.20.far_b = bf16[512,768]{1,0:T(8,128)(2,1)} collective-permute-done((bf16[512,768]{1,0:T(8,128)(2,1)}, bf16[512,768]{1,0:T(8,128)(2,1)}, u32[]{:S(2)}, u32[]{:S(2)}) %collective-permute-start.20) | collective-permute-done | bytes 786464 | tf_op jit(solution)/shard_map/ppermute | solution.py:426
  162.0 9.9 %project_memory_kernel.1 = (bf16[2048,768]{1,0:T(8,128)(2,1)}, bf16[2048,768]{1,0:T(8,128)(2,1)}) custom-call(s32[4]{0:T(128)} %pad_add_fusion.refs_0_.place_ref, bf16[1024,768]{1,0:T(8,128)(2,1)} %bitcast.45, bf16[512,768]{1,0:T(8,128)(2,1)} %copy-done.15, bf16[512,768]{1,0:T(8,128)(2,1)} %collective-permute-done.20.far_b, ...), custom_call_target="tpu_custom_call" | custom-call | flops 6000000000 | bytes 1000 | tf_op jit(solution)/shard_map/project_memory_kernel/pallas_call | solution.py:850
  171.9 22.2 %cross_forward.1 = (bf16[512,768]{1,0:T(8,128)(2,1)}, f32[6,1,1,1024]{3,2,1,0:T(1,128)}) custom-call(s32[1]{0:T(128)} %bitcast.5.refs_0_, s32[1,4]{1,0:T(1,128)} %refs_2_.13, s32[1,4]{1,0:T(1,128)} %refs_2_.11, bf16[512,768]{1,0:T(8,128)(2,1)} %get-tuple-element.123.refs_3_, bf16[2048,768]{1,0:T(8,128)(2,1)} %get-tuple-element.124.refs_4_, ...), custom_call_target="tpu_custom_call" | custom-call | flops 20000000000 | bytes 1000 | tf_op jit(solution)/shard_map/cross_forward/pallas_call | solution.py:338
  194.1 27.7 %feed_forward_kernel.1 = (bf16[512,768]{1,0:T(8,128)(2,1)}, f32[512,768]{1,0:T(8,128)}, bf16[512,768]{1,0:T(8,128)(2,1)}, f32[1,768]{1,0:T(1,128)}, bf16[16,2,1152,128]{3,2,1,0:T(8,128)(2,1)}) custom-call(s32[4]{0:T(128)} %pad_add_fusion.refs_0_.place_ref, f32[512,768]{1,0:T(8,128)} %get-tuple-element.122.refs_1_, ...), custom_call_target="tpu_custom_call" | custom-call | flops 6000000000 | bytes 1000 | tf_op jit(solution)/shard_map/feed_forward_kernel/pallas_call | solution.py:461
  221.9 37.8 %cross_backward.1 = (bf16[512,768]{1,0:T(8,128)(2,1)}, bf16[2048,768]{1,0:T(8,128)(2,1)}, bf16[2048,768]{1,0:T(8,128)(2,1)}) custom-call(s32[1]{0:T(128)} %bitcast.5.refs_0_, s32[1,4]{1,0:T(1,128)} %refs_2_.13, s32[1,4]{1,0:T(1,128)} %refs_2_.11, bf16[512,768]{1,0:T(8,128)(2,1)} %get-tuple-element.123.refs_3_, bf16[2048,768]{1,0:T(8,128)(2,1)} %get-tuple-element.124.refs_4_, ...), custom_call_target="tpu_custom_call" | custom-call | flops 20000000000 | bytes 1000 | tf_op jit(solution)/shard_map/cross_backward/pallas_call | solution.py:390
  259.6 19.2 %memory_backward_kernel.1 = (f32[1024,768]{1,0:T(8,128)}, bf16[512,768]{1,0:T(8,128)(2,1)}, bf16[512,768]{1,0:T(8,128)(2,1)}, bf16[4,2,2,288,128]{4,3,2,1,0:T(8,128)(2,1)}, bf16[4,2,2,288,128]{4,3,2,1,0:T(8,128)(2,1)}) custom-call(s32[4]{0:T(128)} %pad_add_fusion.refs_0_.place_ref, bf16[2048,768]{1,0:T(8,128)(2,1)} %get-tuple-element.134.dk_ref, ...), custom_call_target="tpu_custom_call" | custom-call | flops 6000000000 | bytes 1000 | tf_op jit(solution)/shard_map/memory_backward_kernel/pallas_call | solution.py:1086
  278.9 1.8 collective-permute-start.23
  280.7 10.3 %after_cross_kernel.1 = (f32[512,768]{1,0:T(8,128)}, bf16[512,768]{1,0:T(8,128)(2,1)}, f32[1,768]{1,0:T(1,128)}, bf16[4,2,2,432,128]{4,3,2,1,0:T(8,128)(2,1)}, bf16[4,2,2,432,128]{4,3,2,1,0:T(8,128)(2,1)}) custom-call(s32[4]{0:T(128)} %pad_add_fusion.refs_0_.place_ref, f32[512,768]{1,0:T(8,128)} %get-tuple-element.122.refs_1_, ...), custom_call_target="tpu_custom_call" | custom-call | flops 6000000000 | bytes 1000 | tf_op jit(solution)/shard_map/after_cross_kernel/pallas_call | solution.py:461
  291.5 13.6 %self_backward.2 = (bf16[512,384]{1,0:T(8,128)(2,1)}, bf16[1024,384]{1,0:T(8,128)(2,1)}, bf16[1024,384]{1,0:T(8,128)(2,1)}, f32[3,2,1280]{2,1,0:T(2,128)}) custom-call(s32[1]{0:T(128)} %bitcast.5.refs_0_, s32[1,4]{1,0:T(1,128)} %refs_2_.13, s32[1,4]{1,0:T(1,128)} %refs_2_.13, bf16[512,768]{1,0:T(8,128)(2,1)} %get-tuple-element.110.refs_5_.refs_3_, ...), custom_call_target="tpu_custom_call" | custom-call | flops 20000000000 | bytes 1000 | tf_op jit(solution)/shard_map/self_backward/pallas_call | solution.py:390
  306.6 4.8 %scatter_step.4 = (bf16[4,2,288,128]{3,2,1,0:T(8,128)(2,1)}, bf16[4,2,288,128]{3,2,1,0:T(8,128)(2,1)}, bf16[4,2,432,128]{3,2,1,0:T(8,128)(2,1)}, bf16[4,2,432,128]{3,2,1,0:T(8,128)(2,1)}) custom-call(bf16[4,2,2,288,128]{4,3,2,1,0:T(8,128)(2,1)} %get-tuple-element.144.refs_0_, bf16[4,2,2,288,128]{4,3,2,1,0:T(8,128)(2,1)} %copy-done.8, ...), custom_call_target="tpu_custom_call" | custom-call | flops 100000 | bytes 1000 | tf_op jit(solution)/shard_map/scatter_step/pallas_call | solution.py:461
  311.7 1.7 collective-permute-start.27
  314.3 13.8 %self_backward.3 = (bf16[512,384]{1,0:T(8,128)(2,1)}, bf16[1024,384]{1,0:T(8,128)(2,1)}, bf16[1024,384]{1,0:T(8,128)(2,1)}, f32[3,2,1280]{2,1,0:T(2,128)}) custom-call(s32[1]{0:T(128)} %bitcast.5.refs_0_, s32[1,4]{1,0:T(1,128)} %refs_2_.13, s32[1,4]{1,0:T(1,128)} %refs_2_.13, bf16[512,768]{1,0:T(8,128)(2,1)} %get-tuple-element.110.refs_5_.refs_3_, ...), custom_call_target="tpu_custom_call" | custom-call | flops 20000000000 | bytes 1000 | tf_op jit(solution)/shard_map/self_backward/pallas_call | solution.py:390
  328.2 8.1 %self_row_grads_kernel.1 = (f32[512,768]{1,0:T(8,128)}, bf16[512,768]{1,0:T(8,128)(2,1)}, f32[1,768]{1,0:T(1,128)}) custom-call(s32[4]{0:T(128)} %pad_add_fusion.refs_0_.place_ref, bf16[512,768]{1,0:T(8,128)(2,1)} %bitcast.60, bf16[512,768]{1,0:T(8,128)(2,1)} %copy-done.14, bf16[512,384]{1,0:T(8,128)(2,1)} %get-tuple-element.141.refs_4_.refs_10_.refs_3_.refs_1_, ...), custom_call_target="tpu_custom_call" | custom-call | flops 6000000000 | bytes 1000 | tf_op jit(solution)/shard_map/self_row_grads_kernel/pallas_call | solution.py:461
  338.4 9.6 %collective-permute-done.27.refs_5_.refs_2_ = bf16[512,768]{1,0:T(8,128)(2,1)S(1)} collective-permute-done((bf16[512,768]{1,0:T(8,128)(2,1)}, bf16[512,768]{1,0:T(8,128)(2,1)S(1)}, u32[]{:S(2)}, u32[]{:S(2)}) %collective-permute-start.27) | collective-permute-done | bytes 786464 | tf_op jit(solution)/shard_map/ppermute | solution.py:426
  349.1 3.9 scatter_step.5
  353.0 7.8 %self_weight_grads_kernel.1 = (bf16[4,2,2,240,128]{4,3,2,1,0:T(8,128)(2,1)}, bf16[4,2,2,240,128]{4,3,2,1,0:T(8,128)(2,1)}, bf16[4,2,2,192,128]{4,3,2,1,0:T(8,128)(2,1)}, bf16[4,2,2,192,128]{4,3,2,1,0:T(8,128)(2,1)}) custom-call(s32[4]{0:T(128)} %pad_add_fusion.refs_0_.place_ref, bf16[512,384]{1,0:T(8,128)(2,1)} %get-tuple-element.141.refs_4_.refs_10_.refs_3_.refs_1_, ...), custom_call_target="tpu_custom_call" | custom-call | flops 6000000000 | bytes 1000 | tf_op jit(solution)/shard_map/self_weight_grads_kernel/pallas_call | solution.py:461
  361.6 1.5 collective-permute-start.31
  363.0 1.8 collective-permute-done.32.refs_3_
  369.2 4.1 scatter_step.6
  373.3 1.7 collective-permute-start.33
  376.1 1.6 collective-permute-start.37
  377.7 3.9 collective-permute-done.37.refs_3_
  382.8 9.7 %collective-permute-done.38.refs_1_ = bf16[4,288,128]{2,1,0:T(8,128)(2,1)S(1)} collective-permute-done((bf16[4,288,128]{2,1,0:T(8,128)(2,1)}, bf16[4,288,128]{2,1,0:T(8,128)(2,1)S(1)}, u32[]{:S(2)}, u32[]{:S(2)}) %collective-permute-start.38) | collective-permute-done | bytes 294944 | tf_op jit(solution)/shard_map/ppermute | solution.py:422
  392.5 8.3 %collective-permute-done.39.refs_3_ = bf16[4,432,128]{2,1,0:T(8,128)(2,1)S(1)} collective-permute-done((bf16[4,432,128]{2,1,0:T(8,128)(2,1)S(1)}, bf16[4,432,128]{2,1,0:T(8,128)(2,1)S(1)}, u32[]{:S(2)}, u32[]{:S(2)}) %collective-permute-start.39) | collective-permute-done | bytes 442400 | tf_op jit(solution)/shard_map/ppermute | solution.py:426
  401.6 2.2 scatter_to_line.2
  407.1 4.6 %add_rows.1.refs_4_ = f32[1024,768]{1,0:T(8,128)} custom-call(f32[1024,768]{1,0:T(8,128)} %get-tuple-element.175.refs_0_, bf16[512,768]{1,0:T(8,128)(2,1)} %copy-done.13, bf16[512,768]{1,0:T(8,128)(2,1)} %copy-done.2, f32[21,128]{1,0:T(8,128)} %sum_small.4.refs_3_.refs_0_), custom_call_target="tpu_custom_call" | custom-call | flops 100000 | bytes 1000 | tf_op jit(solution)/shard_map/add_rows/pallas_call | solution.py:461
  411.7 2.6 collective-permute-start.43
  415.1 3.5 scatter_step.7
  419.8 4.2 finish_rows_kernel.1.refs_4_
  426.0 2.1 scatter_to_line.3
  428.5 1.5 collective-permute-start.47
  430.0 2.5 collective-permute-start.48
  432.5 1.8 collective-permute-start.40
  435.0 2.0 scatter_end.3
  442.4 1.8 scatter_end.4
  444.2 1.8 scatter_end.5
  (237 shorter events, 50.8 us)
Async XLA Ops:
  7.2 19.2 %copy-start = (bf16[2,48,1024]{2,1,0:T(8,128)(2,1)S(1)}, bf16[2,48,1024]{2,1,0:T(8,128)(2,1)}, u32[]{:S(2)}) copy-start(bf16[2,48,1024]{2,1,0:T(8,128)(2,1)} %param.25) | copy-start | bytes 589828
  7.2 186.9 %all-gather.3.cloned.1.call-start = ((), (), s32[]{:S(2)}) async-start(), calls=%async_computation.2 | async-start | bytes 9732096 | tf_op jit(solution)/shard_map/all_gather | solution.py:1395
  7.2 25.5 %collective-permute-start = (bf16[512,768]{1,0:T(8,128)(2,1)}, bf16[512,768]{1,0:T(8,128)(2,1)S(1)}, u32[]{:S(2)}, u32[]{:S(2)}) collective-permute-start(bf16[512,768]{1,0:T(8,128)(2,1)} %bitcast.57), channel_id=1, source_target_pairs={{0,1},{1,0},{2,3},{3,2},{4,5},{5,4},{6,7},{7,6},{8,9},{9,8},{10,11... | collective-permute-start | bytes 2359304 | tf_op jit(solution)/shard_map/ppermute | solution.py:426
  10.2 10.2 %collective-permute-start.2 = (bf16[3,48,384]{2,1,0:T(8,128)(2,1)}, bf16[3,48,384]{2,1,0:T(8,128)(2,1)S(1)}, u32[]{:S(2)}, u32[]{:S(2)}) collective-permute-start(bf16[3,48,384]{2,1,0:T(8,128)(2,1)} %refs_1_.7), channel_id=1, source_target_pairs={{0,16},{2,18},{4,20},{6,22},{8,24},{10,26},{12,28},{14,30},{16,0},... | collective-permute-start | bytes 331784 | tf_op jit(solution)/shard_map/ppermute | solution.py:422
  12.8 7.6 %collective-permute-start.1 = (bf16[3,48,384]{2,1,0:T(8,128)(2,1)}, bf16[3,48,384]{2,1,0:T(8,128)(2,1)S(1)}, u32[]{:S(2)}, u32[]{:S(2)}) collective-permute-start(bf16[3,48,384]{2,1,0:T(8,128)(2,1)} %refs_1_.7), channel_id=1, source_target_pairs={{0,8},{2,10},{4,12},{6,14},{8,0},{10,2},{12,4},{14,6},{16,24},{18,... | collective-permute-start | bytes 331784 | tf_op jit(solution)/shard_map/ppermute | solution.py:422
  14.4 7.3 %collective-permute-start.3 = (bf16[3,48,384]{2,1,0:T(8,128)(2,1)}, bf16[3,48,384]{2,1,0:T(8,128)(2,1)S(1)}, u32[]{:S(2)}, u32[]{:S(2)}) collective-permute-start(bf16[3,48,384]{2,1,0:T(8,128)(2,1)} %refs_1_.7), channel_id=1, source_target_pairs={{0,24},{2,26},{4,28},{6,30},{8,16},{10,18},{12,20},{14,22},{16,8},... | collective-permute-start | bytes 331784 | tf_op jit(solution)/shard_map/ppermute | solution.py:422
  15.8 24.9 %copy-start.5 = (bf16[1,1024,768]{2,1,0:T(8,128)(2,1)S(1)}, bf16[1,1024,768]{2,1,0:T(8,128)(2,1)}, u32[]{:S(2)}) copy-start(bf16[1,1024,768]{2,1,0:T(8,128)(2,1)} %param.15) | copy-start | bytes 4718596
  24.3 8.4 %collective-permute-start.4 = (bf16[2,3,48,384]{3,2,1,0:T(8,128)(2,1)}, bf16[2,3,48,384]{3,2,1,0:T(8,128)(2,1)S(1)}, u32[]{:S(2)}, u32[]{:S(2)}) collective-permute-start(bf16[2,3,48,384]{3,2,1,0:T(8,128)(2,1)} %get-tuple-element.104.refs_1_), channel_id=1, source_target_pairs={{0,1},{1,0},{2,3},{3,2},{4,5},{5,4},{6,7},{7,6},{8,9},{9,8},{10,11... | collective-permute-start | bytes 663560 | tf_op jit(solution)/shard_map/ppermute | solution.py:426
  24.8 7.9 %collective-permute-start.5 = (bf16[2,3,48,384]{3,2,1,0:T(8,128)(2,1)}, bf16[2,3,48,384]{3,2,1,0:T(8,128)(2,1)S(1)}, u32[]{:S(2)}, u32[]{:S(2)}) collective-permute-start(bf16[2,3,48,384]{3,2,1,0:T(8,128)(2,1)} %get-tuple-element.105.refs_3_.refs_2_), channel_id=1, source_target_pairs={{0,4},{2,6},{4,0},{6,2},{8,12},{10,14},{12,8},{14,10},{16,20},{18,... | collective-permute-start | bytes 663560 | tf_op jit(solution)/shard_map/ppermute | solution.py:422
  36.6 11.6 %collective-permute-start.6 = (bf16[2,2,3,48,384]{4,3,2,1,0:T(8,128)(2,1)}, bf16[2,2,3,48,384]{4,3,2,1,0:T(8,128)(2,1)S(1)}, u32[]{:S(2)}, u32[]{:S(2)}) collective-permute-start(bf16[2,2,3,48,384]{4,3,2,1,0:T(8,128)(2,1)} %get-tuple-element.106.refs_1_), channel_id=1, source_target_pairs={{0,4},{2,6},{4,0},{6,2},{8,12},{10,14},{12,8},{14,10},{16,20},{18,... | collective-permute-start | bytes 1327112 | tf_op jit(solution)/shard_map/ppermute | solution.py:422
  38.4 11.0 %collective-permute-start.7 = (bf16[2,2,3,48,384]{4,3,2,1,0:T(8,128)(2,1)}, bf16[2,2,3,48,384]{4,3,2,1,0:T(8,128)(2,1)S(1)}, u32[]{:S(2)}, u32[]{:S(2)}) collective-permute-start(bf16[2,2,3,48,384]{4,3,2,1,0:T(8,128)(2,1)} %get-tuple-element.107.refs_3_), channel_id=1, source_target_pairs={{0,1},{1,0},{2,3},{3,2},{4,5},{5,4},{6,7},{7,6},{8,9},{9,8},{10,11... | collective-permute-start | bytes 1327112 | tf_op jit(solution)/shard_map/ppermute | solution.py:426
  53.0 391.2 %reduce-scatter.2.cloned.1.call-start = ((), (), s32[]{:S(2)}) async-start(), calls=%async_computation.1 | async-start | bytes 9732096 | tf_op jit(solution)/shard_map/reduce_scatter | solution.py:1435
  54.0 7.0 %collective-permute-start.8 = (bf16[2,2,2,3,48,384]{5,4,3,2,1,0:T(8,128)(2,1)S(1)}, bf16[2,2,2,3,48,384]{5,4,3,2,1,0:T(8,128)(2,1)}, u32[]{:S(2)}, u32[]{:S(2)}) collective-permute-start(bf16[2,2,2,3,48,384]{5,4,3,2,1,0:T(8,128)(2,1)S(1)} %copy-done.10), channel_id=1, source_target_pairs={{0,2},{2,0},{4,6},{6,4},{8,10},{10,8},{12,14},{14,12},{16,18},{18,... | collective-permute-start | bytes 2654216 | tf_op jit(solution)/shard_map/ppermute | solution.py:422
  54.3 8.2 %collective-permute-start.9 = (bf16[2,2,2,3,48,384]{5,4,3,2,1,0:T(8,128)(2,1)S(1)}, bf16[2,2,2,3,48,384]{5,4,3,2,1,0:T(8,128)(2,1)}, u32[]{:S(2)}, u32[]{:S(2)}) collective-permute-start(bf16[2,2,2,3,48,384]{5,4,3,2,1,0:T(8,128)(2,1)S(1)} %copy-done.11), channel_id=1, source_target_pairs={{0,2},{2,0},{4,6},{6,4},{8,10},{10,8},{12,14},{14,12},{16,18},{18,... | collective-permute-start | bytes 2654216 | tf_op jit(solution)/shard_map/ppermute | solution.py:422
  56.7 14.0 %collective-permute-start.12 = (bf16[5,48,384]{2,1,0:T(8,128)(2,1)}, bf16[5,48,384]{2,1,0:T(8,128)(2,1)S(1)}, u32[]{:S(2)}, u32[]{:S(2)}) collective-permute-start(bf16[5,48,384]{2,1,0:T(8,128)(2,1)} %hold.4.refs_1_), channel_id=1, source_target_pairs={{0,24},{2,26},{4,28},{6,30},{8,16},{10,18},{12,20},{14,22},{16,8},... | collective-permute-start | bytes 552968 | tf_op jit(solution)/shard_map/ppermute | solution.py:422
  60.3 22.9 %collective-permute-start.11 = (bf16[5,48,384]{2,1,0:T(8,128)(2,1)}, bf16[5,48,384]{2,1,0:T(8,128)(2,1)S(1)}, u32[]{:S(2)}, u32[]{:S(2)}) collective-permute-start(bf16[5,48,384]{2,1,0:T(8,128)(2,1)} %hold.4.refs_1_), channel_id=1, source_target_pairs={{0,16},{2,18},{4,20},{6,22},{8,24},{10,26},{12,28},{14,30},{16,0},... | collective-permute-start | bytes 552968 | tf_op jit(solution)/shard_map/ppermute | solution.py:422
  60.3 22.9 %collective-permute-start.10 = (bf16[5,48,384]{2,1,0:T(8,128)(2,1)}, bf16[5,48,384]{2,1,0:T(8,128)(2,1)S(1)}, u32[]{:S(2)}, u32[]{:S(2)}) collective-permute-start(bf16[5,48,384]{2,1,0:T(8,128)(2,1)} %hold.4.refs_1_), channel_id=1, source_target_pairs={{0,8},{2,10},{4,12},{6,14},{8,0},{10,2},{12,4},{14,6},{16,24},{18,... | collective-permute-start | bytes 552968 | tf_op jit(solution)/shard_map/ppermute | solution.py:422
  61.0 36.4 %collective-permute-start.15 = (bf16[512,768]{1,0:T(8,128)(2,1)S(1)}, bf16[512,768]{1,0:T(8,128)(2,1)S(1)}, u32[]{:S(2)}, u32[]{:S(2)}) collective-permute-start(bf16[512,768]{1,0:T(8,128)(2,1)S(1)} %copy-done.3), channel_id=1, source_target_pairs={{0,1},{1,0},{2,3},{3,2},{4,5},{5,4},{6,7},{7,6},{8,9},{9,8},{10,11... | collective-permute-start | bytes 2359304 | tf_op jit(solution)/shard_map/ppermute | solution.py:426
  70.7 12.5 %copy-start.35 = (bf16[5,48,384]{2,1,0:T(8,128)(2,1)}, bf16[5,48,384]{2,1,0:T(8,128)(2,1)S(1)}, u32[]{:S(2)}) copy-start(bf16[5,48,384]{2,1,0:T(8,128)(2,1)S(1)} %collective-permute-done.12.refs_4_) | copy-start | bytes 552964
  86.1 18.7 %collective-permute-start.13 = (bf16[2,5,48,384]{3,2,1,0:T(8,128)(2,1)}, bf16[2,5,48,384]{3,2,1,0:T(8,128)(2,1)S(1)}, u32[]{:S(2)}, u32[]{:S(2)}) collective-permute-start(bf16[2,5,48,384]{3,2,1,0:T(8,128)(2,1)} %get-tuple-element.113.refs_7_.refs_1_), channel_id=1, source_target_pairs={{0,1},{1,0},{2,3},{3,2},{4,5},{5,4},{6,7},{7,6},{8,9},{9,8},{10,11... | collective-permute-start | bytes 1105928 | tf_op jit(solution)/shard_map/ppermute | solution.py:426
  87.3 17.5 %collective-permute-start.14 = (bf16[2,5,48,384]{3,2,1,0:T(8,128)(2,1)}, bf16[2,5,48,384]{3,2,1,0:T(8,128)(2,1)S(1)}, u32[]{:S(2)}, u32[]{:S(2)}) collective-permute-start(bf16[2,5,48,384]{3,2,1,0:T(8,128)(2,1)} %get-tuple-element.114.refs_8_.refs_3_), channel_id=1, source_target_pairs={{0,4},{2,6},{4,0},{6,2},{8,12},{10,14},{12,8},{14,10},{16,20},{18,... | collective-permute-start | bytes 1105928 | tf_op jit(solution)/shard_map/ppermute | solution.py:422
  108.3 26.7 %collective-permute-start.16 = (bf16[2,2,5,48,384]{4,3,2,1,0:T(8,128)(2,1)}, bf16[2,2,5,48,384]{4,3,2,1,0:T(8,128)(2,1)S(1)}, u32[]{:S(2)}, u32[]{:S(2)}) collective-permute-start(bf16[2,2,5,48,384]{4,3,2,1,0:T(8,128)(2,1)} %get-tuple-element.117.refs_7_.refs_1_), channel_id=1, source_target_pairs={{0,4},{2,6},{4,0},{6,2},{8,12},{10,14},{12,8},{14,10},{16,20},{18,... | collective-permute-start | bytes 2211848 | tf_op jit(solution)/shard_map/ppermute | solution.py:422
  109.1 27.6 %collective-permute-start.17 = (bf16[2,2,5,48,384]{4,3,2,1,0:T(8,128)(2,1)}, bf16[2,2,5,48,384]{4,3,2,1,0:T(8,128)(2,1)S(1)}, u32[]{:S(2)}, u32[]{:S(2)}) collective-permute-start(bf16[2,2,5,48,384]{4,3,2,1,0:T(8,128)(2,1)} %get-tuple-element.118.refs_8_.refs_3_), channel_id=1, source_target_pairs={{0,1},{1,0},{2,3},{3,2},{4,5},{5,4},{6,7},{7,6},{8,9},{9,8},{10,11... | collective-permute-start | bytes 2211848 | tf_op jit(solution)/shard_map/ppermute | solution.py:426
  141.1 3.5 collective-permute-start.18
  141.1 6.2 %collective-permute-start.19 = (bf16[2,2,2,5,48,384]{5,4,3,2,1,0:T(8,128)(2,1)}, bf16[2,2,2,5,48,384]{5,4,3,2,1,0:T(8,128)(2,1)S(1)}, u32[]{:S(2)}, u32[]{:S(2)}) collective-permute-start(bf16[2,2,2,5,48,384]{5,4,3,2,1,0:T(8,128)(2,1)} %get-tuple-element.121.refs_7_.refs_11_.refs_2_.refs_6_.refs_15_), channel_id=1, source_target_pairs={{0,2},{2,0},{4,6},{6,4},{8,10},{10,8},{12,14},{14,12},{16,18},{18,... | collective-permute-start | bytes 4423688 | tf_op jit(solution)/shard_map/ppermute | solution.py:422
  141.6 20.4 %collective-permute-start.20 = (bf16[512,768]{1,0:T(8,128)(2,1)}, bf16[512,768]{1,0:T(8,128)(2,1)}, u32[]{:S(2)}, u32[]{:S(2)}) collective-permute-start(bf16[512,768]{1,0:T(8,128)(2,1)} %hold.6), channel_id=1, source_target_pairs={{0,1},{1,0},{2,3},{3,2},{4,5},{5,4},{6,7},{7,6},{8,9},{9,8},{10,11... | collective-permute-start | bytes 2359304 | tf_op jit(solution)/shard_map/ppermute | solution.py:426
  278.9 34.6 %collective-permute-start.23 = (bf16[512,768]{1,0:T(8,128)(2,1)}, bf16[512,768]{1,0:T(8,128)(2,1)S(1)}, u32[]{:S(2)}, u32[]{:S(2)}) collective-permute-start(bf16[512,768]{1,0:T(8,128)(2,1)} %get-tuple-element.136.refs_17_), channel_id=1, source_target_pairs={{0,1},{1,0},{2,3},{3,2},{4,5},{5,4},{6,7},{7,6},{8,9},{9,8},{10,11... | collective-permute-start | bytes 2359304 | tf_op jit(solution)/shard_map/ppermute | solution.py:426
  280.7 24.4 %collective-permute-start.21 = (bf16[4,2,2,288,128]{4,3,2,1,0:T(8,128)(2,1)}, bf16[4,2,2,288,128]{4,3,2,1,0:T(8,128)(2,1)S(1)}, u32[]{:S(2)}, u32[]{:S(2)}) collective-permute-start(bf16[4,2,2,288,128]{4,3,2,1,0:T(8,128)(2,1)} %get-tuple-element.145), channel_id=1, source_target_pairs={{0,2},{2,0},{4,6},{6,4},{8,10},{10,8},{12,14},{14,12},{16,18},{18,... | collective-permute-start | bytes 3538952 | tf_op jit(solution)/shard_map/ppermute | solution.py:422
  291.0 14.1 %collective-permute-start.22 = (bf16[4,2,2,432,128]{4,3,2,1,0:T(8,128)(2,1)}, bf16[4,2,2,432,128]{4,3,2,1,0:T(8,128)(2,1)S(1)}, u32[]{:S(2)}, u32[]{:S(2)}) collective-permute-start(bf16[4,2,2,432,128]{4,3,2,1,0:T(8,128)(2,1)} %get-tuple-element.146), channel_id=1, source_target_pairs={{0,2},{2,0},{4,6},{6,4},{8,10},{10,8},{12,14},{14,12},{16,18},{18,... | collective-permute-start | bytes 5308424 | tf_op jit(solution)/shard_map/ppermute | solution.py:422
  311.4 26.9 %collective-permute-start.25 = (bf16[4,2,288,128]{3,2,1,0:T(8,128)(2,1)}, bf16[4,2,288,128]{3,2,1,0:T(8,128)(2,1)S(1)}, u32[]{:S(2)}, u32[]{:S(2)}) collective-permute-start(bf16[4,2,288,128]{3,2,1,0:T(8,128)(2,1)} %get-tuple-element.157), channel_id=1, source_target_pairs={{0,1},{1,0},{2,3},{3,2},{4,5},{5,4},{6,7},{7,6},{8,9},{9,8},{10,11... | collective-permute-start | bytes 1769480 | tf_op jit(solution)/shard_map/ppermute | solution.py:426
  311.7 36.2 %collective-permute-start.27 = (bf16[512,768]{1,0:T(8,128)(2,1)}, bf16[512,768]{1,0:T(8,128)(2,1)S(1)}, u32[]{:S(2)}, u32[]{:S(2)}) collective-permute-start(bf16[512,768]{1,0:T(8,128)(2,1)} %hold.7), channel_id=1, source_target_pairs={{0,1},{1,0},{2,3},{3,2},{4,5},{5,4},{6,7},{7,6},{8,9},{9,8},{10,11... | collective-permute-start | bytes 2359304 | tf_op jit(solution)/shard_map/ppermute | solution.py:426
  313.5 34.5 %collective-permute-start.26 = (bf16[4,2,432,128]{3,2,1,0:T(8,128)(2,1)}, bf16[4,2,432,128]{3,2,1,0:T(8,128)(2,1)S(1)}, u32[]{:S(2)}, u32[]{:S(2)}) collective-permute-start(bf16[4,2,432,128]{3,2,1,0:T(8,128)(2,1)} %get-tuple-element.159), channel_id=1, source_target_pairs={{0,4},{2,6},{4,0},{6,2},{8,12},{10,14},{12,8},{14,10},{16,20},{18,... | collective-permute-start | bytes 2654216 | tf_op jit(solution)/shard_map/ppermute | solution.py:422
  328.2 8.8 %copy-start.52 = (f32[3,2,1280]{2,1,0:T(2,128)S(1)}, f32[3,2,1280]{2,1,0:T(2,128)}, u32[]{:S(2)}) copy-start(f32[3,2,1280]{2,1,0:T(2,128)} %get-tuple-element.165) | copy-start | bytes 92164
  328.2 8.8 %copy-start.53 = (f32[3,2,1280]{2,1,0:T(2,128)S(1)}, f32[3,2,1280]{2,1,0:T(2,128)}, u32[]{:S(2)}) copy-start(f32[3,2,1280]{2,1,0:T(2,128)} %get-tuple-element.166) | copy-start | bytes 92164
  328.2 8.9 %copy-start.39 = (pred[1024,32]{1,0:T(32,128)(4,1)S(1)}, pred[1024,32]{1,0:T(32,128)(4,1)}, u32[]{:S(2)}) copy-start(pred[1024,32]{1,0:T(32,128)(4,1)} %copy-done.38) | copy-start | bytes 98308
  338.4 9.6 %copy-start.19 = (bf16[4,2,288,128]{3,2,1,0:T(8,128)(2,1)}, bf16[4,2,288,128]{3,2,1,0:T(8,128)(2,1)S(1)}, u32[]{:S(2)}) copy-start(bf16[4,2,288,128]{3,2,1,0:T(8,128)(2,1)S(1)} %collective-permute-done.25.refs_1_) | copy-start | bytes 1769476
  353.0 8.3 %copy-start.64 = (bf16[512,768]{1,0:T(8,128)(2,1)S(1)}, bf16[512,768]{1,0:T(8,128)(2,1)}, u32[]{:S(2)}) copy-start(bf16[512,768]{1,0:T(8,128)(2,1)} %get-tuple-element.154) | copy-start | bytes 2359300
  353.0 8.6 %copy-start.49 = (f32[21,128]{1,0:T(8,128)S(1)}, f32[21,128]{1,0:T(8,128)}, u32[]{:S(2)}) copy-start(f32[21,128]{1,0:T(8,128)} %maximum_bitcast_fusion.refs_9_.refs_0_) | copy-start | bytes 32260
  360.8 7.1 %collective-permute-start.28 = (bf16[4,2,2,240,128]{4,3,2,1,0:T(8,128)(2,1)}, bf16[4,2,2,240,128]{4,3,2,1,0:T(8,128)(2,1)S(1)}, u32[]{:S(2)}, u32[]{:S(2)}) collective-permute-start(bf16[4,2,2,240,128]{4,3,2,1,0:T(8,128)(2,1)} %get-tuple-element.168), channel_id=1, source_target_pairs={{0,2},{2,0},{4,6},{6,4},{8,10},{10,8},{12,14},{14,12},{16,18},{18,... | collective-permute-start | bytes 2949128 | tf_op jit(solution)/shard_map/ppermute | solution.py:422
  360.8 7.1 %collective-permute-start.29 = (bf16[4,2,2,192,128]{4,3,2,1,0:T(8,128)(2,1)}, bf16[4,2,2,192,128]{4,3,2,1,0:T(8,128)(2,1)S(1)}, u32[]{:S(2)}, u32[]{:S(2)}) collective-permute-start(bf16[4,2,2,192,128]{4,3,2,1,0:T(8,128)(2,1)} %get-tuple-element.170), channel_id=1, source_target_pairs={{0,2},{2,0},{4,6},{6,4},{8,10},{10,8},{12,14},{14,12},{16,18},{18,... | collective-permute-start | bytes 2359304 | tf_op jit(solution)/shard_map/ppermute | solution.py:422
  361.3 57.6 %collective-permute-start.24 = (bf16[512,768]{1,0:T(8,128)(2,1)S(1)}, bf16[512,768]{1,0:T(8,128)(2,1)S(1)}, u32[]{:S(2)}, u32[]{:S(2)}) collective-permute-start(bf16[512,768]{1,0:T(8,128)(2,1)S(1)} %copy-done.64), channel_id=1, source_target_pairs={{0,1},{1,0},{2,3},{3,2},{4,5},{5,4},{6,7},{7,6},{8,9},{9,8},{10,11... | collective-permute-start | bytes 2359304 | tf_op jit(solution)/shard_map/ppermute | solution.py:426
  361.6 3.2 collective-permute-start.32
  361.6 3.7 collective-permute-start.31
  364.8 1.2 collective-permute-start.30
  373.3 41.1 %collective-permute-start.33 = (bf16[4,2,240,128]{3,2,1,0:T(8,128)(2,1)}, bf16[4,2,240,128]{3,2,1,0:T(8,128)(2,1)S(1)}, u32[]{:S(2)}, u32[]{:S(2)}) collective-permute-start(bf16[4,2,240,128]{3,2,1,0:T(8,128)(2,1)} %get-tuple-element.172), channel_id=1, source_target_pairs={{0,1},{1,0},{2,3},{3,2},{4,5},{5,4},{6,7},{7,6},{8,9},{9,8},{10,11... | collective-permute-start | bytes 1474568 | tf_op jit(solution)/shard_map/ppermute | solution.py:426
  375.0 25.8 %collective-permute-start.39 = (bf16[4,432,128]{2,1,0:T(8,128)(2,1)S(1)}, bf16[4,432,128]{2,1,0:T(8,128)(2,1)S(1)}, u32[]{:S(2)}, u32[]{:S(2)}) collective-permute-start(bf16[4,432,128]{2,1,0:T(8,128)(2,1)S(1)} %copy-done.66), channel_id=1, source_target_pairs={{0,1},{1,0},{2,3},{3,2},{4,5},{5,4},{6,7},{7,6},{8,9},{9,8},{10,11... | collective-permute-start | bytes 1327112 | tf_op jit(solution)/shard_map/ppermute | solution.py:426
  375.3 36.4 %collective-permute-start.34 = (bf16[4,2,192,128]{3,2,1,0:T(8,128)(2,1)}, bf16[4,2,192,128]{3,2,1,0:T(8,128)(2,1)S(1)}, u32[]{:S(2)}, u32[]{:S(2)}) collective-permute-start(bf16[4,2,192,128]{3,2,1,0:T(8,128)(2,1)} %get-tuple-element.174), channel_id=1, source_target_pairs={{0,4},{2,6},{4,0},{6,2},{8,12},{10,14},{12,8},{14,10},{16,20},{18,... | collective-permute-start | bytes 1179656 | tf_op jit(solution)/shard_map/ppermute | solution.py:422
  376.1 5.5 %collective-permute-start.37 = (f32[21,128]{1,0:T(8,128)S(1)}, f32[21,128]{1,0:T(8,128)S(1)}, u32[]{:S(2)}, u32[]{:S(2)}) collective-permute-start(f32[21,128]{1,0:T(8,128)S(1)} %copy-done.48), channel_id=1, source_target_pairs={{0,24},{1,25},{2,26},{3,27},{4,28},{5,29},{6,30},{7,31},{8,16},{9,... | collective-permute-start | bytes 32264 | tf_op jit(solution)/shard_map/ppermute | solution.py:614
  381.6 23.6 %copy-start.58 = (f32[21,128]{1,0:T(8,128)}, f32[21,128]{1,0:T(8,128)S(1)}, u32[]{:S(2)}) copy-start(f32[21,128]{1,0:T(8,128)S(1)} %collective-permute-done.37.refs_3_) | copy-start | bytes 32260
  381.6 11.0 %collective-permute-start.38 = (bf16[4,288,128]{2,1,0:T(8,128)(2,1)}, bf16[4,288,128]{2,1,0:T(8,128)(2,1)S(1)}, u32[]{:S(2)}, u32[]{:S(2)}) collective-permute-start(bf16[4,288,128]{2,1,0:T(8,128)(2,1)} %get-tuple-element.176), channel_id=1, source_target_pairs={{0,4},{2,6},{4,0},{6,2},{8,12},{10,14},{12,8},{14,10},{16,20},{18,... | collective-permute-start | bytes 884744 | tf_op jit(solution)/shard_map/ppermute | solution.py:422
  392.5 8.3 %copy-start.27 = (bf16[4,288,128]{2,1,0:T(8,128)(2,1)}, bf16[4,288,128]{2,1,0:T(8,128)(2,1)S(1)}, u32[]{:S(2)}) copy-start(bf16[4,288,128]{2,1,0:T(8,128)(2,1)S(1)} %collective-permute-done.38.refs_1_) | copy-start | bytes 884740
  392.5 11.3 %collective-permute-start.36 = (f32[21,128]{1,0:T(8,128)S(1)}, f32[21,128]{1,0:T(8,128)S(1)}, u32[]{:S(2)}, u32[]{:S(2)}) collective-permute-start(f32[21,128]{1,0:T(8,128)S(1)} %copy-done.48), channel_id=1, source_target_pairs={{0,16},{1,17},{2,18},{3,19},{4,20},{5,21},{6,22},{7,23},{8,24},{9,... | collective-permute-start | bytes 32264 | tf_op jit(solution)/shard_map/ppermute | solution.py:614
  400.8 4.3 collective-permute-start.35
  403.8 26.2 %collective-permute-start.41 = (bf16[720,128]{1,0:T(8,128)(2,1)}, bf16[720,128]{1,0:T(8,128)(2,1)S(1)}, u32[]{:S(2)}, u32[]{:S(2)}) collective-permute-start(bf16[720,128]{1,0:T(8,128)(2,1)} %get-tuple-element.181), channel_id=1, source_target_pairs={{0,8},{2,10},{4,12},{6,14},{8,0},{10,2},{12,4},{14,6},{16,24},{18,... | collective-permute-start | bytes 552968 | tf_op jit(solution)/shard_map/ppermute | solution.py:422
  405.1 27.4 %collective-permute-start.42 = (bf16[720,128]{1,0:T(8,128)(2,1)}, bf16[720,128]{1,0:T(8,128)(2,1)S(1)}, u32[]{:S(2)}, u32[]{:S(2)}) collective-permute-start(bf16[720,128]{1,0:T(8,128)(2,1)} %get-tuple-element.182), channel_id=1, source_target_pairs={{0,16},{2,18},{4,20},{6,22},{8,24},{10,26},{12,28},{14,30},{16,0},... | collective-permute-start | bytes 552968 | tf_op jit(solution)/shard_map/ppermute | solution.py:422
  411.7 22.6 %collective-permute-start.43 = (bf16[720,128]{1,0:T(8,128)(2,1)S(1)}, bf16[720,128]{1,0:T(8,128)(2,1)S(1)}, u32[]{:S(2)}, u32[]{:S(2)}) collective-permute-start(bf16[720,128]{1,0:T(8,128)(2,1)S(1)} %copy-done.67), channel_id=1, source_target_pairs={{0,24},{2,26},{4,28},{6,30},{8,16},{10,18},{12,20},{14,22},{16,8},... | collective-permute-start | bytes 552968 | tf_op jit(solution)/shard_map/ppermute | solution.py:422
  418.6 5.9 %collective-permute-start.45 = (bf16[4,192,128]{2,1,0:T(8,128)(2,1)}, bf16[4,192,128]{2,1,0:T(8,128)(2,1)S(1)}, u32[]{:S(2)}, u32[]{:S(2)}) collective-permute-start(bf16[4,192,128]{2,1,0:T(8,128)(2,1)} %get-tuple-element.186), channel_id=1, source_target_pairs={{0,1},{1,0},{2,3},{3,2},{4,5},{5,4},{6,7},{7,6},{8,9},{9,8},{10,11... | collective-permute-start | bytes 589832 | tf_op jit(solution)/shard_map/ppermute | solution.py:426
  418.9 6.4 %collective-permute-start.44 = (bf16[4,240,128]{2,1,0:T(8,128)(2,1)}, bf16[4,240,128]{2,1,0:T(8,128)(2,1)S(1)}, u32[]{:S(2)}, u32[]{:S(2)}) collective-permute-start(bf16[4,240,128]{2,1,0:T(8,128)(2,1)} %get-tuple-element.184), channel_id=1, source_target_pairs={{0,4},{2,6},{4,0},{6,2},{8,12},{10,14},{12,8},{14,10},{16,20},{18,... | collective-permute-start | bytes 737288 | tf_op jit(solution)/shard_map/ppermute | solution.py:422
  424.0 8.5 %copy-start.40 = (f32[21,128]{1,0:T(8,128)S(1)}, f32[21,128]{1,0:T(8,128)}, u32[]{:S(2)}) copy-start(f32[21,128]{1,0:T(8,128)} %sum_small.4.refs_3_.refs_0_) | copy-start | bytes 32260
  426.0 20.0 %copy-start.1 = (bf16[2,48,1024]{2,1,0:T(8,128)(2,1)S(1)}, bf16[2,48,1024]{2,1,0:T(8,128)(2,1)}, u32[]{:S(2)}) copy-start(bf16[2,48,1024]{2,1,0:T(8,128)(2,1)} %param.25) | copy-start | bytes 589828
  428.1 13.5 %collective-permute-start.46 = (bf16[432,128]{1,0:T(8,128)(2,1)}, bf16[432,128]{1,0:T(8,128)(2,1)S(1)}, u32[]{:S(2)}, u32[]{:S(2)}) collective-permute-start(bf16[432,128]{1,0:T(8,128)(2,1)} %get-tuple-element.189), channel_id=1, source_target_pairs={{0,8},{2,10},{4,12},{6,14},{8,0},{10,2},{12,4},{14,6},{16,24},{18,... | collective-permute-start | bytes 331784 | tf_op jit(solution)/shard_map/ppermute | solution.py:422
  428.5 13.2 %collective-permute-start.47 = (bf16[432,128]{1,0:T(8,128)(2,1)}, bf16[432,128]{1,0:T(8,128)(2,1)S(1)}, u32[]{:S(2)}, u32[]{:S(2)}) collective-permute-start(bf16[432,128]{1,0:T(8,128)(2,1)} %get-tuple-element.190), channel_id=1, source_target_pairs={{0,16},{2,18},{4,20},{6,22},{8,24},{10,26},{12,28},{14,30},{16,0},... | collective-permute-start | bytes 331784 | tf_op jit(solution)/shard_map/ppermute | solution.py:422
  430.0 11.7 %collective-permute-start.48 = (bf16[432,128]{1,0:T(8,128)(2,1)}, bf16[432,128]{1,0:T(8,128)(2,1)S(1)}, u32[]{:S(2)}, u32[]{:S(2)}) collective-permute-start(bf16[432,128]{1,0:T(8,128)(2,1)} %get-tuple-element.191), channel_id=1, source_target_pairs={{0,24},{2,26},{4,28},{6,30},{8,16},{10,18},{12,20},{14,22},{16,8},... | collective-permute-start | bytes 331784 | tf_op jit(solution)/shard_map/ppermute | solution.py:422
  432.5 4.5 collective-permute-start.40
  (56 other events, 107.7 us)
Sparse Core Ops, SparseCore 0:
  53.1 103.1 all-gather.2
  222.0 147.4 reduce-scatter.1

commit v4 on v3

--- a/solution.py
+++ b/solution.py
@@ -625,18 +625,12 @@
 def add_rows(block, far, after):
     rows, width = block.shape
 
-    def body(one_ref, far_a, far_b, out_ref):
-        other = jnp.where(pl.program_id(0) < 2, far_a[...], far_b[...])
-        out_ref[...] = one_ref[...] + other.astype(F32)
-
-    part = (rows // 4, width)
-    spec = pl.BlockSpec(part, lambda i: (i, 0))
-    halves = [
-        pl.BlockSpec(part, lambda i: (jnp.minimum(i, 1), 0)),
-        pl.BlockSpec(part, lambda i: (jnp.maximum(i - 2, 0), 0)),
-    ]
+    def body(one_ref, two_ref, out_ref):
+        out_ref[...] = one_ref[...] + two_ref[...].astype(F32)
+
+    spec = pl.BlockSpec((rows // 4, width), lambda i: (i, 0))
     shape = jax.ShapeDtypeStruct(block.shape, F32)
-    return kernel_call(body, "add_rows", (4,), [spec, *halves], spec, shape, (block, *far), after=after)
+    return kernel_call(body, "add_rows", (4,), [spec, spec], spec, shape, (block, far), after=after)
 
 
 def chosen(block, axis, index):
@@ -816,7 +810,7 @@
         q_ref[...] = mm(normed, matrix_of(place_ref, q_weight)).astype(BF16)
 
     return kernel_call(
-        body, "after_self_kernel", (1,),
+        body, "after_self", (1,),
         [smem(), whole_spec(own.shape), whole_spec(gains.shape), *specs_of(attn)]
         + weight_specs(pack, 3) + weight_specs(pack, 0),
         [whole_spec(own.shape)] * 3,
@@ -829,6 +823,10 @@
     )
 
 
+def halves_of(block):
+    return [pl.BlockSpec(block, lambda *_: (0, 0)), pl.BlockSpec(block, lambda *_: (1, 0))]
+
+
 def three_way(step, own_ref, far_a, far_b):
     return jnp.where(step < 2, own_ref[...], jnp.where(step == 2, far_a[...], far_b[...]))
 
@@ -838,10 +836,16 @@
     step = rows // 2
 
     def body(place_ref, own_ref, far_a, far_b, *refs):
-        k_ref, v_ref = refs[8:]
+        k_ref, v_ref, key_weight, value_weight = refs[8:]
+
+        @pl.when(pl.program_id(0) == 0)
+        def once():
+            key_weight[...] = matrix_of(place_ref, refs[:4])
+            value_weight[...] = matrix_of(place_ref, refs[4:8])
+
         source = three_way(pl.program_id(0), own_ref, far_a, far_b)
-        k_ref[...] = mm(source, matrix_of(place_ref, refs[:4])).astype(BF16)
-        v_ref[...] = mm(source, matrix_of(place_ref, refs[4:8])).astype(BF16)
+        k_ref[...] = mm(source, key_weight[...]).astype(BF16)
+        v_ref[...] = mm(source, value_weight[...]).astype(BF16)
 
     def result(i, place_ref):
         return ((place_ref[3] ^ (i // 2)) * 2 + i % 2, 0)
@@ -854,17 +858,17 @@
             grid=(4,),
             in_specs=[
                 pl.BlockSpec((step, width), lambda i, _: (jnp.minimum(i, 1), 0)),
-                whole_spec((step, width)),
-                whole_spec((step, width)),
+                *halves_of((step, width)),
             ]
             + weight_specs(pack, 1) + weight_specs(pack, 2),
             out_specs=[pl.BlockSpec((step, width), result)] * 2,
+            scratch_shapes=[pltpu.VMEM((width, width), BF16)] * 2,
         ),
         out_shape=[shape, shape],
         compiler_params=pltpu.CompilerParams(vmem_limit_bytes=60 << 20),
         cost_estimate=MEDIUM,
         name="project_memory_kernel",
-    )(place, own, *far, *pack, *pack)
+    )(place, own, far, far, *pack, *pack)
 
 
 def feed_forward(place, middle_one, attn, cotangent, gains, pack, wide, half):
@@ -1044,7 +1048,8 @@
         place_ref, dk_ref, dv_ref, own_ref, far_a, far_b, *refs,
     ):
         k_refs, v_refs = refs[:4], refs[4:8]
-        grad_own_ref, grad_far_a, grad_far_b, keep_ref, send_ref, key_total, value_total = refs[8:]
+        grad_own_ref, grad_far_ref, keep_ref, send_ref = refs[8:12]
+        key_total, value_total, key_weight, value_weight = refs[12:]
         i = pl.program_id(0)
         source = three_way(i ^ 2, own_ref, far_a, far_b)
         source_t = source.T
@@ -1053,21 +1058,17 @@
         def clear():
             key_total[...] = jnp.zeros_like(key_total)
             value_total[...] = jnp.zeros_like(value_total)
+            key_weight[...] = matrix_of(place_ref, k_refs)
+            value_weight[...] = matrix_of(place_ref, v_refs)
 
         grad_key, grad_value = dk_ref[...], dv_ref[...]
         key_total[...] += mm(source_t, grad_key)
         value_total[...] += mm(source_t, grad_value)
-        grads = mm_t(grad_key, matrix_of(place_ref, k_refs)) + mm_t(
-            grad_value, matrix_of(place_ref, v_refs)
-        )
-
-        @pl.when(i == 0)
-        def there_first():
-            grad_far_a[...] = grads.astype(BF16)
-
-        @pl.when(i == 1)
-        def there_second():
-            grad_far_b[...] = grads.astype(BF16)
+        grads = mm_t(grad_key, key_weight[...]) + mm_t(grad_value, value_weight[...])
+
+        @pl.when(i < 2)
+        def there():
+            grad_far_ref[...] = grads.astype(BF16)
 
         @pl.when(i >= 2)
         def here():
@@ -1091,30 +1092,28 @@
             in_specs=[
                 *[pl.BlockSpec((step, width), block)] * 2,
                 pl.BlockSpec((step, width), lambda i, _: (jnp.maximum(i - 2, 0), 0)),
-                whole_spec((step, width)),
-                whole_spec((step, width)),
+                *halves_of((step, width)),
             ]
             + weight_specs(pack, 1) + weight_specs(pack, 2),
             out_specs=[
                 pl.BlockSpec((step, width), lambda i, _: (jnp.maximum(i - 2, 0), 0)),
-                whole_spec((step, width)),
-                whole_spec((step, width)),
+                pl.BlockSpec((step, width), lambda i, _: (jnp.minimum(i, 1), 0)),
                 whole_spec(pieces.shape),
                 whole_spec(pieces.shape),
             ],
-            scratch_shapes=[pltpu.VMEM((width, width), F32), pltpu.VMEM((width, width), F32)],
+            scratch_shapes=[pltpu.VMEM((width, width), F32)] * 2
+            + [pltpu.VMEM((width, width), BF16)] * 2,
         ),
         out_shape=[
             jax.ShapeDtypeStruct((rows, width), F32),
-            jax.ShapeDtypeStruct((step, width), BF16),
-            jax.ShapeDtypeStruct((step, width), BF16),
+            jax.ShapeDtypeStruct((rows, width), BF16),
             pieces,
             pieces,
         ],
         compiler_params=pltpu.CompilerParams(vmem_limit_bytes=60 << 20),
         cost_estimate=MEDIUM,
         name="memory_backward_kernel",
-    )(place, grad_key, grad_value, own, *far, *pack, *pack)
+    )(place, grad_key, grad_value, own, far, far, *pack, *pack)
 
 
 def self_weight_grads(place, grad_query, grad_key, grad_value, normed, z_count, after):
@@ -1388,12 +1387,8 @@
     (second,) = hold((second,), (low, high))
     line = line_of(second)
     low, high = gather_first(spot, low, high, (far,))
-    low, high = gather_second(spot, low, high)
-    middle = own_memory.shape[0] // 2
-    memory_a, wide = hold((own_memory[:middle], wide), (low, high))
-    far_memory_a = send_mem(memory_a)
-    wide = lax.all_gather(wide, ("batch", "mem"), axis=0, tiled=False)
-    wide = wide.reshape(batch_count, mem_count, *wide.shape[1:])
+    next_low, next_high = place_line(spot, line, (low, high))
+    low, high = gather_second(spot, low, high, (next_low, next_high))
     self_pack = gather_cores(low, high)
 
     distance_table, one_hot = bias_window(
@@ -1412,13 +1407,14 @@
             distance_table, head_width, key_count, span, after, cost,
         )
 
-    low, high = place_line(spot, line, (query_self,))
+    low, high = gather_first(spot, next_low, next_high, (query_self,))
+    memory_start, wide = hold((own_memory, wide), (low, high))
+    wide = lax.all_gather(wide, ("batch", "mem"), axis=0, tiled=False)
+    wide = wide.reshape(batch_count, mem_count, *wide.shape[1:])
+    far_memory = send_mem(memory_start)
     one = self_forward(halves[0], (low, high), LONG)
-    low, high = gather_first(spot, low, high, (one[0], far_memory_a))
-    two = self_forward(halves[1], (low, high), LONG)
+    two = self_forward(halves[1], (one[0], memory_start), LONG)
     low, high = gather_second(spot, low, high, (two[0],))
-    (memory_b,) = hold((own_memory[middle:],), (low, high))
-    far_memory = (far_memory_a, send_mem(memory_b))
     square_pack = gather_cores(low, high)
     attn_self, self_totals, tiles = zip(one, two)
     middle_one, normed_cross, query_cross = after_self(spot, own, attn_self, norm_gains, square_pack)
@@ -1440,12 +1436,12 @@
         first, decoder_lengths, memory_lengths, query_cross, key_memory, value_memory,
         grad_attn_cross, cross_totals, None, head_width, key_memory.shape[0], (0, pairs),
     )
-    memory_own, memory_far_a, memory_far_b, kv_keep, kv_send = memory_backward(
+    memory_own, memory_far, kv_keep, kv_send = memory_backward(
         spot, grad_key_memory, grad_value_memory, own_memory, far_memory, square_pack
     )
     grad_middle_one, grad_attn_self, gain_two, qo_keep, qo_send = after_cross(
         spot, (grad_query_cross,), middle_one, grad_middle_two, normed_cross, attn_self, attn_cross,
-        norm_gains, square_pack, (memory_far_a,),
+        norm_gains, square_pack, (memory_far,),
     )
 
     def self_backward(half, after):
@@ -1458,16 +1454,15 @@
     (kv_keep, kv_send), (qo_keep, qo_send) = scatter_step(
         ((kv_keep, send_batch(kv_send, 1)), (qo_keep, send_batch(qo_send, 1))), (one[0],), (2, 1)
     )
-    (memory_far_b,) = hold((memory_far_b,), (kv_keep, qo_keep))
-    memory_far = (send_mem(memory_far_a), send_mem(memory_far_b))
-    two = self_backward(1, (kv_keep, one[0], memory_far[0]))
+    memory_far = send_mem(memory_far)
+    two = self_backward(1, (kv_keep, one[0]))
     grad_query_self, grad_key_self, grad_value_self, diagonals = zip(one, two)
     rows_own, rows_far, gain_one = self_row_grads(
         spot, own, far, norm_gains, grad_query_self, grad_key_self, grad_value_self, self_pack, ()
     )
     (kv_keep, kv_send), (qo_keep, qo_send) = scatter_step(
         ((kv_keep, send_mem(kv_send)), (qo_keep, send_batch(qo_send, 2))),
-        (rows_own, memory_far[1]), (1, 1),
+        (rows_own, memory_far), (1, 1),
     )
     rows_far = send_mem(rows_far)
     bias_partial = bias_gradient(jnp.concatenate(diagonals, axis=0), one_hot)
@@ -1476,14 +1471,14 @@
     keep_a, send_a, keep_b, send_b = self_weight_grads(
         spot, grad_query_self, grad_key_self, grad_value_self, normed_self, z_count, (kv_keep, sums)
     )
-    sums = sum_small(sums, (2, 4, 6), (keep_a,))
+    line = scatter_to_line(
+        ((kv_keep, send_batch(kv_send, 2)), (qo_keep, send_mem(qo_send))), (keep_a,)
+    )
+    sums = sum_small(sums, (2, 4, 6), (line[0],))
     (keep_a, send_a), (keep_b, send_b) = scatter_step(
         ((keep_a, send_batch(send_a, 1)), (keep_b, send_batch(send_b, 1))), (sums,), (2, 1)
     )
-    line = scatter_to_line(
-        ((kv_keep, send_batch(kv_send, 2)), (qo_keep, send_mem(qo_send))), (keep_a,)
-    )
-    sums = sum_small(sums, (8, 16, 24), (line[0],))
+    sums = sum_small(sums, (8, 16, 24), (keep_a,))
     memory_gradient = add_rows(memory_own, memory_far, (sums,))
     (keep_a, send_a), (keep_b, send_b) = scatter_step(
         ((keep_a, send_mem(send_a)), (keep_b, send_batch(send_b, 2))), (memory_gradient,), (1, 1)

time: 459 us -> 437 us (0.952)
  waiting for transfers between devices: 103 us -> 85.6 us
    ppermute x28, waiting for transfers between devices: 53.6 us -> 27.4 us  [send_batch(): lax.ppermute(block, 'batch', [(i, i ^ distance) for i in range(count)])]
    ppermute x7, waiting for transfers between devices: 6.6 us -> 15.1 us  [sum_small(): parts.append(lax.ppermute(block, ('batch', 'mem'), pairs))]
    ppermute x14 -> x12, starting transfers between devices: 17.9 us -> 14.5 us  [send_mem(): return lax.ppermute(block, 'mem', [(0, 1), (1, 0)])]
    unnamed x140 -> x141, local copies, waits for them, and re-layouts: 20.6 us -> 18.2 us
    ppermute x14 -> x12, waiting for transfers between devices: 43.3 us -> 43.1 us  [send_mem(): return lax.ppermute(block, 'mem', [(0, 1), (1, 0)])]
  transfers between devices with their start and end apart: 51 -> 49, of which waited for: 21 -> 18; matrix products, arithmetic and copies ran while one was open for 2% -> 2% of each run, Pallas kernels for 49% -> 51%
where the time goes in v4:
time: 437 us; the launch traced here: 431 us
  Pallas kernels  256 us (59%)
  waiting for transfers between devices  85.6 us (20%)
  starting transfers between devices  48.4 us (11%)
  local copies, waits for them, and re-layouts  21.3 us (5%)
  between operations  14.8 us (3%)
    pallas_call x26, Pallas kernels, kernel_call(): pl.pallas_call(ignoring(body, len(args), len(after)), grid=grid, in_specs...  121 us
    pallas_call x3, Pallas kernels, attention_backward(): pl.pallas_call(ignoring(functools.partial(backward_kernel, causal, step,...  65.2 us
    ppermute x12, waiting for transfers between devices, send_mem(): return lax.ppermute(block, 'mem', [(0, 1), (1, 0)])  43.1 us
    pallas_call x3, Pallas kernels, attention_forward(): pl.pallas_call(ignoring(functools.partial(forward_kernel, causal, step, w...  40.3 us
    ppermute x28, starting transfers between devices, send_batch(): lax.ppermute(block, 'batch', [(i, i ^ distance) for i in range(count)])  27.7 us
    ppermute x28, waiting for transfers between devices, send_batch(): lax.ppermute(block, 'batch', [(i, i ^ distance) for i in range(count)])  27.4 us
    pallas_call x1, Pallas kernels, memory_backward(): pl.pallas_call(body, grid_spec=pltpu.PrefetchScalarGridSpec(num_scalar_pr...  19.5 us
    unnamed x141, local copies, waits for them, and re-layouts  18.2 us
  transfers between devices with their start and end apart: 49, of which 18 were waited for; matrix products, arithmetic and copies ran while one was open for 2% of the time, Pallas kernels for 51%

profile of v4, /device:TPU:0, one launch (start us, length us, event | category | flops | bytes accessed | tf_op | source)
XLA Modules:
  0.0 430.9 jit_solution(16551301726921975276)
XLA Ops:
  7.3 3.0 collective-permute-start
  10.3 2.6 collective-permute-start.2
  12.9 1.6 collective-permute-start.1
  15.3 5.1 %collective-permute-done.2.refs_3_ = bf16[3,48,384]{2,1,0:T(8,128)(2,1)S(1)} collective-permute-done((bf16[3,48,384]{2,1,0:T(8,128)(2,1)}, bf16[3,48,384]{2,1,0:T(8,128)(2,1)S(1)}, u32[]{:S(2)}, u32[]{:S(2)}) %collective-permute-start.2) | collective-permute-done | bytes 110624 | tf_op jit(solution)/shard_map/ppermute | solution.py:422
  22.4 1.9 place_line.2
  24.9 1.5 collective-permute-start.5
  26.4 6.4 %collective-permute-done.4.refs_2_ = bf16[2,3,48,384]{3,2,1,0:T(8,128)(2,1)S(1)} collective-permute-done((bf16[2,3,48,384]{3,2,1,0:T(8,128)(2,1)}, bf16[2,3,48,384]{3,2,1,0:T(8,128)(2,1)S(1)}, u32[]{:S(2)}, u32[]{:S(2)}) %collective-permute-start.4) | collective-permute-done | bytes 221216 | tf_op jit(solution)/shard_map/ppermute | solution.py:426
  34.4 2.2 place_pairs.4
  36.7 1.8 collective-permute-start.6
  38.4 1.5 collective-permute-start.7
  40.6 3.6 collective-permute-start.10
  45.0 5.2 %collective-permute-done.10.refs_4_ = bf16[5,48,384]{2,1,0:T(8,128)(2,1)S(1)} collective-permute-done((bf16[5,48,384]{2,1,0:T(8,128)(2,1)}, bf16[5,48,384]{2,1,0:T(8,128)(2,1)S(1)}, u32[]{:S(2)}, u32[]{:S(2)}) %collective-permute-start.10) | collective-permute-done | bytes 184352 | tf_op jit(solution)/shard_map/ppermute | solution.py:422
  50.2 8.5 %collective-permute-done.9.refs_3_ = bf16[5,48,384]{2,1,0:T(8,128)(2,1)S(1)} collective-permute-done((bf16[5,48,384]{2,1,0:T(8,128)(2,1)}, bf16[5,48,384]{2,1,0:T(8,128)(2,1)S(1)}, u32[]{:S(2)}, u32[]{:S(2)}) %collective-permute-start.9) | collective-permute-done | bytes 184352 | tf_op jit(solution)/shard_map/ppermute | solution.py:422
  60.0 2.2 place_line.3
  63.1 2.8 place_pairs.5
  70.0 8.1 %project_self_kernel.1 = (bf16[512,768]{1,0:T(8,128)(2,1)}, bf16[1024,768]{1,0:T(8,128)(2,1)}, bf16[1024,768]{1,0:T(8,128)(2,1)}, bf16[1024,768]{1,0:T(8,128)(2,1)}) custom-call(s32[4]{0:T(128)} %pad_add_fusion.refs_0_.place_ref, bf16[512,768]{1,0:T(8,128)(2,1)} %bitcast.46, bf16[512,768]{1,0:T(8,128)(2,1)} %copy-done.13, f32[3,768]{1,0:T(4,128)} %refs_4_.3, ...), custom_call_target="tpu_custom_call" | custom-call | flops 6000000000 | bytes 1000 | tf_op jit(solution)/shard_map/project_self_kernel/pallas_call | solution.py:461
  80.5 2.5 place_pairs.6
  87.7 9.2 %self_forward.2 = (bf16[512,384]{1,0:T(8,128)(2,1)}, f32[3,1,1,1024]{3,2,1,0:T(1,128)}, f32[3,4,256,512]{3,2,1,0:T(8,128)}) custom-call(s32[1]{0:T(128)} %bitcast.5.refs_0_, s32[1,4]{1,0:T(1,128)} %refs_2_.13, s32[1,4]{1,0:T(1,128)} %refs_2_.13, bf16[512,768]{1,0:T(8,128)(2,1)} %get-tuple-element.111.refs_5_.refs_3_, ...), custom_call_target="tpu_custom_call" | custom-call | flops 20000000000 | bytes 1000 | tf_op jit(solution)/shard_map/self_forward/pallas_call | solution.py:338
  96.8 9.0 %self_forward.3 = (bf16[512,384]{1,0:T(8,128)(2,1)}, f32[3,1,1,1024]{3,2,1,0:T(1,128)}, f32[3,4,256,512]{3,2,1,0:T(8,128)}) custom-call(s32[1]{0:T(128)} %bitcast.5.refs_0_, s32[1,4]{1,0:T(1,128)} %refs_2_.13, s32[1,4]{1,0:T(1,128)} %refs_2_.13, bf16[512,768]{1,0:T(8,128)(2,1)} %get-tuple-element.111.refs_5_.refs_3_, ...), custom_call_target="tpu_custom_call" | custom-call | flops 20000000000 | bytes 1000 | tf_op jit(solution)/shard_map/self_forward/pallas_call | solution.py:338
  108.0 3.7 place_pairs.7
  112.2 3.0 collective-permute-done.17.refs_6_.refs_10_.refs_1_.refs_5_.refs_14_
  115.2 2.1 collective-permute-done.18.refs_8_.refs_12_.refs_3_.refs_7_.refs_16_
  118.4 4.9 %after_self.1 = (f32[512,768]{1,0:T(8,128)}, bf16[512,768]{1,0:T(8,128)(2,1)}, bf16[512,768]{1,0:T(8,128)(2,1)}) custom-call(s32[4]{0:T(128)} %pad_add_fusion.refs_0_.place_ref, bf16[512,768]{1,0:T(8,128)(2,1)} %bitcast.47, f32[3,768]{1,0:T(4,128)} %refs_4_.3, bf16[512,384]{1,0:T(8,128)(2,1)} %get-tuple-element.116.refs_7_.refs_3_, ...), custom_call_target="tpu_custom_call" | custom-call | flops 100000 | bytes 1000 | tf_op jit(solution)/shard_map/after_self/pallas_call | solution.py:461
  123.3 28.9 %collective-permute-done.19.far_a.far_b = bf16[1024,768]{1,0:T(8,128)(2,1)} collective-permute-done((bf16[1024,768]{1,0:T(8,128)(2,1)}, bf16[1024,768]{1,0:T(8,128)(2,1)}, u32[]{:S(2)}, u32[]{:S(2)}) %collective-permute-start.19) | collective-permute-done | bytes 1572896 | tf_op jit(solution)/shard_map/ppermute | solution.py:426
  152.2 10.1 %project_memory_kernel.1 = (bf16[2048,768]{1,0:T(8,128)(2,1)}, bf16[2048,768]{1,0:T(8,128)(2,1)}) custom-call(s32[4]{0:T(128)} %pad_add_fusion.refs_0_.place_ref, bf16[1024,768]{1,0:T(8,128)(2,1)} %bitcast.41, bf16[1024,768]{1,0:T(8,128)(2,1)} %collective-permute-done.19.far_a.far_b, bf16[1024,768]{1,0:T(8,128)(2,1)} %collective-permute-done.19.far_a.far_b, ...), custom_call_target="tpu_custom_call" | custom-call | flops 6000000000 | bytes 1000 | tf_op jit(solution)/shard_map/project_memory_kernel/pallas_call | solution.py:854
  162.4 22.2 %cross_forward.1 = (bf16[512,768]{1,0:T(8,128)(2,1)}, f32[6,1,1,1024]{3,2,1,0:T(1,128)}) custom-call(s32[1]{0:T(128)} %bitcast.5.refs_0_, s32[1,4]{1,0:T(1,128)} %refs_2_.13, s32[1,4]{1,0:T(1,128)} %refs_2_.11, bf16[512,768]{1,0:T(8,128)(2,1)} %get-tuple-element.122.refs_3_, bf16[2048,768]{1,0:T(8,128)(2,1)} %get-tuple-element.123.refs_4_, ...), custom_call_target="tpu_custom_call" | custom-call | flops 20000000000 | bytes 1000 | tf_op jit(solution)/shard_map/cross_forward/pallas_call | solution.py:338
  184.5 27.7 %feed_forward_kernel.1 = (bf16[512,768]{1,0:T(8,128)(2,1)}, f32[512,768]{1,0:T(8,128)}, bf16[512,768]{1,0:T(8,128)(2,1)}, f32[1,768]{1,0:T(1,128)}, bf16[16,2,1152,128]{3,2,1,0:T(8,128)(2,1)}) custom-call(s32[4]{0:T(128)} %pad_add_fusion.refs_0_.place_ref, f32[512,768]{1,0:T(8,128)} %get-tuple-element.121.refs_1_, ...), custom_call_target="tpu_custom_call" | custom-call | flops 6000000000 | bytes 1000 | tf_op jit(solution)/shard_map/feed_forward_kernel/pallas_call | solution.py:461
  212.3 37.8 %cross_backward.1 = (bf16[512,768]{1,0:T(8,128)(2,1)}, bf16[2048,768]{1,0:T(8,128)(2,1)}, bf16[2048,768]{1,0:T(8,128)(2,1)}) custom-call(s32[1]{0:T(128)} %bitcast.5.refs_0_, s32[1,4]{1,0:T(1,128)} %refs_2_.13, s32[1,4]{1,0:T(1,128)} %refs_2_.11, bf16[512,768]{1,0:T(8,128)(2,1)} %get-tuple-element.122.refs_3_, bf16[2048,768]{1,0:T(8,128)(2,1)} %get-tuple-element.123.refs_4_, ...), custom_call_target="tpu_custom_call" | custom-call | flops 20000000000 | bytes 1000 | tf_op jit(solution)/shard_map/cross_backward/pallas_call | solution.py:390
  250.1 19.5 %memory_backward_kernel.1 = (f32[1024,768]{1,0:T(8,128)}, bf16[1024,768]{1,0:T(8,128)(2,1)}, bf16[4,2,2,288,128]{4,3,2,1,0:T(8,128)(2,1)}, bf16[4,2,2,288,128]{4,3,2,1,0:T(8,128)(2,1)}) custom-call(s32[4]{0:T(128)} %pad_add_fusion.refs_0_.place_ref, bf16[2048,768]{1,0:T(8,128)(2,1)} %get-tuple-element.133.dk_ref, ...), custom_call_target="tpu_custom_call" | custom-call | flops 6000000000 | bytes 1000 | tf_op jit(solution)/shard_map/memory_backward_kernel/pallas_call | solution.py:1087
  269.7 2.0 collective-permute-start.25
  271.7 10.2 %after_cross_kernel.1 = (f32[512,768]{1,0:T(8,128)}, bf16[512,768]{1,0:T(8,128)(2,1)}, f32[1,768]{1,0:T(1,128)}, bf16[4,2,2,432,128]{4,3,2,1,0:T(8,128)(2,1)}, bf16[4,2,2,432,128]{4,3,2,1,0:T(8,128)(2,1)}) custom-call(s32[4]{0:T(128)} %pad_add_fusion.refs_0_.place_ref, f32[512,768]{1,0:T(8,128)} %get-tuple-element.121.refs_1_, ...), custom_call_target="tpu_custom_call" | custom-call | flops 6000000000 | bytes 1000 | tf_op jit(solution)/shard_map/after_cross_kernel/pallas_call | solution.py:461
  282.1 13.6 %self_backward.2 = (bf16[512,384]{1,0:T(8,128)(2,1)}, bf16[1024,384]{1,0:T(8,128)(2,1)}, bf16[1024,384]{1,0:T(8,128)(2,1)}, f32[3,2,1280]{2,1,0:T(2,128)}) custom-call(s32[1]{0:T(128)} %bitcast.5.refs_0_, s32[1,4]{1,0:T(1,128)} %refs_2_.13, s32[1,4]{1,0:T(1,128)} %refs_2_.13, bf16[512,768]{1,0:T(8,128)(2,1)} %get-tuple-element.111.refs_5_.refs_3_, ...), custom_call_target="tpu_custom_call" | custom-call | flops 20000000000 | bytes 1000 | tf_op jit(solution)/shard_map/self_backward/pallas_call | solution.py:390
  296.9 4.8 %scatter_step.4 = (bf16[4,2,288,128]{3,2,1,0:T(8,128)(2,1)}, bf16[4,2,288,128]{3,2,1,0:T(8,128)(2,1)}, bf16[4,2,432,128]{3,2,1,0:T(8,128)(2,1)}, bf16[4,2,432,128]{3,2,1,0:T(8,128)(2,1)}) custom-call(bf16[4,2,2,288,128]{4,3,2,1,0:T(8,128)(2,1)} %get-tuple-element.143.refs_0_, bf16[4,2,2,288,128]{4,3,2,1,0:T(8,128)(2,1)} %collective-permute-done.20.refs_1_, ...), custom_call_target="tpu_custom_call" | custom-call | flops 100000 | bytes 1000 | tf_op jit(solution)/shard_map/scatter_step/pallas_call | solution.py:461
  303.3 13.8 %self_backward.3 = (bf16[512,384]{1,0:T(8,128)(2,1)}, bf16[1024,384]{1,0:T(8,128)(2,1)}, bf16[1024,384]{1,0:T(8,128)(2,1)}, f32[3,2,1280]{2,1,0:T(2,128)}) custom-call(s32[1]{0:T(128)} %bitcast.5.refs_0_, s32[1,4]{1,0:T(1,128)} %refs_2_.13, s32[1,4]{1,0:T(1,128)} %refs_2_.13, bf16[512,768]{1,0:T(8,128)(2,1)} %get-tuple-element.111.refs_5_.refs_3_, ...), custom_call_target="tpu_custom_call" | custom-call | flops 20000000000 | bytes 1000 | tf_op jit(solution)/shard_map/self_backward/pallas_call | solution.py:390
  317.1 8.1 %self_row_grads_kernel.1 = (f32[512,768]{1,0:T(8,128)}, bf16[512,768]{1,0:T(8,128)(2,1)}, f32[1,768]{1,0:T(1,128)}) custom-call(s32[4]{0:T(128)} %pad_add_fusion.refs_0_.place_ref, bf16[512,768]{1,0:T(8,128)(2,1)} %bitcast.48, bf16[512,768]{1,0:T(8,128)(2,1)} %copy-done.13, bf16[512,384]{1,0:T(8,128)(2,1)} %get-tuple-element.140.refs_4_.refs_10_.refs_3_.refs_1_, ...), custom_call_target="tpu_custom_call" | custom-call | flops 6000000000 | bytes 1000 | tf_op jit(solution)/shard_map/self_row_grads_kernel/pallas_call | solution.py:461
  327.3 5.4 %collective-permute-done.23.refs_1_ = bf16[4,2,288,128]{3,2,1,0:T(8,128)(2,1)S(1)} collective-permute-done((bf16[4,2,288,128]{3,2,1,0:T(8,128)(2,1)}, bf16[4,2,288,128]{3,2,1,0:T(8,128)(2,1)S(1)}, u32[]{:S(2)}, u32[]{:S(2)}) %collective-permute-start.23) | collective-permute-done | bytes 589856 | tf_op jit(solution)/shard_map/ppermute | solution.py:426
  333.8 3.9 scatter_step.5
  337.8 7.8 %self_weight_grads_kernel.1 = (bf16[4,2,2,240,128]{4,3,2,1,0:T(8,128)(2,1)}, bf16[4,2,2,240,128]{4,3,2,1,0:T(8,128)(2,1)}, bf16[4,2,2,192,128]{4,3,2,1,0:T(8,128)(2,1)}, bf16[4,2,2,192,128]{4,3,2,1,0:T(8,128)(2,1)}) custom-call(s32[4]{0:T(128)} %pad_add_fusion.refs_0_.place_ref, bf16[512,384]{1,0:T(8,128)(2,1)} %get-tuple-element.140.refs_4_.refs_10_.refs_3_.refs_1_, ...), custom_call_target="tpu_custom_call" | custom-call | flops 6000000000 | bytes 1000 | tf_op jit(solution)/shard_map/self_weight_grads_kernel/pallas_call | solution.py:461
  346.8 1.4 collective-permute-start.31
  348.2 8.7 %collective-permute-done.30.refs_3_ = f32[21,128]{1,0:T(8,128)S(1)} collective-permute-done((f32[21,128]{1,0:T(8,128)S(1)}, f32[21,128]{1,0:T(8,128)S(1)}, u32[]{:S(2)}, u32[]{:S(2)}) %collective-permute-start.30) | collective-permute-done | bytes 10784 | tf_op jit(solution)/shard_map/ppermute | solution.py:614
  357.0 1.4 collective-permute-start.22
  358.4 2.0 collective-permute-start.29
  361.2 2.2 scatter_to_line.2
  364.0 1.4 sum_small.3.refs_4_.refs_0_
  366.6 4.1 scatter_step.6
  371.4 1.3 collective-permute-start.34
  372.8 3.3 collective-permute-start.37
  376.1 2.2 collective-permute-done.37.refs_3_
  378.3 2.4 collective-permute-done.36.refs_2_
  380.7 1.4 collective-permute-done.35.refs_1_
  382.1 1.9 collective-permute-start.40
  384.0 1.4 sum_small.4.refs_2_.refs_0_
  385.3 4.5 %add_rows.1.refs_4_ = f32[1024,768]{1,0:T(8,128)} custom-call(f32[1024,768]{1,0:T(8,128)} %get-tuple-element.177.refs_0_, bf16[1024,768]{1,0:T(8,128)(2,1)} %copy-done.5, f32[21,128]{1,0:T(8,128)} %sum_small.4.refs_2_.refs_0_), custom_call_target="tpu_custom_call" | custom-call | flops 100000 | bytes 1000 | tf_op jit(solution)/shard_map/add_rows/pallas_call | solution.py:461
  389.8 2.0 collective-permute-start.41
  392.6 3.5 scatter_step.7
  396.1 1.4 collective-permute-start.43
  398.1 4.2 finish_rows_kernel.1.refs_4_
  402.3 1.6 collective-permute-done.42.refs_1_
  404.6 2.1 scatter_to_line.3
  406.7 2.5 collective-permute-start.45
  409.2 1.9 collective-permute-start.46
  412.5 2.0 scatter_end.3
  420.3 1.8 scatter_end.4
  422.1 1.8 scatter_end.5
  (231 shorter events, 43.7 us)
Async XLA Ops:
  7.2 60.7 %copy-start = (bf16[2,48,1024]{2,1,0:T(8,128)(2,1)S(1)}, bf16[2,48,1024]{2,1,0:T(8,128)(2,1)}, u32[]{:S(2)}) copy-start(bf16[2,48,1024]{2,1,0:T(8,128)(2,1)} %param.25) | copy-start | bytes 589828
  7.2 32.7 %copy-start.49 = (bf16[48,384]{1,0:T(8,128)(2,1)S(1)}, bf16[48,384]{1,0:T(8,128)(2,1)}, u32[]{:S(2)}) copy-start(bf16[48,384]{1,0:T(8,128)(2,1)} %param.24) | copy-start | bytes 110596
  7.2 32.7 %copy-start.39 = (bf16[3,48,384]{2,1,0:T(8,128)(2,1)S(1)}, bf16[3,48,384]{2,1,0:T(8,128)(2,1)}, u32[]{:S(2)}) copy-start(bf16[3,48,384]{2,1,0:T(8,128)(2,1)} %param.23) | copy-start | bytes 331780
  7.2 32.7 %copy-start.50 = (bf16[48,384]{1,0:T(8,128)(2,1)S(1)}, bf16[48,384]{1,0:T(8,128)(2,1)}, u32[]{:S(2)}) copy-start(bf16[48,384]{1,0:T(8,128)(2,1)} %param.22) | copy-start | bytes 110596
  7.2 177.3 %all-gather.3.cloned.1.call-start = ((), (), s32[]{:S(2)}) async-start(), calls=%async_computation.2 | async-start | bytes 9732096 | tf_op jit(solution)/shard_map/all_gather | solution.py:1412
  7.3 25.5 %collective-permute-start = (bf16[512,768]{1,0:T(8,128)(2,1)}, bf16[512,768]{1,0:T(8,128)(2,1)S(1)}, u32[]{:S(2)}, u32[]{:S(2)}) collective-permute-start(bf16[512,768]{1,0:T(8,128)(2,1)} %bitcast.45), channel_id=1, source_target_pairs={{0,1},{1,0},{2,3},{3,2},{4,5},{5,4},{6,7},{7,6},{8,9},{9,8},{10,11... | collective-permute-start | bytes 2359304 | tf_op jit(solution)/shard_map/ppermute | solution.py:426
  10.3 10.2 %collective-permute-start.2 = (bf16[3,48,384]{2,1,0:T(8,128)(2,1)}, bf16[3,48,384]{2,1,0:T(8,128)(2,1)S(1)}, u32[]{:S(2)}, u32[]{:S(2)}) collective-permute-start(bf16[3,48,384]{2,1,0:T(8,128)(2,1)} %refs_1_.7), channel_id=1, source_target_pairs={{0,16},{2,18},{4,20},{6,22},{8,24},{10,26},{12,28},{14,30},{16,0},... | collective-permute-start | bytes 331784 | tf_op jit(solution)/shard_map/ppermute | solution.py:422
  12.9 7.6 %collective-permute-start.1 = (bf16[3,48,384]{2,1,0:T(8,128)(2,1)}, bf16[3,48,384]{2,1,0:T(8,128)(2,1)S(1)}, u32[]{:S(2)}, u32[]{:S(2)}) collective-permute-start(bf16[3,48,384]{2,1,0:T(8,128)(2,1)} %refs_1_.7), channel_id=1, source_target_pairs={{0,8},{2,10},{4,12},{6,14},{8,0},{10,2},{12,4},{14,6},{16,24},{18,... | collective-permute-start | bytes 331784 | tf_op jit(solution)/shard_map/ppermute | solution.py:422
  14.4 7.3 %collective-permute-start.3 = (bf16[3,48,384]{2,1,0:T(8,128)(2,1)}, bf16[3,48,384]{2,1,0:T(8,128)(2,1)S(1)}, u32[]{:S(2)}, u32[]{:S(2)}) collective-permute-start(bf16[3,48,384]{2,1,0:T(8,128)(2,1)} %refs_1_.7), channel_id=1, source_target_pairs={{0,24},{2,26},{4,28},{6,30},{8,16},{10,18},{12,20},{14,22},{16,8},... | collective-permute-start | bytes 331784 | tf_op jit(solution)/shard_map/ppermute | solution.py:422
  24.3 8.4 %collective-permute-start.4 = (bf16[2,3,48,384]{3,2,1,0:T(8,128)(2,1)}, bf16[2,3,48,384]{3,2,1,0:T(8,128)(2,1)S(1)}, u32[]{:S(2)}, u32[]{:S(2)}) collective-permute-start(bf16[2,3,48,384]{3,2,1,0:T(8,128)(2,1)} %get-tuple-element.103.refs_1_), channel_id=1, source_target_pairs={{0,1},{1,0},{2,3},{3,2},{4,5},{5,4},{6,7},{7,6},{8,9},{9,8},{10,11... | collective-permute-start | bytes 663560 | tf_op jit(solution)/shard_map/ppermute | solution.py:426
  24.9 7.9 %collective-permute-start.5 = (bf16[2,3,48,384]{3,2,1,0:T(8,128)(2,1)}, bf16[2,3,48,384]{3,2,1,0:T(8,128)(2,1)S(1)}, u32[]{:S(2)}, u32[]{:S(2)}) collective-permute-start(bf16[2,3,48,384]{3,2,1,0:T(8,128)(2,1)} %get-tuple-element.104.refs_3_.refs_2_), channel_id=1, source_target_pairs={{0,4},{2,6},{4,0},{6,2},{8,12},{10,14},{12,8},{14,10},{16,20},{18,... | collective-permute-start | bytes 663560 | tf_op jit(solution)/shard_map/ppermute | solution.py:422
  36.7 25.6 %collective-permute-start.6 = (bf16[2,2,3,48,384]{4,3,2,1,0:T(8,128)(2,1)}, bf16[2,2,3,48,384]{4,3,2,1,0:T(8,128)(2,1)S(1)}, u32[]{:S(2)}, u32[]{:S(2)}) collective-permute-start(bf16[2,2,3,48,384]{4,3,2,1,0:T(8,128)(2,1)} %get-tuple-element.105.refs_5_.refs_1_), channel_id=1, source_target_pairs={{0,4},{2,6},{4,0},{6,2},{8,12},{10,14},{12,8},{14,10},{16,20},{18,... | collective-permute-start | bytes 1327112 | tf_op jit(solution)/shard_map/ppermute | solution.py:422
  38.4 23.8 %collective-permute-start.7 = (bf16[2,2,3,48,384]{4,3,2,1,0:T(8,128)(2,1)}, bf16[2,2,3,48,384]{4,3,2,1,0:T(8,128)(2,1)S(1)}, u32[]{:S(2)}, u32[]{:S(2)}) collective-permute-start(bf16[2,2,3,48,384]{4,3,2,1,0:T(8,128)(2,1)} %get-tuple-element.106.refs_6_.refs_3_), channel_id=1, source_target_pairs={{0,1},{1,0},{2,3},{3,2},{4,5},{5,4},{6,7},{7,6},{8,9},{9,8},{10,11... | collective-permute-start | bytes 1327112 | tf_op jit(solution)/shard_map/ppermute | solution.py:426
  40.6 9.6 %collective-permute-start.10 = (bf16[5,48,384]{2,1,0:T(8,128)(2,1)}, bf16[5,48,384]{2,1,0:T(8,128)(2,1)S(1)}, u32[]{:S(2)}, u32[]{:S(2)}) collective-permute-start(bf16[5,48,384]{2,1,0:T(8,128)(2,1)} %hold.2.refs_1_), channel_id=1, source_target_pairs={{0,24},{2,26},{4,28},{6,30},{8,16},{10,18},{12,20},{14,22},{16,8},... | collective-permute-start | bytes 552968 | tf_op jit(solution)/shard_map/ppermute | solution.py:422
  44.2 14.4 %collective-permute-start.9 = (bf16[5,48,384]{2,1,0:T(8,128)(2,1)}, bf16[5,48,384]{2,1,0:T(8,128)(2,1)S(1)}, u32[]{:S(2)}, u32[]{:S(2)}) collective-permute-start(bf16[5,48,384]{2,1,0:T(8,128)(2,1)} %hold.2.refs_1_), channel_id=1, source_target_pairs={{0,16},{2,18},{4,20},{6,22},{8,24},{10,26},{12,28},{14,30},{16,0},... | collective-permute-start | bytes 552968 | tf_op jit(solution)/shard_map/ppermute | solution.py:422
  44.2 14.4 %collective-permute-start.8 = (bf16[5,48,384]{2,1,0:T(8,128)(2,1)}, bf16[5,48,384]{2,1,0:T(8,128)(2,1)S(1)}, u32[]{:S(2)}, u32[]{:S(2)}) collective-permute-start(bf16[5,48,384]{2,1,0:T(8,128)(2,1)} %hold.2.refs_1_), channel_id=1, source_target_pairs={{0,8},{2,10},{4,12},{6,14},{8,0},{10,2},{12,4},{14,6},{16,24},{18,... | collective-permute-start | bytes 552968 | tf_op jit(solution)/shard_map/ppermute | solution.py:422
  50.2 8.5 %copy-start.30 = (bf16[5,48,384]{2,1,0:T(8,128)(2,1)}, bf16[5,48,384]{2,1,0:T(8,128)(2,1)S(1)}, u32[]{:S(2)}) copy-start(bf16[5,48,384]{2,1,0:T(8,128)(2,1)S(1)} %collective-permute-done.10.refs_4_) | copy-start | bytes 552964
  65.9 4.1 collective-permute-start.11
  65.9 4.1 collective-permute-start.12
  68.7 10.5 %collective-permute-start.13 = (bf16[2,5,48,384]{3,2,1,0:T(8,128)(2,1)S(1)}, bf16[2,5,48,384]{3,2,1,0:T(8,128)(2,1)S(1)}, u32[]{:S(2)}, u32[]{:S(2)}) collective-permute-start(bf16[2,5,48,384]{3,2,1,0:T(8,128)(2,1)S(1)} %copy-done.9), channel_id=1, source_target_pairs={{0,1},{1,0},{2,3},{3,2},{4,5},{5,4},{6,7},{7,6},{8,9},{9,8},{10,11... | collective-permute-start | bytes 1105928 | tf_op jit(solution)/shard_map/ppermute | solution.py:426
  69.5 10.2 %collective-permute-start.14 = (bf16[2,5,48,384]{3,2,1,0:T(8,128)(2,1)S(1)}, bf16[2,5,48,384]{3,2,1,0:T(8,128)(2,1)S(1)}, u32[]{:S(2)}, u32[]{:S(2)}) collective-permute-start(bf16[2,5,48,384]{3,2,1,0:T(8,128)(2,1)S(1)} %copy-done.10), channel_id=1, source_target_pairs={{0,4},{2,6},{4,0},{6,2},{8,12},{10,14},{12,8},{14,10},{16,20},{18,... | collective-permute-start | bytes 1105928 | tf_op jit(solution)/shard_map/ppermute | solution.py:422
  83.1 339.0 %reduce-scatter.2.cloned.1.call-start = ((), (), s32[]{:S(2)}) async-start(), calls=%async_computation.1 | async-start | bytes 9732096 | tf_op jit(solution)/shard_map/reduce_scatter | solution.py:1431
  84.0 12.9 %copy-start.36 = (pred[1024,32]{1,0:T(32,128)(4,1)}, pred[1024,32]{1,0:T(32,128)(4,1)S(1)}, u32[]{:S(2)}) copy-start(pred[1024,32]{1,0:T(32,128)(4,1)S(1)} %iota_compare_fusion) | copy-start | bytes 98308
  85.1 20.7 %collective-permute-start.15 = (bf16[2,2,5,48,384]{4,3,2,1,0:T(8,128)(2,1)S(1)}, bf16[2,2,5,48,384]{4,3,2,1,0:T(8,128)(2,1)S(1)}, u32[]{:S(2)}, u32[]{:S(2)}) collective-permute-start(bf16[2,2,5,48,384]{4,3,2,1,0:T(8,128)(2,1)S(1)} %copy-done.6), channel_id=1, source_target_pairs={{0,4},{2,6},{4,0},{6,2},{8,12},{10,14},{12,8},{14,10},{16,20},{18,... | collective-permute-start | bytes 2211848 | tf_op jit(solution)/shard_map/ppermute | solution.py:422
  85.6 21.5 %collective-permute-start.16 = (bf16[2,2,5,48,384]{4,3,2,1,0:T(8,128)(2,1)S(1)}, bf16[2,2,5,48,384]{4,3,2,1,0:T(8,128)(2,1)S(1)}, u32[]{:S(2)}, u32[]{:S(2)}) collective-permute-start(bf16[2,2,5,48,384]{4,3,2,1,0:T(8,128)(2,1)S(1)} %copy-done.7), channel_id=1, source_target_pairs={{0,1},{1,0},{2,3},{3,2},{4,5},{5,4},{6,7},{7,6},{8,9},{9,8},{10,11... | collective-permute-start | bytes 2211848 | tf_op jit(solution)/shard_map/ppermute | solution.py:426
  86.8 65.4 %collective-permute-start.19 = (bf16[1024,768]{1,0:T(8,128)(2,1)}, bf16[1024,768]{1,0:T(8,128)(2,1)}, u32[]{:S(2)}, u32[]{:S(2)}) collective-permute-start(bf16[1024,768]{1,0:T(8,128)(2,1)} %get-tuple-element.117.refs_8_), channel_id=1, source_target_pairs={{0,1},{1,0},{2,3},{3,2},{4,5},{5,4},{6,7},{7,6},{8,9},{9,8},{10,11... | collective-permute-start | bytes 4718600 | tf_op jit(solution)/shard_map/ppermute | solution.py:426
  111.7 3.5 collective-permute-start.17
  111.7 5.6 %collective-permute-start.18 = (bf16[2,2,2,5,48,384]{5,4,3,2,1,0:T(8,128)(2,1)}, bf16[2,2,2,5,48,384]{5,4,3,2,1,0:T(8,128)(2,1)S(1)}, u32[]{:S(2)}, u32[]{:S(2)}) collective-permute-start(bf16[2,2,2,5,48,384]{5,4,3,2,1,0:T(8,128)(2,1)} %get-tuple-element.120.refs_7_.refs_11_.refs_2_.refs_6_.refs_15_), channel_id=1, source_target_pairs={{0,2},{2,0},{4,6},{6,4},{8,10},{10,8},{12,14},{14,12},{16,18},{18,... | collective-permute-start | bytes 4423688 | tf_op jit(solution)/shard_map/ppermute | solution.py:422
  269.6 26.1 %collective-permute-start.20 = (bf16[4,2,2,288,128]{4,3,2,1,0:T(8,128)(2,1)}, bf16[4,2,2,288,128]{4,3,2,1,0:T(8,128)(2,1)}, u32[]{:S(2)}, u32[]{:S(2)}) collective-permute-start(bf16[4,2,2,288,128]{4,3,2,1,0:T(8,128)(2,1)} %get-tuple-element.144), channel_id=1, source_target_pairs={{0,2},{2,0},{4,6},{6,4},{8,10},{10,8},{12,14},{14,12},{16,18},{18,... | collective-permute-start | bytes 3538952 | tf_op jit(solution)/shard_map/ppermute | solution.py:422
  269.7 57.7 %collective-permute-start.25 = (bf16[1024,768]{1,0:T(8,128)(2,1)}, bf16[1024,768]{1,0:T(8,128)(2,1)S(1)}, u32[]{:S(2)}, u32[]{:S(2)}) collective-permute-start(bf16[1024,768]{1,0:T(8,128)(2,1)} %get-tuple-element.135.refs_17_), channel_id=1, source_target_pairs={{0,1},{1,0},{2,3},{3,2},{4,5},{5,4},{6,7},{7,6},{8,9},{9,8},{10,11... | collective-permute-start | bytes 4718600 | tf_op jit(solution)/shard_map/ppermute | solution.py:426
  281.9 13.8 %collective-permute-start.21 = (bf16[4,2,2,432,128]{4,3,2,1,0:T(8,128)(2,1)}, bf16[4,2,2,432,128]{4,3,2,1,0:T(8,128)(2,1)S(1)}, u32[]{:S(2)}, u32[]{:S(2)}) collective-permute-start(bf16[4,2,2,432,128]{4,3,2,1,0:T(8,128)(2,1)} %get-tuple-element.145), channel_id=1, source_target_pairs={{0,2},{2,0},{4,6},{6,4},{8,10},{10,8},{12,14},{14,12},{16,18},{18,... | collective-permute-start | bytes 5308424 | tf_op jit(solution)/shard_map/ppermute | solution.py:422
  301.7 31.0 %collective-permute-start.23 = (bf16[4,2,288,128]{3,2,1,0:T(8,128)(2,1)}, bf16[4,2,288,128]{3,2,1,0:T(8,128)(2,1)S(1)}, u32[]{:S(2)}, u32[]{:S(2)}) collective-permute-start(bf16[4,2,288,128]{3,2,1,0:T(8,128)(2,1)} %get-tuple-element.156), channel_id=1, source_target_pairs={{0,1},{1,0},{2,3},{3,2},{4,5},{5,4},{6,7},{7,6},{8,9},{9,8},{10,11... | collective-permute-start | bytes 1769480 | tf_op jit(solution)/shard_map/ppermute | solution.py:426
  302.1 30.7 %collective-permute-start.24 = (bf16[4,2,432,128]{3,2,1,0:T(8,128)(2,1)}, bf16[4,2,432,128]{3,2,1,0:T(8,128)(2,1)S(1)}, u32[]{:S(2)}, u32[]{:S(2)}) collective-permute-start(bf16[4,2,432,128]{3,2,1,0:T(8,128)(2,1)} %get-tuple-element.158), channel_id=1, source_target_pairs={{0,4},{2,6},{4,0},{6,2},{8,12},{10,14},{12,8},{14,10},{16,20},{18,... | collective-permute-start | bytes 2654216 | tf_op jit(solution)/shard_map/ppermute | solution.py:422
  317.1 8.9 %copy-start.51 = (f32[3,2,1280]{2,1,0:T(2,128)S(1)}, f32[3,2,1280]{2,1,0:T(2,128)}, u32[]{:S(2)}) copy-start(f32[3,2,1280]{2,1,0:T(2,128)} %get-tuple-element.163) | copy-start | bytes 92164
  317.1 8.9 %copy-start.52 = (f32[3,2,1280]{2,1,0:T(2,128)S(1)}, f32[3,2,1280]{2,1,0:T(2,128)}, u32[]{:S(2)}) copy-start(f32[3,2,1280]{2,1,0:T(2,128)} %get-tuple-element.164) | copy-start | bytes 92164
  317.1 9.0 %copy-start.37 = (pred[1024,32]{1,0:T(32,128)(4,1)S(1)}, pred[1024,32]{1,0:T(32,128)(4,1)}, u32[]{:S(2)}) copy-start(pred[1024,32]{1,0:T(32,128)(4,1)} %copy-done.36) | copy-start | bytes 98308
  337.8 10.5 %copy-start.48 = (f32[21,128]{1,0:T(8,128)S(1)}, f32[21,128]{1,0:T(8,128)}, u32[]{:S(2)}) copy-start(f32[21,128]{1,0:T(8,128)} %maximum_bitcast_fusion.refs_9_.refs_0_) | copy-start | bytes 32260
  337.8 19.2 %copy-start.63 = (bf16[512,768]{1,0:T(8,128)(2,1)S(1)}, bf16[512,768]{1,0:T(8,128)(2,1)}, u32[]{:S(2)}) copy-start(bf16[512,768]{1,0:T(8,128)(2,1)} %get-tuple-element.153) | copy-start | bytes 2359300
  345.6 19.8 %collective-permute-start.26 = (bf16[4,2,2,240,128]{4,3,2,1,0:T(8,128)(2,1)}, bf16[4,2,2,240,128]{4,3,2,1,0:T(8,128)(2,1)S(1)}, u32[]{:S(2)}, u32[]{:S(2)}) collective-permute-start(bf16[4,2,2,240,128]{4,3,2,1,0:T(8,128)(2,1)} %get-tuple-element.166), channel_id=1, source_target_pairs={{0,2},{2,0},{4,6},{6,4},{8,10},{10,8},{12,14},{14,12},{16,18},{18,... | collective-permute-start | bytes 2949128 | tf_op jit(solution)/shard_map/ppermute | solution.py:422
  345.6 19.8 %collective-permute-start.27 = (bf16[4,2,2,192,128]{4,3,2,1,0:T(8,128)(2,1)}, bf16[4,2,2,192,128]{4,3,2,1,0:T(8,128)(2,1)S(1)}, u32[]{:S(2)}, u32[]{:S(2)}) collective-permute-start(bf16[4,2,2,192,128]{4,3,2,1,0:T(8,128)(2,1)} %get-tuple-element.168), channel_id=1, source_target_pairs={{0,2},{2,0},{4,6},{6,4},{8,10},{10,8},{12,14},{14,12},{16,18},{18,... | collective-permute-start | bytes 2359304 | tf_op jit(solution)/shard_map/ppermute | solution.py:422
  346.1 14.3 %collective-permute-start.32 = (bf16[4,432,128]{2,1,0:T(8,128)(2,1)S(1)}, bf16[4,432,128]{2,1,0:T(8,128)(2,1)S(1)}, u32[]{:S(2)}, u32[]{:S(2)}) collective-permute-start(bf16[4,432,128]{2,1,0:T(8,128)(2,1)S(1)} %copy-done.64), channel_id=1, source_target_pairs={{0,1},{1,0},{2,3},{3,2},{4,5},{5,4},{6,7},{7,6},{8,9},{9,8},{10,11... | collective-permute-start | bytes 1327112 | tf_op jit(solution)/shard_map/ppermute | solution.py:426
  346.8 11.6 %collective-permute-start.31 = (bf16[4,288,128]{2,1,0:T(8,128)(2,1)}, bf16[4,288,128]{2,1,0:T(8,128)(2,1)S(1)}, u32[]{:S(2)}, u32[]{:S(2)}) collective-permute-start(bf16[4,288,128]{2,1,0:T(8,128)(2,1)} %get-tuple-element.169), channel_id=1, source_target_pairs={{0,4},{2,6},{4,0},{6,2},{8,12},{10,14},{12,8},{14,10},{16,20},{18,... | collective-permute-start | bytes 884744 | tf_op jit(solution)/shard_map/ppermute | solution.py:422
  348.2 8.7 %collective-permute-start.30 = (f32[21,128]{1,0:T(8,128)S(1)}, f32[21,128]{1,0:T(8,128)S(1)}, u32[]{:S(2)}, u32[]{:S(2)}) collective-permute-start(f32[21,128]{1,0:T(8,128)S(1)} %copy-done.48), channel_id=1, source_target_pairs={{0,6},{1,7},{2,4},{3,5},{4,2},{5,3},{6,0},{7,1},{8,14},{9,15},{10,... | collective-permute-start | bytes 32264 | tf_op jit(solution)/shard_map/ppermute | solution.py:614
  357.0 40.5 %collective-permute-start.22 = (bf16[512,768]{1,0:T(8,128)(2,1)S(1)}, bf16[512,768]{1,0:T(8,128)(2,1)}, u32[]{:S(2)}, u32[]{:S(2)}) collective-permute-start(bf16[512,768]{1,0:T(8,128)(2,1)S(1)} %copy-done.63), channel_id=1, source_target_pairs={{0,1},{1,0},{2,3},{3,2},{4,5},{5,4},{6,7},{7,6},{8,9},{9,8},{10,11... | collective-permute-start | bytes 2359304 | tf_op jit(solution)/shard_map/ppermute | solution.py:426
  358.4 5.0 %collective-permute-start.29 = (f32[21,128]{1,0:T(8,128)S(1)}, f32[21,128]{1,0:T(8,128)S(1)}, u32[]{:S(2)}, u32[]{:S(2)}) collective-permute-start(f32[21,128]{1,0:T(8,128)S(1)} %copy-done.48), channel_id=1, source_target_pairs={{0,4},{1,5},{2,6},{3,7},{4,0},{5,1},{6,2},{7,3},{8,12},{9,13},{10,... | collective-permute-start | bytes 32264 | tf_op jit(solution)/shard_map/ppermute | solution.py:614
  360.3 3.1 collective-permute-start.28
  366.6 14.1 %copy-start.67 = (bf16[720,128]{1,0:T(8,128)(2,1)S(1)}, bf16[720,128]{1,0:T(8,128)(2,1)}, u32[]{:S(2)}) copy-start(bf16[720,128]{1,0:T(8,128)(2,1)} %get-tuple-element.179) | copy-start | bytes 552964
  366.6 15.5 %copy-start.66 = (bf16[720,128]{1,0:T(8,128)(2,1)S(1)}, bf16[720,128]{1,0:T(8,128)(2,1)}, u32[]{:S(2)}) copy-start(bf16[720,128]{1,0:T(8,128)(2,1)} %get-tuple-element.180) | copy-start | bytes 552964
  370.7 21.1 %collective-permute-start.33 = (bf16[4,2,240,128]{3,2,1,0:T(8,128)(2,1)}, bf16[4,2,240,128]{3,2,1,0:T(8,128)(2,1)S(1)}, u32[]{:S(2)}, u32[]{:S(2)}) collective-permute-start(bf16[4,2,240,128]{3,2,1,0:T(8,128)(2,1)} %get-tuple-element.174), channel_id=1, source_target_pairs={{0,1},{1,0},{2,3},{3,2},{4,5},{5,4},{6,7},{7,6},{8,9},{9,8},{10,11... | collective-permute-start | bytes 1474568 | tf_op jit(solution)/shard_map/ppermute | solution.py:426
  371.4 18.4 %collective-permute-start.34 = (bf16[4,2,192,128]{3,2,1,0:T(8,128)(2,1)}, bf16[4,2,192,128]{3,2,1,0:T(8,128)(2,1)S(1)}, u32[]{:S(2)}, u32[]{:S(2)}) collective-permute-start(bf16[4,2,192,128]{3,2,1,0:T(8,128)(2,1)} %get-tuple-element.176), channel_id=1, source_target_pairs={{0,4},{2,6},{4,0},{6,2},{8,12},{10,14},{12,8},{14,10},{16,20},{18,... | collective-permute-start | bytes 1179656 | tf_op jit(solution)/shard_map/ppermute | solution.py:422
  372.8 5.5 %collective-permute-start.37 = (f32[21,128]{1,0:T(8,128)S(1)}, f32[21,128]{1,0:T(8,128)S(1)}, u32[]{:S(2)}, u32[]{:S(2)}) collective-permute-start(f32[21,128]{1,0:T(8,128)S(1)} %copy-done.46), channel_id=1, source_target_pairs={{0,24},{1,25},{2,26},{3,27},{4,28},{5,29},{6,30},{7,31},{8,16},{9,... | collective-permute-start | bytes 32264 | tf_op jit(solution)/shard_map/ppermute | solution.py:614
  376.1 4.6 %collective-permute-start.36 = (f32[21,128]{1,0:T(8,128)S(1)}, f32[21,128]{1,0:T(8,128)S(1)}, u32[]{:S(2)}, u32[]{:S(2)}) collective-permute-start(f32[21,128]{1,0:T(8,128)S(1)} %copy-done.46), channel_id=1, source_target_pairs={{0,16},{1,17},{2,18},{3,19},{4,20},{5,21},{6,22},{7,23},{8,24},{9,... | collective-permute-start | bytes 32264 | tf_op jit(solution)/shard_map/ppermute | solution.py:614
  378.3 3.8 collective-permute-start.35
  380.7 28.5 %collective-permute-start.39 = (bf16[720,128]{1,0:T(8,128)(2,1)S(1)}, bf16[720,128]{1,0:T(8,128)(2,1)S(1)}, u32[]{:S(2)}, u32[]{:S(2)}) collective-permute-start(bf16[720,128]{1,0:T(8,128)(2,1)S(1)} %copy-done.67), channel_id=1, source_target_pairs={{0,8},{2,10},{4,12},{6,14},{8,0},{10,2},{12,4},{14,6},{16,24},{18,... | collective-permute-start | bytes 552968 | tf_op jit(solution)/shard_map/ppermute | solution.py:422
  382.1 29.0 %collective-permute-start.40 = (bf16[720,128]{1,0:T(8,128)(2,1)S(1)}, bf16[720,128]{1,0:T(8,128)(2,1)S(1)}, u32[]{:S(2)}, u32[]{:S(2)}) collective-permute-start(bf16[720,128]{1,0:T(8,128)(2,1)S(1)} %copy-done.66), channel_id=1, source_target_pairs={{0,16},{2,18},{4,20},{6,22},{8,24},{10,26},{12,28},{14,30},{16,0},... | collective-permute-start | bytes 552968 | tf_op jit(solution)/shard_map/ppermute | solution.py:422
  389.8 22.0 %collective-permute-start.41 = (bf16[720,128]{1,0:T(8,128)(2,1)S(1)}, bf16[720,128]{1,0:T(8,128)(2,1)S(1)}, u32[]{:S(2)}, u32[]{:S(2)}) collective-permute-start(bf16[720,128]{1,0:T(8,128)(2,1)S(1)} %copy-done.65), channel_id=1, source_target_pairs={{0,24},{2,26},{4,28},{6,30},{8,16},{10,18},{12,20},{14,22},{16,8},... | collective-permute-start | bytes 552968 | tf_op jit(solution)/shard_map/ppermute | solution.py:422
  396.1 6.2 %collective-permute-start.43 = (bf16[4,192,128]{2,1,0:T(8,128)(2,1)}, bf16[4,192,128]{2,1,0:T(8,128)(2,1)S(1)}, u32[]{:S(2)}, u32[]{:S(2)}) collective-permute-start(bf16[4,192,128]{2,1,0:T(8,128)(2,1)} %get-tuple-element.184), channel_id=1, source_target_pairs={{0,1},{1,0},{2,3},{3,2},{4,5},{5,4},{6,7},{7,6},{8,9},{9,8},{10,11... | collective-permute-start | bytes 589832 | tf_op jit(solution)/shard_map/ppermute | solution.py:426
  397.5 6.4 %collective-permute-start.42 = (bf16[4,240,128]{2,1,0:T(8,128)(2,1)}, bf16[4,240,128]{2,1,0:T(8,128)(2,1)S(1)}, u32[]{:S(2)}, u32[]{:S(2)}) collective-permute-start(bf16[4,240,128]{2,1,0:T(8,128)(2,1)} %get-tuple-element.182), channel_id=1, source_target_pairs={{0,4},{2,6},{4,0},{6,2},{8,12},{10,14},{12,8},{14,10},{16,20},{18,... | collective-permute-start | bytes 737288 | tf_op jit(solution)/shard_map/ppermute | solution.py:422
  402.3 8.8 %copy-start.38 = (f32[21,128]{1,0:T(8,128)S(1)}, f32[21,128]{1,0:T(8,128)}, u32[]{:S(2)}) copy-start(f32[21,128]{1,0:T(8,128)} %sum_small.4.refs_2_.refs_0_) | copy-start | bytes 32260
  404.6 19.3 %copy-start.1 = (bf16[2,48,1024]{2,1,0:T(8,128)(2,1)S(1)}, bf16[2,48,1024]{2,1,0:T(8,128)(2,1)}, u32[]{:S(2)}) copy-start(bf16[2,48,1024]{2,1,0:T(8,128)(2,1)} %param.25) | copy-start | bytes 589828
  406.7 12.9 %collective-permute-start.44 = (bf16[432,128]{1,0:T(8,128)(2,1)}, bf16[432,128]{1,0:T(8,128)(2,1)S(1)}, u32[]{:S(2)}, u32[]{:S(2)}) collective-permute-start(bf16[432,128]{1,0:T(8,128)(2,1)} %get-tuple-element.187), channel_id=1, source_target_pairs={{0,8},{2,10},{4,12},{6,14},{8,0},{10,2},{12,4},{14,6},{16,24},{18,... | collective-permute-start | bytes 331784 | tf_op jit(solution)/shard_map/ppermute | solution.py:422
  406.7 12.8 %collective-permute-start.45 = (bf16[432,128]{1,0:T(8,128)(2,1)}, bf16[432,128]{1,0:T(8,128)(2,1)S(1)}, u32[]{:S(2)}, u32[]{:S(2)}) collective-permute-start(bf16[432,128]{1,0:T(8,128)(2,1)} %get-tuple-element.188), channel_id=1, source_target_pairs={{0,16},{2,18},{4,20},{6,22},{8,24},{10,26},{12,28},{14,30},{16,0},... | collective-permute-start | bytes 331784 | tf_op jit(solution)/shard_map/ppermute | solution.py:422
  409.2 10.4 %collective-permute-start.46 = (bf16[432,128]{1,0:T(8,128)(2,1)}, bf16[432,128]{1,0:T(8,128)(2,1)S(1)}, u32[]{:S(2)}, u32[]{:S(2)}) collective-permute-start(bf16[432,128]{1,0:T(8,128)(2,1)} %get-tuple-element.189), channel_id=1, source_target_pairs={{0,24},{2,26},{4,28},{6,30},{8,16},{10,18},{12,20},{14,22},{16,8},... | collective-permute-start | bytes 331784 | tf_op jit(solution)/shard_map/ppermute | solution.py:422
  411.1 3.8 collective-permute-start.38
  (54 other events, 114.2 us)
Sparse Core Ops, SparseCore 0:
  83.2 92.2 all-gather.2
  212.4 151.8 reduce-scatter.1

commit v5 on v4

--- a/solution.py
+++ b/solution.py
@@ -823,19 +823,10 @@
     )
 
 
-def halves_of(block):
-    return [pl.BlockSpec(block, lambda *_: (0, 0)), pl.BlockSpec(block, lambda *_: (1, 0))]
-
-
-def three_way(step, own_ref, far_a, far_b):
-    return jnp.where(step < 2, own_ref[...], jnp.where(step == 2, far_a[...], far_b[...]))
-
-
 def project_memory(place, own, far, pack):
     rows, width = own.shape
-    step = rows // 2
-
-    def body(place_ref, own_ref, far_a, far_b, *refs):
+
+    def body(place_ref, own_ref, far_ref, *refs):
         k_ref, v_ref, key_weight, value_weight = refs[8:]
 
         @pl.when(pl.program_id(0) == 0)
@@ -843,39 +834,39 @@
             key_weight[...] = matrix_of(place_ref, refs[:4])
             value_weight[...] = matrix_of(place_ref, refs[4:8])
 
-        source = three_way(pl.program_id(0), own_ref, far_a, far_b)
+        source = jnp.where(pl.program_id(0) == 0, own_ref[...], far_ref[...])
         k_ref[...] = mm(source, key_weight[...]).astype(BF16)
         v_ref[...] = mm(source, value_weight[...]).astype(BF16)
 
     def result(i, place_ref):
-        return ((place_ref[3] ^ (i // 2)) * 2 + i % 2, 0)
+        return (place_ref[3] ^ i, 0)
 
     shape = jax.ShapeDtypeStruct((2 * rows, width), BF16)
     return pl.pallas_call(
         body,
         grid_spec=pltpu.PrefetchScalarGridSpec(
             num_scalar_prefetch=1,
-            grid=(4,),
+            grid=(2,),
             in_specs=[
-                pl.BlockSpec((step, width), lambda i, _: (jnp.minimum(i, 1), 0)),
-                *halves_of((step, width)),
+                whole_spec((rows, width)),
+                whole_spec((rows, width)),
             ]
             + weight_specs(pack, 1) + weight_specs(pack, 2),
-            out_specs=[pl.BlockSpec((step, width), result)] * 2,
+            out_specs=[pl.BlockSpec((rows, width), result)] * 2,
             scratch_shapes=[pltpu.VMEM((width, width), BF16)] * 2,
         ),
         out_shape=[shape, shape],
         compiler_params=pltpu.CompilerParams(vmem_limit_bytes=60 << 20),
         cost_estimate=MEDIUM,
         name="project_memory_kernel",
-    )(place, own, far, far, *pack, *pack)
+    )(place, own, far, *pack, *pack)
 
 
 def feed_forward(place, middle_one, attn, cotangent, gains, pack, wide, half):
     rows, width = cotangent.shape
     batch_count = wide.shape[0]
     slab = width // batch_count
-    chunk = half // 2
+    chunk = half
     across = chunk // 128
     down_rows = half * 2 // batch_count
     down_across = width // 256
@@ -932,7 +923,7 @@
         grad_up = (grad_act * gelu).astype(BF16)
         grad_normed[...] += mm_t(grad_gate, gate_weight) + mm_t(grad_up, up_weight)
         down_grad = t_mm(act, cot).astype(BF16)
-        gate_rows = 2 * across * slab
+        gate_rows = across * slab
         for block in range(chunk // down_rows):
             for x in range(2):
                 for index in range(down_across):
@@ -944,10 +935,8 @@
         for which, grad in enumerate((grad_gate, grad_up)):
             whole = mm(normed_t[...], grad).astype(BF16).reshape(batch_count, slab, chunk)
             for index in range(across):
-                start_row = pl.multiple_of(
-                    which * gate_rows + (step % 2) * across * slab + index * slab, slab
-                )
-                wide_grad[:, step // 2, pl.ds(start_row, slab), :] = whole[
+                start_row = which * gate_rows + index * slab
+                wide_grad[:, step, pl.ds(start_row, slab), :] = whole[
                     :, :, index * 128 : (index + 1) * 128
                 ]
 
@@ -963,13 +952,13 @@
 
     row_shape = (rows, width)
     wide_spec = lambda which: pl.BlockSpec(
-        (batch_count, 1, across * slab, 128), lambda i: (0, i // 2, 2 * which + i % 2, 0)
+        (batch_count, 1, across * slab, 128), lambda i: (0, i, which, 0)
     )
     down_spec = pl.BlockSpec(
-        (chunk // down_rows, 2, down_units, 128), lambda i: (i, 0, 4 * across * slab // down_units, 0)
+        (chunk // down_rows, 2, down_units, 128), lambda i: (i, 0, 2 * across * slab // down_units, 0)
     )
     return kernel_call(
-        body, "feed_forward_kernel", (4,),
+        body, "feed_forward_kernel", (2,),
         [smem(), *[whole_spec(row_shape)] * 3, whole_spec(gains.shape)] + weight_specs(pack, 4) + [wide_spec(0), wide_spec(1), down_spec],
         [whole_spec(row_shape)] * 3 + [whole_spec((1, width)), whole_spec(wide.shape)],
         [
@@ -1040,18 +1029,17 @@
 
 def memory_backward(place, grad_key, grad_value, own, far, pack):
     rows, width = own.shape
-    step = rows // 2
     z_count = pack[0].shape[2] * 2
     slab = pack[0].shape[4]
 
     def body(
-        place_ref, dk_ref, dv_ref, own_ref, far_a, far_b, *refs,
+        place_ref, dk_ref, dv_ref, own_ref, far_ref, *refs,
     ):
         k_refs, v_refs = refs[:4], refs[4:8]
         grad_own_ref, grad_far_ref, keep_ref, send_ref = refs[8:12]
         key_total, value_total, key_weight, value_weight = refs[12:]
         i = pl.program_id(0)
-        source = three_way(i ^ 2, own_ref, far_a, far_b)
+        source = jnp.where(i == 0, far_ref[...], own_ref[...])
         source_t = source.T
 
         @pl.when(i == 0)
@@ -1066,38 +1054,38 @@
         value_total[...] += mm(source_t, grad_value)
         grads = mm_t(grad_key, key_weight[...]) + mm_t(grad_value, value_weight[...])
 
-        @pl.when(i < 2)
+        @pl.when(i == 0)
         def there():
             grad_far_ref[...] = grads.astype(BF16)
 
-        @pl.when(i >= 2)
+        @pl.when(i == 1)
         def here():
             grad_own_ref[...] = grads
 
-        @pl.when(i == 3)
+        @pl.when(i == 1)
         def finish():
             for index, total in enumerate((key_total, value_total)):
                 targets = [(keep_ref, send_ref, (3 * index + part) * slab) for part in range(3)]
                 store_square(place_ref, targets, total[...], z_count)
 
     def block(i, place_ref):
-        return ((place_ref[3] ^ (1 - i // 2)) * 2 + i % 2, 0)
+        return (place_ref[3] ^ (1 - i), 0)
 
     pieces = piece_shape(z_count, 6 * slab)
     return pl.pallas_call(
         body,
         grid_spec=pltpu.PrefetchScalarGridSpec(
             num_scalar_prefetch=1,
-            grid=(4,),
+            grid=(2,),
             in_specs=[
-                *[pl.BlockSpec((step, width), block)] * 2,
-                pl.BlockSpec((step, width), lambda i, _: (jnp.maximum(i - 2, 0), 0)),
-                *halves_of((step, width)),
+                *[pl.BlockSpec((rows, width), block)] * 2,
+                whole_spec((rows, width)),
+                whole_spec((rows, width)),
             ]
             + weight_specs(pack, 1) + weight_specs(pack, 2),
             out_specs=[
-                pl.BlockSpec((step, width), lambda i, _: (jnp.maximum(i - 2, 0), 0)),
-                pl.BlockSpec((step, width), lambda i, _: (jnp.minimum(i, 1), 0)),
+                whole_spec((rows, width)),
+                whole_spec((rows, width)),
                 whole_spec(pieces.shape),
                 whole_spec(pieces.shape),
             ],
@@ -1113,7 +1101,7 @@
         compiler_params=pltpu.CompilerParams(vmem_limit_bytes=60 << 20),
         cost_estimate=MEDIUM,
         name="memory_backward_kernel",
-    )(place, grad_key, grad_value, own, far, far, *pack, *pack)
+    )(place, grad_key, grad_value, own, far, *pack, *pack)
 
 
 def self_weight_grads(place, grad_query, grad_key, grad_value, normed, z_count, after):
@@ -1474,7 +1462,7 @@
     line = scatter_to_line(
         ((kv_keep, send_batch(kv_send, 2)), (qo_keep, send_mem(qo_send))), (keep_a,)
     )
-    sums = sum_small(sums, (2, 4, 6), (line[0],))
+    sums = sum_small(sums, (2,), (line[0],))
     (keep_a, send_a), (keep_b, send_b) = scatter_step(
         ((keep_a, send_batch(send_a, 1)), (keep_b, send_batch(send_b, 1))), (sums,), (2, 1)
     )
@@ -1494,7 +1482,7 @@
         square_moves(units, slab, columns, ((0, 1), (0, 2), (0, 0), (1, None), (2, None))),
         (self_line[0],),
     )
-    sums = sum_small(sums, (1,), (cross_grad,)).reshape(-1)
+    sums = sum_small(sums, (1, 4, 5), (cross_grad,)).reshape(-1)
     units = [(0, unit // 3, unit % 3) for unit in range(9)]
     (self_grad,) = scatter_end(
         (send_line(self_line),), (self_weights.shape,),

time: 437 us -> 441 us (level)
  waiting for transfers between devices: 85.6 us -> 91.7 us
    ppermute x28, waiting for transfers between devices: 27.4 us -> 35.2 us  [send_batch(): lax.ppermute(block, 'batch', [(i, i ^ distance) for i in range(count)])]
    ppermute x7, waiting for transfers between devices: 15.1 us -> 9.76 us  [sum_small(): parts.append(lax.ppermute(block, ('batch', 'mem'), pairs))]
  transfers between devices with their start and end apart: 49 -> 49, of which waited for: 18 -> 20; matrix products, arithmetic and copies ran while one was open for 2% -> 2% of each run, Pallas kernels for 51% -> 50%
where the time goes in v5:
time: 441 us; the launch traced here: 436 us
  Pallas kernels  256 us (58%)
  waiting for transfers between devices  91.7 us (21%)
  starting transfers between devices  48.3 us (11%)
  local copies, waits for them, and re-layouts  20.5 us (5%)
  between operations  15 us (3%)
    pallas_call x26, Pallas kernels, kernel_call(): pl.pallas_call(ignoring(body, len(args), len(after)), grid=grid, in_specs...  120 us
    pallas_call x3, Pallas kernels, attention_backward(): pl.pallas_call(ignoring(functools.partial(backward_kernel, causal, step,...  65.4 us
    ppermute x12, waiting for transfers between devices, send_mem(): return lax.ppermute(block, 'mem', [(0, 1), (1, 0)])  46.7 us
    pallas_call x3, Pallas kernels, attention_forward(): pl.pallas_call(ignoring(functools.partial(forward_kernel, causal, step, w...  40.6 us
    ppermute x28, waiting for transfers between devices, send_batch(): lax.ppermute(block, 'batch', [(i, i ^ distance) for i in range(count)])  35.2 us
    ppermute x28, starting transfers between devices, send_batch(): lax.ppermute(block, 'batch', [(i, i ^ distance) for i in range(count)])  27.5 us
    pallas_call x1, Pallas kernels, memory_backward(): pl.pallas_call(body, grid_spec=pltpu.PrefetchScalarGridSpec(num_scalar_pr...  19.9 us
    unnamed x141, local copies, waits for them, and re-layouts  17.4 us
  transfers between devices with their start and end apart: 49, of which 20 were waited for; matrix products, arithmetic and copies ran while one was open for 2% of the time, Pallas kernels for 50%

profile of v5, /device:TPU:0, one launch (start us, length us, event | category | flops | bytes accessed | tf_op | source)
XLA Modules:
  0.0 436.1 jit_solution(10131516431225823789)
XLA Ops:
  7.3 3.0 collective-permute-start
  10.3 2.6 collective-permute-start.2
  12.9 1.6 collective-permute-start.1
  15.3 5.1 %collective-permute-done.2.refs_3_ = bf16[3,48,384]{2,1,0:T(8,128)(2,1)S(1)} collective-permute-done((bf16[3,48,384]{2,1,0:T(8,128)(2,1)}, bf16[3,48,384]{2,1,0:T(8,128)(2,1)S(1)}, u32[]{:S(2)}, u32[]{:S(2)}) %collective-permute-start.2) | collective-permute-done | bytes 110624 | tf_op jit(solution)/shard_map/ppermute | solution.py:422
  22.4 1.9 place_line.2
  24.9 1.5 collective-permute-start.5
  26.4 6.4 %collective-permute-done.4.refs_2_ = bf16[2,3,48,384]{3,2,1,0:T(8,128)(2,1)S(1)} collective-permute-done((bf16[2,3,48,384]{3,2,1,0:T(8,128)(2,1)}, bf16[2,3,48,384]{3,2,1,0:T(8,128)(2,1)S(1)}, u32[]{:S(2)}, u32[]{:S(2)}) %collective-permute-start.4) | collective-permute-done | bytes 221216 | tf_op jit(solution)/shard_map/ppermute | solution.py:426
  34.4 2.2 place_pairs.4
  36.7 1.8 collective-permute-start.6
  38.4 1.5 collective-permute-start.7
  40.6 3.6 collective-permute-start.10
  45.0 5.2 %collective-permute-done.10.refs_4_ = bf16[5,48,384]{2,1,0:T(8,128)(2,1)S(1)} collective-permute-done((bf16[5,48,384]{2,1,0:T(8,128)(2,1)}, bf16[5,48,384]{2,1,0:T(8,128)(2,1)S(1)}, u32[]{:S(2)}, u32[]{:S(2)}) %collective-permute-start.10) | collective-permute-done | bytes 184352 | tf_op jit(solution)/shard_map/ppermute | solution.py:422
  50.2 8.5 %collective-permute-done.9.refs_3_ = bf16[5,48,384]{2,1,0:T(8,128)(2,1)S(1)} collective-permute-done((bf16[5,48,384]{2,1,0:T(8,128)(2,1)}, bf16[5,48,384]{2,1,0:T(8,128)(2,1)S(1)}, u32[]{:S(2)}, u32[]{:S(2)}) %collective-permute-start.9) | collective-permute-done | bytes 184352 | tf_op jit(solution)/shard_map/ppermute | solution.py:422
  60.0 2.2 place_line.3
  63.1 2.8 place_pairs.5
  70.0 8.1 %project_self_kernel.1 = (bf16[512,768]{1,0:T(8,128)(2,1)}, bf16[1024,768]{1,0:T(8,128)(2,1)}, bf16[1024,768]{1,0:T(8,128)(2,1)}, bf16[1024,768]{1,0:T(8,128)(2,1)}) custom-call(s32[4]{0:T(128)} %pad_add_fusion.refs_0_.place_ref, bf16[512,768]{1,0:T(8,128)(2,1)} %bitcast.46, bf16[512,768]{1,0:T(8,128)(2,1)} %copy-done.13, f32[3,768]{1,0:T(4,128)} %refs_4_.3, ...), custom_call_target="tpu_custom_call" | custom-call | flops 6000000000 | bytes 1000 | tf_op jit(solution)/shard_map/project_self_kernel/pallas_call | solution.py:461
  80.5 2.5 place_pairs.6
  87.7 9.0 %self_forward.2 = (bf16[512,384]{1,0:T(8,128)(2,1)}, f32[3,1,1,1024]{3,2,1,0:T(1,128)}, f32[3,4,256,512]{3,2,1,0:T(8,128)}) custom-call(s32[1]{0:T(128)} %bitcast.5.refs_0_, s32[1,4]{1,0:T(1,128)} %refs_2_.13, s32[1,4]{1,0:T(1,128)} %refs_2_.13, bf16[512,768]{1,0:T(8,128)(2,1)} %get-tuple-element.111.refs_5_.refs_3_, ...), custom_call_target="tpu_custom_call" | custom-call | flops 20000000000 | bytes 1000 | tf_op jit(solution)/shard_map/self_forward/pallas_call | solution.py:338
  96.6 9.0 %self_forward.3 = (bf16[512,384]{1,0:T(8,128)(2,1)}, f32[3,1,1,1024]{3,2,1,0:T(1,128)}, f32[3,4,256,512]{3,2,1,0:T(8,128)}) custom-call(s32[1]{0:T(128)} %bitcast.5.refs_0_, s32[1,4]{1,0:T(1,128)} %refs_2_.13, s32[1,4]{1,0:T(1,128)} %refs_2_.13, bf16[512,768]{1,0:T(8,128)(2,1)} %get-tuple-element.111.refs_5_.refs_3_, ...), custom_call_target="tpu_custom_call" | custom-call | flops 20000000000 | bytes 1000 | tf_op jit(solution)/shard_map/self_forward/pallas_call | solution.py:338
  105.7 1.5 collective-permute-done.16.refs_4_
  108.0 3.7 place_pairs.7
  112.2 3.0 collective-permute-done.17.refs_6_.refs_10_.refs_1_.refs_5_.refs_14_
  115.2 2.1 collective-permute-done.18.refs_8_.refs_12_.refs_3_.refs_7_.refs_16_
  118.4 4.9 %after_self.1 = (f32[512,768]{1,0:T(8,128)}, bf16[512,768]{1,0:T(8,128)(2,1)}, bf16[512,768]{1,0:T(8,128)(2,1)}) custom-call(s32[4]{0:T(128)} %pad_add_fusion.refs_0_.place_ref, bf16[512,768]{1,0:T(8,128)(2,1)} %bitcast.47, f32[3,768]{1,0:T(4,128)} %refs_4_.3, bf16[512,384]{1,0:T(8,128)(2,1)} %get-tuple-element.116.refs_7_.refs_3_, ...), custom_call_target="tpu_custom_call" | custom-call | flops 100000 | bytes 1000 | tf_op jit(solution)/shard_map/after_self/pallas_call | solution.py:461
  123.3 28.9 %collective-permute-done.19.far_ref = bf16[1024,768]{1,0:T(8,128)(2,1)} collective-permute-done((bf16[1024,768]{1,0:T(8,128)(2,1)}, bf16[1024,768]{1,0:T(8,128)(2,1)}, u32[]{:S(2)}, u32[]{:S(2)}) %collective-permute-start.19) | collective-permute-done | bytes 1572896 | tf_op jit(solution)/shard_map/ppermute | solution.py:426
  152.2 10.0 %project_memory_kernel.1 = (bf16[2048,768]{1,0:T(8,128)(2,1)}, bf16[2048,768]{1,0:T(8,128)(2,1)}) custom-call(s32[4]{0:T(128)} %pad_add_fusion.refs_0_.place_ref, bf16[1024,768]{1,0:T(8,128)(2,1)} %bitcast.41, bf16[1024,768]{1,0:T(8,128)(2,1)} %collective-permute-done.19.far_ref, ...), custom_call_target="tpu_custom_call" | custom-call | flops 6000000000 | bytes 1000 | tf_op jit(solution)/shard_map/project_memory_kernel/pallas_call | solution.py:845
  162.2 22.6 %cross_forward.1 = (bf16[512,768]{1,0:T(8,128)(2,1)}, f32[6,1,1,1024]{3,2,1,0:T(1,128)}) custom-call(s32[1]{0:T(128)} %bitcast.5.refs_0_, s32[1,4]{1,0:T(1,128)} %refs_2_.13, s32[1,4]{1,0:T(1,128)} %refs_2_.11, bf16[512,768]{1,0:T(8,128)(2,1)} %get-tuple-element.122.refs_3_, bf16[2048,768]{1,0:T(8,128)(2,1)} %get-tuple-element.123.refs_4_, ...), custom_call_target="tpu_custom_call" | custom-call | flops 20000000000 | bytes 1000 | tf_op jit(solution)/shard_map/cross_forward/pallas_call | solution.py:338
  184.8 26.7 %feed_forward_kernel.1 = (bf16[512,768]{1,0:T(8,128)(2,1)}, f32[512,768]{1,0:T(8,128)}, bf16[512,768]{1,0:T(8,128)(2,1)}, f32[1,768]{1,0:T(1,128)}, bf16[16,2,1152,128]{3,2,1,0:T(8,128)(2,1)}) custom-call(s32[4]{0:T(128)} %pad_add_fusion.refs_0_.place_ref, f32[512,768]{1,0:T(8,128)} %get-tuple-element.121.refs_1_, ...), custom_call_target="tpu_custom_call" | custom-call | flops 6000000000 | bytes 1000 | tf_op jit(solution)/shard_map/feed_forward_kernel/pallas_call | solution.py:461
  211.5 38.0 %cross_backward.1 = (bf16[512,768]{1,0:T(8,128)(2,1)}, bf16[2048,768]{1,0:T(8,128)(2,1)}, bf16[2048,768]{1,0:T(8,128)(2,1)}) custom-call(s32[1]{0:T(128)} %bitcast.5.refs_0_, s32[1,4]{1,0:T(1,128)} %refs_2_.13, s32[1,4]{1,0:T(1,128)} %refs_2_.11, bf16[512,768]{1,0:T(8,128)(2,1)} %get-tuple-element.122.refs_3_, bf16[2048,768]{1,0:T(8,128)(2,1)} %get-tuple-element.123.refs_4_, ...), custom_call_target="tpu_custom_call" | custom-call | flops 20000000000 | bytes 1000 | tf_op jit(solution)/shard_map/cross_backward/pallas_call | solution.py:390
  249.5 19.9 %memory_backward_kernel.1 = (f32[1024,768]{1,0:T(8,128)}, bf16[1024,768]{1,0:T(8,128)(2,1)}, bf16[4,2,2,288,128]{4,3,2,1,0:T(8,128)(2,1)}, bf16[4,2,2,288,128]{4,3,2,1,0:T(8,128)(2,1)}) custom-call(s32[4]{0:T(128)} %pad_add_fusion.refs_0_.place_ref, bf16[2048,768]{1,0:T(8,128)(2,1)} %get-tuple-element.133.dk_ref, ...), custom_call_target="tpu_custom_call" | custom-call | flops 6000000000 | bytes 1000 | tf_op jit(solution)/shard_map/memory_backward_kernel/pallas_call | solution.py:1075
  269.5 2.0 collective-permute-start.25
  271.5 10.2 %after_cross_kernel.1 = (f32[512,768]{1,0:T(8,128)}, bf16[512,768]{1,0:T(8,128)(2,1)}, f32[1,768]{1,0:T(1,128)}, bf16[4,2,2,432,128]{4,3,2,1,0:T(8,128)(2,1)}, bf16[4,2,2,432,128]{4,3,2,1,0:T(8,128)(2,1)}) custom-call(s32[4]{0:T(128)} %pad_add_fusion.refs_0_.place_ref, f32[512,768]{1,0:T(8,128)} %get-tuple-element.121.refs_1_, ...), custom_call_target="tpu_custom_call" | custom-call | flops 6000000000 | bytes 1000 | tf_op jit(solution)/shard_map/after_cross_kernel/pallas_call | solution.py:461
  281.9 13.6 %self_backward.2 = (bf16[512,384]{1,0:T(8,128)(2,1)}, bf16[1024,384]{1,0:T(8,128)(2,1)}, bf16[1024,384]{1,0:T(8,128)(2,1)}, f32[3,2,1280]{2,1,0:T(2,128)}) custom-call(s32[1]{0:T(128)} %bitcast.5.refs_0_, s32[1,4]{1,0:T(1,128)} %refs_2_.13, s32[1,4]{1,0:T(1,128)} %refs_2_.13, bf16[512,768]{1,0:T(8,128)(2,1)} %get-tuple-element.111.refs_5_.refs_3_, ...), custom_call_target="tpu_custom_call" | custom-call | flops 20000000000 | bytes 1000 | tf_op jit(solution)/shard_map/self_backward/pallas_call | solution.py:390
  296.7 4.8 %scatter_step.4 = (bf16[4,2,288,128]{3,2,1,0:T(8,128)(2,1)}, bf16[4,2,288,128]{3,2,1,0:T(8,128)(2,1)}, bf16[4,2,432,128]{3,2,1,0:T(8,128)(2,1)}, bf16[4,2,432,128]{3,2,1,0:T(8,128)(2,1)}) custom-call(bf16[4,2,2,288,128]{4,3,2,1,0:T(8,128)(2,1)} %get-tuple-element.143.refs_0_, bf16[4,2,2,288,128]{4,3,2,1,0:T(8,128)(2,1)} %collective-permute-done.20.refs_1_, ...), custom_call_target="tpu_custom_call" | custom-call | flops 100000 | bytes 1000 | tf_op jit(solution)/shard_map/scatter_step/pallas_call | solution.py:461
  303.1 13.8 %self_backward.3 = (bf16[512,384]{1,0:T(8,128)(2,1)}, bf16[1024,384]{1,0:T(8,128)(2,1)}, bf16[1024,384]{1,0:T(8,128)(2,1)}, f32[3,2,1280]{2,1,0:T(2,128)}) custom-call(s32[1]{0:T(128)} %bitcast.5.refs_0_, s32[1,4]{1,0:T(1,128)} %refs_2_.13, s32[1,4]{1,0:T(1,128)} %refs_2_.13, bf16[512,768]{1,0:T(8,128)(2,1)} %get-tuple-element.111.refs_5_.refs_3_, ...), custom_call_target="tpu_custom_call" | custom-call | flops 20000000000 | bytes 1000 | tf_op jit(solution)/shard_map/self_backward/pallas_call | solution.py:390
  317.0 8.1 %self_row_grads_kernel.1 = (f32[512,768]{1,0:T(8,128)}, bf16[512,768]{1,0:T(8,128)(2,1)}, f32[1,768]{1,0:T(1,128)}) custom-call(s32[4]{0:T(128)} %pad_add_fusion.refs_0_.place_ref, bf16[512,768]{1,0:T(8,128)(2,1)} %bitcast.48, bf16[512,768]{1,0:T(8,128)(2,1)} %copy-done.13, bf16[512,384]{1,0:T(8,128)(2,1)} %get-tuple-element.140.refs_4_.refs_10_.refs_3_.refs_1_, ...), custom_call_target="tpu_custom_call" | custom-call | flops 6000000000 | bytes 1000 | tf_op jit(solution)/shard_map/self_row_grads_kernel/pallas_call | solution.py:461
  327.1 5.7 %collective-permute-done.23.refs_1_ = bf16[4,2,288,128]{3,2,1,0:T(8,128)(2,1)S(1)} collective-permute-done((bf16[4,2,288,128]{3,2,1,0:T(8,128)(2,1)}, bf16[4,2,288,128]{3,2,1,0:T(8,128)(2,1)S(1)}, u32[]{:S(2)}, u32[]{:S(2)}) %collective-permute-start.23) | collective-permute-done | bytes 589856 | tf_op jit(solution)/shard_map/ppermute | solution.py:426
  333.9 4.0 scatter_step.5
  337.9 7.8 %self_weight_grads_kernel.1 = (bf16[4,2,2,240,128]{4,3,2,1,0:T(8,128)(2,1)}, bf16[4,2,2,240,128]{4,3,2,1,0:T(8,128)(2,1)}, bf16[4,2,2,192,128]{4,3,2,1,0:T(8,128)(2,1)}, bf16[4,2,2,192,128]{4,3,2,1,0:T(8,128)(2,1)}) custom-call(s32[4]{0:T(128)} %pad_add_fusion.refs_0_.place_ref, bf16[512,384]{1,0:T(8,128)(2,1)} %get-tuple-element.140.refs_4_.refs_10_.refs_3_.refs_1_, ...), custom_call_target="tpu_custom_call" | custom-call | flops 6000000000 | bytes 1000 | tf_op jit(solution)/shard_map/self_weight_grads_kernel/pallas_call | solution.py:461
  349.8 7.7 %collective-permute-done.29.refs_1_ = bf16[4,288,128]{2,1,0:T(8,128)(2,1)S(1)} collective-permute-done((bf16[4,288,128]{2,1,0:T(8,128)(2,1)}, bf16[4,288,128]{2,1,0:T(8,128)(2,1)S(1)}, u32[]{:S(2)}, u32[]{:S(2)}) %collective-permute-start.29) | collective-permute-done | bytes 294944 | tf_op jit(solution)/shard_map/ppermute | solution.py:422
  357.5 3.2 collective-permute-done.30.refs_3_
  361.5 2.2 scatter_to_line.2
  366.9 4.1 scatter_step.6
  371.6 1.5 collective-permute-start.32
  373.1 3.2 collective-permute-start.35
  376.3 2.3 collective-permute-done.35.refs_3_
  378.6 2.3 collective-permute-done.34.refs_2_
  380.9 1.5 collective-permute-done.33.refs_1_
  382.4 1.8 collective-permute-start.40
  384.2 1.4 sum_small.4.refs_2_.refs_0_
  385.5 4.5 %add_rows.1.refs_4_ = f32[1024,768]{1,0:T(8,128)} custom-call(f32[1024,768]{1,0:T(8,128)} %get-tuple-element.177.refs_0_, bf16[1024,768]{1,0:T(8,128)(2,1)} %copy-done.4, f32[21,128]{1,0:T(8,128)} %sum_small.4.refs_2_.refs_0_), custom_call_target="tpu_custom_call" | custom-call | flops 100000 | bytes 1000 | tf_op jit(solution)/shard_map/add_rows/pallas_call | solution.py:461
  390.1 2.0 collective-permute-start.41
  392.8 3.5 scatter_step.7
  396.3 1.5 collective-permute-start.43
  398.4 4.2 finish_rows_kernel.1.refs_4_
  402.6 1.7 collective-permute-done.42.refs_1_
  404.9 2.1 scatter_to_line.3
  407.1 2.4 collective-permute-start.45
  409.5 1.9 collective-permute-start.46
  412.1 1.5 collective-permute-start.37
  413.5 2.6 collective-permute-done.38.refs_3_
  416.7 2.0 scatter_end.3
  425.3 1.8 scatter_end.4
  427.1 1.8 scatter_end.5
  (231 shorter events, 46.8 us)
Async XLA Ops:
  7.2 60.7 %copy-start = (bf16[2,48,1024]{2,1,0:T(8,128)(2,1)S(1)}, bf16[2,48,1024]{2,1,0:T(8,128)(2,1)}, u32[]{:S(2)}) copy-start(bf16[2,48,1024]{2,1,0:T(8,128)(2,1)} %param.25) | copy-start | bytes 589828
  7.2 32.7 %copy-start.49 = (bf16[48,384]{1,0:T(8,128)(2,1)S(1)}, bf16[48,384]{1,0:T(8,128)(2,1)}, u32[]{:S(2)}) copy-start(bf16[48,384]{1,0:T(8,128)(2,1)} %param.24) | copy-start | bytes 110596
  7.2 32.7 %copy-start.39 = (bf16[3,48,384]{2,1,0:T(8,128)(2,1)S(1)}, bf16[3,48,384]{2,1,0:T(8,128)(2,1)}, u32[]{:S(2)}) copy-start(bf16[3,48,384]{2,1,0:T(8,128)(2,1)} %param.23) | copy-start | bytes 331780
  7.2 32.7 %copy-start.50 = (bf16[48,384]{1,0:T(8,128)(2,1)S(1)}, bf16[48,384]{1,0:T(8,128)(2,1)}, u32[]{:S(2)}) copy-start(bf16[48,384]{1,0:T(8,128)(2,1)} %param.22) | copy-start | bytes 110596
  7.2 177.5 %all-gather.3.cloned.1.call-start = ((), (), s32[]{:S(2)}) async-start(), calls=%async_computation.2 | async-start | bytes 9732096 | tf_op jit(solution)/shard_map/all_gather | solution.py:1400
  7.3 25.5 %collective-permute-start = (bf16[512,768]{1,0:T(8,128)(2,1)}, bf16[512,768]{1,0:T(8,128)(2,1)S(1)}, u32[]{:S(2)}, u32[]{:S(2)}) collective-permute-start(bf16[512,768]{1,0:T(8,128)(2,1)} %bitcast.45), channel_id=1, source_target_pairs={{0,1},{1,0},{2,3},{3,2},{4,5},{5,4},{6,7},{7,6},{8,9},{9,8},{10,11... | collective-permute-start | bytes 2359304 | tf_op jit(solution)/shard_map/ppermute | solution.py:426
  10.3 10.2 %collective-permute-start.2 = (bf16[3,48,384]{2,1,0:T(8,128)(2,1)}, bf16[3,48,384]{2,1,0:T(8,128)(2,1)S(1)}, u32[]{:S(2)}, u32[]{:S(2)}) collective-permute-start(bf16[3,48,384]{2,1,0:T(8,128)(2,1)} %refs_1_.7), channel_id=1, source_target_pairs={{0,16},{2,18},{4,20},{6,22},{8,24},{10,26},{12,28},{14,30},{16,0},... | collective-permute-start | bytes 331784 | tf_op jit(solution)/shard_map/ppermute | solution.py:422
  12.9 7.6 %collective-permute-start.1 = (bf16[3,48,384]{2,1,0:T(8,128)(2,1)}, bf16[3,48,384]{2,1,0:T(8,128)(2,1)S(1)}, u32[]{:S(2)}, u32[]{:S(2)}) collective-permute-start(bf16[3,48,384]{2,1,0:T(8,128)(2,1)} %refs_1_.7), channel_id=1, source_target_pairs={{0,8},{2,10},{4,12},{6,14},{8,0},{10,2},{12,4},{14,6},{16,24},{18,... | collective-permute-start | bytes 331784 | tf_op jit(solution)/shard_map/ppermute | solution.py:422
  14.4 7.3 %collective-permute-start.3 = (bf16[3,48,384]{2,1,0:T(8,128)(2,1)}, bf16[3,48,384]{2,1,0:T(8,128)(2,1)S(1)}, u32[]{:S(2)}, u32[]{:S(2)}) collective-permute-start(bf16[3,48,384]{2,1,0:T(8,128)(2,1)} %refs_1_.7), channel_id=1, source_target_pairs={{0,24},{2,26},{4,28},{6,30},{8,16},{10,18},{12,20},{14,22},{16,8},... | collective-permute-start | bytes 331784 | tf_op jit(solution)/shard_map/ppermute | solution.py:422
  24.3 8.4 %collective-permute-start.4 = (bf16[2,3,48,384]{3,2,1,0:T(8,128)(2,1)}, bf16[2,3,48,384]{3,2,1,0:T(8,128)(2,1)S(1)}, u32[]{:S(2)}, u32[]{:S(2)}) collective-permute-start(bf16[2,3,48,384]{3,2,1,0:T(8,128)(2,1)} %get-tuple-element.103.refs_1_), channel_id=1, source_target_pairs={{0,1},{1,0},{2,3},{3,2},{4,5},{5,4},{6,7},{7,6},{8,9},{9,8},{10,11... | collective-permute-start | bytes 663560 | tf_op jit(solution)/shard_map/ppermute | solution.py:426
  24.9 7.9 %collective-permute-start.5 = (bf16[2,3,48,384]{3,2,1,0:T(8,128)(2,1)}, bf16[2,3,48,384]{3,2,1,0:T(8,128)(2,1)S(1)}, u32[]{:S(2)}, u32[]{:S(2)}) collective-permute-start(bf16[2,3,48,384]{3,2,1,0:T(8,128)(2,1)} %get-tuple-element.104.refs_3_.refs_2_), channel_id=1, source_target_pairs={{0,4},{2,6},{4,0},{6,2},{8,12},{10,14},{12,8},{14,10},{16,20},{18,... | collective-permute-start | bytes 663560 | tf_op jit(solution)/shard_map/ppermute | solution.py:422
  36.7 25.6 %collective-permute-start.6 = (bf16[2,2,3,48,384]{4,3,2,1,0:T(8,128)(2,1)}, bf16[2,2,3,48,384]{4,3,2,1,0:T(8,128)(2,1)S(1)}, u32[]{:S(2)}, u32[]{:S(2)}) collective-permute-start(bf16[2,2,3,48,384]{4,3,2,1,0:T(8,128)(2,1)} %get-tuple-element.105.refs_5_.refs_1_), channel_id=1, source_target_pairs={{0,4},{2,6},{4,0},{6,2},{8,12},{10,14},{12,8},{14,10},{16,20},{18,... | collective-permute-start | bytes 1327112 | tf_op jit(solution)/shard_map/ppermute | solution.py:422
  38.4 23.8 %collective-permute-start.7 = (bf16[2,2,3,48,384]{4,3,2,1,0:T(8,128)(2,1)}, bf16[2,2,3,48,384]{4,3,2,1,0:T(8,128)(2,1)S(1)}, u32[]{:S(2)}, u32[]{:S(2)}) collective-permute-start(bf16[2,2,3,48,384]{4,3,2,1,0:T(8,128)(2,1)} %get-tuple-element.106.refs_6_.refs_3_), channel_id=1, source_target_pairs={{0,1},{1,0},{2,3},{3,2},{4,5},{5,4},{6,7},{7,6},{8,9},{9,8},{10,11... | collective-permute-start | bytes 1327112 | tf_op jit(solution)/shard_map/ppermute | solution.py:426
  40.6 9.6 %collective-permute-start.10 = (bf16[5,48,384]{2,1,0:T(8,128)(2,1)}, bf16[5,48,384]{2,1,0:T(8,128)(2,1)S(1)}, u32[]{:S(2)}, u32[]{:S(2)}) collective-permute-start(bf16[5,48,384]{2,1,0:T(8,128)(2,1)} %hold.2.refs_1_), channel_id=1, source_target_pairs={{0,24},{2,26},{4,28},{6,30},{8,16},{10,18},{12,20},{14,22},{16,8},... | collective-permute-start | bytes 552968 | tf_op jit(solution)/shard_map/ppermute | solution.py:422
  44.2 14.4 %collective-permute-start.9 = (bf16[5,48,384]{2,1,0:T(8,128)(2,1)}, bf16[5,48,384]{2,1,0:T(8,128)(2,1)S(1)}, u32[]{:S(2)}, u32[]{:S(2)}) collective-permute-start(bf16[5,48,384]{2,1,0:T(8,128)(2,1)} %hold.2.refs_1_), channel_id=1, source_target_pairs={{0,16},{2,18},{4,20},{6,22},{8,24},{10,26},{12,28},{14,30},{16,0},... | collective-permute-start | bytes 552968 | tf_op jit(solution)/shard_map/ppermute | solution.py:422
  44.2 14.4 %collective-permute-start.8 = (bf16[5,48,384]{2,1,0:T(8,128)(2,1)}, bf16[5,48,384]{2,1,0:T(8,128)(2,1)S(1)}, u32[]{:S(2)}, u32[]{:S(2)}) collective-permute-start(bf16[5,48,384]{2,1,0:T(8,128)(2,1)} %hold.2.refs_1_), channel_id=1, source_target_pairs={{0,8},{2,10},{4,12},{6,14},{8,0},{10,2},{12,4},{14,6},{16,24},{18,... | collective-permute-start | bytes 552968 | tf_op jit(solution)/shard_map/ppermute | solution.py:422
  50.2 8.5 %copy-start.30 = (bf16[5,48,384]{2,1,0:T(8,128)(2,1)}, bf16[5,48,384]{2,1,0:T(8,128)(2,1)S(1)}, u32[]{:S(2)}) copy-start(bf16[5,48,384]{2,1,0:T(8,128)(2,1)S(1)} %collective-permute-done.10.refs_4_) | copy-start | bytes 552964
  65.9 4.1 collective-permute-start.11
  65.9 4.1 collective-permute-start.12
  68.7 10.5 %collective-permute-start.13 = (bf16[2,5,48,384]{3,2,1,0:T(8,128)(2,1)S(1)}, bf16[2,5,48,384]{3,2,1,0:T(8,128)(2,1)S(1)}, u32[]{:S(2)}, u32[]{:S(2)}) collective-permute-start(bf16[2,5,48,384]{3,2,1,0:T(8,128)(2,1)S(1)} %copy-done.9), channel_id=1, source_target_pairs={{0,1},{1,0},{2,3},{3,2},{4,5},{5,4},{6,7},{7,6},{8,9},{9,8},{10,11... | collective-permute-start | bytes 1105928 | tf_op jit(solution)/shard_map/ppermute | solution.py:426
  69.5 10.2 %collective-permute-start.14 = (bf16[2,5,48,384]{3,2,1,0:T(8,128)(2,1)S(1)}, bf16[2,5,48,384]{3,2,1,0:T(8,128)(2,1)S(1)}, u32[]{:S(2)}, u32[]{:S(2)}) collective-permute-start(bf16[2,5,48,384]{3,2,1,0:T(8,128)(2,1)S(1)} %copy-done.10), channel_id=1, source_target_pairs={{0,4},{2,6},{4,0},{6,2},{8,12},{10,14},{12,8},{14,10},{16,20},{18,... | collective-permute-start | bytes 1105928 | tf_op jit(solution)/shard_map/ppermute | solution.py:422
  83.1 343.9 %reduce-scatter.2.cloned.1.call-start = ((), (), s32[]{:S(2)}) async-start(), calls=%async_computation.1 | async-start | bytes 9732096 | tf_op jit(solution)/shard_map/reduce_scatter | solution.py:1419
  84.0 12.7 %copy-start.36 = (pred[1024,32]{1,0:T(32,128)(4,1)}, pred[1024,32]{1,0:T(32,128)(4,1)S(1)}, u32[]{:S(2)}) copy-start(pred[1024,32]{1,0:T(32,128)(4,1)S(1)} %iota_compare_fusion) | copy-start | bytes 98308
  85.1 20.5 %collective-permute-start.15 = (bf16[2,2,5,48,384]{4,3,2,1,0:T(8,128)(2,1)S(1)}, bf16[2,2,5,48,384]{4,3,2,1,0:T(8,128)(2,1)S(1)}, u32[]{:S(2)}, u32[]{:S(2)}) collective-permute-start(bf16[2,2,5,48,384]{4,3,2,1,0:T(8,128)(2,1)S(1)} %copy-done.5), channel_id=1, source_target_pairs={{0,4},{2,6},{4,0},{6,2},{8,12},{10,14},{12,8},{14,10},{16,20},{18,... | collective-permute-start | bytes 2211848 | tf_op jit(solution)/shard_map/ppermute | solution.py:422
  85.6 21.5 %collective-permute-start.16 = (bf16[2,2,5,48,384]{4,3,2,1,0:T(8,128)(2,1)S(1)}, bf16[2,2,5,48,384]{4,3,2,1,0:T(8,128)(2,1)S(1)}, u32[]{:S(2)}, u32[]{:S(2)}) collective-permute-start(bf16[2,2,5,48,384]{4,3,2,1,0:T(8,128)(2,1)S(1)} %copy-done.6), channel_id=1, source_target_pairs={{0,1},{1,0},{2,3},{3,2},{4,5},{5,4},{6,7},{7,6},{8,9},{9,8},{10,11... | collective-permute-start | bytes 2211848 | tf_op jit(solution)/shard_map/ppermute | solution.py:426
  86.8 65.4 %collective-permute-start.19 = (bf16[1024,768]{1,0:T(8,128)(2,1)}, bf16[1024,768]{1,0:T(8,128)(2,1)}, u32[]{:S(2)}, u32[]{:S(2)}) collective-permute-start(bf16[1024,768]{1,0:T(8,128)(2,1)} %get-tuple-element.117.refs_8_), channel_id=1, source_target_pairs={{0,1},{1,0},{2,3},{3,2},{4,5},{5,4},{6,7},{7,6},{8,9},{9,8},{10,11... | collective-permute-start | bytes 4718600 | tf_op jit(solution)/shard_map/ppermute | solution.py:426
  111.7 3.5 collective-permute-start.17
  111.7 5.6 %collective-permute-start.18 = (bf16[2,2,2,5,48,384]{5,4,3,2,1,0:T(8,128)(2,1)}, bf16[2,2,2,5,48,384]{5,4,3,2,1,0:T(8,128)(2,1)S(1)}, u32[]{:S(2)}, u32[]{:S(2)}) collective-permute-start(bf16[2,2,2,5,48,384]{5,4,3,2,1,0:T(8,128)(2,1)} %get-tuple-element.120.refs_7_.refs_11_.refs_2_.refs_6_.refs_15_), channel_id=1, source_target_pairs={{0,2},{2,0},{4,6},{6,4},{8,10},{10,8},{12,14},{14,12},{16,18},{18,... | collective-permute-start | bytes 4423688 | tf_op jit(solution)/shard_map/ppermute | solution.py:422
  269.4 26.1 %collective-permute-start.20 = (bf16[4,2,2,288,128]{4,3,2,1,0:T(8,128)(2,1)}, bf16[4,2,2,288,128]{4,3,2,1,0:T(8,128)(2,1)}, u32[]{:S(2)}, u32[]{:S(2)}) collective-permute-start(bf16[4,2,2,288,128]{4,3,2,1,0:T(8,128)(2,1)} %get-tuple-element.144), channel_id=1, source_target_pairs={{0,2},{2,0},{4,6},{6,4},{8,10},{10,8},{12,14},{14,12},{16,18},{18,... | collective-permute-start | bytes 3538952 | tf_op jit(solution)/shard_map/ppermute | solution.py:422
  269.5 57.6 %collective-permute-start.25 = (bf16[1024,768]{1,0:T(8,128)(2,1)}, bf16[1024,768]{1,0:T(8,128)(2,1)S(1)}, u32[]{:S(2)}, u32[]{:S(2)}) collective-permute-start(bf16[1024,768]{1,0:T(8,128)(2,1)} %get-tuple-element.135.refs_17_), channel_id=1, source_target_pairs={{0,1},{1,0},{2,3},{3,2},{4,5},{5,4},{6,7},{7,6},{8,9},{9,8},{10,11... | collective-permute-start | bytes 4718600 | tf_op jit(solution)/shard_map/ppermute | solution.py:426
  281.8 13.8 %collective-permute-start.21 = (bf16[4,2,2,432,128]{4,3,2,1,0:T(8,128)(2,1)}, bf16[4,2,2,432,128]{4,3,2,1,0:T(8,128)(2,1)S(1)}, u32[]{:S(2)}, u32[]{:S(2)}) collective-permute-start(bf16[4,2,2,432,128]{4,3,2,1,0:T(8,128)(2,1)} %get-tuple-element.145), channel_id=1, source_target_pairs={{0,2},{2,0},{4,6},{6,4},{8,10},{10,8},{12,14},{14,12},{16,18},{18,... | collective-permute-start | bytes 5308424 | tf_op jit(solution)/shard_map/ppermute | solution.py:422
  301.5 31.3 %collective-permute-start.23 = (bf16[4,2,288,128]{3,2,1,0:T(8,128)(2,1)}, bf16[4,2,288,128]{3,2,1,0:T(8,128)(2,1)S(1)}, u32[]{:S(2)}, u32[]{:S(2)}) collective-permute-start(bf16[4,2,288,128]{3,2,1,0:T(8,128)(2,1)} %get-tuple-element.156), channel_id=1, source_target_pairs={{0,1},{1,0},{2,3},{3,2},{4,5},{5,4},{6,7},{7,6},{8,9},{9,8},{10,11... | collective-permute-start | bytes 1769480 | tf_op jit(solution)/shard_map/ppermute | solution.py:426
  301.8 31.0 %collective-permute-start.24 = (bf16[4,2,432,128]{3,2,1,0:T(8,128)(2,1)}, bf16[4,2,432,128]{3,2,1,0:T(8,128)(2,1)S(1)}, u32[]{:S(2)}, u32[]{:S(2)}) collective-permute-start(bf16[4,2,432,128]{3,2,1,0:T(8,128)(2,1)} %get-tuple-element.158), channel_id=1, source_target_pairs={{0,4},{2,6},{4,0},{6,2},{8,12},{10,14},{12,8},{14,10},{16,20},{18,... | collective-permute-start | bytes 2654216 | tf_op jit(solution)/shard_map/ppermute | solution.py:422
  316.9 8.9 %copy-start.51 = (f32[3,2,1280]{2,1,0:T(2,128)S(1)}, f32[3,2,1280]{2,1,0:T(2,128)}, u32[]{:S(2)}) copy-start(f32[3,2,1280]{2,1,0:T(2,128)} %get-tuple-element.163) | copy-start | bytes 92164
  316.9 8.9 %copy-start.52 = (f32[3,2,1280]{2,1,0:T(2,128)S(1)}, f32[3,2,1280]{2,1,0:T(2,128)}, u32[]{:S(2)}) copy-start(f32[3,2,1280]{2,1,0:T(2,128)} %get-tuple-element.164) | copy-start | bytes 92164
  316.9 9.0 %copy-start.37 = (pred[1024,32]{1,0:T(32,128)(4,1)S(1)}, pred[1024,32]{1,0:T(32,128)(4,1)}, u32[]{:S(2)}) copy-start(pred[1024,32]{1,0:T(32,128)(4,1)} %copy-done.36) | copy-start | bytes 98308
  337.9 10.5 %copy-start.63 = (bf16[512,768]{1,0:T(8,128)(2,1)S(1)}, bf16[512,768]{1,0:T(8,128)(2,1)}, u32[]{:S(2)}) copy-start(bf16[512,768]{1,0:T(8,128)(2,1)} %get-tuple-element.153) | copy-start | bytes 2359300
  337.9 19.6 %copy-start.48 = (f32[21,128]{1,0:T(8,128)S(1)}, f32[21,128]{1,0:T(8,128)}, u32[]{:S(2)}) copy-start(f32[21,128]{1,0:T(8,128)} %maximum_bitcast_fusion.refs_9_.refs_0_) | copy-start | bytes 32260
  345.7 19.9 %collective-permute-start.26 = (bf16[4,2,2,240,128]{4,3,2,1,0:T(8,128)(2,1)}, bf16[4,2,2,240,128]{4,3,2,1,0:T(8,128)(2,1)S(1)}, u32[]{:S(2)}, u32[]{:S(2)}) collective-permute-start(bf16[4,2,2,240,128]{4,3,2,1,0:T(8,128)(2,1)} %get-tuple-element.166), channel_id=1, source_target_pairs={{0,2},{2,0},{4,6},{6,4},{8,10},{10,8},{12,14},{14,12},{16,18},{18,... | collective-permute-start | bytes 2949128 | tf_op jit(solution)/shard_map/ppermute | solution.py:422
  345.8 19.9 %collective-permute-start.27 = (bf16[4,2,2,192,128]{4,3,2,1,0:T(8,128)(2,1)}, bf16[4,2,2,192,128]{4,3,2,1,0:T(8,128)(2,1)S(1)}, u32[]{:S(2)}, u32[]{:S(2)}) collective-permute-start(bf16[4,2,2,192,128]{4,3,2,1,0:T(8,128)(2,1)} %get-tuple-element.168), channel_id=1, source_target_pairs={{0,2},{2,0},{4,6},{6,4},{8,10},{10,8},{12,14},{14,12},{16,18},{18,... | collective-permute-start | bytes 2359304 | tf_op jit(solution)/shard_map/ppermute | solution.py:422
  346.2 14.4 %collective-permute-start.30 = (bf16[4,432,128]{2,1,0:T(8,128)(2,1)S(1)}, bf16[4,432,128]{2,1,0:T(8,128)(2,1)S(1)}, u32[]{:S(2)}, u32[]{:S(2)}) collective-permute-start(bf16[4,432,128]{2,1,0:T(8,128)(2,1)S(1)} %copy-done.64), channel_id=1, source_target_pairs={{0,1},{1,0},{2,3},{3,2},{4,5},{5,4},{6,7},{7,6},{8,9},{9,8},{10,11... | collective-permute-start | bytes 1327112 | tf_op jit(solution)/shard_map/ppermute | solution.py:426
  347.2 10.3 %collective-permute-start.29 = (bf16[4,288,128]{2,1,0:T(8,128)(2,1)}, bf16[4,288,128]{2,1,0:T(8,128)(2,1)S(1)}, u32[]{:S(2)}, u32[]{:S(2)}) collective-permute-start(bf16[4,288,128]{2,1,0:T(8,128)(2,1)} %get-tuple-element.169), channel_id=1, source_target_pairs={{0,4},{2,6},{4,0},{6,2},{8,12},{10,14},{12,8},{14,10},{16,20},{18,... | collective-permute-start | bytes 884744 | tf_op jit(solution)/shard_map/ppermute | solution.py:422
  348.4 49.4 %collective-permute-start.22 = (bf16[512,768]{1,0:T(8,128)(2,1)S(1)}, bf16[512,768]{1,0:T(8,128)(2,1)}, u32[]{:S(2)}, u32[]{:S(2)}) collective-permute-start(bf16[512,768]{1,0:T(8,128)(2,1)S(1)} %copy-done.63), channel_id=1, source_target_pairs={{0,1},{1,0},{2,3},{3,2},{4,5},{5,4},{6,7},{7,6},{8,9},{9,8},{10,11... | collective-permute-start | bytes 2359304 | tf_op jit(solution)/shard_map/ppermute | solution.py:426
  357.5 6.3 %collective-permute-start.28 = (f32[21,128]{1,0:T(8,128)S(1)}, f32[21,128]{1,0:T(8,128)S(1)}, u32[]{:S(2)}, u32[]{:S(2)}) collective-permute-start(f32[21,128]{1,0:T(8,128)S(1)} %copy-done.48), channel_id=1, source_target_pairs={{0,2},{1,3},{2,0},{3,1},{4,6},{5,7},{6,4},{7,5},{8,10},{9,11},{10,... | collective-permute-start | bytes 32264 | tf_op jit(solution)/shard_map/ppermute | solution.py:614
  366.9 14.0 %copy-start.67 = (bf16[720,128]{1,0:T(8,128)(2,1)S(1)}, bf16[720,128]{1,0:T(8,128)(2,1)}, u32[]{:S(2)}) copy-start(bf16[720,128]{1,0:T(8,128)(2,1)} %get-tuple-element.179) | copy-start | bytes 552964
  366.9 15.5 %copy-start.66 = (bf16[720,128]{1,0:T(8,128)(2,1)S(1)}, bf16[720,128]{1,0:T(8,128)(2,1)}, u32[]{:S(2)}) copy-start(bf16[720,128]{1,0:T(8,128)(2,1)} %get-tuple-element.180) | copy-start | bytes 552964
  370.9 21.1 %collective-permute-start.31 = (bf16[4,2,240,128]{3,2,1,0:T(8,128)(2,1)}, bf16[4,2,240,128]{3,2,1,0:T(8,128)(2,1)S(1)}, u32[]{:S(2)}, u32[]{:S(2)}) collective-permute-start(bf16[4,2,240,128]{3,2,1,0:T(8,128)(2,1)} %get-tuple-element.174), channel_id=1, source_target_pairs={{0,1},{1,0},{2,3},{3,2},{4,5},{5,4},{6,7},{7,6},{8,9},{9,8},{10,11... | collective-permute-start | bytes 1474568 | tf_op jit(solution)/shard_map/ppermute | solution.py:426
  371.6 18.5 %collective-permute-start.32 = (bf16[4,2,192,128]{3,2,1,0:T(8,128)(2,1)}, bf16[4,2,192,128]{3,2,1,0:T(8,128)(2,1)S(1)}, u32[]{:S(2)}, u32[]{:S(2)}) collective-permute-start(bf16[4,2,192,128]{3,2,1,0:T(8,128)(2,1)} %get-tuple-element.176), channel_id=1, source_target_pairs={{0,4},{2,6},{4,0},{6,2},{8,12},{10,14},{12,8},{14,10},{16,20},{18,... | collective-permute-start | bytes 1179656 | tf_op jit(solution)/shard_map/ppermute | solution.py:422
  373.1 5.5 %collective-permute-start.35 = (f32[21,128]{1,0:T(8,128)S(1)}, f32[21,128]{1,0:T(8,128)S(1)}, u32[]{:S(2)}, u32[]{:S(2)}) collective-permute-start(f32[21,128]{1,0:T(8,128)S(1)} %copy-done.46), channel_id=1, source_target_pairs={{0,24},{1,25},{2,26},{3,27},{4,28},{5,29},{6,30},{7,31},{8,16},{9,... | collective-permute-start | bytes 32264 | tf_op jit(solution)/shard_map/ppermute | solution.py:614
  376.3 4.6 %collective-permute-start.34 = (f32[21,128]{1,0:T(8,128)S(1)}, f32[21,128]{1,0:T(8,128)S(1)}, u32[]{:S(2)}, u32[]{:S(2)}) collective-permute-start(f32[21,128]{1,0:T(8,128)S(1)} %copy-done.46), channel_id=1, source_target_pairs={{0,16},{1,17},{2,18},{3,19},{4,20},{5,21},{6,22},{7,23},{8,24},{9,... | collective-permute-start | bytes 32264 | tf_op jit(solution)/shard_map/ppermute | solution.py:614
  378.6 3.8 collective-permute-start.33
  380.9 28.6 %collective-permute-start.39 = (bf16[720,128]{1,0:T(8,128)(2,1)S(1)}, bf16[720,128]{1,0:T(8,128)(2,1)S(1)}, u32[]{:S(2)}, u32[]{:S(2)}) collective-permute-start(bf16[720,128]{1,0:T(8,128)(2,1)S(1)} %copy-done.67), channel_id=1, source_target_pairs={{0,8},{2,10},{4,12},{6,14},{8,0},{10,2},{12,4},{14,6},{16,24},{18,... | collective-permute-start | bytes 552968 | tf_op jit(solution)/shard_map/ppermute | solution.py:422
  382.4 29.1 %collective-permute-start.40 = (bf16[720,128]{1,0:T(8,128)(2,1)S(1)}, bf16[720,128]{1,0:T(8,128)(2,1)S(1)}, u32[]{:S(2)}, u32[]{:S(2)}) collective-permute-start(bf16[720,128]{1,0:T(8,128)(2,1)S(1)} %copy-done.66), channel_id=1, source_target_pairs={{0,16},{2,18},{4,20},{6,22},{8,24},{10,26},{12,28},{14,30},{16,0},... | collective-permute-start | bytes 552968 | tf_op jit(solution)/shard_map/ppermute | solution.py:422
  390.1 22.0 %collective-permute-start.41 = (bf16[720,128]{1,0:T(8,128)(2,1)S(1)}, bf16[720,128]{1,0:T(8,128)(2,1)S(1)}, u32[]{:S(2)}, u32[]{:S(2)}) collective-permute-start(bf16[720,128]{1,0:T(8,128)(2,1)S(1)} %copy-done.65), channel_id=1, source_target_pairs={{0,24},{2,26},{4,28},{6,30},{8,16},{10,18},{12,20},{14,22},{16,8},... | collective-permute-start | bytes 552968 | tf_op jit(solution)/shard_map/ppermute | solution.py:422
  396.3 6.2 %collective-permute-start.43 = (bf16[4,192,128]{2,1,0:T(8,128)(2,1)}, bf16[4,192,128]{2,1,0:T(8,128)(2,1)S(1)}, u32[]{:S(2)}, u32[]{:S(2)}) collective-permute-start(bf16[4,192,128]{2,1,0:T(8,128)(2,1)} %get-tuple-element.184), channel_id=1, source_target_pairs={{0,1},{1,0},{2,3},{3,2},{4,5},{5,4},{6,7},{7,6},{8,9},{9,8},{10,11... | collective-permute-start | bytes 589832 | tf_op jit(solution)/shard_map/ppermute | solution.py:426
  397.8 6.4 %collective-permute-start.42 = (bf16[4,240,128]{2,1,0:T(8,128)(2,1)}, bf16[4,240,128]{2,1,0:T(8,128)(2,1)S(1)}, u32[]{:S(2)}, u32[]{:S(2)}) collective-permute-start(bf16[4,240,128]{2,1,0:T(8,128)(2,1)} %get-tuple-element.182), channel_id=1, source_target_pairs={{0,4},{2,6},{4,0},{6,2},{8,12},{10,14},{12,8},{14,10},{16,20},{18,... | collective-permute-start | bytes 737288 | tf_op jit(solution)/shard_map/ppermute | solution.py:422
  402.6 8.9 %copy-start.38 = (f32[21,128]{1,0:T(8,128)S(1)}, f32[21,128]{1,0:T(8,128)}, u32[]{:S(2)}) copy-start(f32[21,128]{1,0:T(8,128)} %sum_small.4.refs_2_.refs_0_) | copy-start | bytes 32260
  404.9 23.9 %copy-start.1 = (bf16[2,48,1024]{2,1,0:T(8,128)(2,1)S(1)}, bf16[2,48,1024]{2,1,0:T(8,128)(2,1)}, u32[]{:S(2)}) copy-start(bf16[2,48,1024]{2,1,0:T(8,128)(2,1)} %param.25) | copy-start | bytes 589828
  407.1 17.5 %collective-permute-start.44 = (bf16[432,128]{1,0:T(8,128)(2,1)}, bf16[432,128]{1,0:T(8,128)(2,1)S(1)}, u32[]{:S(2)}, u32[]{:S(2)}) collective-permute-start(bf16[432,128]{1,0:T(8,128)(2,1)} %get-tuple-element.187), channel_id=1, source_target_pairs={{0,8},{2,10},{4,12},{6,14},{8,0},{10,2},{12,4},{14,6},{16,24},{18,... | collective-permute-start | bytes 331784 | tf_op jit(solution)/shard_map/ppermute | solution.py:422
  407.1 17.5 %collective-permute-start.45 = (bf16[432,128]{1,0:T(8,128)(2,1)}, bf16[432,128]{1,0:T(8,128)(2,1)S(1)}, u32[]{:S(2)}, u32[]{:S(2)}) collective-permute-start(bf16[432,128]{1,0:T(8,128)(2,1)} %get-tuple-element.188), channel_id=1, source_target_pairs={{0,16},{2,18},{4,20},{6,22},{8,24},{10,26},{12,28},{14,30},{16,0},... | collective-permute-start | bytes 331784 | tf_op jit(solution)/shard_map/ppermute | solution.py:422
  409.5 15.0 %collective-permute-start.46 = (bf16[432,128]{1,0:T(8,128)(2,1)}, bf16[432,128]{1,0:T(8,128)(2,1)S(1)}, u32[]{:S(2)}, u32[]{:S(2)}) collective-permute-start(bf16[432,128]{1,0:T(8,128)(2,1)} %get-tuple-element.189), channel_id=1, source_target_pairs={{0,24},{2,26},{4,28},{6,30},{8,16},{10,18},{12,20},{14,22},{16,8},... | collective-permute-start | bytes 331784 | tf_op jit(solution)/shard_map/ppermute | solution.py:422
  411.5 4.7 %collective-permute-start.38 = (f32[21,128]{1,0:T(8,128)S(1)}, f32[21,128]{1,0:T(8,128)S(1)}, u32[]{:S(2)}, u32[]{:S(2)}) collective-permute-start(f32[21,128]{1,0:T(8,128)S(1)} %copy-done.38), channel_id=1, source_target_pairs={{0,5},{1,4},{2,7},{3,6},{4,1},{5,0},{6,3},{7,2},{8,13},{9,12},{10,... | collective-permute-start | bytes 32264 | tf_op jit(solution)/shard_map/ppermute | solution.py:614
  412.1 6.6 %collective-permute-start.37 = (f32[21,128]{1,0:T(8,128)S(1)}, f32[21,128]{1,0:T(8,128)S(1)}, u32[]{:S(2)}, u32[]{:S(2)}) collective-permute-start(f32[21,128]{1,0:T(8,128)S(1)} %copy-done.38), channel_id=1, source_target_pairs={{0,4},{1,5},{2,6},{3,7},{4,0},{5,1},{6,2},{7,3},{8,12},{9,13},{10,... | collective-permute-start | bytes 32264 | tf_op jit(solution)/shard_map/ppermute | solution.py:614
  416.1 3.7 collective-permute-start.36
  (54 other events, 126.5 us)
Sparse Core Ops, SparseCore 0:
  83.2 92.2 all-gather.2
  211.6 150.9 reduce-scatter.1
